TPU v7x, 32 devices: a whole 2x2x4 slice. The times are simulated.
32 devices in a mesh: azim: 4 (over z), beam: 2 (over y), sweep: 4 (over x, core).
Axes of the slice: x: 2, y: 2, z: 4, core: 2. Of those that a mesh axis runs over, the one named last changes fastest.
Arguments:
- features: bfloat16 [256, 4, 4, 256], P('azim', 'sweep', 'beam'), may hold values from -16 to 16
- cotangent: bfloat16 [256, 4, 4, 256], P('azim', 'sweep', 'beam'), may hold values from -6 to 6
- w_query: bfloat16 [256, 256], replicated
- w_key: bfloat16 [256, 256], replicated
- w_value: bfloat16 [256, 256], replicated, may hold values from -0.375 to 0.375
- w_out: bfloat16 [256, 256], replicated, may hold values from -0.375 to 0.375
- w_conv: bfloat16 [256, 27, 256], replicated, may hold values from -0.078125 to 0.078125
- sector_mask: int32 [4, 4], replicated, may hold values from 0 to 1, as said below
Outputs:
- features_grad: bfloat16 [256, 4, 4, 256], P('azim', 'sweep', 'beam')
- weight_grads: float32 [256, 31, 256], P('azim', None, ('beam', 'sweep'))
Inputs may be any that keep to these rules, and one draw needn't show every extreme that they name: `sector_mask`: entry [i, j] is 1 where query sector i may attend to key sector j, else 0; every diagonal entry is 1.
All inputs are finite; a program needn't handle non-finite values.
Results may differ from a plain program's by a relative error of at most 0.012.
The roundings to bfloat16 on the way count: a program that leaves them out, or rounds other values in their place, can miss the bound.
Values may be sent and summed in bfloat16 or wider, within the bound.
No kernel may reach another device: no remote copies, remote signals or barrier semaphores. Data moves between devices by JAX's collectives and lax.ppermute only.
A program may use at most 128 MiB of HBM per device.

v0:
```python
import jax
import jax.numpy as jnp
from jax import lax
from jax.sharding import PartitionSpec as P

HEADS = 8
SECTOR = 64
TAPS = 27


highest = lax.Precision.HIGHEST
masked_score = -1e30


def padded_2(block, sides, width):
    for axis, dim in sides:
        count = lax.axis_size(axis)
        forward = [(i, i + 1) for i in range(count - 1)]
        forward.append((count - 1, 0))
        backward = [(target, source) for source, target in forward]
        low = lax.ppermute(
            lax.slice_in_dim(block, block.shape[dim] - width, None, axis=dim), axis, forward
        )
        high = lax.ppermute(lax.slice_in_dim(block, 0, width, axis=dim), axis, backward)
        block = jnp.concatenate([low, block, high], axis=dim)
    return block


def sector_onehot(first_row, row_total, sectors):
    sector_of = (first_row + jnp.arange(row_total, dtype=jnp.int32)) // SECTOR
    return (sector_of[:, None] == jnp.arange(sectors, dtype=jnp.int32)[None, :]).astype(jnp.float32)


def allowed_table(sector_mask, query_first, query_total, key_first, key_total):
    sectors = sector_mask.shape[0]
    query_hot = sector_onehot(query_first, query_total, sectors)
    key_hot = sector_onehot(key_first, key_total, sectors)
    lookup = jnp.dot(jnp.dot(query_hot, sector_mask.astype(jnp.float32)), key_hot.T)
    return lookup > 0.5


def split_heads(tensor):
    return tensor.reshape(tensor.shape[:3] + (HEADS, tensor.shape[3] // HEADS))


def project(flat_rows, weight):
    return jnp.dot(flat_rows, weight, preferred_element_type=jnp.float32).astype(jnp.bfloat16)


def scores_of(queries, key_rows, allowed):
    score_scale = (queries.shape[3] // HEADS) ** (-0.5)
    raw_scores = jnp.einsum(
        "asbhe,ksbhe->sbhak",
        split_heads(queries),
        split_heads(key_rows),
        preferred_element_type=jnp.float32,
    )
    return jnp.where(allowed, raw_scores * score_scale, masked_score)


def key_side(queries, grad_attended, logsum, row_delta, key_rows, value_rows, allowed):
    score_scale = (queries.shape[3] // HEADS) ** (-0.5)
    scores = scores_of(queries, key_rows, allowed)
    weights_full = jnp.where(allowed, jnp.exp(scores - logsum[..., None]), 0.0)
    grad_prob = jnp.einsum(
        "asbhe,ksbhe->sbhak",
        split_heads(grad_attended),
        split_heads(value_rows),
        preferred_element_type=jnp.float32,
    )
    grad_score = (weights_full * (grad_prob - row_delta[..., None])).astype(jnp.bfloat16)
    grad_key = (
        jnp.einsum(
            "sbhak,asbhe->ksbhe",
            grad_score,
            split_heads(queries),
            preferred_element_type=jnp.float32,
        )
        * score_scale
    )
    grad_value = jnp.einsum(
        "sbhak,asbhe->ksbhe",
        weights_full.astype(jnp.bfloat16),
        split_heads(grad_attended),
        preferred_element_type=jnp.float32,
    )
    return (grad_key.reshape(key_rows.shape), grad_value.reshape(key_rows.shape))


def edge_factors(position, devices, length):
    lower_keep = jnp.where(position > 0, 1.0, 0.0).astype(jnp.bfloat16)
    upper_keep = jnp.where(position < devices - 1, 1.0, 0.0).astype(jnp.bfloat16)
    middle = jnp.ones((length,), jnp.bfloat16)
    return jnp.concatenate([lower_keep[None], middle, upper_keep[None]])


def gather_taps(padded, col_count, sweeps, beam_rows, direction):
    pieces = []
    for offset_one in (-1, 0, 1):
        for offset_two in (-1, 0, 1):
            for offset_three in (-1, 0, 1):
                first_at = 1 + direction * offset_one
                second_at = 1 + direction * offset_two
                third_at = 1 + direction * offset_three
                pieces.append(
                    padded[
                        first_at : first_at + col_count,
                        second_at : second_at + sweeps,
                        third_at : third_at + beam_rows,
                    ]
                )
    return jnp.stack(pieces, axis=3)


def per_device(features, cotangent, w_query, w_key, w_value, w_out, w_conv, sector_mask):
    col_count, sweeps, beam_rows, channels = features.shape
    row_count = col_count * sweeps * beam_rows
    flat_in = features.reshape(row_count, channels)
    keep_edges = (
        edge_factors(lax.axis_index("sweep"), lax.axis_size("sweep"), sweeps)[:, None, None]
        * edge_factors(lax.axis_index("beam"), lax.axis_size("beam"), beam_rows)[None, :, None]
    )
    queries = project(flat_in, w_query).reshape(features.shape)
    key_proj = project(flat_in, w_key).reshape(features.shape)
    values = project(flat_in, w_value).reshape(features.shape)
    col_first = lax.axis_index("azim") * col_count
    key_all, value_all = (
        lax.all_gather(key_proj, "azim", axis=0, tiled=True),
        lax.all_gather(values, "azim", axis=0, tiled=True),
    )
    allowed_all = allowed_table(sector_mask, col_first, col_count, 0, key_all.shape[0])
    scores = scores_of(queries, key_all, allowed_all)
    peak_score = jnp.max(scores, axis=-1)
    logsum = peak_score + jnp.log(jnp.sum(jnp.exp(scores - peak_score[..., None]), axis=-1))
    weights_full = jnp.where(allowed_all, jnp.exp(scores - logsum[..., None]), 0.0)
    attended = jnp.einsum(
        "sbhak,ksbhe->asbhe",
        weights_full.astype(jnp.bfloat16),
        split_heads(value_all),
        preferred_element_type=jnp.float32,
    )
    attended = attended.reshape(features.shape).astype(jnp.bfloat16)
    attended_flat = attended.reshape(row_count, channels)
    mixed_out = flat_in.astype(jnp.float32) + jnp.dot(
        attended_flat, w_out, preferred_element_type=jnp.float32
    )
    layer_out = mixed_out.reshape(features.shape).astype(jnp.bfloat16)
    both_pad = (
        padded_2(jnp.stack([layer_out, cotangent]), (("azim", 1), ("beam", 3), ("sweep", 2)), 1)
        * keep_edges
    )
    layer_pad = both_pad[0]
    cot_pad = both_pad[1]
    cot_flat = cotangent.reshape(row_count, channels)
    cot_taps = gather_taps(cot_pad, col_count, sweeps, beam_rows, -1).reshape(
        row_count, TAPS, channels
    )
    grad_layer = cot_flat.astype(jnp.float32) + jnp.einsum(
        "nto,ito->ni", cot_taps, w_conv, preferred_element_type=jnp.float32
    )
    layer_taps = gather_taps(layer_pad, col_count, sweeps, beam_rows, 1).reshape(
        row_count, TAPS, channels
    )
    grad_layer_bf = grad_layer.astype(jnp.bfloat16)
    grad_attended = (
        jnp.dot(grad_layer_bf, w_out.T, preferred_element_type=jnp.float32)
        .astype(jnp.bfloat16)
        .reshape(features.shape)
    )
    row_delta = jnp.einsum(
        "asbhe,asbhe->sbha",
        split_heads(grad_attended),
        split_heads(attended),
        preferred_element_type=jnp.float32,
    )
    grad_prob = jnp.einsum(
        "asbhe,ksbhe->sbhak",
        split_heads(grad_attended),
        split_heads(value_all),
        preferred_element_type=jnp.float32,
    )
    grad_score = (weights_full * (grad_prob - row_delta[..., None])).astype(jnp.bfloat16)
    score_scale = (channels // HEADS) ** (-0.5)
    grad_query = (
        jnp.einsum(
            "sbhak,ksbhe->asbhe",
            grad_score,
            split_heads(key_all),
            preferred_element_type=jnp.float32,
        )
        * score_scale
    )
    grad_query = grad_query.reshape(row_count, channels)
    allowed = allowed_table(
        sector_mask, col_first, col_count, jnp.int32(0), lax.axis_size("azim") * col_count
    )
    grad_key_part, grad_value_part = key_side(
        queries, grad_attended, logsum, row_delta, key_all, value_all, allowed
    )
    key_grads = lax.psum_scatter(
        jnp.concatenate([grad_key_part, grad_value_part], axis=3),
        "azim",
        scatter_dimension=0,
        tiled=True,
    )
    grad_key = key_grads[..., :channels]
    grad_value = key_grads[..., channels:]
    grad_key_flat = grad_key.reshape(row_count, channels)
    grad_value_flat = grad_value.reshape(row_count, channels)
    grad_in = grad_layer + jnp.dot(grad_query, w_query.astype(jnp.float32).T, precision=highest)
    grad_in = grad_in + jnp.dot(grad_key_flat, w_key.astype(jnp.float32).T, precision=highest)
    grad_in = grad_in + jnp.dot(grad_value_flat, w_value.astype(jnp.float32).T, precision=highest)
    features_grad = grad_in.astype(jnp.bfloat16).reshape(features.shape)
    flat_wide = flat_in.astype(jnp.float32)
    projection_terms = jnp.stack(
        [
            jnp.einsum("ni,no->io", flat_wide, grad_query, precision=highest),
            jnp.einsum("ni,no->io", flat_wide, grad_key_flat, precision=highest),
            jnp.einsum("ni,no->io", flat_wide, grad_value_flat, precision=highest),
            jnp.einsum(
                "ni,no->io", attended_flat, grad_layer_bf, preferred_element_type=jnp.float32
            ),
        ],
        axis=1,
    )
    conv_terms = jnp.einsum("nti,no->ito", layer_taps, cot_flat, preferred_element_type=jnp.float32)
    weight_rows = lax.psum_scatter(
        jnp.concatenate([projection_terms, conv_terms], axis=1),
        "azim",
        scatter_dimension=0,
        tiled=True,
    )
    weight_grads = lax.psum_scatter(weight_rows, ("beam", "sweep"), scatter_dimension=2, tiled=True)
    return (features_grad, weight_grads)


def solution(mesh):
    in_specs = (
        P("azim", "sweep", "beam", None),
        P("azim", "sweep", "beam", None),
        P(),
        P(),
        P(),
        P(),
        P(),
        P(),
    )
    out_specs = (P("azim", "sweep", "beam", None), P("azim", None, ("beam", "sweep")))
    return jax.shard_map(
        per_device, mesh=mesh, in_specs=in_specs, out_specs=out_specs, check_vma=False
    )
```

profile of v0, /device:TPU:0, one launch (start us, length us, event | category | flops | bytes accessed | tf_op | source)
XLA Modules:
  0.0 498.9 jit_solution(9875512611837250144)
XLA Ops:
  7.8 1.8 copy.172
  11.1 1.7 convolution_convert_fusion.4
  14.3 17.5 %all_gather.6 = bf16[256,1,2,256]{3,2,1,0:T(2,128)(2,1)} all-gather(bf16[64,1,2,256]{3,2,1,0:T(2,128)(2,1)} %bitcast.301), channel_id=1, replica_groups=mesh['azim'=4,'beam'=2,'sweep'=4] {'azim'}, dimensions={0}, use_global_device_ids=true | all-gather | bytes 327680 | tf_op jit(solution)/shard_map/all_gather | solution.py:129
  31.8 1.8 copy.105
  33.6 1.7 convolution_convert_fusion.3
  35.3 1.7 reshape.293
  37.1 1.8 copy.108
  38.9 1.7 convolution_convert_fusion.2
  42.2 15.0 %all_gather.7 = bf16[256,1,2,256]{3,2,1,0:T(2,128)(2,1)} all-gather(bf16[64,1,2,256]{3,2,1,0:T(2,128)(2,1)} %bitcast.302), channel_id=1, replica_groups=mesh['azim'=4,'beam'=2,'sweep'=4] {'azim'}, dimensions={0}, use_global_device_ids=true | all-gather | bytes 327680 | tf_op jit(solution)/shard_map/all_gather | solution.py:128
  57.1 1.8 copy.107
  64.1 1.8 copy.109
  65.9 1.8 convert_element_type.105
  67.7 1.7 fusion.8
  73.8 2.3 collective-permute-start.1
  77.7 4.1 collective-permute-done
  85.5 1.7 collective-permute-done.3
  88.7 1.7 pad_maximum_fusion.1
  93.7 3.5 collective-permute-done.5
  97.2 2.8 collective-permute-done.4
  215.3 2.8 fusion.6
  219.5 1.8 reshape.296
  221.3 1.9 copy.139
  223.2 1.8 bitcast_convert_fusion
  224.9 2.0 copy.161
  228.1 2.4 fusion.17
  233.0 2.0 copy.140
  235.0 1.9 reshape.298
  236.9 2.0 copy.144
  239.0 2.0 copy.143
  241.0 2.3 pad_maximum_fusion
  243.5 1.9 convolution_bitcast_fusion.3
  245.5 1.8 copy.150
  277.3 1.9 convolution_bitcast_fusion.2
  279.3 1.8 copy.151
  281.1 1.9 convolution_bitcast_fusion.1
  283.0 1.8 copy.152
  284.8 1.7 constant_dynamic-update-slice_fusion.55
  286.5 1.7 constant_dynamic-update-slice_fusion.54
  288.1 1.9 fusion.5
  290.0 5.4 %bitcast_dynamic-update-slice_fusion = f32[256,31,256]{2,0,1:T(8,128)} fusion(f32[256,31,256]{2,0,1:T(8,128)} %fusion.5, bf16[64,1,2,27,256]{4,0,2,3,1:T(8,128)(2,1)} %constant_dynamic-update-slice_fusion.27, bf16[64,2,256]{2,1,0:T(2,128)(2,1)} %bitcast.298), kind=kOutput, calls=%fused_computation | convolution fusion | flops 452984832 | bytes 8912896 | tf_op jit(solution)/shard_map/nti,no->ito/dot_general | solution.py:226
  295.5 137.0 %reduce-scatter.6.cloned.1.call-done = f32[64,31,256]{2,0,1:T(8,128)} async-done(((f32[256,31,256]{2,0,1:T(8,128)}), f32[64,31,256]{2,0,1:T(8,128)}) %reduce-scatter.6.cloned.1.call-update) | async-done | bytes 2031632 | tf_op jit(solution)/shard_map/reduce_scatter | solution.py:227
  432.5 5.5 %copy.153 = f32[64,31,256]{0,1,2:T(8,128)} copy(f32[64,31,256]{2,0,1:T(8,128)} %reduce-scatter.6.cloned.1.call-done) | data formatting | bytes 4063232 | tf_op jit(solution)/shard_map/reduce_scatter | solution.py:227
  438.1 2.0 convolution_add_fusion.3
  444.1 1.7 copy.146
  445.8 1.7 reshape.302
  448.8 1.9 fusion.7
  452.3 37.9 %reduce-scatter.8.cloned.1.call-done = f32[64,31,32]{0,1,2:T(8,128)} async-done(((f32[64,31,256]{0,1,2:T(8,128)}), f32[64,31,32]{0,1,2:T(8,128)}) %reduce-scatter.8.cloned.1.call-update) | async-done | bytes 253968 | tf_op jit(solution)/shard_map/reduce_scatter | solution.py:233
  490.2 2.1 copy.155
  (217 shorter events, 182.2 us)
Async XLA Ops:
  7.2 208.1 %copy-start = (bf16[256,27,256]{2,0,1:T(8,128)(2,1)S(1)}, bf16[256,27,256]{2,0,1:T(8,128)(2,1)}, u32[]{:S(2)}) copy-start(bf16[256,27,256]{2,0,1:T(8,128)(2,1)} %param.14) | copy-start | bytes 10616836
  7.2 270.2 %reduce-scatter.4.cloned.1.call-start = ((), (), s32[]{:S(2)}) async-start(), calls=%async_computation.3 | async-start | bytes 1310720 | tf_op jit(solution)/shard_map/reduce_scatter | solution.py:200
  60.6 2.5 copy-start.4
  62.1 1.0 copy-start.1
  62.5 1.6 copy-start.28
  71.8 0.6 copy-start.8
  73.8 3.9 collective-permute-start.1
  76.1 5.7 %collective-permute-start = (bf16[2,1,1,2,256]{4,1,3,2,0:T(2,128)(2,1)}, bf16[2,1,1,2,256]{4,1,3,2,0:T(2,128)(2,1)}, u32[]{:S(2)}, u32[]{:S(2)}) collective-permute-start(bf16[2,1,1,2,256]{4,1,3,2,0:T(2,128)(2,1)} %get-tuple-element.41), channel_id=1, source_target_pairs={{0,8},{8,16},{16,24},{24,0},{1,9},{9,17},{17,25},{25,1},{2,10},{10... | collective-permute-start | bytes 6152 | tf_op jit(solution)/shard_map/ppermute | solution.py:21
  82.8 4.4 collective-permute-start.3
  84.3 4.4 collective-permute-start.2
  87.2 1.5 copy-start.14
  88.7 1.7 copy-start.15
  90.4 6.8 %collective-permute-start.5 = (bf16[2,66,1,4,256]{4,1,3,2,0:T(8,128)(2,1)}, bf16[2,66,1,4,256]{4,1,3,2,0:T(8,128)(2,1)}, u32[]{:S(2)}, u32[]{:S(2)}) collective-permute-start(bf16[2,66,1,4,256]{4,1,3,2,0:T(8,128)(2,1)} %pad_maximum_fusion.1), channel_id=1, source_target_pairs={{1,0},{2,1},{3,2},{0,3},{5,4},{6,5},{7,6},{4,7},{9,8},{10,9},{11,1... | collective-permute-start | bytes 811016 | tf_op jit(solution)/shard_map/ppermute | solution.py:24
  90.4 9.6 %collective-permute-start.4 = (bf16[2,66,1,4,256]{4,1,3,2,0:T(8,128)(2,1)}, bf16[2,66,1,4,256]{4,1,3,2,0:T(8,128)(2,1)}, u32[]{:S(2)}, u32[]{:S(2)}) collective-permute-start(bf16[2,66,1,4,256]{4,1,3,2,0:T(8,128)(2,1)} %pad_maximum_fusion.1), channel_id=1, source_target_pairs={{0,1},{1,2},{2,3},{3,0},{4,5},{5,6},{6,7},{7,4},{8,9},{9,10},{10,1... | collective-permute-start | bytes 811016 | tf_op jit(solution)/shard_map/ppermute | solution.py:21
  186.8 20.8 %copy-start.16 = (bf16[128,1,256]{2,0,1:T(8,128)(2,1)S(1)}, bf16[128,1,256]{2,0,1:T(8,128)(2,1)}, u32[]{:S(2)}) copy-start(bf16[128,1,256]{2,0,1:T(8,128)(2,1)} %stack.204) | copy-start | bytes 196612
  186.9 21.4 %copy-start.17 = (bf16[128,1,256]{2,0,1:T(8,128)(2,1)S(1)}, bf16[128,1,256]{2,0,1:T(8,128)(2,1)}, u32[]{:S(2)}) copy-start(bf16[128,1,256]{2,0,1:T(8,128)(2,1)} %stack.205) | copy-start | bytes 196612
  186.9 22.1 %copy-start.18 = (bf16[128,1,256]{2,0,1:T(8,128)(2,1)S(1)}, bf16[128,1,256]{2,0,1:T(8,128)(2,1)}, u32[]{:S(2)}) copy-start(bf16[128,1,256]{2,0,1:T(8,128)(2,1)} %stack.206) | copy-start | bytes 196612
  186.9 22.7 %copy-start.19 = (bf16[128,1,256]{2,0,1:T(8,128)(2,1)S(1)}, bf16[128,1,256]{2,0,1:T(8,128)(2,1)}, u32[]{:S(2)}) copy-start(bf16[128,1,256]{2,0,1:T(8,128)(2,1)} %stack.207) | copy-start | bytes 196612
  186.9 23.3 %copy-start.20 = (bf16[128,1,256]{2,0,1:T(8,128)(2,1)S(1)}, bf16[128,1,256]{2,0,1:T(8,128)(2,1)}, u32[]{:S(2)}) copy-start(bf16[128,1,256]{2,0,1:T(8,128)(2,1)} %stack.208) | copy-start | bytes 196612
  186.9 23.9 %copy-start.21 = (bf16[128,1,256]{2,0,1:T(8,128)(2,1)S(1)}, bf16[128,1,256]{2,0,1:T(8,128)(2,1)}, u32[]{:S(2)}) copy-start(bf16[128,1,256]{2,0,1:T(8,128)(2,1)} %stack.209) | copy-start | bytes 196612
  186.9 24.6 %copy-start.22 = (bf16[128,1,256]{2,0,1:T(8,128)(2,1)S(1)}, bf16[128,1,256]{2,0,1:T(8,128)(2,1)}, u32[]{:S(2)}) copy-start(bf16[128,1,256]{2,0,1:T(8,128)(2,1)} %stack.210) | copy-start | bytes 196612
  186.9 25.2 %copy-start.23 = (bf16[128,1,256]{2,0,1:T(8,128)(2,1)S(1)}, bf16[128,1,256]{2,0,1:T(8,128)(2,1)}, u32[]{:S(2)}) copy-start(bf16[128,1,256]{2,0,1:T(8,128)(2,1)} %stack.211) | copy-start | bytes 196612
  186.9 25.8 %copy-start.24 = (bf16[128,1,256]{2,0,1:T(8,128)(2,1)S(1)}, bf16[128,1,256]{2,0,1:T(8,128)(2,1)}, u32[]{:S(2)}) copy-start(bf16[128,1,256]{2,0,1:T(8,128)(2,1)} %stack.212) | copy-start | bytes 196612
  186.9 26.4 %copy-start.25 = (bf16[128,1,256]{2,0,1:T(8,128)(2,1)S(1)}, bf16[128,1,256]{2,0,1:T(8,128)(2,1)}, u32[]{:S(2)}) copy-start(bf16[128,1,256]{2,0,1:T(8,128)(2,1)} %stack.213) | copy-start | bytes 196612
  186.9 27.1 %copy-start.26 = (bf16[128,1,256]{2,0,1:T(8,128)(2,1)S(1)}, bf16[128,1,256]{2,0,1:T(8,128)(2,1)}, u32[]{:S(2)}) copy-start(bf16[128,1,256]{2,0,1:T(8,128)(2,1)} %stack.214) | copy-start | bytes 196612
  186.9 27.7 %copy-start.27 = (bf16[128,1,256]{2,0,1:T(8,128)(2,1)S(1)}, bf16[128,1,256]{2,0,1:T(8,128)(2,1)}, u32[]{:S(2)}) copy-start(bf16[128,1,256]{2,0,1:T(8,128)(2,1)} %stack.215) | copy-start | bytes 196612
  186.9 28.3 %copy-start.12 = (f32[128,256]{1,0:T(8,128)S(1)}, f32[128,256]{1,0:T(8,128)}, u32[]{:S(2)}) copy-start(f32[128,256]{1,0:T(8,128)} %reshape.309) | copy-start | bytes 393220
  215.3 3.4 copy-start.13
  218.1 0.7 copy-start.7
  226.9 3.6 copy-start.2
  226.9 3.6 copy-start.5
  226.9 3.6 copy-start.10
  226.9 3.6 copy-start.29
  228.1 3.0 copy-start.6
  230.5 1.5 copy-start.9
  243.3 189.2 %reduce-scatter.6.cloned.1.call-start = ((), (), s32[]{:S(2)}) async-start(), calls=%async_computation.4 | async-start | bytes 10158080 | tf_op jit(solution)/shard_map/reduce_scatter | solution.py:227
  247.3 21.0 %copy-start.3 = (bf16[66,3,4,256]{3,0,2,1:T(8,128)(2,1)S(1)}, bf16[66,3,4,256]{3,0,2,1:T(8,128)(2,1)}, u32[]{:S(2)}) copy-start(bf16[66,3,4,256]{3,0,2,1:T(8,128)(2,1)} %get-tuple-element.8) | copy-start | bytes 1216516
  247.3 23.6 %copy-start.11 = (f32[256,1,256]{2,0,1:T(8,128)S(1)}, f32[256,1,256]{2,0,1:T(8,128)}, u32[]{:S(2)}) copy-start(f32[256,1,256]{2,0,1:T(8,128)} %copy.150) | copy-start | bytes 786436
  295.4 194.8 %reduce-scatter.8.cloned.1.call-start = ((), (), s32[]{:S(2)}) async-start(), calls=%async_computation.5 | async-start | bytes 4718592 | tf_op jit(solution)/shard_map/reduce_scatter | solution.py:233
Sparse Core Ops, SparseCore 0:
  243.4 23.7 reduce-scatter.3
  295.6 136.8 reduce-scatter.5
  438.2 51.9 reduce-scatter.7
where the time goes:
time: 505 us; the launch traced here: 499 us
  local copies, waits for them, and re-layouts  205 us (41%)
  waiting for transfers between devices  190 us (38%)
  matrix products  37.4 us (7%)
  blocking collectives  32.4 us (6%)
  other arithmetic  14.1 us (3%)
  between operations  14.1 us (3%)
  starting transfers between devices  5.25 us (1%)
    reduce_scatter x1, waiting for transfers between devices, per_device(): lax.psum_scatter(jnp.concatenate([projection_terms, conv_terms], axis=1),...  137 us
    unnamed x118, local copies, waits for them, and re-layouts  69.6 us
    slice x29, local copies, waits for them, and re-layouts, gather_taps(): padded[first_at:first_at + col_count, second_at:second_at + sweeps, third...  42.6 us
    another operation x29, local copies, waits for them, and re-layouts, gather_taps(): return jnp.stack(pieces, axis=3)  41.7 us
    reduce_scatter x1, waiting for transfers between devices, per_device(): lax.psum_scatter(weight_rows, ('beam', 'sweep'), scatter_dimension=2, til...  37.9 us
    all_gather x1, blocking collectives, per_device(): lax.all_gather(values, 'azim', axis=0, tiled=True)  17.5 us
    all_gather x1, blocking collectives, per_device(): lax.all_gather(key_proj, 'azim', axis=0, tiled=True)  15 us
  transfers between devices with their start and end apart: 9, of which 8 were waited for; matrix products, arithmetic and copies ran while one was open for 10% of the time, Pallas kernels for 0%

commit v1 on v0

v1 whole, which is shorter than its diff:
```python
import functools

import jax
import jax.numpy as jnp
from jax import lax
from jax.experimental import pallas as pl
from jax.experimental.pallas import tpu as pltpu
from jax.sharding import PartitionSpec as P

HEADS = 8
SECTOR = 64
TAPS = 27
MASKED = -1e30
GROUP = ("beam", "sweep")

NN = ((1,), (0,))
NT = ((1,), (1,))
TN = ((0,), (0,))

VMEM = pl.BlockSpec(memory_space=pltpu.VMEM)
SMEM = pl.BlockSpec(memory_space=pltpu.SMEM)
BF = jnp.bfloat16
F32 = jnp.float32


def dot(left, right, dims=NN):
    return lax.dot_general(left, right, (dims, ((), ())), preferred_element_type=F32)


def call(kernel, outs, in_specs, scratch=(), limit=40):
    return pl.pallas_call(
        kernel,
        out_shape=[jax.ShapeDtypeStruct(shape, dtype) for shape, dtype in outs],
        in_specs=in_specs,
        out_specs=[VMEM] * len(outs),
        scratch_shapes=list(scratch),
        compiler_params=pltpu.CompilerParams(vmem_limit_bytes=limit << 20),
    )


def slot_of(other, own):
    differ = other ^ own
    return (differ & 1) * 4 + (differ >> 1)


def group_index():
    return lax.axis_index("beam") * lax.axis_size("sweep") + lax.axis_index("sweep")


def prep_kernel(features_ref, cot_ref, features_out, cot_out):
    for source, target in ((features_ref, features_out), (cot_ref, cot_out)):
        wide = source[...].astype(F32)
        for b in range(wide.shape[1]):
            target[b] = wide[:, b, :].astype(BF)


def slices_kernel(even_ref, odd_ref, slices_out, first_out, last_out):
    me = group_index()
    _, beams, cols, channels = even_ref.shape
    width = channels // 8
    for out, col in ((first_out, 0), (last_out, cols - 1)):
        base = col // 16 * 16
        rows = []
        for ref in (even_ref, odd_ref):
            for block in range(4):
                for b in range(beams):
                    part = ref[block, b, base : base + 16, :].astype(F32)
                    rows.append(part[col - base : col - base + 1])
        out[...] = jnp.concatenate(rows, axis=0).astype(BF)
    channel = lax.broadcasted_iota(jnp.int32, (channels, 4 * width), 0) - width * me
    lane = lax.broadcasted_iota(jnp.int32, (channels, 4 * width), 1)
    total = [None] * 4
    for b in range(4):
        pick = jnp.where(channel + width * b == lane, 1.0, 0.0)
        pick = jnp.where((channel >= 0) & (channel < width), pick, 0.0).astype(BF)
        for s in range(4):
            slot = slot_of((b // beams) * 4 + s, me)
            odd = slot // 4
            block = lax.rem(slot, 4)
            value = jnp.where(odd == 1, odd_ref[block, b % beams], even_ref[block, b % beams])
            part = dot(value, pick)
            total[s] = part if total[s] is None else total[s] + part
    for s in range(4):
        slices_out[:, 4 * width * s : 4 * width * (s + 1)] = total[s].astype(BF)


def conv_kernel(even_ref, odd_ref, below_ref, above_ref, w_ref, w_out_ref, layer_out, layer_bf_out, attended_out,
                padded, edges, shifted):
    me = group_index()
    sweep = lax.axis_index("sweep")
    beam = lax.axis_index("beam")
    _, beams, cols, channels = even_ref.shape
    edges[0] = below_ref[...].astype(F32)
    edges[1] = above_ref[...].astype(F32)
    for j in range(3):
        other_sweep = sweep + (j - 1)
        sweep_ok = (other_sweep >= 0) & (other_sweep < 4)
        for m in range(beams + 2):
            other_beam = beam + (-1 if m == 0 else (1 if m == beams + 1 else 0))
            within = (m - 1) % beams
            ok = sweep_ok & (other_beam >= 0) & (other_beam < 2)
            keep = jnp.where(ok, 1.0, 0.0)
            other = jnp.where(ok, other_beam * 4 + other_sweep, me)
            slot = slot_of(other, me)
            odd = slot // 4
            block = lax.rem(slot, 4)
            value = jnp.where(odd == 1, odd_ref[block, within], even_ref[block, within])
            padded[j, m, 8 : 8 + cols, :] = value.astype(F32) * keep
            row = slot * beams + within
            padded[j, m, 7:8, :] = edges[0, pl.ds(row, 1), :] * keep
            padded[j, m, 8 + cols : 9 + cols, :] = edges[1, pl.ds(row, 1), :] * keep
    for i in (-1, 0, 1):
        for j in range(3):
            for m in range(beams + 2):
                shifted[i + 1, j, m * cols : (m + 1) * cols, :] = padded[j, m, 8 - i : 8 - i + cols, :].astype(BF)
    total = even_ref[0].reshape(beams * cols, channels).astype(F32)
    for i in (-1, 0, 1):
        for j in (-1, 0, 1):
            for k in (-1, 0, 1):
                rows = shifted[i + 1, 1 - j, (1 - k) * cols : (1 - k + beams) * cols, :]
                total = total + dot(rows, w_ref[9 * (i + 1) + 3 * (j + 1) + (k + 1)], NT)
    rounded = total.astype(BF)
    layer_out[...] = total.reshape(beams, cols, channels)
    layer_bf_out[...] = rounded.reshape(beams, cols, channels)
    attended_out[...] = dot(rounded, w_out_ref[...], NT).astype(BF).reshape(beams, cols, channels)


def allowed_row(mask_ref, count, cols):
    me = lax.axis_index("azim")
    block = lax.broadcasted_iota(jnp.int32, (1, count * cols), 1) // cols
    row = jnp.zeros((1, count * cols), jnp.int32)
    for ahead in range(count):
        row = jnp.where(block == ahead, mask_ref[me, lax.rem(me + ahead, count)], row)
    return row > 0


def by_head(rows):
    cols, channels = rows.shape
    head = lax.broadcasted_iota(jnp.int32, rows.shape, 1) // (channels // HEADS)
    wide = rows.astype(F32)
    return jnp.concatenate([jnp.where(head == h, wide, 0.0).astype(BF) for h in range(HEADS)], axis=0)


def own_head(stacked):
    cols = stacked.shape[0] // HEADS
    channels = stacked.shape[1]
    head = lax.broadcasted_iota(jnp.int32, (cols, channels), 1) // (channels // HEADS)
    total = jnp.zeros((cols, channels), F32)
    for h in range(HEADS):
        total = jnp.where(head == h, stacked[h * cols : (h + 1) * cols], total)
    return total


def weights_of(queries_by_head, keys, allowed):
    scale = (queries_by_head.shape[1] // HEADS) ** (-0.5)
    scores = jnp.where(allowed, dot(queries_by_head, keys, NT) * scale, MASKED)
    peak = jnp.max(scores, axis=-1, keepdims=True)
    logsum = peak + jnp.log(jnp.sum(jnp.exp(scores - peak), axis=-1, keepdims=True))
    return jnp.where(allowed, jnp.exp(scores - logsum), 0.0)


def forward_kernel(count, *refs):
    mask_ref = refs[0]
    feature_refs = refs[1 : 1 + count]
    w_query, w_key, w_value, w_out = refs[1 + count : 5 + count]
    all_out, query_out, key_out, value_out, attended_out, pieces_out = refs[5 + count :]
    beams, cols, channels = feature_refs[0].shape
    for ahead in range(count):
        all_out[:, ahead * cols : (ahead + 1) * cols, :] = feature_refs[ahead][...]
    own = feature_refs[0][...].reshape(beams * cols, channels)
    every = all_out[...].reshape(beams * count * cols, channels)
    query_out[...] = dot(own, w_query[...]).astype(BF).reshape(beams, cols, channels)
    key_out[...] = dot(every, w_key[...]).astype(BF).reshape(beams, count * cols, channels)
    value_out[...] = dot(every, w_value[...]).astype(BF).reshape(beams, count * cols, channels)
    allowed = allowed_row(mask_ref, count, cols)
    for b in range(beams):
        weights = weights_of(by_head(query_out[b]), key_out[b], allowed)
        attended_out[b] = own_head(dot(weights.astype(BF), value_out[b])).astype(BF)
    mixed = own.astype(F32) + dot(attended_out[...].reshape(beams * cols, channels), w_out[...])
    me = lax.axis_index("azim")
    width = channels // count
    for owner in range(count):
        part = [mixed[b * cols : (b + 1) * cols, owner * width : (owner + 1) * width] for b in range(beams)]
        pieces_out[lax.rem(owner + count - me, count)] = jnp.concatenate(part, axis=1).astype(BF)


def backward_kernel(count, mask_ref, all_ref, query_ref, key_ref, value_ref, attended_ref, grad_ref, layer_bf_ref,
                    layer_ref, w_query, w_key, w_value, base_out, send_out, keep_out, pass_out,
                    grad_query, grad_key, grad_value, sums):
    beams, cols, channels = query_ref.shape
    scale = (channels // HEADS) ** (-0.5)
    allowed = allowed_row(mask_ref, count, cols)
    for b in range(beams):
        queries = by_head(query_ref[b])
        keys = key_ref[b]
        weights = weights_of(queries, keys, allowed)
        grads = by_head(grad_ref[b])
        attended = jnp.concatenate([attended_ref[b].astype(F32)] * HEADS, axis=0)
        delta = jnp.sum(grads.astype(F32) * attended, axis=-1, keepdims=True)
        grad_score = (weights * (dot(grads, value_ref[b], NT) - delta)).astype(BF)
        grad_query[b] = (own_head(dot(grad_score, keys)) * scale).astype(BF)
        grad_key[b] = (dot(grad_score, queries, TN) * scale).astype(BF)
        grad_value[b] = dot(weights.astype(BF), grads, TN).astype(BF)
    own_rows = beams * cols
    all_rows = beams * count * cols
    query_flat = grad_query[...].reshape(own_rows, channels)
    key_flat = grad_key[...].reshape(all_rows, channels)
    value_flat = grad_value[...].reshape(all_rows, channels)
    own = dot(query_flat, w_query[...], NT).reshape(beams, cols, channels) + layer_ref[...]
    spread = dot(key_flat, w_key[...], NT) + dot(value_flat, w_value[...], NT)
    spread = spread.reshape(beams, count, cols, channels)
    base_out[...] = own + spread[:, 0]
    for ahead in range(1, count):
        send_out[ahead - 1] = spread[:, ahead].astype(BF)
    every = all_ref[...].reshape(all_rows, channels)
    mine = all_ref[:, :cols, :].reshape(own_rows, channels)
    width = channels // 8
    for index, (left, right) in enumerate(
        (
            (query_flat, mine),
            (key_flat, every),
            (value_flat, every),
            (layer_bf_ref[...].reshape(own_rows, channels), attended_ref[...].reshape(own_rows, channels)),
        )
    ):
        sums[index] = dot(left, right, TN).astype(BF).reshape(8, width, channels)
    me = group_index()
    for differ in range(8):
        target = pass_out if differ & 1 else keep_out
        for index in range(4):
            target[differ >> 1, index * width : (index + 1) * width, :] = sums[index, me ^ differ]


def pieces_kernel(count, keep_ref, come_ref, pieces_out):
    me = lax.axis_index("azim")
    total = keep_ref[...].astype(F32) + come_ref[...].astype(F32)
    rows, channels = total.shape
    width = channels // count
    half = rows // 2
    for owner in range(count):
        part = total[:, owner * width : (owner + 1) * width]
        pieces_out[lax.rem(owner + count - me, count)] = jnp.concatenate([part[:half], part[half:]], axis=1).astype(BF)


def last_kernel(count, *refs):
    even_ref, odd_ref, own_ref = refs[:3]
    packed_refs = refs[3 : 2 + count]
    own_piece = refs[2 + count]
    piece_refs = refs[3 + count : 2 + 2 * count]
    base_ref = refs[2 + 2 * count]
    come_refs = refs[3 + 2 * count : 2 + 3 * count]
    features_out, weights_out, layers, turned = refs[2 + 3 * count :]
    me = group_index()
    total = base_ref[...]
    for ref in come_refs:
        total = total + ref[...].astype(F32)
    features_out[...] = jnp.stack([total[b] for b in range(total.shape[0])], axis=1).astype(BF)
    piece = own_piece[0].astype(F32)
    for ref in piece_refs:
        piece = piece + ref[...].astype(F32)
    lanes = piece.shape[1] // 2
    width = piece.shape[0] // 2
    for index in range(4):
        weights_out[index] = piece[
            (index % 2) * width : (index % 2 + 1) * width, (index // 2) * lanes : (index // 2 + 1) * lanes
        ]
    rows = own_ref.shape[0]
    for s in range(4):
        for y in range(2):
            slot = slot_of(y * 4 + s, me)
            odd = slot // 4
            block = lax.rem(slot, 4)
            value = jnp.where(odd == 1, odd_ref[block], even_ref[block])
            layers[s, :, y * 2 * lanes : (y + 1) * 2 * lanes] = value.reshape(count * rows, 2 * lanes)
    span = own_ref.shape[1]
    cots = [own_ref[...]] + [ref[:, :span] for ref in packed_refs]
    wide = jnp.concatenate(cots, axis=0).astype(F32).T
    for i in (-1, 0, 1):
        moved = wide if i == 0 else pltpu.roll(wide, i % wide.shape[1], 1)
        turned[i + 1] = moved.astype(BF)
    per_sweep = span // 4
    for i in (-1, 0, 1):
        for j in (-1, 0, 1):
            found = None
            for s in range(4):
                if 0 <= s - j < 4:
                    part = dot(turned[i + 1, (s - j) * per_sweep : (s - j + 1) * per_sweep, :], layers[s])
                    found = part if found is None else found + part
            for k in (-1, 0, 1):
                tap = None
                for b in range(4):
                    if 0 <= b + k < 4:
                        part = found[b * width : (b + 1) * width, (b + k) * lanes : (b + k + 1) * lanes]
                        tap = part if tap is None else tap + part
                weights_out[4 + 9 * (i + 1) + 3 * (j + 1) + (k + 1)] = tap


def shift(value, ahead):
    count = lax.axis_size("azim")
    return lax.ppermute(value, "azim", [(i, (i + ahead) % count) for i in range(count)])


def swap(value, bits):
    return lax.ppermute(value, GROUP, [(i, i ^ bits) for i in range(8)])


def group_gather(value):
    even = jnp.stack([value, swap(value, 2), swap(value, 4), swap(value, 6)])
    return even, swap(even, 1)


def add(left, right):
    return (left.astype(F32) + right.astype(F32)).astype(BF)


def per_device(features, cotangent, w_query, w_key, w_value, w_out, w_conv, sector_mask):
    cols, sweeps, beams, channels = features.shape
    count = lax.axis_size("azim")
    assert sweeps == 1 and beams == 2 and cols == SECTOR
    assert lax.axis_size("beam") == 2 and lax.axis_size("sweep") == 4
    width = channels // 8
    lanes = channels // count
    block = (beams, cols, channels)
    whole = (beams, count * cols, channels)

    own_features, own_cot = call(prep_kernel, [(block, BF)] * 2, [VMEM] * 2)(
        features.reshape(cols, beams, channels), cotangent.reshape(cols, beams, channels)
    )
    come = [shift(own_features, ahead) for ahead in range(1, count)]
    all_features = [own_features] + come[::-1]
    even, odd = group_gather(own_cot)

    edge = (8 * beams, channels)
    slices, first, last = call(
        slices_kernel, [((cols, 16 * width), BF), (edge, BF), (edge, BF)], [VMEM] * 2
    )(even, odd)
    below = shift(last, 1)
    above = shift(first, count - 1)

    every, queries, keys, values, attended, pieces = call(
        functools.partial(forward_kernel, count),
        [(whole, BF), (block, BF), (whole, BF), (whole, BF), (block, BF), ((count, cols, beams * lanes), BF)],
        [SMEM] + [VMEM] * (count + 4),
    )(sector_mask, *all_features, w_query, w_key, w_value, w_out)

    span = 16 * width
    packed = [shift(jnp.concatenate([slices, pieces[ahead]], axis=1), ahead) for ahead in range(1, count)][::-1]
    layer_block = jnp.stack([pieces[0]] + [part[:, span:] for part in packed])
    even_layers, odd_layers = group_gather(layer_block)

    grad_layer, grad_layer_bf, grad_attended = call(
        conv_kernel,
        [(block, F32), (block, BF), (block, BF)],
        [VMEM] * 6,
        scratch=[
            pltpu.VMEM((3, beams + 2, cols + 16, channels), F32),
            pltpu.VMEM((2,) + edge, F32),
            pltpu.VMEM((3, 3, (beams + 2) * cols, channels), BF),
        ],
    )(even, odd, below, above, w_conv.transpose(1, 0, 2), w_out)

    quarter = (4, 4 * width, channels)
    base, send, keep, give = call(
        functools.partial(backward_kernel, count),
        [(block, F32), ((count - 1,) + block, BF), (quarter, BF), (quarter, BF)],
        [SMEM] + [VMEM] * 11,
        scratch=[
            pltpu.VMEM(block, BF),
            pltpu.VMEM(whole, BF),
            pltpu.VMEM(whole, BF),
            pltpu.VMEM((4, 8, width, channels), BF),
        ],
    )(
        sector_mask, every, queries, keys, values, attended, grad_attended, grad_layer_bf, grad_layer,
        w_query, w_key, w_value,
    )
    come_grads = [shift(send[ahead - 1], ahead) for ahead in range(1, count)]

    sums = add(keep, swap(give, 1)).reshape(2, 2, 4 * width, channels)
    sums = add(sums[:, 0], swap(sums[:, 1], 2))
    sum_pieces = call(
        functools.partial(pieces_kernel, count), [((count, 2 * width, 2 * lanes), BF)], [VMEM] * 2
    )(sums[0], swap(sums[1], 4))[0]
    come_pieces = [shift(sum_pieces[ahead], ahead) for ahead in range(1, count)]

    features_grad, weight_grads = call(
        functools.partial(last_kernel, count),
        [((cols, beams, channels), BF), ((4 + TAPS, width, lanes), F32)],
        [VMEM] * (2 + 3 * count),
        scratch=[
            pltpu.VMEM((4, count * cols, 4 * lanes), BF),
            pltpu.VMEM((3, span, count * cols), BF),
        ],
    )(even_layers, odd_layers, slices, *packed, sum_pieces, *come_pieces, base, *come_grads)
    return features_grad.reshape(features.shape), weight_grads.transpose(2, 0, 1)


def solution(mesh):
    token = P("azim", "sweep", "beam", None)
    in_specs = (token, token, P(), P(), P(), P(), P(), P())
    out_specs = (token, P("azim", None, ("beam", "sweep")))
    return jax.shard_map(per_device, mesh=mesh, in_specs=in_specs, out_specs=out_specs, check_vma=False)
```

time: 505 us -> 64.3 us (0.13); the launches traced: 499 us -> 64 us
  local copies, waits for them, and re-layouts: 205 us -> 9 us
  waiting for transfers between devices: 190 us -> 14.1 us
  matrix products: 37.4 us -> 0 us
  blocking collectives: 32.4 us -> 0 us
  starting transfers between devices: 5.25 us -> 31.3 us
  other arithmetic: 14.1 us -> 0.21 us
  between operations: 14.1 us -> 0.91 us
  Pallas kernels: 0 us -> 8.47 us
    reduce_scatter x3 -> x0, waiting for transfers between devices: 175 us -> none  [the longest x1 137 us: per_device(): lax.psum_scatter(jnp.concatenate([projection_terms, conv_terms], axis=1),...]
    unnamed x118 -> x26, local copies, waits for them, and re-layouts: 69.6 us -> 8.94 us
    another operation x35 -> x3, local copies, waits for them, and re-layouts: 50.7 us -> 0.01 us  [per_device(): layer_block = jnp.stack([pieces[0]] + [part[:, span:] for part in packed])]
    slice x33 -> x1, local copies, waits for them, and re-layouts: 46.7 us -> 0.01 us  [per_device(): layer_block = jnp.stack([pieces[0]] + [part[:, span:] for part in packed])]
    dot_general x21 -> x0, matrix products: 37.4 us -> none  [the longest x1 5.43 us: per_device(): jnp.einsum('nti,no->ito', layer_taps, cot_flat, preferred_element_type=jn...]
    all_gather x2 -> x0, blocking collectives: 32.4 us -> none  [the longest x1 17.5 us: per_device(): lax.all_gather(values, 'azim', axis=0, tiled=True)]
    ppermute x6 -> x25, starting transfers between devices: 4.95 us -> 31.3 us  [the longest x14 19.9 us: shift(): lax.ppermute(value, 'azim', [(i, (i + ahead) % count) for i in range(coun...]
    reshape x11 -> x0, local copies, waits for them, and re-layouts: 18.8 us -> none
  transfers between devices with their start and end apart: 9 -> 25, of which waited for: 8 -> 11; matrix products, arithmetic and copies ran while one was open for 10% -> 0% of each run, Pallas kernels for 0% -> 9%
where the time goes in v1:
time: 64.3 us; the launch traced here: 64 us
  starting transfers between devices  31.3 us (49%)
  waiting for transfers between devices  14.1 us (22%)
  local copies, waits for them, and re-layouts  9 us (14%)
  Pallas kernels  8.47 us (13%)
  between operations  0.91 us (1%)
    ppermute x14, starting transfers between devices, shift(): lax.ppermute(value, 'azim', [(i, (i + ahead) % count) for i in range(coun...  19.9 us
    ppermute x11, starting transfers between devices, swap(): return lax.ppermute(value, GROUP, [(i, i ^ bits) for i in range(8)])  11.5 us
    ppermute x14, waiting for transfers between devices, shift(): lax.ppermute(value, 'azim', [(i, (i + ahead) % count) for i in range(coun...  9.56 us
    unnamed x26, local copies, waits for them, and re-layouts  8.94 us
    ppermute x11, waiting for transfers between devices, swap(): return lax.ppermute(value, GROUP, [(i, i ^ bits) for i in range(8)])  4.5 us
    pallas_call x1, Pallas kernels, per_device(): call(functools.partial(backward_kernel, count), [(block, F32), ((count -...  2.4 us
    pallas_call x1, Pallas kernels, per_device(): call(functools.partial(last_kernel, count), [((cols, beams, channels), BF...  1.95 us
    pallas_call x1, Pallas kernels, per_device(): call(functools.partial(forward_kernel, count), [(whole, BF), (block, BF),...  1.88 us
  transfers between devices with their start and end apart: 25, of which 11 were waited for; matrix products, arithmetic and copies ran while one was open for 0% of the time, Pallas kernels for 9%

profile of v1, /device:TPU:0, one launch (start us, length us, event | category | flops | bytes accessed | tf_op | source)
XLA Modules:
  0.0 64.0 jit_solution(1532961771575284039)
XLA Ops:
  0.7 0.9 %copy-done.9 = bf16[64,1,2,256]{3,2,1,0:T(2,128)(2,1)S(1)} copy-done((bf16[64,1,2,256]{3,2,1,0:T(2,128)(2,1)S(1)}, bf16[64,1,2,256]{3,2,1,0:T(2,128)(2,1)}, u32[]{:S(2)}) %copy-start.9) | copy-done | bytes 65560
  1.6 0.8 %copy-done.10 = bf16[64,1,2,256]{3,2,1,0:T(2,128)(2,1)S(1)} copy-done((bf16[64,1,2,256]{3,2,1,0:T(2,128)(2,1)S(1)}, bf16[64,1,2,256]{3,2,1,0:T(2,128)(2,1)}, u32[]{:S(2)}) %copy-start.10) | copy-done | bytes 65560
  2.4 0.3 shard_map.95
  2.7 3.0 %collective-permute-start.3 = (bf16[2,64,256]{2,1,0:T(8,128)(2,1)S(1)}, bf16[2,64,256]{2,1,0:T(8,128)(2,1)S(1)}, u32[]{:S(2)}, u32[]{:S(2)}) collective-permute-start(bf16[2,64,256]{2,1,0:T(8,128)(2,1)S(1)} %get-tuple-element.24), channel_id=1, source_target_pairs={{0,2},{1,3},{2,0},{3,1},{4,6},{5,7},{6,4},{7,5},{8,10},{9,11},{10,... | collective-permute-start | bytes 196616 | tf_op jit(solution)/shard_map/ppermute | solution.py:304
  5.8 1.5 %collective-permute-start.4 = (bf16[2,64,256]{2,1,0:T(8,128)(2,1)S(1)}, bf16[2,64,256]{2,1,0:T(8,128)(2,1)S(1)}, u32[]{:S(2)}, u32[]{:S(2)}) collective-permute-start(bf16[2,64,256]{2,1,0:T(8,128)(2,1)S(1)} %get-tuple-element.24), channel_id=1, source_target_pairs={{0,4},{1,5},{2,6},{3,7},{4,0},{5,1},{6,2},{7,3},{8,12},{9,13},{10,... | collective-permute-start | bytes 196616 | tf_op jit(solution)/shard_map/ppermute | solution.py:304
  7.3 4.1 %collective-permute-start = (bf16[2,64,256]{2,1,0:T(8,128)(2,1)S(1)}, bf16[2,64,256]{2,1,0:T(8,128)(2,1)S(1)}, u32[]{:S(2)}, u32[]{:S(2)}) collective-permute-start(bf16[2,64,256]{2,1,0:T(8,128)(2,1)S(1)} %get-tuple-element.22.refs_1_), channel_id=1, source_target_pairs={{0,24},{8,0},{16,8},{24,16},{1,25},{9,1},{17,9},{25,17},{2,26},{10... | collective-permute-start | bytes 196616 | tf_op jit(solution)/shard_map/ppermute | solution.py:300
  11.4 1.0 %collective-permute-start.2 = (bf16[2,64,256]{2,1,0:T(8,128)(2,1)S(1)}, bf16[2,64,256]{2,1,0:T(8,128)(2,1)S(1)}, u32[]{:S(2)}, u32[]{:S(2)}) collective-permute-start(bf16[2,64,256]{2,1,0:T(8,128)(2,1)S(1)} %get-tuple-element.22.refs_1_), channel_id=1, source_target_pairs={{0,8},{8,16},{16,24},{24,0},{1,9},{9,17},{17,25},{25,1},{2,10},{10... | collective-permute-start | bytes 196616 | tf_op jit(solution)/shard_map/ppermute | solution.py:300
  12.5 0.1 collective-permute-start.6
  12.6 0.7 %collective-permute-done.refs_2_ = bf16[2,64,256]{2,1,0:T(8,128)(2,1)S(1)} collective-permute-done((bf16[2,64,256]{2,1,0:T(8,128)(2,1)S(1)}, bf16[2,64,256]{2,1,0:T(8,128)(2,1)S(1)}, u32[]{:S(2)}, u32[]{:S(2)}) %collective-permute-start) | collective-permute-done | bytes 65568 | tf_op jit(solution)/shard_map/ppermute | solution.py:300
  13.3 3.2 %collective-permute-done.1.refs_3_ = bf16[2,64,256]{2,1,0:T(8,128)(2,1)S(1)} collective-permute-done((bf16[2,64,256]{2,1,0:T(8,128)(2,1)S(1)}, bf16[2,64,256]{2,1,0:T(8,128)(2,1)S(1)}, u32[]{:S(2)}, u32[]{:S(2)}) %collective-permute-start.1) | collective-permute-done | bytes 65568 | tf_op jit(solution)/shard_map/ppermute | solution.py:300
  16.5 0.9 %collective-permute-done.2.refs_4_ = bf16[2,64,256]{2,1,0:T(8,128)(2,1)S(1)} collective-permute-done((bf16[2,64,256]{2,1,0:T(8,128)(2,1)S(1)}, bf16[2,64,256]{2,1,0:T(8,128)(2,1)S(1)}, u32[]{:S(2)}, u32[]{:S(2)}) %collective-permute-start.2) | collective-permute-done | bytes 65568 | tf_op jit(solution)/shard_map/ppermute | solution.py:300
  17.4 0.9 %copy-done.1 = bf16[256,256]{1,0:T(8,128)(2,1)S(1)} copy-done((bf16[256,256]{1,0:T(8,128)(2,1)S(1)}, bf16[256,256]{1,0:T(8,128)(2,1)}, u32[]{:S(2)}) %copy-start.1) | copy-done | bytes 131096
  18.3 0.9 %copy-done.3 = bf16[256,256]{1,0:T(8,128)(2,1)S(1)} copy-done((bf16[256,256]{1,0:T(8,128)(2,1)S(1)}, bf16[256,256]{1,0:T(8,128)(2,1)}, u32[]{:S(2)}) %copy-start.3) | copy-done | bytes 131096
  19.2 0.9 %copy-done.5 = bf16[256,256]{1,0:T(8,128)(2,1)S(1)} copy-done((bf16[256,256]{1,0:T(8,128)(2,1)S(1)}, bf16[256,256]{1,0:T(8,128)(2,1)}, u32[]{:S(2)}) %copy-start.5) | copy-done | bytes 131096
  20.1 0.9 %copy-done.7 = bf16[256,256]{1,0:T(8,128)(2,1)S(1)} copy-done((bf16[256,256]{1,0:T(8,128)(2,1)S(1)}, bf16[256,256]{1,0:T(8,128)(2,1)}, u32[]{:S(2)}) %copy-start.7) | copy-done | bytes 131096
  21.0 0.7 %copy-done.11 = s32[4,4]{1,0:T(4,128)S(1)} copy-done((s32[4,4]{1,0:T(4,128)S(1)}, s32[4,4]{1,0:T(4,128)}, u32[]{:S(2)}) %copy-start.11) | copy-done | bytes 88
  21.7 1.9 %shard_map.96 = (bf16[2,256,256]{2,1,0:T(8,128)(2,1)S(1)}, bf16[2,64,256]{2,1,0:T(8,128)(2,1)S(1)}, bf16[2,256,256]{2,1,0:T(8,128)(2,1)S(1)}, bf16[2,256,256]{2,...) custom-call(s32[4,4]{1,0:T(4,128)S(1)} %copy-done.11, ...), custom_call_target="tpu_custom_call" | custom-call | tf_op jit(solution)/shard_map/pallas_call | solution.py:340
  23.6 0.4 shard_map.97
  24.1 1.9 %collective-permute-start.14 = (bf16[16,256]{1,0:T(8,128)(2,1)S(1)}, bf16[16,256]{1,0:T(8,128)(2,1)S(1)}, u32[]{:S(2)}, u32[]{:S(2)}) collective-permute-start(bf16[16,256]{1,0:T(8,128)(2,1)S(1)} %get-tuple-element.31), channel_id=1, source_target_pairs={{0,8},{8,16},{16,24},{24,0},{1,9},{9,17},{17,25},{25,1},{2,10},{10... | collective-permute-start | bytes 24584 | tf_op jit(solution)/shard_map/ppermute | solution.py:300
  26.1 2.0 %collective-permute-start.15 = (bf16[16,256]{1,0:T(8,128)(2,1)S(1)}, bf16[16,256]{1,0:T(8,128)(2,1)S(1)}, u32[]{:S(2)}, u32[]{:S(2)}) collective-permute-start(bf16[16,256]{1,0:T(8,128)(2,1)S(1)} %get-tuple-element.32), channel_id=1, source_target_pairs={{0,24},{8,0},{16,8},{24,16},{1,25},{9,1},{17,9},{25,17},{2,26},{10... | collective-permute-start | bytes 24584 | tf_op jit(solution)/shard_map/ppermute | solution.py:300
  28.0 0.5 collective-permute-start.8
  28.5 2.0 %collective-permute-start.7 = (bf16[64,640]{1,0:T(8,128)(2,1)S(1)}, bf16[64,640]{1,0:T(8,128)(2,1)S(1)}, u32[]{:S(2)}, u32[]{:S(2)}) collective-permute-start(bf16[64,640]{1,0:T(8,128)(2,1)S(1)} %get-tuple-element.60), channel_id=1, source_target_pairs={{0,24},{8,0},{16,8},{24,16},{1,25},{9,1},{17,9},{25,17},{2,26},{10... | collective-permute-start | bytes 245768 | tf_op jit(solution)/shard_map/ppermute | solution.py:300
  30.4 0.9 %collective-permute-done.14.below_ref = bf16[16,256]{1,0:T(8,128)(2,1)S(1)} collective-permute-done((bf16[16,256]{1,0:T(8,128)(2,1)S(1)}, bf16[16,256]{1,0:T(8,128)(2,1)S(1)}, u32[]{:S(2)}, u32[]{:S(2)}) %collective-permute-start.14) | collective-permute-done | bytes 8224 | tf_op jit(solution)/shard_map/ppermute | solution.py:300
  31.4 2.0 %copy-done = bf16[256,27,256]{2,0,1:T(8,128)(2,1)S(1)} copy-done((bf16[256,27,256]{2,0,1:T(8,128)(2,1)S(1)}, bf16[256,27,256]{2,0,1:T(8,128)(2,1)}, u32[]{:S(2)}) %copy-start) | copy-done | bytes 3538968
  33.4 0.9 %copy-done.2 = bf16[256,256]{1,0:T(8,128)(2,1)S(1)} copy-done((bf16[256,256]{1,0:T(8,128)(2,1)S(1)}, bf16[256,256]{1,0:T(8,128)(2,1)}, u32[]{:S(2)}) %copy-start.2) | copy-done | bytes 131096
  34.3 1.4 %shard_map.98 = (f32[2,64,256]{2,1,0:T(8,128)S(1)}, bf16[2,64,256]{2,1,0:T(8,128)(2,1)S(1)}, bf16[2,64,256]{2,1,0:T(8,128)(2,1)S(1)}) custom-call(bf16[4,2,64,256]{3,2,1,0:T(8,128)(2,1)S(1)} %pad_maximum_fusion.even_ref, bf16[4,2,64,256]{3,2,1,0:T(8,128)(2,1)S(1)} %collective-permute-done.6.odd_ref, bf16[16,256]{1,0:T(8,128)(2,1)S(1)} %collective-permute-done.14.below_ref, ...), custom_call_target="tpu_custom_call" | custom-call | tf_op jit(solution)/shard_map/pallas_call | solution.py:351
  35.8 2.4 %shard_map.99 = (f32[2,64,256]{2,1,0:T(8,128)S(1)}, bf16[3,2,64,256]{3,2,1,0:T(8,128)(2,1)S(1)}, bf16[4,128,256]{2,1,0:T(8,128)(2,1)S(1)}, bf16[4,128,256]{2,1,0:T(8,128)(2,1)S(1)}) custom-call(s32[4,4]{1,0:T(4,128)S(1)} %copy-done.12, bf16[2,256,256]{2,1,0:T(8,128)(2,1)S(1)} %get-tuple-element.26.all_ref, ...), custom_call_target="tpu_custom_call" | custom-call | tf_op jit(solution)/shard_map/pallas_call | solution.py:363
  38.2 0.1 collective-permute-start.16
  38.4 1.6 %collective-permute-start.10 = (bf16[4,64,128]{2,1,0:T(8,128)(2,1)S(1)}, bf16[4,64,128]{2,1,0:T(8,128)(2,1)S(1)}, u32[]{:S(2)}, u32[]{:S(2)}) collective-permute-start(bf16[4,64,128]{2,1,0:T(8,128)(2,1)S(1)} %get-tuple-element.55), channel_id=1, source_target_pairs={{0,2},{1,3},{2,0},{3,1},{4,6},{5,7},{6,4},{7,5},{8,10},{9,11},{10,... | collective-permute-start | bytes 196616 | tf_op jit(solution)/shard_map/ppermute | solution.py:304
  39.9 1.5 %collective-permute-start.11 = (bf16[4,64,128]{2,1,0:T(8,128)(2,1)S(1)}, bf16[4,64,128]{2,1,0:T(8,128)(2,1)S(1)}, u32[]{:S(2)}, u32[]{:S(2)}) collective-permute-start(bf16[4,64,128]{2,1,0:T(8,128)(2,1)S(1)} %get-tuple-element.55), channel_id=1, source_target_pairs={{0,4},{1,5},{2,6},{3,7},{4,0},{5,1},{6,2},{7,3},{8,12},{9,13},{10,... | collective-permute-start | bytes 196616 | tf_op jit(solution)/shard_map/ppermute | solution.py:304
  41.4 0.5 collective-permute-start.12
  42.0 1.6 %collective-permute-start.17 = (bf16[2,128,256]{2,1,0:T(8,128)(2,1)S(1)}, bf16[2,128,256]{2,1,0:T(8,128)(2,1)S(1)}, u32[]{:S(2)}, u32[]{:S(2)}) collective-permute-start(bf16[2,128,256]{2,1,0:T(8,128)(2,1)S(1)} %slice_bitcast_fusion), channel_id=1, source_target_pairs={{0,2},{1,3},{2,0},{3,1},{4,6},{5,7},{6,4},{7,5},{8,10},{9,11},{10,... | collective-permute-start | bytes 393224 | tf_op jit(solution)/shard_map/ppermute | solution.py:304
  43.6 0.6 collective-permute-done.11
  44.2 3.1 %collective-permute-done.12 = bf16[4,64,128]{2,1,0:T(8,128)(2,1)S(1)} collective-permute-done((bf16[4,64,128]{2,1,0:T(8,128)(2,1)S(1)}, bf16[4,64,128]{2,1,0:T(8,128)(2,1)S(1)}, u32[]{:S(2)}, u32[]{:S(2)}) %collective-permute-start.12) | collective-permute-done | bytes 65568 | tf_op jit(solution)/shard_map/ppermute | solution.py:304
  47.3 0.1 collective-permute-start.13
  47.4 0.7 %collective-permute-done.17 = bf16[2,128,256]{2,1,0:T(8,128)(2,1)S(1)} collective-permute-done((bf16[2,128,256]{2,1,0:T(8,128)(2,1)S(1)}, bf16[2,128,256]{2,1,0:T(8,128)(2,1)S(1)}, u32[]{:S(2)}, u32[]{:S(2)}) %collective-permute-start.17) | collective-permute-done | bytes 131104 | tf_op jit(solution)/shard_map/ppermute | solution.py:304
  48.2 1.6 %collective-permute-start.18 = (bf16[128,256]{1,0:T(8,128)(2,1)S(1)}, bf16[128,256]{1,0:T(8,128)(2,1)S(1)}, u32[]{:S(2)}, u32[]{:S(2)}) collective-permute-start(bf16[128,256]{1,0:T(8,128)(2,1)S(1)} %get-tuple-element.49), channel_id=1, source_target_pairs={{0,4},{1,5},{2,6},{3,7},{4,0},{5,1},{6,2},{7,3},{8,12},{9,13},{10,... | collective-permute-start | bytes 196616 | tf_op jit(solution)/shard_map/ppermute | solution.py:304
  49.8 0.5 collective-permute-start.22
  50.2 2.2 %collective-permute-start.23 = (bf16[2,64,256]{2,1,0:T(8,128)(2,1)S(1)}, bf16[2,64,256]{2,1,0:T(8,128)(2,1)S(1)}, u32[]{:S(2)}, u32[]{:S(2)}) collective-permute-start(bf16[2,64,256]{2,1,0:T(8,128)(2,1)S(1)} %get-tuple-element.47), channel_id=1, source_target_pairs={{0,16},{8,24},{16,0},{24,8},{1,17},{9,25},{17,1},{25,9},{2,18},{10... | collective-permute-start | bytes 196616 | tf_op jit(solution)/shard_map/ppermute | solution.py:300
  52.4 1.2 %collective-permute-start.24 = (bf16[2,64,256]{2,1,0:T(8,128)(2,1)S(1)}, bf16[2,64,256]{2,1,0:T(8,128)(2,1)S(1)}, u32[]{:S(2)}, u32[]{:S(2)}) collective-permute-start(bf16[2,64,256]{2,1,0:T(8,128)(2,1)S(1)} %get-tuple-element.46), channel_id=1, source_target_pairs={{0,24},{8,0},{16,8},{24,16},{1,25},{9,1},{17,9},{25,17},{2,26},{10... | collective-permute-start | bytes 196616 | tf_op jit(solution)/shard_map/ppermute | solution.py:300
  53.6 0.1 shard_map.100.refs_6_
  53.8 0.9 %collective-permute-start.19 = (bf16[64,128]{1,0:T(8,128)(2,1)S(1)}, bf16[64,128]{1,0:T(8,128)(2,1)S(1)}, u32[]{:S(2)}, u32[]{:S(2)}) collective-permute-start(bf16[64,128]{1,0:T(8,128)(2,1)S(1)} %get-tuple-element.53), channel_id=1, source_target_pairs={{0,8},{8,16},{16,24},{24,0},{1,9},{9,17},{17,25},{25,1},{2,10},{10... | collective-permute-start | bytes 49160 | tf_op jit(solution)/shard_map/ppermute | solution.py:300
  54.6 1.4 %collective-permute-done.22.refs_11_ = bf16[2,64,256]{2,1,0:T(8,128)(2,1)S(1)} collective-permute-done((bf16[2,64,256]{2,1,0:T(8,128)(2,1)S(1)}, bf16[2,64,256]{2,1,0:T(8,128)(2,1)S(1)}, u32[]{:S(2)}, u32[]{:S(2)}) %collective-permute-start.22) | collective-permute-done | bytes 65568 | tf_op jit(solution)/shard_map/ppermute | solution.py:300
  56.0 0.8 %collective-permute-start.20 = (bf16[64,128]{1,0:T(8,128)(2,1)S(1)}, bf16[64,128]{1,0:T(8,128)(2,1)S(1)}, u32[]{:S(2)}, u32[]{:S(2)}) collective-permute-start(bf16[64,128]{1,0:T(8,128)(2,1)S(1)} %get-tuple-element.52), channel_id=1, source_target_pairs={{0,16},{8,24},{16,0},{24,8},{1,17},{9,25},{17,1},{25,9},{2,18},{10... | collective-permute-start | bytes 49160 | tf_op jit(solution)/shard_map/ppermute | solution.py:300
  56.8 1.0 %collective-permute-done.23.refs_12_ = bf16[2,64,256]{2,1,0:T(8,128)(2,1)S(1)} collective-permute-done((bf16[2,64,256]{2,1,0:T(8,128)(2,1)S(1)}, bf16[2,64,256]{2,1,0:T(8,128)(2,1)S(1)}, u32[]{:S(2)}, u32[]{:S(2)}) %collective-permute-start.23) | collective-permute-done | bytes 65568 | tf_op jit(solution)/shard_map/ppermute | solution.py:300
  57.8 2.8 %collective-permute-start.21 = (bf16[64,128]{1,0:T(8,128)(2,1)S(1)}, bf16[64,128]{1,0:T(8,128)(2,1)S(1)}, u32[]{:S(2)}, u32[]{:S(2)}) collective-permute-start(bf16[64,128]{1,0:T(8,128)(2,1)S(1)} %get-tuple-element.51), channel_id=1, source_target_pairs={{0,24},{8,0},{16,8},{24,16},{1,25},{9,1},{17,9},{25,17},{2,26},{10... | collective-permute-start | bytes 49160 | tf_op jit(solution)/shard_map/ppermute | solution.py:300
  60.6 1.4 %collective-permute-done.21.refs_9_ = bf16[64,128]{1,0:T(8,128)(2,1)S(1)} collective-permute-done((bf16[64,128]{1,0:T(8,128)(2,1)S(1)}, bf16[64,128]{1,0:T(8,128)(2,1)S(1)}, u32[]{:S(2)}, u32[]{:S(2)}) %collective-permute-start.21) | collective-permute-done | bytes 16416 | tf_op jit(solution)/shard_map/ppermute | solution.py:300
  62.0 2.0 %shard_map.101 = (bf16[64,2,256]{2,1,0:T(2,128)(2,1)}, f32[31,32,64]{2,1,0:T(8,128)}) custom-call(bf16[4,4,64,128]{3,2,1,0:T(8,128)(2,1)S(1)} %pad_maximum_fusion.1.refs_0_, bf16[4,4,64,128]{3,2,1,0:T(8,128)(2,1)S(1)} %collective-permute-done.13.refs_1_, bf16[64,512]{1,0:T(8,128)(2,1)S(1)} %get-tuple-element.25.refs_2_, ...), custom_call_target="tpu_custom_call" | custom-call | tf_op jit(solution)/shard_map/pallas_call | solution.py:386
  (49 shorter events, 0.5 us)
Async XLA Ops:
  0.6 35.1 %copy-start.4 = (bf16[256,256]{1,0:T(8,128)(2,1)S(1)}, bf16[256,256]{1,0:T(8,128)(2,1)}, u32[]{:S(2)}) copy-start(bf16[256,256]{1,0:T(8,128)(2,1)} %w_query.1) | copy-start | bytes 393220
  0.6 35.1 %copy-start.6 = (bf16[256,256]{1,0:T(8,128)(2,1)S(1)}, bf16[256,256]{1,0:T(8,128)(2,1)}, u32[]{:S(2)}) copy-start(bf16[256,256]{1,0:T(8,128)(2,1)} %w_key.1) | copy-start | bytes 393220
  0.7 35.1 %copy-start.8 = (bf16[256,256]{1,0:T(8,128)(2,1)S(1)}, bf16[256,256]{1,0:T(8,128)(2,1)}, u32[]{:S(2)}) copy-start(bf16[256,256]{1,0:T(8,128)(2,1)} %w_value.1) | copy-start | bytes 393220
  0.7 0.9 %copy-start.9 = (bf16[64,1,2,256]{3,2,1,0:T(2,128)(2,1)S(1)}, bf16[64,1,2,256]{3,2,1,0:T(2,128)(2,1)}, u32[]{:S(2)}) copy-start(bf16[64,1,2,256]{3,2,1,0:T(2,128)(2,1)} %param.8) | copy-start | bytes 196612
  1.6 0.8 %copy-start.10 = (bf16[64,1,2,256]{3,2,1,0:T(2,128)(2,1)S(1)}, bf16[64,1,2,256]{3,2,1,0:T(2,128)(2,1)}, u32[]{:S(2)}) copy-start(bf16[64,1,2,256]{3,2,1,0:T(2,128)(2,1)} %param.9) | copy-start | bytes 196612
  2.4 33.4 %copy-start.12 = (s32[4,4]{1,0:T(4,128)S(1)}, s32[4,4]{1,0:T(4,128)}, u32[]{:S(2)}) copy-start(s32[4,4]{1,0:T(4,128)} %mask_ref.1) | copy-start | bytes 196
  2.7 8.6 %collective-permute-start.3 = (bf16[2,64,256]{2,1,0:T(8,128)(2,1)S(1)}, bf16[2,64,256]{2,1,0:T(8,128)(2,1)S(1)}, u32[]{:S(2)}, u32[]{:S(2)}) collective-permute-start(bf16[2,64,256]{2,1,0:T(8,128)(2,1)S(1)} %get-tuple-element.24), channel_id=1, source_target_pairs={{0,2},{1,3},{2,0},{3,1},{4,6},{5,7},{6,4},{7,5},{8,10},{9,11},{10,... | collective-permute-start | bytes 196616 | tf_op jit(solution)/shard_map/ppermute | solution.py:304
  5.8 6.6 %collective-permute-start.4 = (bf16[2,64,256]{2,1,0:T(8,128)(2,1)S(1)}, bf16[2,64,256]{2,1,0:T(8,128)(2,1)S(1)}, u32[]{:S(2)}, u32[]{:S(2)}) collective-permute-start(bf16[2,64,256]{2,1,0:T(8,128)(2,1)S(1)} %get-tuple-element.24), channel_id=1, source_target_pairs={{0,4},{1,5},{2,6},{3,7},{4,0},{5,1},{6,2},{7,3},{8,12},{9,13},{10,... | collective-permute-start | bytes 196616 | tf_op jit(solution)/shard_map/ppermute | solution.py:304
  7.3 5.2 %collective-permute-start.5 = (bf16[2,64,256]{2,1,0:T(8,128)(2,1)S(1)}, bf16[2,64,256]{2,1,0:T(8,128)(2,1)S(1)}, u32[]{:S(2)}, u32[]{:S(2)}) collective-permute-start(bf16[2,64,256]{2,1,0:T(8,128)(2,1)S(1)} %get-tuple-element.24), channel_id=1, source_target_pairs={{0,6},{1,7},{2,4},{3,5},{4,2},{5,3},{6,0},{7,1},{8,14},{9,15},{10,... | collective-permute-start | bytes 196616 | tf_op jit(solution)/shard_map/ppermute | solution.py:304
  7.3 6.0 %collective-permute-start = (bf16[2,64,256]{2,1,0:T(8,128)(2,1)S(1)}, bf16[2,64,256]{2,1,0:T(8,128)(2,1)S(1)}, u32[]{:S(2)}, u32[]{:S(2)}) collective-permute-start(bf16[2,64,256]{2,1,0:T(8,128)(2,1)S(1)} %get-tuple-element.22.refs_1_), channel_id=1, source_target_pairs={{0,24},{8,0},{16,8},{24,16},{1,25},{9,1},{17,9},{25,17},{2,26},{10... | collective-permute-start | bytes 196616 | tf_op jit(solution)/shard_map/ppermute | solution.py:300
  11.4 5.2 %collective-permute-start.1 = (bf16[2,64,256]{2,1,0:T(8,128)(2,1)S(1)}, bf16[2,64,256]{2,1,0:T(8,128)(2,1)S(1)}, u32[]{:S(2)}, u32[]{:S(2)}) collective-permute-start(bf16[2,64,256]{2,1,0:T(8,128)(2,1)S(1)} %get-tuple-element.22.refs_1_), channel_id=1, source_target_pairs={{0,16},{8,24},{16,0},{24,8},{1,17},{9,25},{17,1},{25,9},{2,18},{10... | collective-permute-start | bytes 196616 | tf_op jit(solution)/shard_map/ppermute | solution.py:300
  11.4 6.1 %collective-permute-start.2 = (bf16[2,64,256]{2,1,0:T(8,128)(2,1)S(1)}, bf16[2,64,256]{2,1,0:T(8,128)(2,1)S(1)}, u32[]{:S(2)}, u32[]{:S(2)}) collective-permute-start(bf16[2,64,256]{2,1,0:T(8,128)(2,1)S(1)} %get-tuple-element.22.refs_1_), channel_id=1, source_target_pairs={{0,8},{8,16},{16,24},{24,0},{1,9},{9,17},{17,25},{25,1},{2,10},{10... | collective-permute-start | bytes 196616 | tf_op jit(solution)/shard_map/ppermute | solution.py:300
  12.5 11.2 %collective-permute-start.6 = (bf16[4,2,64,256]{3,2,1,0:T(8,128)(2,1)S(1)}, bf16[4,2,64,256]{3,2,1,0:T(8,128)(2,1)S(1)}, u32[]{:S(2)}, u32[]{:S(2)}) collective-permute-start(bf16[4,2,64,256]{3,2,1,0:T(8,128)(2,1)S(1)} %pad_maximum_fusion.even_ref), channel_id=1, source_target_pairs={{0,1},{1,0},{2,3},{3,2},{4,5},{5,4},{6,7},{7,6},{8,9},{9,8},{10,11... | collective-permute-start | bytes 786440 | tf_op jit(solution)/shard_map/ppermute | solution.py:304
  17.4 0.9 %copy-start.1 = (bf16[256,256]{1,0:T(8,128)(2,1)S(1)}, bf16[256,256]{1,0:T(8,128)(2,1)}, u32[]{:S(2)}) copy-start(bf16[256,256]{1,0:T(8,128)(2,1)} %w_out_ref.1) | copy-start | bytes 393220
  18.3 0.9 %copy-start.3 = (bf16[256,256]{1,0:T(8,128)(2,1)S(1)}, bf16[256,256]{1,0:T(8,128)(2,1)}, u32[]{:S(2)}) copy-start(bf16[256,256]{1,0:T(8,128)(2,1)} %w_query.1) | copy-start | bytes 393220
  19.2 0.9 %copy-start.5 = (bf16[256,256]{1,0:T(8,128)(2,1)S(1)}, bf16[256,256]{1,0:T(8,128)(2,1)}, u32[]{:S(2)}) copy-start(bf16[256,256]{1,0:T(8,128)(2,1)} %w_key.1) | copy-start | bytes 393220
  20.1 0.9 %copy-start.7 = (bf16[256,256]{1,0:T(8,128)(2,1)S(1)}, bf16[256,256]{1,0:T(8,128)(2,1)}, u32[]{:S(2)}) copy-start(bf16[256,256]{1,0:T(8,128)(2,1)} %w_value.1) | copy-start | bytes 393220
  21.0 0.7 %copy-start.11 = (s32[4,4]{1,0:T(4,128)S(1)}, s32[4,4]{1,0:T(4,128)}, u32[]{:S(2)}) copy-start(s32[4,4]{1,0:T(4,128)} %mask_ref.1) | copy-start | bytes 196
  24.0 14.2 %collective-permute-start.9 = (bf16[64,640]{1,0:T(8,128)(2,1)S(1)}, bf16[64,640]{1,0:T(8,128)(2,1)S(1)}, u32[]{:S(2)}, u32[]{:S(2)}) collective-permute-start(bf16[64,640]{1,0:T(8,128)(2,1)S(1)} %get-tuple-element.62), channel_id=1, source_target_pairs={{0,8},{8,16},{16,24},{24,0},{1,9},{9,17},{17,25},{25,1},{2,10},{10... | collective-permute-start | bytes 245768 | tf_op jit(solution)/shard_map/ppermute | solution.py:300
  24.1 7.3 %collective-permute-start.14 = (bf16[16,256]{1,0:T(8,128)(2,1)S(1)}, bf16[16,256]{1,0:T(8,128)(2,1)S(1)}, u32[]{:S(2)}, u32[]{:S(2)}) collective-permute-start(bf16[16,256]{1,0:T(8,128)(2,1)S(1)} %get-tuple-element.31), channel_id=1, source_target_pairs={{0,8},{8,16},{16,24},{24,0},{1,9},{9,17},{17,25},{25,1},{2,10},{10... | collective-permute-start | bytes 24584 | tf_op jit(solution)/shard_map/ppermute | solution.py:300
  26.1 5.3 %collective-permute-start.15 = (bf16[16,256]{1,0:T(8,128)(2,1)S(1)}, bf16[16,256]{1,0:T(8,128)(2,1)S(1)}, u32[]{:S(2)}, u32[]{:S(2)}) collective-permute-start(bf16[16,256]{1,0:T(8,128)(2,1)S(1)} %get-tuple-element.32), channel_id=1, source_target_pairs={{0,24},{8,0},{16,8},{24,16},{1,25},{9,1},{17,9},{25,17},{2,26},{10... | collective-permute-start | bytes 24584 | tf_op jit(solution)/shard_map/ppermute | solution.py:300
  28.0 10.3 %collective-permute-start.8 = (bf16[64,640]{1,0:T(8,128)(2,1)S(1)}, bf16[64,640]{1,0:T(8,128)(2,1)S(1)}, u32[]{:S(2)}, u32[]{:S(2)}) collective-permute-start(bf16[64,640]{1,0:T(8,128)(2,1)S(1)} %get-tuple-element.61), channel_id=1, source_target_pairs={{0,16},{8,24},{16,0},{24,8},{1,17},{9,25},{17,1},{25,9},{2,18},{10... | collective-permute-start | bytes 245768 | tf_op jit(solution)/shard_map/ppermute | solution.py:300
  28.5 9.8 %collective-permute-start.7 = (bf16[64,640]{1,0:T(8,128)(2,1)S(1)}, bf16[64,640]{1,0:T(8,128)(2,1)S(1)}, u32[]{:S(2)}, u32[]{:S(2)}) collective-permute-start(bf16[64,640]{1,0:T(8,128)(2,1)S(1)} %get-tuple-element.60), channel_id=1, source_target_pairs={{0,24},{8,0},{16,8},{24,16},{1,25},{9,1},{17,9},{25,17},{2,26},{10... | collective-permute-start | bytes 245768 | tf_op jit(solution)/shard_map/ppermute | solution.py:300
  31.4 2.0 %copy-start = (bf16[256,27,256]{2,0,1:T(8,128)(2,1)S(1)}, bf16[256,27,256]{2,0,1:T(8,128)(2,1)}, u32[]{:S(2)}) copy-start(bf16[256,27,256]{2,0,1:T(8,128)(2,1)} %param.14) | copy-start | bytes 10616836
  33.4 0.9 %copy-start.2 = (bf16[256,256]{1,0:T(8,128)(2,1)S(1)}, bf16[256,256]{1,0:T(8,128)(2,1)}, u32[]{:S(2)}) copy-start(bf16[256,256]{1,0:T(8,128)(2,1)} %w_out_ref.1) | copy-start | bytes 393220
  38.2 3.7 %collective-permute-start.16 = (bf16[4,128,256]{2,1,0:T(8,128)(2,1)S(1)}, bf16[4,128,256]{2,1,0:T(8,128)(2,1)S(1)}, u32[]{:S(2)}, u32[]{:S(2)}) collective-permute-start(bf16[4,128,256]{2,1,0:T(8,128)(2,1)S(1)} %get-tuple-element.37), channel_id=1, source_target_pairs={{0,1},{1,0},{2,3},{3,2},{4,5},{5,4},{6,7},{7,6},{8,9},{9,8},{10,11... | collective-permute-start | bytes 786440 | tf_op jit(solution)/shard_map/ppermute | solution.py:304
  38.4 5.2 %collective-permute-start.10 = (bf16[4,64,128]{2,1,0:T(8,128)(2,1)S(1)}, bf16[4,64,128]{2,1,0:T(8,128)(2,1)S(1)}, u32[]{:S(2)}, u32[]{:S(2)}) collective-permute-start(bf16[4,64,128]{2,1,0:T(8,128)(2,1)S(1)} %get-tuple-element.55), channel_id=1, source_target_pairs={{0,2},{1,3},{2,0},{3,1},{4,6},{5,7},{6,4},{7,5},{8,10},{9,11},{10,... | collective-permute-start | bytes 196616 | tf_op jit(solution)/shard_map/ppermute | solution.py:304
  39.9 4.3 %collective-permute-start.11 = (bf16[4,64,128]{2,1,0:T(8,128)(2,1)S(1)}, bf16[4,64,128]{2,1,0:T(8,128)(2,1)S(1)}, u32[]{:S(2)}, u32[]{:S(2)}) collective-permute-start(bf16[4,64,128]{2,1,0:T(8,128)(2,1)S(1)} %get-tuple-element.55), channel_id=1, source_target_pairs={{0,4},{1,5},{2,6},{3,7},{4,0},{5,1},{6,2},{7,3},{8,12},{9,13},{10,... | collective-permute-start | bytes 196616 | tf_op jit(solution)/shard_map/ppermute | solution.py:304
  41.4 5.9 %collective-permute-start.12 = (bf16[4,64,128]{2,1,0:T(8,128)(2,1)S(1)}, bf16[4,64,128]{2,1,0:T(8,128)(2,1)S(1)}, u32[]{:S(2)}, u32[]{:S(2)}) collective-permute-start(bf16[4,64,128]{2,1,0:T(8,128)(2,1)S(1)} %get-tuple-element.55), channel_id=1, source_target_pairs={{0,6},{1,7},{2,4},{3,5},{4,2},{5,3},{6,0},{7,1},{8,14},{9,15},{10,... | collective-permute-start | bytes 196616 | tf_op jit(solution)/shard_map/ppermute | solution.py:304
  42.0 6.1 %collective-permute-start.17 = (bf16[2,128,256]{2,1,0:T(8,128)(2,1)S(1)}, bf16[2,128,256]{2,1,0:T(8,128)(2,1)S(1)}, u32[]{:S(2)}, u32[]{:S(2)}) collective-permute-start(bf16[2,128,256]{2,1,0:T(8,128)(2,1)S(1)} %slice_bitcast_fusion), channel_id=1, source_target_pairs={{0,2},{1,3},{2,0},{3,1},{4,6},{5,7},{6,4},{7,5},{8,10},{9,11},{10,... | collective-permute-start | bytes 393224 | tf_op jit(solution)/shard_map/ppermute | solution.py:304
  47.3 13.3 %collective-permute-start.13 = (bf16[4,4,64,128]{3,2,1,0:T(8,128)(2,1)S(1)}, bf16[4,4,64,128]{3,2,1,0:T(8,128)(2,1)S(1)}, u32[]{:S(2)}, u32[]{:S(2)}) collective-permute-start(bf16[4,4,64,128]{3,2,1,0:T(8,128)(2,1)S(1)} %pad_maximum_fusion.1.refs_0_), channel_id=1, source_target_pairs={{0,1},{1,0},{2,3},{3,2},{4,5},{5,4},{6,7},{7,6},{8,9},{9,8},{10,11... | collective-permute-start | bytes 786440 | tf_op jit(solution)/shard_map/ppermute | solution.py:304
  48.2 5.5 %collective-permute-start.18 = (bf16[128,256]{1,0:T(8,128)(2,1)S(1)}, bf16[128,256]{1,0:T(8,128)(2,1)S(1)}, u32[]{:S(2)}, u32[]{:S(2)}) collective-permute-start(bf16[128,256]{1,0:T(8,128)(2,1)S(1)} %get-tuple-element.49), channel_id=1, source_target_pairs={{0,4},{1,5},{2,6},{3,7},{4,0},{5,1},{6,2},{7,3},{8,12},{9,13},{10,... | collective-permute-start | bytes 196616 | tf_op jit(solution)/shard_map/ppermute | solution.py:304
  49.8 6.2 %collective-permute-start.22 = (bf16[2,64,256]{2,1,0:T(8,128)(2,1)S(1)}, bf16[2,64,256]{2,1,0:T(8,128)(2,1)S(1)}, u32[]{:S(2)}, u32[]{:S(2)}) collective-permute-start(bf16[2,64,256]{2,1,0:T(8,128)(2,1)S(1)} %get-tuple-element.48), channel_id=1, source_target_pairs={{0,8},{8,16},{16,24},{24,0},{1,9},{9,17},{17,25},{25,1},{2,10},{10... | collective-permute-start | bytes 196616 | tf_op jit(solution)/shard_map/ppermute | solution.py:300
  50.2 7.5 %collective-permute-start.23 = (bf16[2,64,256]{2,1,0:T(8,128)(2,1)S(1)}, bf16[2,64,256]{2,1,0:T(8,128)(2,1)S(1)}, u32[]{:S(2)}, u32[]{:S(2)}) collective-permute-start(bf16[2,64,256]{2,1,0:T(8,128)(2,1)S(1)} %get-tuple-element.47), channel_id=1, source_target_pairs={{0,16},{8,24},{16,0},{24,8},{1,17},{9,25},{17,1},{25,9},{2,18},{10... | collective-permute-start | bytes 196616 | tf_op jit(solution)/shard_map/ppermute | solution.py:300
  52.4 8.2 %collective-permute-start.24 = (bf16[2,64,256]{2,1,0:T(8,128)(2,1)S(1)}, bf16[2,64,256]{2,1,0:T(8,128)(2,1)S(1)}, u32[]{:S(2)}, u32[]{:S(2)}) collective-permute-start(bf16[2,64,256]{2,1,0:T(8,128)(2,1)S(1)} %get-tuple-element.46), channel_id=1, source_target_pairs={{0,24},{8,0},{16,8},{24,16},{1,25},{9,1},{17,9},{25,17},{2,26},{10... | collective-permute-start | bytes 196616 | tf_op jit(solution)/shard_map/ppermute | solution.py:300
  53.8 6.9 %collective-permute-start.19 = (bf16[64,128]{1,0:T(8,128)(2,1)S(1)}, bf16[64,128]{1,0:T(8,128)(2,1)S(1)}, u32[]{:S(2)}, u32[]{:S(2)}) collective-permute-start(bf16[64,128]{1,0:T(8,128)(2,1)S(1)} %get-tuple-element.53), channel_id=1, source_target_pairs={{0,8},{8,16},{16,24},{24,0},{1,9},{9,17},{17,25},{25,1},{2,10},{10... | collective-permute-start | bytes 49160 | tf_op jit(solution)/shard_map/ppermute | solution.py:300
  56.0 4.7 %collective-permute-start.20 = (bf16[64,128]{1,0:T(8,128)(2,1)S(1)}, bf16[64,128]{1,0:T(8,128)(2,1)S(1)}, u32[]{:S(2)}, u32[]{:S(2)}) collective-permute-start(bf16[64,128]{1,0:T(8,128)(2,1)S(1)} %get-tuple-element.52), channel_id=1, source_target_pairs={{0,16},{8,24},{16,0},{24,8},{1,17},{9,25},{17,1},{25,9},{2,18},{10... | collective-permute-start | bytes 49160 | tf_op jit(solution)/shard_map/ppermute | solution.py:300
  57.8 4.3 %collective-permute-start.21 = (bf16[64,128]{1,0:T(8,128)(2,1)S(1)}, bf16[64,128]{1,0:T(8,128)(2,1)S(1)}, u32[]{:S(2)}, u32[]{:S(2)}) collective-permute-start(bf16[64,128]{1,0:T(8,128)(2,1)S(1)} %get-tuple-element.51), channel_id=1, source_target_pairs={{0,24},{8,0},{16,8},{24,16},{1,25},{9,1},{17,9},{25,17},{2,26},{10... | collective-permute-start | bytes 49160 | tf_op jit(solution)/shard_map/ppermute | solution.py:300

commit v2 on v1

--- a/solution.py
+++ b/solution.py
@@ -9,6 +9,7 @@
 
 HEADS = 8
 SECTOR = 64
+LANES = 128
 TAPS = 27
 MASKED = -1e30
 GROUP = ("beam", "sweep")
@@ -18,7 +19,7 @@
 TN = ((0,), (0,))
 
 VMEM = pl.BlockSpec(memory_space=pltpu.VMEM)
-SMEM = pl.BlockSpec(memory_space=pltpu.SMEM)
+HBM = pl.BlockSpec(memory_space=pltpu.HBM)
 BF = jnp.bfloat16
 F32 = jnp.float32
 
@@ -47,11 +48,36 @@
     return lax.axis_index("beam") * lax.axis_size("sweep") + lax.axis_index("sweep")
 
 
-def prep_kernel(features_ref, cot_ref, features_out, cot_out):
-    for source, target in ((features_ref, features_out), (cot_ref, cot_out)):
+def prep_kernel(count, features_hbm, cot_hbm, mask_hbm, *refs):
+    weights_hbm = refs[:4]
+    features_out, cot_out, allowed_out = refs[4:7]
+    weights_out = refs[7:11]
+    features, cot, mask, sems = refs[11:]
+    copies = [
+        pltpu.make_async_copy(source, target, sems.at[index])
+        for index, (source, target) in enumerate(
+            zip((features_hbm, cot_hbm, mask_hbm) + weights_hbm, (features, cot, mask) + weights_out)
+        )
+    ]
+    for copy in copies:
+        copy.start()
+    for copy, source, target in ((copies[0], features, features_out), (copies[1], cot, cot_out)):
+        copy.wait()
         wide = source[...].astype(F32)
         for b in range(wide.shape[1]):
             target[b] = wide[:, b, :].astype(BF)
+    copies[2].wait()
+    me = lax.axis_index("azim")
+    square = mask[...].astype(F32)
+    row = lax.broadcasted_iota(jnp.int32, square.shape, 0)
+    own = jnp.sum(jnp.where(row == me, square, 0.0), axis=0, keepdims=True)
+    keys = allowed_out.shape[1]
+    sector = lax.broadcasted_iota(jnp.int32, (count, keys), 0)
+    block = lax.broadcasted_iota(jnp.int32, (count, keys), 1) // SECTOR
+    spread = jnp.where(sector == lax.rem(block + me, count), 1.0, 0.0).astype(BF)
+    allowed_out[...] = dot(jnp.broadcast_to(own, (8, count)).astype(BF), spread)
+    for copy in copies[3:]:
+        copy.wait()
 
 
 def slices_kernel(even_ref, odd_ref, slices_out, first_out, last_out):
@@ -66,7 +92,10 @@
                 for b in range(beams):
                     part = ref[block, b, base : base + 16, :].astype(F32)
                     rows.append(part[col - base : col - base + 1])
-        out[...] = jnp.concatenate(rows, axis=0).astype(BF)
+        edge = jnp.concatenate(rows, axis=0).astype(BF)
+        count = edge.shape[0]
+        for half in range(out.shape[0] // count):
+            out[half * count : (half + 1) * count] = edge[:, half * LANES : (half + 1) * LANES]
     channel = lax.broadcasted_iota(jnp.int32, (channels, 4 * width), 0) - width * me
     lane = lax.broadcasted_iota(jnp.int32, (channels, 4 * width), 1)
     total = [None] * 4
@@ -81,7 +110,7 @@
             part = dot(value, pick)
             total[s] = part if total[s] is None else total[s] + part
     for s in range(4):
-        slices_out[:, 4 * width * s : 4 * width * (s + 1)] = total[s].astype(BF)
+        slices_out[cols * s : cols * (s + 1), :] = total[s].astype(BF)
 
 
 def conv_kernel(even_ref, odd_ref, below_ref, above_ref, w_ref, w_out_ref, layer_out, layer_bf_out, attended_out,
@@ -90,8 +119,13 @@
     sweep = lax.axis_index("sweep")
     beam = lax.axis_index("beam")
     _, beams, cols, channels = even_ref.shape
-    edges[0] = below_ref[...].astype(F32)
-    edges[1] = above_ref[...].astype(F32)
+    count = 8 * beams
+    start = below_ref.shape[0] - count * (channels // LANES)
+    for index, ref in enumerate((below_ref, above_ref)):
+        for half in range(channels // LANES):
+            edges[index, :, half * LANES : (half + 1) * LANES] = ref[
+                start + half * count : start + (half + 1) * count, :
+            ].astype(F32)
     for j in range(3):
         other_sweep = sweep + (j - 1)
         sweep_ok = (other_sweep >= 0) & (other_sweep < 4)
@@ -125,15 +159,6 @@
     attended_out[...] = dot(rounded, w_out_ref[...], NT).astype(BF).reshape(beams, cols, channels)
 
 
-def allowed_row(mask_ref, count, cols):
-    me = lax.axis_index("azim")
-    block = lax.broadcasted_iota(jnp.int32, (1, count * cols), 1) // cols
-    row = jnp.zeros((1, count * cols), jnp.int32)
-    for ahead in range(count):
-        row = jnp.where(block == ahead, mask_ref[me, lax.rem(me + ahead, count)], row)
-    return row > 0
-
-
 def by_head(rows):
     cols, channels = rows.shape
     head = lax.broadcasted_iota(jnp.int32, rows.shape, 1) // (channels // HEADS)
@@ -160,10 +185,12 @@
 
 
 def forward_kernel(count, *refs):
-    mask_ref = refs[0]
+    allowed_ref = refs[0]
     feature_refs = refs[1 : 1 + count]
-    w_query, w_key, w_value, w_out = refs[1 + count : 5 + count]
-    all_out, query_out, key_out, value_out, attended_out, pieces_out = refs[5 + count :]
+    w_query, w_key, w_value, w_out, w_conv_hbm = refs[1 + count : 6 + count]
+    all_out, query_out, key_out, value_out, attended_out, pieces_out, w_conv_out, sem = refs[6 + count :]
+    copy = pltpu.make_async_copy(w_conv_hbm, w_conv_out, sem)
+    copy.start()
     beams, cols, channels = feature_refs[0].shape
     for ahead in range(count):
         all_out[:, ahead * cols : (ahead + 1) * cols, :] = feature_refs[ahead][...]
@@ -172,7 +199,7 @@
     query_out[...] = dot(own, w_query[...]).astype(BF).reshape(beams, cols, channels)
     key_out[...] = dot(every, w_key[...]).astype(BF).reshape(beams, count * cols, channels)
     value_out[...] = dot(every, w_value[...]).astype(BF).reshape(beams, count * cols, channels)
-    allowed = allowed_row(mask_ref, count, cols)
+    allowed = allowed_ref[0:1, :] > 0.5
     for b in range(beams):
         weights = weights_of(by_head(query_out[b]), key_out[b], allowed)
         attended_out[b] = own_head(dot(weights.astype(BF), value_out[b])).astype(BF)
@@ -181,15 +208,19 @@
     width = channels // count
     for owner in range(count):
         part = [mixed[b * cols : (b + 1) * cols, owner * width : (owner + 1) * width] for b in range(beams)]
+        spare = pieces_out.shape[2] - beams * width
+        if spare:
+            part.append(jnp.zeros((cols, spare), F32))
         pieces_out[lax.rem(owner + count - me, count)] = jnp.concatenate(part, axis=1).astype(BF)
-
-
-def backward_kernel(count, mask_ref, all_ref, query_ref, key_ref, value_ref, attended_ref, grad_ref, layer_bf_ref,
+    copy.wait()
+
+
+def backward_kernel(count, allowed_ref, all_ref, query_ref, key_ref, value_ref, attended_ref, grad_ref, layer_bf_ref,
                     layer_ref, w_query, w_key, w_value, base_out, send_out, keep_out, pass_out,
                     grad_query, grad_key, grad_value, sums):
     beams, cols, channels = query_ref.shape
     scale = (channels // HEADS) ** (-0.5)
-    allowed = allowed_row(mask_ref, count, cols)
+    allowed = allowed_ref[0:1, :] > 0.5
     for b in range(beams):
         queries = by_head(query_ref[b])
         keys = key_ref[b]
@@ -264,21 +295,20 @@
         weights_out[index] = piece[
             (index % 2) * width : (index % 2 + 1) * width, (index // 2) * lanes : (index // 2 + 1) * lanes
         ]
-    rows = own_ref.shape[0]
+    per_sweep, rows = own_ref.shape[1], own_ref.shape[0] // 4
     for s in range(4):
         for y in range(2):
             slot = slot_of(y * 4 + s, me)
             odd = slot // 4
             block = lax.rem(slot, 4)
             value = jnp.where(odd == 1, odd_ref[block], even_ref[block])
-            layers[s, :, y * 2 * lanes : (y + 1) * 2 * lanes] = value.reshape(count * rows, 2 * lanes)
-    span = own_ref.shape[1]
-    cots = [own_ref[...]] + [ref[:, :span] for ref in packed_refs]
-    wide = jnp.concatenate(cots, axis=0).astype(F32).T
-    for i in (-1, 0, 1):
-        moved = wide if i == 0 else pltpu.roll(wide, i % wide.shape[1], 1)
-        turned[i + 1] = moved.astype(BF)
-    per_sweep = span // 4
+            layers[s, :, y * 2 * lanes : (y + 1) * 2 * lanes] = value.reshape(count * rows, -1)[:, : 2 * lanes]
+    for s in range(4):
+        cots = [ref[s * rows : (s + 1) * rows, :] for ref in (own_ref,) + tuple(packed_refs)]
+        wide = jnp.concatenate(cots, axis=0).astype(F32).T
+        for i in (-1, 0, 1):
+            moved = wide if i == 0 else pltpu.roll(wide, i % wide.shape[1], 1)
+            turned[i + 1, s * per_sweep : (s + 1) * per_sweep, :] = moved.astype(BF)
     for i in (-1, 0, 1):
         for j in (-1, 0, 1):
             found = None
@@ -295,6 +325,10 @@
                 weights_out[4 + 9 * (i + 1) + 3 * (j + 1) + (k + 1)] = tap
 
 
+def in_hbm(value):
+    return pltpu.with_memory_space_constraint(value, pltpu.HBM)
+
+
 def shift(value, ahead):
     count = lax.axis_size("azim")
     return lax.ppermute(value, "azim", [(i, (i + ahead) % count) for i in range(count)])
@@ -323,29 +357,51 @@
     block = (beams, cols, channels)
     whole = (beams, count * cols, channels)
 
-    own_features, own_cot = call(prep_kernel, [(block, BF)] * 2, [VMEM] * 2)(
-        features.reshape(cols, beams, channels), cotangent.reshape(cols, beams, channels)
-    )
+    token = (cols, beams, channels)
+    square = (channels, channels)
+    own_features, own_cot, allowed, w_query, w_key, w_value, w_out = call(
+        functools.partial(prep_kernel, count),
+        [(block, BF), (block, BF), ((8, count * cols), F32)] + [(square, BF)] * 4,
+        [HBM] * 7,
+        scratch=[
+            pltpu.VMEM(token, BF),
+            pltpu.VMEM(token, BF),
+            pltpu.VMEM(sector_mask.shape, jnp.int32),
+            pltpu.SemaphoreType.DMA((7,)),
+        ],
+    )(*map(in_hbm, (features.reshape(token), cotangent.reshape(token), sector_mask, w_query, w_key, w_value, w_out)))
     come = [shift(own_features, ahead) for ahead in range(1, count)]
     all_features = [own_features] + come[::-1]
     even, odd = group_gather(own_cot)
 
+    spread = (4 * cols, 4 * width)
     edge = (8 * beams, channels)
+    edge_rows = (8 * beams * channels // LANES, LANES)
     slices, first, last = call(
-        slices_kernel, [((cols, 16 * width), BF), (edge, BF), (edge, BF)], [VMEM] * 2
+        slices_kernel, [(spread, BF), (edge_rows, BF), (edge_rows, BF)], [VMEM] * 2
     )(even, odd)
-    below = shift(last, 1)
-    above = shift(first, count - 1)
-
-    every, queries, keys, values, attended, pieces = call(
+
+    pieces_shape = (count, cols, max(LANES, beams * lanes))
+    every, queries, keys, values, attended, pieces, w_conv = call(
         functools.partial(forward_kernel, count),
-        [(whole, BF), (block, BF), (whole, BF), (whole, BF), (block, BF), ((count, cols, beams * lanes), BF)],
-        [SMEM] + [VMEM] * (count + 4),
-    )(sector_mask, *all_features, w_query, w_key, w_value, w_out)
-
-    span = 16 * width
-    packed = [shift(jnp.concatenate([slices, pieces[ahead]], axis=1), ahead) for ahead in range(1, count)][::-1]
-    layer_block = jnp.stack([pieces[0]] + [part[:, span:] for part in packed])
+        [(whole, BF), (block, BF), (whole, BF), (whole, BF), (block, BF), (pieces_shape, BF),
+         ((TAPS,) + square, BF)],
+        [VMEM] * (count + 5) + [HBM],
+        scratch=[pltpu.SemaphoreType.DMA],
+    )(allowed, *all_features, w_query, w_key, w_value, w_out, in_hbm(w_conv.transpose(1, 0, 2)))
+
+    packed = []
+    for ahead in range(1, count):
+        parts = [slices, pieces[ahead]]
+        if ahead == 1:
+            parts.append(last)
+        if ahead == count - 1:
+            parts.append(first)
+        packed.append(shift(jnp.concatenate(parts, axis=0), ahead))
+    packed = packed[::-1]
+    below, above = packed[-1], packed[0]
+    start = 4 * cols
+    layer_block = jnp.stack([pieces[0]] + [part[start : start + cols] for part in packed])
     even_layers, odd_layers = group_gather(layer_block)
 
     grad_layer, grad_layer_bf, grad_attended = call(
@@ -357,13 +413,13 @@
             pltpu.VMEM((2,) + edge, F32),
             pltpu.VMEM((3, 3, (beams + 2) * cols, channels), BF),
         ],
-    )(even, odd, below, above, w_conv.transpose(1, 0, 2), w_out)
+    )(even, odd, below, above, w_conv, w_out)
 
     quarter = (4, 4 * width, channels)
     base, send, keep, give = call(
         functools.partial(backward_kernel, count),
         [(block, F32), ((count - 1,) + block, BF), (quarter, BF), (quarter, BF)],
-        [SMEM] + [VMEM] * 11,
+        [VMEM] * 12,
         scratch=[
             pltpu.VMEM(block, BF),
             pltpu.VMEM(whole, BF),
@@ -371,7 +427,7 @@
             pltpu.VMEM((4, 8, width, channels), BF),
         ],
     )(
-        sector_mask, every, queries, keys, values, attended, grad_attended, grad_layer_bf, grad_layer,
+        allowed, every, queries, keys, values, attended, grad_attended, grad_layer_bf, grad_layer,
         w_query, w_key, w_value,
     )
     come_grads = [shift(send[ahead - 1], ahead) for ahead in range(1, count)]
@@ -389,7 +445,7 @@
         [VMEM] * (2 + 3 * count),
         scratch=[
             pltpu.VMEM((4, count * cols, 4 * lanes), BF),
-            pltpu.VMEM((3, span, count * cols), BF),
+            pltpu.VMEM((3, 16 * width, count * cols), BF),
         ],
     )(even_layers, odd_layers, slices, *packed, sum_pieces, *come_pieces, base, *come_grads)
     return features_grad.reshape(features.shape), weight_grads.transpose(2, 0, 1)

time: 64.3 us -> 57.2 us (0.89)
  local copies, waits for them, and re-layouts: 9 us -> 0.06 us
  waiting for transfers between devices: 14.1 us -> 19.6 us
  starting transfers between devices: 31.3 us -> 26.9 us
  Pallas kernels: 8.47 us -> 9.4 us
    unnamed x26 -> x0, local copies, waits for them, and re-layouts: 8.94 us -> none
    ppermute x14 -> x12, waiting for transfers between devices: 9.56 us -> 15.1 us  [shift(): lax.ppermute(value, 'azim', [(i, (i + ahead) % count) for i in range(coun...]
    ppermute x14 -> x12, starting transfers between devices: 19.9 us -> 15.4 us  [shift(): lax.ppermute(value, 'azim', [(i, (i + ahead) % count) for i in range(coun...]
    pallas_call x2, Pallas kernels: 0.71 us -> 1.77 us  [the longest x1 1.39 us: per_device(): call(functools.partial(prep_kernel, count), [(block, BF), (block, BF), ((...]
  transfers between devices with their start and end apart: 25 -> 23, of which waited for: 11 -> 15; matrix products, arithmetic and copies ran while one was open for 0% -> 0% of each run, Pallas kernels for 9% -> 4%
where the time goes in v2:
time: 57.2 us; the launch traced here: 57 us
  starting transfers between devices  26.9 us (47%)
  waiting for transfers between devices  19.6 us (34%)
  Pallas kernels  9.4 us (16%)
  between operations  0.82 us (1%)
    ppermute x12, starting transfers between devices, shift(): lax.ppermute(value, 'azim', [(i, (i + ahead) % count) for i in range(coun...  15.4 us
    ppermute x12, waiting for transfers between devices, shift(): lax.ppermute(value, 'azim', [(i, (i + ahead) % count) for i in range(coun...  15.1 us
    ppermute x11, starting transfers between devices, swap(): return lax.ppermute(value, GROUP, [(i, i ^ bits) for i in range(8)])  11.5 us
    ppermute x11, waiting for transfers between devices, swap(): return lax.ppermute(value, GROUP, [(i, i ^ bits) for i in range(8)])  4.5 us
    pallas_call x1, Pallas kernels, per_device(): call(functools.partial(forward_kernel, count), [(whole, BF), (block, BF),...  2.28 us
    pallas_call x1, Pallas kernels, per_device(): call(functools.partial(last_kernel, count), [((cols, beams, channels), BF...  1.96 us
    pallas_call x1, Pallas kernels, per_device(): call(functools.partial(backward_kernel, count), [(block, F32), ((count -...  1.85 us
    pallas_call x1, Pallas kernels, per_device(): call(conv_kernel, [(block, F32), (block, BF), (block, BF)], [VMEM] * 6, s...  1.45 us
  transfers between devices with their start and end apart: 23, of which 15 were waited for; matrix products, arithmetic and copies ran while one was open for 0% of the time, Pallas kernels for 4%

profile of v2, /device:TPU:0, one launch (start us, length us, event | category | flops | bytes accessed | tf_op | source)
XLA Modules:
  0.0 57.0 jit_solution(6873282721870998369)
XLA Ops:
  0.6 1.4 %shard_map.95 = (bf16[2,64,256]{2,1,0:T(8,128)(2,1)S(1)}, bf16[2,64,256]{2,1,0:T(8,128)(2,1)S(1)}, f32[8,256]{1,0:T(8,128)S(1)}, bf16[256,256]{1,0:T(8,128)(2,1)...) custom-call(bf16[64,2,256]{2,1,0:T(2,128)(2,1)} %bitcast.60, ...), custom_call_target="tpu_custom_call" | custom-call | tf_op jit(solution)/shard_map/pallas_call | solution.py:362
  2.0 3.0 %collective-permute-start.3 = (bf16[2,64,256]{2,1,0:T(8,128)(2,1)S(1)}, bf16[2,64,256]{2,1,0:T(8,128)(2,1)S(1)}, u32[]{:S(2)}, u32[]{:S(2)}) collective-permute-start(bf16[2,64,256]{2,1,0:T(8,128)(2,1)S(1)} %get-tuple-element.35), channel_id=1, source_target_pairs={{0,2},{1,3},{2,0},{3,1},{4,6},{5,7},{6,4},{7,5},{8,10},{9,11},{10,... | collective-permute-start | bytes 196616 | tf_op jit(solution)/shard_map/ppermute | solution.py:338
  5.0 1.5 %collective-permute-start.4 = (bf16[2,64,256]{2,1,0:T(8,128)(2,1)S(1)}, bf16[2,64,256]{2,1,0:T(8,128)(2,1)S(1)}, u32[]{:S(2)}, u32[]{:S(2)}) collective-permute-start(bf16[2,64,256]{2,1,0:T(8,128)(2,1)S(1)} %get-tuple-element.35), channel_id=1, source_target_pairs={{0,4},{1,5},{2,6},{3,7},{4,0},{5,1},{6,2},{7,3},{8,12},{9,13},{10,... | collective-permute-start | bytes 196616 | tf_op jit(solution)/shard_map/ppermute | solution.py:338
  6.6 0.0 collective-permute-start.5
  6.6 4.1 %collective-permute-start = (bf16[2,64,256]{2,1,0:T(8,128)(2,1)S(1)}, bf16[2,64,256]{2,1,0:T(8,128)(2,1)S(1)}, u32[]{:S(2)}, u32[]{:S(2)}) collective-permute-start(bf16[2,64,256]{2,1,0:T(8,128)(2,1)S(1)} %get-tuple-element.29.refs_1_), channel_id=1, source_target_pairs={{0,24},{8,0},{16,8},{24,16},{1,25},{9,1},{17,9},{25,17},{2,26},{10... | collective-permute-start | bytes 196616 | tf_op jit(solution)/shard_map/ppermute | solution.py:334
  10.6 1.0 %collective-permute-start.2 = (bf16[2,64,256]{2,1,0:T(8,128)(2,1)S(1)}, bf16[2,64,256]{2,1,0:T(8,128)(2,1)S(1)}, u32[]{:S(2)}, u32[]{:S(2)}) collective-permute-start(bf16[2,64,256]{2,1,0:T(8,128)(2,1)S(1)} %get-tuple-element.29.refs_1_), channel_id=1, source_target_pairs={{0,8},{8,16},{16,24},{24,0},{1,9},{9,17},{17,25},{25,1},{2,10},{10... | collective-permute-start | bytes 196616 | tf_op jit(solution)/shard_map/ppermute | solution.py:334
  11.7 0.1 collective-permute-done.5
  11.8 0.1 collective-permute-start.6
  11.8 0.7 %collective-permute-done.refs_2_ = bf16[2,64,256]{2,1,0:T(8,128)(2,1)S(1)} collective-permute-done((bf16[2,64,256]{2,1,0:T(8,128)(2,1)S(1)}, bf16[2,64,256]{2,1,0:T(8,128)(2,1)S(1)}, u32[]{:S(2)}, u32[]{:S(2)}) %collective-permute-start) | collective-permute-done | bytes 65568 | tf_op jit(solution)/shard_map/ppermute | solution.py:334
  12.6 3.2 %collective-permute-done.1.refs_3_ = bf16[2,64,256]{2,1,0:T(8,128)(2,1)S(1)} collective-permute-done((bf16[2,64,256]{2,1,0:T(8,128)(2,1)S(1)}, bf16[2,64,256]{2,1,0:T(8,128)(2,1)S(1)}, u32[]{:S(2)}, u32[]{:S(2)}) %collective-permute-start.1) | collective-permute-done | bytes 65568 | tf_op jit(solution)/shard_map/ppermute | solution.py:334
  15.8 0.9 %collective-permute-done.2.refs_4_ = bf16[2,64,256]{2,1,0:T(8,128)(2,1)S(1)} collective-permute-done((bf16[2,64,256]{2,1,0:T(8,128)(2,1)S(1)}, bf16[2,64,256]{2,1,0:T(8,128)(2,1)S(1)}, u32[]{:S(2)}, u32[]{:S(2)}) %collective-permute-start.2) | collective-permute-done | bytes 65568 | tf_op jit(solution)/shard_map/ppermute | solution.py:334
  16.7 2.3 %shard_map.96 = (bf16[2,256,256]{2,1,0:T(8,128)(2,1)S(1)}, bf16[2,64,256]{2,1,0:T(8,128)(2,1)S(1)}, bf16[2,256,256]{2,1,0:T(8,128)(2,1)S(1)}, bf16[2,256,256]{2,...) custom-call(f32[8,256]{1,0:T(8,128)S(1)} %get-tuple-element.28.refs_, ...), custom_call_target="tpu_custom_call" | custom-call | tf_op jit(solution)/shard_map/pallas_call | solution.py:385
  19.0 0.0 collective-permute-done.6.odd_ref
  19.0 0.4 shard_map.97
  19.4 1.5 %collective-permute-start.8 = (bf16[320,128]{1,0:T(8,128)(2,1)S(1)}, bf16[320,128]{1,0:T(8,128)(2,1)S(1)}, u32[]{:S(2)}, u32[]{:S(2)}) collective-permute-start(bf16[320,128]{1,0:T(8,128)(2,1)S(1)} %pad_maximum_fusion.4), channel_id=1, source_target_pairs={{0,16},{8,24},{16,0},{24,8},{1,17},{9,25},{17,1},{25,9},{2,18},{10... | collective-permute-start | bytes 245768 | tf_op jit(solution)/shard_map/ppermute | solution.py:334
  20.9 0.8 %collective-permute-start.7 = (bf16[352,128]{1,0:T(8,128)(2,1)S(1)}, bf16[352,128]{1,0:T(8,128)(2,1)S(1)}, u32[]{:S(2)}, u32[]{:S(2)}) collective-permute-start(bf16[352,128]{1,0:T(8,128)(2,1)S(1)} %get-tuple-element.72), channel_id=1, source_target_pairs={{0,24},{8,0},{16,8},{24,16},{1,25},{9,1},{17,9},{25,17},{2,26},{10... | collective-permute-start | bytes 270344 | tf_op jit(solution)/shard_map/ppermute | solution.py:334
  21.7 1.3 %collective-permute-start.9 = (bf16[352,128]{1,0:T(8,128)(2,1)S(1)}, bf16[352,128]{1,0:T(8,128)(2,1)S(1)}, u32[]{:S(2)}, u32[]{:S(2)}) collective-permute-start(bf16[352,128]{1,0:T(8,128)(2,1)S(1)} %get-tuple-element.73), channel_id=1, source_target_pairs={{0,8},{8,16},{16,24},{24,0},{1,9},{9,17},{17,25},{25,1},{2,10},{10... | collective-permute-start | bytes 270344 | tf_op jit(solution)/shard_map/ppermute | solution.py:334
  23.0 3.6 %collective-permute-done.8.refs_4_ = bf16[320,128]{1,0:T(8,128)(2,1)S(1)} collective-permute-done((bf16[320,128]{1,0:T(8,128)(2,1)S(1)}, bf16[320,128]{1,0:T(8,128)(2,1)S(1)}, u32[]{:S(2)}, u32[]{:S(2)}) %collective-permute-start.8) | collective-permute-done | bytes 81952 | tf_op jit(solution)/shard_map/ppermute | solution.py:334
  26.5 0.7 %collective-permute-done.7.above_ref.refs_3_ = bf16[352,128]{1,0:T(8,128)(2,1)S(1)} collective-permute-done((bf16[352,128]{1,0:T(8,128)(2,1)S(1)}, bf16[352,128]{1,0:T(8,128)(2,1)S(1)}, u32[]{:S(2)}, u32[]{:S(2)}) %collective-permute-start.7) | collective-permute-done | bytes 90144 | tf_op jit(solution)/shard_map/ppermute | solution.py:334
  27.2 0.9 %collective-permute-done.9.below_ref.refs_5_ = bf16[352,128]{1,0:T(8,128)(2,1)S(1)} collective-permute-done((bf16[352,128]{1,0:T(8,128)(2,1)S(1)}, bf16[352,128]{1,0:T(8,128)(2,1)S(1)}, u32[]{:S(2)}, u32[]{:S(2)}) %collective-permute-start.9) | collective-permute-done | bytes 90144 | tf_op jit(solution)/shard_map/ppermute | solution.py:334
  28.1 1.5 %shard_map.98 = (f32[2,64,256]{2,1,0:T(8,128)S(1)}, bf16[2,64,256]{2,1,0:T(8,128)(2,1)S(1)}, bf16[2,64,256]{2,1,0:T(8,128)(2,1)S(1)}) custom-call(bf16[4,2,64,256]{3,2,1,0:T(8,128)(2,1)S(1)} %pad_maximum_fusion.even_ref, bf16[4,2,64,256]{3,2,1,0:T(8,128)(2,1)S(1)} %collective-permute-done.6.odd_ref, ...), custom_call_target="tpu_custom_call" | custom-call | tf_op jit(solution)/shard_map/pallas_call | solution.py:407
  29.6 1.9 %shard_map.99 = (f32[2,64,256]{2,1,0:T(8,128)S(1)}, bf16[3,2,64,256]{3,2,1,0:T(8,128)(2,1)S(1)}, bf16[4,128,256]{2,1,0:T(8,128)(2,1)S(1)}, bf16[4,128,256]{2,1,0:T(8,128)(2,1)S(1)}) custom-call(f32[8,256]{1,0:T(8,128)S(1)} %get-tuple-element.28.refs_0_.allowed_ref, bf16[2,256,256]{2,1,0:T(8,128)(2,1)S(1)} %get-tuple-element.39.all_ref, ...), custom_call_target="tpu_custom_call" | custom-call | tf_op jit(solution)/shard_map/pallas_call | solution.py:419
  31.4 0.1 collective-permute-start.14
  31.6 1.6 %collective-permute-start.10 = (bf16[4,64,128]{2,1,0:T(8,128)(2,1)S(1)}, bf16[4,64,128]{2,1,0:T(8,128)(2,1)S(1)}, u32[]{:S(2)}, u32[]{:S(2)}) collective-permute-start(bf16[4,64,128]{2,1,0:T(8,128)(2,1)S(1)} %get-tuple-element.67), channel_id=1, source_target_pairs={{0,2},{1,3},{2,0},{3,1},{4,6},{5,7},{6,4},{7,5},{8,10},{9,11},{10,... | collective-permute-start | bytes 196616 | tf_op jit(solution)/shard_map/ppermute | solution.py:338
  33.1 1.5 %collective-permute-start.11 = (bf16[4,64,128]{2,1,0:T(8,128)(2,1)S(1)}, bf16[4,64,128]{2,1,0:T(8,128)(2,1)S(1)}, u32[]{:S(2)}, u32[]{:S(2)}) collective-permute-start(bf16[4,64,128]{2,1,0:T(8,128)(2,1)S(1)} %get-tuple-element.67), channel_id=1, source_target_pairs={{0,4},{1,5},{2,6},{3,7},{4,0},{5,1},{6,2},{7,3},{8,12},{9,13},{10,... | collective-permute-start | bytes 196616 | tf_op jit(solution)/shard_map/ppermute | solution.py:338
  34.6 0.5 collective-permute-start.12
  35.1 0.0 collective-permute-done.14
  35.1 0.1 add_convert_fusion
  35.2 1.6 %collective-permute-start.15 = (bf16[2,128,256]{2,1,0:T(8,128)(2,1)S(1)}, bf16[2,128,256]{2,1,0:T(8,128)(2,1)S(1)}, u32[]{:S(2)}, u32[]{:S(2)}) collective-permute-start(bf16[2,128,256]{2,1,0:T(8,128)(2,1)S(1)} %slice_bitcast_fusion), channel_id=1, source_target_pairs={{0,2},{1,3},{2,0},{3,1},{4,6},{5,7},{6,4},{7,5},{8,10},{9,11},{10,... | collective-permute-start | bytes 393224 | tf_op jit(solution)/shard_map/ppermute | solution.py:338
  36.8 0.0 collective-permute-done.10
  36.8 0.6 %collective-permute-done.11 = bf16[4,64,128]{2,1,0:T(8,128)(2,1)S(1)} collective-permute-done((bf16[4,64,128]{2,1,0:T(8,128)(2,1)S(1)}, bf16[4,64,128]{2,1,0:T(8,128)(2,1)S(1)}, u32[]{:S(2)}, u32[]{:S(2)}) %collective-permute-start.11) | collective-permute-done | bytes 65568 | tf_op jit(solution)/shard_map/ppermute | solution.py:338
  37.4 3.1 %collective-permute-done.12 = bf16[4,64,128]{2,1,0:T(8,128)(2,1)S(1)} collective-permute-done((bf16[4,64,128]{2,1,0:T(8,128)(2,1)S(1)}, bf16[4,64,128]{2,1,0:T(8,128)(2,1)S(1)}, u32[]{:S(2)}, u32[]{:S(2)}) %collective-permute-start.12) | collective-permute-done | bytes 65568 | tf_op jit(solution)/shard_map/ppermute | solution.py:338
  40.6 0.1 collective-permute-start.13
  40.6 0.7 %collective-permute-done.15 = bf16[2,128,256]{2,1,0:T(8,128)(2,1)S(1)} collective-permute-done((bf16[2,128,256]{2,1,0:T(8,128)(2,1)S(1)}, bf16[2,128,256]{2,1,0:T(8,128)(2,1)S(1)}, u32[]{:S(2)}, u32[]{:S(2)}) %collective-permute-start.15) | collective-permute-done | bytes 131104 | tf_op jit(solution)/shard_map/ppermute | solution.py:338
  41.4 1.6 %collective-permute-start.16 = (bf16[128,256]{1,0:T(8,128)(2,1)S(1)}, bf16[128,256]{1,0:T(8,128)(2,1)S(1)}, u32[]{:S(2)}, u32[]{:S(2)}) collective-permute-start(bf16[128,256]{1,0:T(8,128)(2,1)S(1)} %get-tuple-element.61), channel_id=1, source_target_pairs={{0,4},{1,5},{2,6},{3,7},{4,0},{5,1},{6,2},{7,3},{8,12},{9,13},{10,... | collective-permute-start | bytes 196616 | tf_op jit(solution)/shard_map/ppermute | solution.py:338
  43.0 0.9 %collective-permute-start.20 = (bf16[2,64,256]{2,1,0:T(8,128)(2,1)S(1)}, bf16[2,64,256]{2,1,0:T(8,128)(2,1)S(1)}, u32[]{:S(2)}, u32[]{:S(2)}) collective-permute-start(bf16[2,64,256]{2,1,0:T(8,128)(2,1)S(1)} %get-tuple-element.60), channel_id=1, source_target_pairs={{0,8},{8,16},{16,24},{24,0},{1,9},{9,17},{17,25},{25,1},{2,10},{10... | collective-permute-start | bytes 196616 | tf_op jit(solution)/shard_map/ppermute | solution.py:334
  43.9 1.6 %collective-permute-start.21 = (bf16[2,64,256]{2,1,0:T(8,128)(2,1)S(1)}, bf16[2,64,256]{2,1,0:T(8,128)(2,1)S(1)}, u32[]{:S(2)}, u32[]{:S(2)}) collective-permute-start(bf16[2,64,256]{2,1,0:T(8,128)(2,1)S(1)} %get-tuple-element.59), channel_id=1, source_target_pairs={{0,16},{8,24},{16,0},{24,8},{1,17},{9,25},{17,1},{25,9},{2,18},{10... | collective-permute-start | bytes 196616 | tf_op jit(solution)/shard_map/ppermute | solution.py:334
  45.4 2.3 %collective-permute-start.22 = (bf16[2,64,256]{2,1,0:T(8,128)(2,1)S(1)}, bf16[2,64,256]{2,1,0:T(8,128)(2,1)S(1)}, u32[]{:S(2)}, u32[]{:S(2)}) collective-permute-start(bf16[2,64,256]{2,1,0:T(8,128)(2,1)S(1)} %get-tuple-element.58), channel_id=1, source_target_pairs={{0,24},{8,0},{16,8},{24,16},{1,25},{9,1},{17,9},{25,17},{2,26},{10... | collective-permute-start | bytes 196616 | tf_op jit(solution)/shard_map/ppermute | solution.py:334
  47.8 0.1 shard_map.100.refs_6_
  47.9 0.1 collective-permute-start.17
  48.0 1.2 %collective-permute-done.20.refs_11_ = bf16[2,64,256]{2,1,0:T(8,128)(2,1)S(1)} collective-permute-done((bf16[2,64,256]{2,1,0:T(8,128)(2,1)S(1)}, bf16[2,64,256]{2,1,0:T(8,128)(2,1)S(1)}, u32[]{:S(2)}, u32[]{:S(2)}) %collective-permute-start.20) | collective-permute-done | bytes 65568 | tf_op jit(solution)/shard_map/ppermute | solution.py:334
  49.2 0.3 collective-permute-start.18
  49.5 1.8 %collective-permute-done.21.refs_12_ = bf16[2,64,256]{2,1,0:T(8,128)(2,1)S(1)} collective-permute-done((bf16[2,64,256]{2,1,0:T(8,128)(2,1)S(1)}, bf16[2,64,256]{2,1,0:T(8,128)(2,1)S(1)}, u32[]{:S(2)}, u32[]{:S(2)}) %collective-permute-start.21) | collective-permute-done | bytes 65568 | tf_op jit(solution)/shard_map/ppermute | solution.py:334
  51.3 1.6 %collective-permute-start.19 = (bf16[64,128]{1,0:T(8,128)(2,1)S(1)}, bf16[64,128]{1,0:T(8,128)(2,1)S(1)}, u32[]{:S(2)}, u32[]{:S(2)}) collective-permute-start(bf16[64,128]{1,0:T(8,128)(2,1)S(1)} %get-tuple-element.63), channel_id=1, source_target_pairs={{0,24},{8,0},{16,8},{24,16},{1,25},{9,1},{17,9},{25,17},{2,26},{10... | collective-permute-start | bytes 49160 | tf_op jit(solution)/shard_map/ppermute | solution.py:334
  52.9 0.6 %collective-permute-done.17.refs_7_ = bf16[64,128]{1,0:T(8,128)(2,1)S(1)} collective-permute-done((bf16[64,128]{1,0:T(8,128)(2,1)S(1)}, bf16[64,128]{1,0:T(8,128)(2,1)S(1)}, u32[]{:S(2)}, u32[]{:S(2)}) %collective-permute-start.17) | collective-permute-done | bytes 16416 | tf_op jit(solution)/shard_map/ppermute | solution.py:334
  53.5 0.4 collective-permute-done.18.refs_8_
  53.9 1.2 %collective-permute-done.19.refs_9_ = bf16[64,128]{1,0:T(8,128)(2,1)S(1)} collective-permute-done((bf16[64,128]{1,0:T(8,128)(2,1)S(1)}, bf16[64,128]{1,0:T(8,128)(2,1)S(1)}, u32[]{:S(2)}, u32[]{:S(2)}) %collective-permute-start.19) | collective-permute-done | bytes 16416 | tf_op jit(solution)/shard_map/ppermute | solution.py:334
  55.0 2.0 %shard_map.101 = (bf16[64,2,256]{2,1,0:T(2,128)(2,1)}, f32[31,32,64]{2,1,0:T(8,128)}) custom-call(bf16[4,4,64,128]{3,2,1,0:T(8,128)(2,1)S(1)} %pad_maximum_fusion.1.refs_0_, bf16[4,4,64,128]{3,2,1,0:T(8,128)(2,1)S(1)} %collective-permute-done.13.refs_1_, bf16[256,128]{1,0:T(8,128)(2,1)S(1)} %get-tuple-element.36.refs_2_, ...), custom_call_target="tpu_custom_call" | custom-call | tf_op jit(solution)/shard_map/pallas_call | solution.py:442
  (20 shorter events, 0.2 us)
Async XLA Ops:
  2.0 8.6 %collective-permute-start.3 = (bf16[2,64,256]{2,1,0:T(8,128)(2,1)S(1)}, bf16[2,64,256]{2,1,0:T(8,128)(2,1)S(1)}, u32[]{:S(2)}, u32[]{:S(2)}) collective-permute-start(bf16[2,64,256]{2,1,0:T(8,128)(2,1)S(1)} %get-tuple-element.35), channel_id=1, source_target_pairs={{0,2},{1,3},{2,0},{3,1},{4,6},{5,7},{6,4},{7,5},{8,10},{9,11},{10,... | collective-permute-start | bytes 196616 | tf_op jit(solution)/shard_map/ppermute | solution.py:338
  5.0 6.6 %collective-permute-start.4 = (bf16[2,64,256]{2,1,0:T(8,128)(2,1)S(1)}, bf16[2,64,256]{2,1,0:T(8,128)(2,1)S(1)}, u32[]{:S(2)}, u32[]{:S(2)}) collective-permute-start(bf16[2,64,256]{2,1,0:T(8,128)(2,1)S(1)} %get-tuple-element.35), channel_id=1, source_target_pairs={{0,4},{1,5},{2,6},{3,7},{4,0},{5,1},{6,2},{7,3},{8,12},{9,13},{10,... | collective-permute-start | bytes 196616 | tf_op jit(solution)/shard_map/ppermute | solution.py:338
  6.6 5.2 %collective-permute-start.5 = (bf16[2,64,256]{2,1,0:T(8,128)(2,1)S(1)}, bf16[2,64,256]{2,1,0:T(8,128)(2,1)S(1)}, u32[]{:S(2)}, u32[]{:S(2)}) collective-permute-start(bf16[2,64,256]{2,1,0:T(8,128)(2,1)S(1)} %get-tuple-element.35), channel_id=1, source_target_pairs={{0,6},{1,7},{2,4},{3,5},{4,2},{5,3},{6,0},{7,1},{8,14},{9,15},{10,... | collective-permute-start | bytes 196616 | tf_op jit(solution)/shard_map/ppermute | solution.py:338
  6.6 6.0 %collective-permute-start = (bf16[2,64,256]{2,1,0:T(8,128)(2,1)S(1)}, bf16[2,64,256]{2,1,0:T(8,128)(2,1)S(1)}, u32[]{:S(2)}, u32[]{:S(2)}) collective-permute-start(bf16[2,64,256]{2,1,0:T(8,128)(2,1)S(1)} %get-tuple-element.29.refs_1_), channel_id=1, source_target_pairs={{0,24},{8,0},{16,8},{24,16},{1,25},{9,1},{17,9},{25,17},{2,26},{10... | collective-permute-start | bytes 196616 | tf_op jit(solution)/shard_map/ppermute | solution.py:334
  10.6 5.2 %collective-permute-start.1 = (bf16[2,64,256]{2,1,0:T(8,128)(2,1)S(1)}, bf16[2,64,256]{2,1,0:T(8,128)(2,1)S(1)}, u32[]{:S(2)}, u32[]{:S(2)}) collective-permute-start(bf16[2,64,256]{2,1,0:T(8,128)(2,1)S(1)} %get-tuple-element.29.refs_1_), channel_id=1, source_target_pairs={{0,16},{8,24},{16,0},{24,8},{1,17},{9,25},{17,1},{25,9},{2,18},{10... | collective-permute-start | bytes 196616 | tf_op jit(solution)/shard_map/ppermute | solution.py:334
  10.6 6.1 %collective-permute-start.2 = (bf16[2,64,256]{2,1,0:T(8,128)(2,1)S(1)}, bf16[2,64,256]{2,1,0:T(8,128)(2,1)S(1)}, u32[]{:S(2)}, u32[]{:S(2)}) collective-permute-start(bf16[2,64,256]{2,1,0:T(8,128)(2,1)S(1)} %get-tuple-element.29.refs_1_), channel_id=1, source_target_pairs={{0,8},{8,16},{16,24},{24,0},{1,9},{9,17},{17,25},{25,1},{2,10},{10... | collective-permute-start | bytes 196616 | tf_op jit(solution)/shard_map/ppermute | solution.py:334
  11.8 7.3 %collective-permute-start.6 = (bf16[4,2,64,256]{3,2,1,0:T(8,128)(2,1)S(1)}, bf16[4,2,64,256]{3,2,1,0:T(8,128)(2,1)S(1)}, u32[]{:S(2)}, u32[]{:S(2)}) collective-permute-start(bf16[4,2,64,256]{3,2,1,0:T(8,128)(2,1)S(1)} %pad_maximum_fusion.even_ref), channel_id=1, source_target_pairs={{0,1},{1,0},{2,3},{3,2},{4,5},{5,4},{6,7},{7,6},{8,9},{9,8},{10,11... | collective-permute-start | bytes 786440 | tf_op jit(solution)/shard_map/ppermute | solution.py:338
  19.4 7.1 %collective-permute-start.8 = (bf16[320,128]{1,0:T(8,128)(2,1)S(1)}, bf16[320,128]{1,0:T(8,128)(2,1)S(1)}, u32[]{:S(2)}, u32[]{:S(2)}) collective-permute-start(bf16[320,128]{1,0:T(8,128)(2,1)S(1)} %pad_maximum_fusion.4), channel_id=1, source_target_pairs={{0,16},{8,24},{16,0},{24,8},{1,17},{9,25},{17,1},{25,9},{2,18},{10... | collective-permute-start | bytes 245768 | tf_op jit(solution)/shard_map/ppermute | solution.py:334
  20.9 6.3 %collective-permute-start.7 = (bf16[352,128]{1,0:T(8,128)(2,1)S(1)}, bf16[352,128]{1,0:T(8,128)(2,1)S(1)}, u32[]{:S(2)}, u32[]{:S(2)}) collective-permute-start(bf16[352,128]{1,0:T(8,128)(2,1)S(1)} %get-tuple-element.72), channel_id=1, source_target_pairs={{0,24},{8,0},{16,8},{24,16},{1,25},{9,1},{17,9},{25,17},{2,26},{10... | collective-permute-start | bytes 270344 | tf_op jit(solution)/shard_map/ppermute | solution.py:334
  21.7 6.4 %collective-permute-start.9 = (bf16[352,128]{1,0:T(8,128)(2,1)S(1)}, bf16[352,128]{1,0:T(8,128)(2,1)S(1)}, u32[]{:S(2)}, u32[]{:S(2)}) collective-permute-start(bf16[352,128]{1,0:T(8,128)(2,1)S(1)} %get-tuple-element.73), channel_id=1, source_target_pairs={{0,8},{8,16},{16,24},{24,0},{1,9},{9,17},{17,25},{25,1},{2,10},{10... | collective-permute-start | bytes 270344 | tf_op jit(solution)/shard_map/ppermute | solution.py:334
  31.4 3.7 %collective-permute-start.14 = (bf16[4,128,256]{2,1,0:T(8,128)(2,1)S(1)}, bf16[4,128,256]{2,1,0:T(8,128)(2,1)S(1)}, u32[]{:S(2)}, u32[]{:S(2)}) collective-permute-start(bf16[4,128,256]{2,1,0:T(8,128)(2,1)S(1)} %get-tuple-element.49), channel_id=1, source_target_pairs={{0,1},{1,0},{2,3},{3,2},{4,5},{5,4},{6,7},{7,6},{8,9},{9,8},{10,11... | collective-permute-start | bytes 786440 | tf_op jit(solution)/shard_map/ppermute | solution.py:338
  31.6 5.2 %collective-permute-start.10 = (bf16[4,64,128]{2,1,0:T(8,128)(2,1)S(1)}, bf16[4,64,128]{2,1,0:T(8,128)(2,1)S(1)}, u32[]{:S(2)}, u32[]{:S(2)}) collective-permute-start(bf16[4,64,128]{2,1,0:T(8,128)(2,1)S(1)} %get-tuple-element.67), channel_id=1, source_target_pairs={{0,2},{1,3},{2,0},{3,1},{4,6},{5,7},{6,4},{7,5},{8,10},{9,11},{10,... | collective-permute-start | bytes 196616 | tf_op jit(solution)/shard_map/ppermute | solution.py:338
  33.1 4.3 %collective-permute-start.11 = (bf16[4,64,128]{2,1,0:T(8,128)(2,1)S(1)}, bf16[4,64,128]{2,1,0:T(8,128)(2,1)S(1)}, u32[]{:S(2)}, u32[]{:S(2)}) collective-permute-start(bf16[4,64,128]{2,1,0:T(8,128)(2,1)S(1)} %get-tuple-element.67), channel_id=1, source_target_pairs={{0,4},{1,5},{2,6},{3,7},{4,0},{5,1},{6,2},{7,3},{8,12},{9,13},{10,... | collective-permute-start | bytes 196616 | tf_op jit(solution)/shard_map/ppermute | solution.py:338
  34.6 5.9 %collective-permute-start.12 = (bf16[4,64,128]{2,1,0:T(8,128)(2,1)S(1)}, bf16[4,64,128]{2,1,0:T(8,128)(2,1)S(1)}, u32[]{:S(2)}, u32[]{:S(2)}) collective-permute-start(bf16[4,64,128]{2,1,0:T(8,128)(2,1)S(1)} %get-tuple-element.67), channel_id=1, source_target_pairs={{0,6},{1,7},{2,4},{3,5},{4,2},{5,3},{6,0},{7,1},{8,14},{9,15},{10,... | collective-permute-start | bytes 196616 | tf_op jit(solution)/shard_map/ppermute | solution.py:338
  35.2 6.1 %collective-permute-start.15 = (bf16[2,128,256]{2,1,0:T(8,128)(2,1)S(1)}, bf16[2,128,256]{2,1,0:T(8,128)(2,1)S(1)}, u32[]{:S(2)}, u32[]{:S(2)}) collective-permute-start(bf16[2,128,256]{2,1,0:T(8,128)(2,1)S(1)} %slice_bitcast_fusion), channel_id=1, source_target_pairs={{0,2},{1,3},{2,0},{3,1},{4,6},{5,7},{6,4},{7,5},{8,10},{9,11},{10,... | collective-permute-start | bytes 393224 | tf_op jit(solution)/shard_map/ppermute | solution.py:338
  40.6 12.3 %collective-permute-start.13 = (bf16[4,4,64,128]{3,2,1,0:T(8,128)(2,1)S(1)}, bf16[4,4,64,128]{3,2,1,0:T(8,128)(2,1)S(1)}, u32[]{:S(2)}, u32[]{:S(2)}) collective-permute-start(bf16[4,4,64,128]{3,2,1,0:T(8,128)(2,1)S(1)} %pad_maximum_fusion.1.refs_0_), channel_id=1, source_target_pairs={{0,1},{1,0},{2,3},{3,2},{4,5},{5,4},{6,7},{7,6},{8,9},{9,8},{10,11... | collective-permute-start | bytes 786440 | tf_op jit(solution)/shard_map/ppermute | solution.py:338
  41.4 6.4 %collective-permute-start.16 = (bf16[128,256]{1,0:T(8,128)(2,1)S(1)}, bf16[128,256]{1,0:T(8,128)(2,1)S(1)}, u32[]{:S(2)}, u32[]{:S(2)}) collective-permute-start(bf16[128,256]{1,0:T(8,128)(2,1)S(1)} %get-tuple-element.61), channel_id=1, source_target_pairs={{0,4},{1,5},{2,6},{3,7},{4,0},{5,1},{6,2},{7,3},{8,12},{9,13},{10,... | collective-permute-start | bytes 196616 | tf_op jit(solution)/shard_map/ppermute | solution.py:338
  43.0 6.2 %collective-permute-start.20 = (bf16[2,64,256]{2,1,0:T(8,128)(2,1)S(1)}, bf16[2,64,256]{2,1,0:T(8,128)(2,1)S(1)}, u32[]{:S(2)}, u32[]{:S(2)}) collective-permute-start(bf16[2,64,256]{2,1,0:T(8,128)(2,1)S(1)} %get-tuple-element.60), channel_id=1, source_target_pairs={{0,8},{8,16},{16,24},{24,0},{1,9},{9,17},{17,25},{25,1},{2,10},{10... | collective-permute-start | bytes 196616 | tf_op jit(solution)/shard_map/ppermute | solution.py:334
  43.9 7.4 %collective-permute-start.21 = (bf16[2,64,256]{2,1,0:T(8,128)(2,1)S(1)}, bf16[2,64,256]{2,1,0:T(8,128)(2,1)S(1)}, u32[]{:S(2)}, u32[]{:S(2)}) collective-permute-start(bf16[2,64,256]{2,1,0:T(8,128)(2,1)S(1)} %get-tuple-element.59), channel_id=1, source_target_pairs={{0,16},{8,24},{16,0},{24,8},{1,17},{9,25},{17,1},{25,9},{2,18},{10... | collective-permute-start | bytes 196616 | tf_op jit(solution)/shard_map/ppermute | solution.py:334
  45.4 7.5 %collective-permute-start.22 = (bf16[2,64,256]{2,1,0:T(8,128)(2,1)S(1)}, bf16[2,64,256]{2,1,0:T(8,128)(2,1)S(1)}, u32[]{:S(2)}, u32[]{:S(2)}) collective-permute-start(bf16[2,64,256]{2,1,0:T(8,128)(2,1)S(1)} %get-tuple-element.58), channel_id=1, source_target_pairs={{0,24},{8,0},{16,8},{24,16},{1,25},{9,1},{17,9},{25,17},{2,26},{10... | collective-permute-start | bytes 196616 | tf_op jit(solution)/shard_map/ppermute | solution.py:334
  47.9 5.6 %collective-permute-start.17 = (bf16[64,128]{1,0:T(8,128)(2,1)S(1)}, bf16[64,128]{1,0:T(8,128)(2,1)S(1)}, u32[]{:S(2)}, u32[]{:S(2)}) collective-permute-start(bf16[64,128]{1,0:T(8,128)(2,1)S(1)} %get-tuple-element.65), channel_id=1, source_target_pairs={{0,8},{8,16},{16,24},{24,0},{1,9},{9,17},{17,25},{25,1},{2,10},{10... | collective-permute-start | bytes 49160 | tf_op jit(solution)/shard_map/ppermute | solution.py:334
  49.2 4.7 %collective-permute-start.18 = (bf16[64,128]{1,0:T(8,128)(2,1)S(1)}, bf16[64,128]{1,0:T(8,128)(2,1)S(1)}, u32[]{:S(2)}, u32[]{:S(2)}) collective-permute-start(bf16[64,128]{1,0:T(8,128)(2,1)S(1)} %get-tuple-element.64), channel_id=1, source_target_pairs={{0,16},{8,24},{16,0},{24,8},{1,17},{9,25},{17,1},{25,9},{2,18},{10... | collective-permute-start | bytes 49160 | tf_op jit(solution)/shard_map/ppermute | solution.py:334
  51.3 3.7 %collective-permute-start.19 = (bf16[64,128]{1,0:T(8,128)(2,1)S(1)}, bf16[64,128]{1,0:T(8,128)(2,1)S(1)}, u32[]{:S(2)}, u32[]{:S(2)}) collective-permute-start(bf16[64,128]{1,0:T(8,128)(2,1)S(1)} %get-tuple-element.63), channel_id=1, source_target_pairs={{0,24},{8,0},{16,8},{24,16},{1,25},{9,1},{17,9},{25,17},{2,26},{10... | collective-permute-start | bytes 49160 | tf_op jit(solution)/shard_map/ppermute | solution.py:334

commit v3 on v2

--- a/solution.py
+++ b/solution.py
@@ -74,17 +74,17 @@
     keys = allowed_out.shape[1]
     sector = lax.broadcasted_iota(jnp.int32, (count, keys), 0)
     block = lax.broadcasted_iota(jnp.int32, (count, keys), 1) // SECTOR
-    spread = jnp.where(sector == lax.rem(block + me, count), 1.0, 0.0).astype(BF)
+    spread = jnp.where(sector == block ^ me, 1.0, 0.0).astype(BF)
     allowed_out[...] = dot(jnp.broadcast_to(own, (8, count)).astype(BF), spread)
     for copy in copies[3:]:
         copy.wait()
 
 
-def slices_kernel(even_ref, odd_ref, slices_out, first_out, last_out):
+def slices_kernel(even_ref, odd_ref, slices_out, edges_out):
     me = group_index()
     _, beams, cols, channels = even_ref.shape
     width = channels // 8
-    for out, col in ((first_out, 0), (last_out, cols - 1)):
+    for side, col in enumerate((0, cols - 1)):
         base = col // 16 * 16
         rows = []
         for ref in (even_ref, odd_ref):
@@ -92,10 +92,7 @@
                 for b in range(beams):
                     part = ref[block, b, base : base + 16, :].astype(F32)
                     rows.append(part[col - base : col - base + 1])
-        edge = jnp.concatenate(rows, axis=0).astype(BF)
-        count = edge.shape[0]
-        for half in range(out.shape[0] // count):
-            out[half * count : (half + 1) * count] = edge[:, half * LANES : (half + 1) * LANES]
+        edges_out[side] = jnp.concatenate(rows, axis=0).astype(BF)
     channel = lax.broadcasted_iota(jnp.int32, (channels, 4 * width), 0) - width * me
     lane = lax.broadcasted_iota(jnp.int32, (channels, 4 * width), 1)
     total = [None] * 4
@@ -113,19 +110,26 @@
         slices_out[cols * s : cols * (s + 1), :] = total[s].astype(BF)
 
 
-def conv_kernel(even_ref, odd_ref, below_ref, above_ref, w_ref, w_out_ref, layer_out, layer_bf_out, attended_out,
-                padded, edges, shifted):
+def neighbour_distances(count):
+    return [distance for distance in range(1, count) if distance & (distance + 1) == 0]
+
+
+def conv_kernel(count, even_ref, odd_ref, *refs):
+    distances = neighbour_distances(count)
+    edge_refs = refs[: len(distances)]
+    w_ref, w_out_ref, layer_out, layer_bf_out, attended_out, padded, edges, shifted = refs[len(distances) :]
     me = group_index()
+    column = lax.axis_index("azim")
     sweep = lax.axis_index("sweep")
     beam = lax.axis_index("beam")
     _, beams, cols, channels = even_ref.shape
-    count = 8 * beams
-    start = below_ref.shape[0] - count * (channels // LANES)
-    for index, ref in enumerate((below_ref, above_ref)):
-        for half in range(channels // LANES):
-            edges[index, :, half * LANES : (half + 1) * LANES] = ref[
-                start + half * count : start + (half + 1) * count, :
-            ].astype(F32)
+    for index, step in enumerate((count - 1, 1)):
+        partner = lax.rem(column + step, count) ^ column
+        total = None
+        for distance, ref in zip(distances, edge_refs):
+            part = ref[1 - index].astype(F32) * jnp.where(partner == distance, 1.0, 0.0)
+            total = part if total is None else total + part
+        edges[index] = total
     for j in range(3):
         other_sweep = sweep + (j - 1)
         sweep_ok = (other_sweep >= 0) & (other_sweep < 4)
@@ -211,7 +215,7 @@
         spare = pieces_out.shape[2] - beams * width
         if spare:
             part.append(jnp.zeros((cols, spare), F32))
-        pieces_out[lax.rem(owner + count - me, count)] = jnp.concatenate(part, axis=1).astype(BF)
+        pieces_out[owner ^ me] = jnp.concatenate(part, axis=1).astype(BF)
     copy.wait()
 
 
@@ -242,7 +246,11 @@
     spread = spread.reshape(beams, count, cols, channels)
     base_out[...] = own + spread[:, 0]
     for ahead in range(1, count):
-        send_out[ahead - 1] = spread[:, ahead].astype(BF)
+        part = spread[:, ahead].astype(BF).reshape(beams * cols, channels)
+        for half in range(channels // LANES):
+            send_out[ahead - 1, half * beams * cols : (half + 1) * beams * cols, :] = part[
+                :, half * LANES : (half + 1) * LANES
+            ]
     every = all_ref[...].reshape(all_rows, channels)
     mine = all_ref[:, :cols, :].reshape(own_rows, channels)
     width = channels // 8
@@ -259,52 +267,55 @@
     for differ in range(8):
         target = pass_out if differ & 1 else keep_out
         for index in range(4):
-            target[differ >> 1, index * width : (index + 1) * width, :] = sums[index, me ^ differ]
-
-
-def pieces_kernel(count, keep_ref, come_ref, pieces_out):
+            part = sums[index, me ^ differ]
+            for half in range(channels // LANES):
+                row = (half * 4 + index) * width
+                target[differ >> 1, row : row + width, :] = part[:, half * LANES : (half + 1) * LANES]
+
+
+def pieces_kernel(count, keep_ref, *refs):
+    pieces_out = refs[-1]
     me = lax.axis_index("azim")
-    total = keep_ref[...].astype(F32) + come_ref[...].astype(F32)
-    rows, channels = total.shape
-    width = channels // count
+    rows = keep_ref.shape[0]
+    total = keep_ref[...].astype(F32)
+    for ref in refs[:-1]:
+        total = total + ref[ref.shape[0] - rows :, :].astype(F32)
+    halves = 2
+    rows = rows // halves
+    total = jnp.concatenate([total[half * rows : (half + 1) * rows] for half in range(halves)], axis=1)
+    width = total.shape[1] // count
     half = rows // 2
     for owner in range(count):
         part = total[:, owner * width : (owner + 1) * width]
-        pieces_out[lax.rem(owner + count - me, count)] = jnp.concatenate([part[:half], part[half:]], axis=1).astype(BF)
-
-
-def last_kernel(count, *refs):
-    even_ref, odd_ref, own_ref = refs[:3]
-    packed_refs = refs[3 : 2 + count]
-    own_piece = refs[2 + count]
-    piece_refs = refs[3 + count : 2 + 2 * count]
-    base_ref = refs[2 + 2 * count]
-    come_refs = refs[3 + 2 * count : 2 + 3 * count]
-    features_out, weights_out, layers, turned = refs[2 + 3 * count :]
+        part = [part[:half], part[half:]]
+        spare = pieces_out.shape[2] - 2 * width
+        if spare:
+            part.append(jnp.zeros((half, spare), F32))
+        pieces_out[owner ^ me] = jnp.concatenate(part, axis=1).astype(BF)
+
+
+def taps_kernel(count, even_ref, odd_ref, own_ref, *refs):
+    packed_refs = refs[: count - 1]
+    taps_out, layers, turned, held = refs[count - 1 :]
     me = group_index()
-    total = base_ref[...]
-    for ref in come_refs:
-        total = total + ref[...].astype(F32)
-    features_out[...] = jnp.stack([total[b] for b in range(total.shape[0])], axis=1).astype(BF)
-    piece = own_piece[0].astype(F32)
-    for ref in piece_refs:
-        piece = piece + ref[...].astype(F32)
-    lanes = piece.shape[1] // 2
-    width = piece.shape[0] // 2
-    for index in range(4):
-        weights_out[index] = piece[
-            (index % 2) * width : (index % 2 + 1) * width, (index // 2) * lanes : (index // 2 + 1) * lanes
-        ]
+    column = lax.axis_index("azim")
+    lanes = taps_out.shape[2]
+    width = taps_out.shape[1]
     per_sweep, rows = own_ref.shape[1], own_ref.shape[0] // 4
+    held[0] = own_ref[...]
+    for distance in range(1, count):
+        held[distance] = packed_refs[distance - 1][: 4 * rows, :]
     for s in range(4):
         for y in range(2):
             slot = slot_of(y * 4 + s, me)
             odd = slot // 4
             block = lax.rem(slot, 4)
-            value = jnp.where(odd == 1, odd_ref[block], even_ref[block])
-            layers[s, :, y * 2 * lanes : (y + 1) * 2 * lanes] = value.reshape(count * rows, -1)[:, : 2 * lanes]
+            for owner in range(count):
+                place = pl.ds(pl.multiple_of((owner ^ column) * rows, rows), rows)
+                value = jnp.where(odd == 1, odd_ref[block, place, :], even_ref[block, place, :])
+                layers[s, owner * rows : (owner + 1) * rows, y * 2 * lanes : (y + 1) * 2 * lanes] = value[:, : 2 * lanes]
     for s in range(4):
-        cots = [ref[s * rows : (s + 1) * rows, :] for ref in (own_ref,) + tuple(packed_refs)]
+        cots = [held[owner ^ column, s * rows : (s + 1) * rows, :] for owner in range(count)]
         wide = jnp.concatenate(cots, axis=0).astype(F32).T
         for i in (-1, 0, 1):
             moved = wide if i == 0 else pltpu.roll(wide, i % wide.shape[1], 1)
@@ -322,25 +333,47 @@
                     if 0 <= b + k < 4:
                         part = found[b * width : (b + 1) * width, (b + k) * lanes : (b + k + 1) * lanes]
                         tap = part if tap is None else tap + part
-                weights_out[4 + 9 * (i + 1) + 3 * (j + 1) + (k + 1)] = tap
+                taps_out[9 * (i + 1) + 3 * (j + 1) + (k + 1)] = tap
+
+
+def last_kernel(count, own_piece, base_ref, taps_ref, *refs):
+    come_refs = refs[: count - 1]
+    features_out, weights_out = refs[count - 1 :]
+    beams, cols, channels = base_ref.shape
+    rows = beams * cols
+    total = base_ref[...].reshape(rows, channels)
+    piece = own_piece[0].astype(F32)
+    start = rows * (channels // LANES)
+    for ref in come_refs:
+        total = total + jnp.concatenate(
+            [ref[half * rows : (half + 1) * rows, :].astype(F32) for half in range(channels // LANES)], axis=1
+        )
+        piece = piece + ref[start:, :].astype(F32)
+    features_out[...] = jnp.stack([total[b * cols : (b + 1) * cols] for b in range(beams)], axis=1).astype(BF)
+    width, lanes = weights_out.shape[1:]
+    for index in range(4):
+        weights_out[index] = piece[
+            (index % 2) * width : (index % 2 + 1) * width, (index // 2) * lanes : (index // 2 + 1) * lanes
+        ]
+    weights_out[4:] = taps_ref[...]
 
 
 def in_hbm(value):
     return pltpu.with_memory_space_constraint(value, pltpu.HBM)
 
 
-def shift(value, ahead):
+def swap_columns(value, distance):
     count = lax.axis_size("azim")
-    return lax.ppermute(value, "azim", [(i, (i + ahead) % count) for i in range(count)])
+    return lax.ppermute(value, "azim", [(i, i ^ distance) for i in range(count)])
+
+
+def exchange(values):
+    come = {distance: swap_columns(values[distance], distance) for distance in sorted(values, reverse=True)}
+    return [come[distance] for distance in sorted(values)]
 
 
 def swap(value, bits):
     return lax.ppermute(value, GROUP, [(i, i ^ bits) for i in range(8)])
-
-
-def group_gather(value):
-    even = jnp.stack([value, swap(value, 2), swap(value, 4), swap(value, 6)])
-    return even, swap(even, 1)
 
 
 def add(left, right):
@@ -370,16 +403,15 @@
             pltpu.SemaphoreType.DMA((7,)),
         ],
     )(*map(in_hbm, (features.reshape(token), cotangent.reshape(token), sector_mask, w_query, w_key, w_value, w_out)))
-    come = [shift(own_features, ahead) for ahead in range(1, count)]
-    all_features = [own_features] + come[::-1]
-    even, odd = group_gather(own_cot)
+    distances = range(1, count)
+    all_features = [own_features] + exchange({distance: own_features for distance in distances})
+    even = jnp.stack([own_cot] + [swap(own_cot, bits) for bits in (2, 4, 6)])
+    odd = swap(even, 1)
 
     spread = (4 * cols, 4 * width)
     edge = (8 * beams, channels)
-    edge_rows = (8 * beams * channels // LANES, LANES)
-    slices, first, last = call(
-        slices_kernel, [(spread, BF), (edge_rows, BF), (edge_rows, BF)], [VMEM] * 2
-    )(even, odd)
+    slices, edges = call(slices_kernel, [(spread, BF), ((2,) + edge, BF)], [VMEM] * 2)(even, odd)
+    neighbours = exchange({distance: edges for distance in neighbour_distances(count)})
 
     pieces_shape = (count, cols, max(LANES, beams * lanes))
     every, queries, keys, values, attended, pieces, w_conv = call(
@@ -390,35 +422,24 @@
         scratch=[pltpu.SemaphoreType.DMA],
     )(allowed, *all_features, w_query, w_key, w_value, w_out, in_hbm(w_conv.transpose(1, 0, 2)))
 
-    packed = []
-    for ahead in range(1, count):
-        parts = [slices, pieces[ahead]]
-        if ahead == 1:
-            parts.append(last)
-        if ahead == count - 1:
-            parts.append(first)
-        packed.append(shift(jnp.concatenate(parts, axis=0), ahead))
-    packed = packed[::-1]
-    below, above = packed[-1], packed[0]
-    start = 4 * cols
-    layer_block = jnp.stack([pieces[0]] + [part[start : start + cols] for part in packed])
-    even_layers, odd_layers = group_gather(layer_block)
+    packed = exchange({distance: jnp.concatenate([slices, pieces[distance]]) for distance in distances})
+    layer_block = jnp.concatenate([pieces[0]] + [part[4 * cols :] for part in packed])
 
     grad_layer, grad_layer_bf, grad_attended = call(
-        conv_kernel,
+        functools.partial(conv_kernel, count),
         [(block, F32), (block, BF), (block, BF)],
-        [VMEM] * 6,
+        [VMEM] * (4 + len(neighbours)),
         scratch=[
             pltpu.VMEM((3, beams + 2, cols + 16, channels), F32),
             pltpu.VMEM((2,) + edge, F32),
             pltpu.VMEM((3, 3, (beams + 2) * cols, channels), BF),
         ],
-    )(even, odd, below, above, w_conv, w_out)
-
-    quarter = (4, 4 * width, channels)
+    )(even, odd, *neighbours, w_conv, w_out)
+
+    quarter = (4, 4 * width * channels // LANES, LANES)
     base, send, keep, give = call(
         functools.partial(backward_kernel, count),
-        [(block, F32), ((count - 1,) + block, BF), (quarter, BF), (quarter, BF)],
+        [(block, F32), ((count - 1, beams * cols * channels // LANES, LANES), BF), (quarter, BF), (quarter, BF)],
         [VMEM] * 12,
         scratch=[
             pltpu.VMEM(block, BF),
@@ -430,24 +451,33 @@
         allowed, every, queries, keys, values, attended, grad_attended, grad_layer_bf, grad_layer,
         w_query, w_key, w_value,
     )
-    come_grads = [shift(send[ahead - 1], ahead) for ahead in range(1, count)]
-
-    sums = add(keep, swap(give, 1)).reshape(2, 2, 4 * width, channels)
-    sums = add(sums[:, 0], swap(sums[:, 1], 2))
+
+    sums = add(keep, swap(give, 1))
+    both = [swap(jnp.concatenate([layer_block, sums[bits // 2]]), bits) for bits in (2, 4, 6)]
+    even_layers = jnp.stack([layer_block] + [part[: layer_block.shape[0]] for part in both])
+    odd_layers = swap(even_layers, 1)
     sum_pieces = call(
-        functools.partial(pieces_kernel, count), [((count, 2 * width, 2 * lanes), BF)], [VMEM] * 2
-    )(sums[0], swap(sums[1], 4))[0]
-    come_pieces = [shift(sum_pieces[ahead], ahead) for ahead in range(1, count)]
-
+        functools.partial(pieces_kernel, count),
+        [((count, 2 * width, max(LANES, 2 * lanes)), BF)],
+        [VMEM] * 4,
+    )(sums[0], *both)[0]
+    come = exchange({distance: jnp.concatenate([send[distance - 1], sum_pieces[distance]]) for distance in distances})
+
+    taps = call(
+        functools.partial(taps_kernel, count),
+        [((TAPS, width, lanes), F32)],
+        [VMEM] * (2 + count),
+        scratch=[
+            pltpu.VMEM((4, count * cols, 4 * lanes), BF),
+            pltpu.VMEM((3, 16 * width, count * cols), BF),
+            pltpu.VMEM((count,) + spread, BF),
+        ],
+    )(even_layers, odd_layers, slices, *packed)[0]
     features_grad, weight_grads = call(
         functools.partial(last_kernel, count),
         [((cols, beams, channels), BF), ((4 + TAPS, width, lanes), F32)],
-        [VMEM] * (2 + 3 * count),
-        scratch=[
-            pltpu.VMEM((4, count * cols, 4 * lanes), BF),
-            pltpu.VMEM((3, 16 * width, count * cols), BF),
-        ],
-    )(even_layers, odd_layers, slices, *packed, sum_pieces, *come_pieces, base, *come_grads)
+        [VMEM] * (2 + count),
+    )(sum_pieces, base, taps, *come)
     return features_grad.reshape(features.shape), weight_grads.transpose(2, 0, 1)
 
 

time: 57.2 us -> 52.3 us (0.914)
  starting transfers between devices: 26.9 us -> 24.4 us
  waiting for transfers between devices: 19.6 us -> 17.2 us
    ppermute x12 -> x11, waiting for transfers between devices: 15.1 us -> 10.5 us  [swap_columns(): lax.ppermute(value, 'azim', [(i, i ^ distance) for i in range(count)])]
    ppermute x11 -> x9, starting transfers between devices: 11.5 us -> 8.37 us  [swap(): return lax.ppermute(value, GROUP, [(i, i ^ bits) for i in range(8)])]
    ppermute x11 -> x9, waiting for transfers between devices: 4.5 us -> 6.7 us  [swap(): return lax.ppermute(value, GROUP, [(i, i ^ bits) for i in range(8)])]
    pallas_call x3 -> x4, Pallas kernels: 1.92 us -> 3.09 us  [the longest x1 1.46 us: per_device(): call(functools.partial(conv_kernel, count), [(block, F32), (block, BF), (...]
    pallas_call x1, Pallas kernels: 1.96 us -> 0.97 us  [per_device(): call(functools.partial(last_kernel, count), [((cols, beams, channels), BF...]
    ppermute x12 -> x11, starting transfers between devices: 15.4 us -> 16 us  [swap_columns(): lax.ppermute(value, 'azim', [(i, i ^ distance) for i in range(count)])]
  transfers between devices with their start and end apart: 23 -> 20, of which waited for: 15 -> 7; matrix products, arithmetic and copies ran while one was open for 0% -> 0% of each run, Pallas kernels for 4% -> 13%
where the time goes in v3:
time: 52.3 us; the launch traced here: 52.1 us
  starting transfers between devices  24.4 us (47%)
  waiting for transfers between devices  17.2 us (33%)
  Pallas kernels  9.35 us (18%)
  between operations  0.86 us (2%)
    ppermute x11, starting transfers between devices, swap_columns(): lax.ppermute(value, 'azim', [(i, i ^ distance) for i in range(count)])  16 us
    ppermute x11, waiting for transfers between devices, swap_columns(): lax.ppermute(value, 'azim', [(i, i ^ distance) for i in range(count)])  10.5 us
    ppermute x9, starting transfers between devices, swap(): return lax.ppermute(value, GROUP, [(i, i ^ bits) for i in range(8)])  8.37 us
    ppermute x9, waiting for transfers between devices, swap(): return lax.ppermute(value, GROUP, [(i, i ^ bits) for i in range(8)])  6.7 us
    pallas_call x1, Pallas kernels, per_device(): call(functools.partial(forward_kernel, count), [(whole, BF), (block, BF),...  2.01 us
    pallas_call x1, Pallas kernels, per_device(): call(functools.partial(backward_kernel, count), [(block, F32), ((count -...  1.89 us
    pallas_call x1, Pallas kernels, per_device(): call(functools.partial(conv_kernel, count), [(block, F32), (block, BF), (...  1.46 us
    pallas_call x1, Pallas kernels, per_device(): call(functools.partial(prep_kernel, count), [(block, BF), (block, BF), ((...  1.39 us
  transfers between devices with their start and end apart: 20, of which 7 were waited for; matrix products, arithmetic and copies ran while one was open for 0% of the time, Pallas kernels for 13%

profile of v3, /device:TPU:0, one launch (start us, length us, event | category | flops | bytes accessed | tf_op | source)
XLA Modules:
  0.0 52.1 jit_solution(9675031135077491758)
XLA Ops:
  0.6 1.4 %shard_map.95 = (bf16[2,64,256]{2,1,0:T(8,128)(2,1)S(1)}, bf16[2,64,256]{2,1,0:T(8,128)(2,1)S(1)}, f32[8,256]{1,0:T(8,128)S(1)}, bf16[256,256]{1,0:T(8,128)(2,1)...) custom-call(bf16[64,2,256]{2,1,0:T(2,128)(2,1)} %bitcast.61, ...), custom_call_target="tpu_custom_call" | custom-call | tf_op jit(solution)/shard_map/pallas_call | solution.py:395
  2.0 4.0 %collective-permute-start.5 = (bf16[2,64,256]{2,1,0:T(8,128)(2,1)S(1)}, bf16[2,64,256]{2,1,0:T(8,128)(2,1)S(1)}, u32[]{:S(2)}, u32[]{:S(2)}) collective-permute-start(bf16[2,64,256]{2,1,0:T(8,128)(2,1)S(1)} %get-tuple-element.38), channel_id=1, source_target_pairs={{0,6},{1,7},{2,4},{3,5},{4,2},{5,3},{6,0},{7,1},{8,14},{9,15},{10,... | collective-permute-start | bytes 196616 | tf_op jit(solution)/shard_map/ppermute | solution.py:376
  6.0 0.5 collective-permute-start.4
  6.5 0.1 collective-permute-start.3
  6.6 4.0 %collective-permute-start.2 = (bf16[2,64,256]{2,1,0:T(8,128)(2,1)S(1)}, bf16[2,64,256]{2,1,0:T(8,128)(2,1)S(1)}, u32[]{:S(2)}, u32[]{:S(2)}) collective-permute-start(bf16[2,64,256]{2,1,0:T(8,128)(2,1)S(1)} %get-tuple-element.28.refs_1_), channel_id=1, source_target_pairs={{0,24},{8,16},{16,8},{24,0},{1,25},{9,17},{17,9},{25,1},{2,26},{10... | collective-permute-start | bytes 196616 | tf_op jit(solution)/shard_map/ppermute | solution.py:367
  10.6 0.0 collective-permute-start.1
  10.6 0.0 collective-permute-done.5
  10.6 0.6 %collective-permute-start = (bf16[2,64,256]{2,1,0:T(8,128)(2,1)S(1)}, bf16[2,64,256]{2,1,0:T(8,128)(2,1)S(1)}, u32[]{:S(2)}, u32[]{:S(2)}) collective-permute-start(bf16[2,64,256]{2,1,0:T(8,128)(2,1)S(1)} %get-tuple-element.28.refs_1_), channel_id=1, source_target_pairs={{0,8},{8,0},{16,24},{24,16},{1,9},{9,1},{17,25},{25,17},{2,10},{10... | collective-permute-start | bytes 196616 | tf_op jit(solution)/shard_map/ppermute | solution.py:367
  11.2 0.0 collective-permute-done.4
  11.2 0.0 collective-permute-done.3
  11.3 0.1 collective-permute-start.6
  11.3 2.0 %collective-permute-done.2.refs_4_ = bf16[2,64,256]{2,1,0:T(8,128)(2,1)S(1)} collective-permute-done((bf16[2,64,256]{2,1,0:T(8,128)(2,1)S(1)}, bf16[2,64,256]{2,1,0:T(8,128)(2,1)S(1)}, u32[]{:S(2)}, u32[]{:S(2)}) %collective-permute-start.2) | collective-permute-done | bytes 65568 | tf_op jit(solution)/shard_map/ppermute | solution.py:367
  13.4 2.6 %collective-permute-done.1.refs_3_ = bf16[2,64,256]{2,1,0:T(8,128)(2,1)S(1)} collective-permute-done((bf16[2,64,256]{2,1,0:T(8,128)(2,1)S(1)}, bf16[2,64,256]{2,1,0:T(8,128)(2,1)S(1)}, u32[]{:S(2)}, u32[]{:S(2)}) %collective-permute-start.1) | collective-permute-done | bytes 65568 | tf_op jit(solution)/shard_map/ppermute | solution.py:367
  16.0 0.0 collective-permute-done.refs_2_
  16.0 2.0 %shard_map.96 = (bf16[2,256,256]{2,1,0:T(8,128)(2,1)S(1)}, bf16[2,64,256]{2,1,0:T(8,128)(2,1)S(1)}, bf16[2,256,256]{2,1,0:T(8,128)(2,1)S(1)}, bf16[2,256,256]{2,...) custom-call(f32[8,256]{1,0:T(8,128)S(1)} %get-tuple-element.27.refs_, ...), custom_call_target="tpu_custom_call" | custom-call | tf_op jit(solution)/shard_map/pallas_call | solution.py:417
  18.0 0.0 collective-permute-done.6.odd_ref
  18.1 0.4 shard_map.97
  18.4 2.3 %collective-permute-start.8 = (bf16[2,16,256]{2,1,0:T(8,128)(2,1)S(1)}, bf16[2,16,256]{2,1,0:T(8,128)(2,1)S(1)}, u32[]{:S(2)}, u32[]{:S(2)}) collective-permute-start(bf16[2,16,256]{2,1,0:T(8,128)(2,1)S(1)} %get-tuple-element.39), channel_id=1, source_target_pairs={{0,24},{8,16},{16,8},{24,0},{1,25},{9,17},{17,9},{25,1},{2,26},{10... | collective-permute-start | bytes 49160 | tf_op jit(solution)/shard_map/ppermute | solution.py:367
  20.7 0.2 collective-permute-start.7
  20.9 1.5 %collective-permute-start.12 = (bf16[320,128]{1,0:T(8,128)(2,1)S(1)}, bf16[320,128]{1,0:T(8,128)(2,1)S(1)}, u32[]{:S(2)}, u32[]{:S(2)}) collective-permute-start(bf16[320,128]{1,0:T(8,128)(2,1)S(1)} %get-tuple-element.70), channel_id=1, source_target_pairs={{0,24},{8,16},{16,8},{24,0},{1,25},{9,17},{17,9},{25,1},{2,26},{10... | collective-permute-start | bytes 245768 | tf_op jit(solution)/shard_map/ppermute | solution.py:367
  22.4 1.9 %collective-permute-start.11 = (bf16[320,128]{1,0:T(8,128)(2,1)S(1)}, bf16[320,128]{1,0:T(8,128)(2,1)S(1)}, u32[]{:S(2)}, u32[]{:S(2)}) collective-permute-start(bf16[320,128]{1,0:T(8,128)(2,1)S(1)} %get-tuple-element.71), channel_id=1, source_target_pairs={{0,16},{8,24},{16,0},{24,8},{1,17},{9,25},{17,1},{25,9},{2,18},{10... | collective-permute-start | bytes 245768 | tf_op jit(solution)/shard_map/ppermute | solution.py:367
  24.3 1.1 %collective-permute-start.10 = (bf16[320,128]{1,0:T(8,128)(2,1)S(1)}, bf16[320,128]{1,0:T(8,128)(2,1)S(1)}, u32[]{:S(2)}, u32[]{:S(2)}) collective-permute-start(bf16[320,128]{1,0:T(8,128)(2,1)S(1)} %get-tuple-element.72), channel_id=1, source_target_pairs={{0,8},{8,0},{16,24},{24,16},{1,9},{9,1},{17,25},{25,17},{2,10},{10... | collective-permute-start | bytes 245768 | tf_op jit(solution)/shard_map/ppermute | solution.py:367
  25.4 0.0 collective-permute-done.8.refs_1_
  25.4 0.0 collective-permute-done.7.refs_0_
  25.4 1.5 %shard_map.98 = (f32[2,64,256]{2,1,0:T(8,128)S(1)}, bf16[2,64,256]{2,1,0:T(8,128)(2,1)S(1)}, bf16[2,64,256]{2,1,0:T(8,128)(2,1)S(1)}) custom-call(bf16[4,2,64,256]{3,2,1,0:T(8,128)(2,1)S(1)} %pad_maximum_fusion.even_ref, bf16[4,2,64,256]{3,2,1,0:T(8,128)(2,1)S(1)} %collective-permute-done.6.odd_ref, bf16[2,16,256]{2,1,0:T(8,128)(2,1)S(1)} %collective-permute-done.7.refs_0_, ...), custom_call_target="tpu_custom_call" | custom-call | tf_op jit(solution)/shard_map/pallas_call | solution.py:428
  26.8 1.9 %shard_map.99 = (f32[2,64,256]{2,1,0:T(8,128)S(1)}, bf16[3,256,128]{2,1,0:T(8,128)(2,1)S(1)}, bf16[4,256,128]{2,1,0:T(8,128)(2,1)S(1)}, bf16[4,256,128]{2,1,0:T(8,128)(2,1)S(1)}) custom-call(f32[8,256]{1,0:T(8,128)S(1)} %get-tuple-element.27.refs_0_.allowed_ref, bf16[2,256,256]{2,1,0:T(8,128)(2,1)S(1)} %get-tuple-element.33.all_ref, ...), custom_call_target="tpu_custom_call" | custom-call | tf_op jit(solution)/shard_map/pallas_call | solution.py:440
  28.7 0.1 collective-permute-start.9
  28.8 0.8 %collective-permute-done.10.refs_0_ = bf16[320,128]{1,0:T(8,128)(2,1)S(1)} collective-permute-done((bf16[320,128]{1,0:T(8,128)(2,1)S(1)}, bf16[320,128]{1,0:T(8,128)(2,1)S(1)}, u32[]{:S(2)}, u32[]{:S(2)}) %collective-permute-start.10) | collective-permute-done | bytes 81952 | tf_op jit(solution)/shard_map/ppermute | solution.py:367
  29.6 0.0 collective-permute-done.11.refs_1_
  29.7 0.0 collective-permute-done.12.refs_2_
  29.7 0.6 %collective-permute-done.9 = bf16[4,256,128]{2,1,0:T(8,128)(2,1)S(1)} collective-permute-done((bf16[4,256,128]{2,1,0:T(8,128)(2,1)S(1)}, bf16[4,256,128]{2,1,0:T(8,128)(2,1)S(1)}, u32[]{:S(2)}, u32[]{:S(2)}) %collective-permute-start.9) | collective-permute-done | bytes 262176 | tf_op jit(solution)/shard_map/ppermute | solution.py:376
  30.4 0.1 add_convert_fusion
  30.5 1.6 %collective-permute-start.13 = (bf16[512,128]{1,0:T(8,128)(2,1)S(1)}, bf16[512,128]{1,0:T(8,128)(2,1)S(1)}, u32[]{:S(2)}, u32[]{:S(2)}) collective-permute-start(bf16[512,128]{1,0:T(8,128)(2,1)S(1)} %fusion.2), channel_id=1, source_target_pairs={{0,2},{1,3},{2,0},{3,1},{4,6},{5,7},{6,4},{7,5},{8,10},{9,11},{10,... | collective-permute-start | bytes 393224 | tf_op jit(solution)/shard_map/ppermute | solution.py:376
  32.0 1.5 %collective-permute-start.14 = (bf16[512,128]{1,0:T(8,128)(2,1)S(1)}, bf16[512,128]{1,0:T(8,128)(2,1)S(1)}, u32[]{:S(2)}, u32[]{:S(2)}) collective-permute-start(bf16[512,128]{1,0:T(8,128)(2,1)S(1)} %fusion.1), channel_id=1, source_target_pairs={{0,4},{1,5},{2,6},{3,7},{4,0},{5,1},{6,2},{7,3},{8,12},{9,13},{10,... | collective-permute-start | bytes 393224 | tf_op jit(solution)/shard_map/ppermute | solution.py:376
  33.6 0.5 collective-permute-start.15
  34.0 2.4 %collective-permute-done.13.refs_0_ = bf16[512,128]{1,0:T(8,128)(2,1)S(1)} collective-permute-done((bf16[512,128]{1,0:T(8,128)(2,1)S(1)}, bf16[512,128]{1,0:T(8,128)(2,1)S(1)}, u32[]{:S(2)}, u32[]{:S(2)}) %collective-permute-start.13) | collective-permute-done | bytes 131104 | tf_op jit(solution)/shard_map/ppermute | solution.py:376
  36.4 3.7 %collective-permute-done.14.refs_1_ = bf16[512,128]{1,0:T(8,128)(2,1)S(1)} collective-permute-done((bf16[512,128]{1,0:T(8,128)(2,1)S(1)}, bf16[512,128]{1,0:T(8,128)(2,1)S(1)}, u32[]{:S(2)}, u32[]{:S(2)}) %collective-permute-start.14) | collective-permute-done | bytes 131104 | tf_op jit(solution)/shard_map/ppermute | solution.py:376
  40.1 0.0 collective-permute-done.15.refs_2_
  40.1 0.1 shard_map.100.own_piece
  40.2 1.0 %collective-permute-start.17 = (bf16[320,128]{1,0:T(8,128)(2,1)S(1)}, bf16[320,128]{1,0:T(8,128)(2,1)S(1)}, u32[]{:S(2)}, u32[]{:S(2)}) collective-permute-start(bf16[320,128]{1,0:T(8,128)(2,1)S(1)} %pad_maximum_fusion.5), channel_id=1, source_target_pairs={{0,8},{8,0},{16,24},{24,16},{1,9},{9,1},{17,25},{25,17},{2,10},{10... | collective-permute-start | bytes 245768 | tf_op jit(solution)/shard_map/ppermute | solution.py:367
  41.4 0.1 collective-permute-start.16
  41.5 1.1 %collective-permute-start.18 = (bf16[320,128]{1,0:T(8,128)(2,1)S(1)}, bf16[320,128]{1,0:T(8,128)(2,1)S(1)}, u32[]{:S(2)}, u32[]{:S(2)}) collective-permute-start(bf16[320,128]{1,0:T(8,128)(2,1)S(1)} %pad_maximum_fusion.6), channel_id=1, source_target_pairs={{0,16},{8,24},{16,0},{24,8},{1,17},{9,25},{17,1},{25,9},{2,18},{10... | collective-permute-start | bytes 245768 | tf_op jit(solution)/shard_map/ppermute | solution.py:367
  42.6 2.4 %collective-permute-start.19 = (bf16[320,128]{1,0:T(8,128)(2,1)S(1)}, bf16[320,128]{1,0:T(8,128)(2,1)S(1)}, u32[]{:S(2)}, u32[]{:S(2)}) collective-permute-start(bf16[320,128]{1,0:T(8,128)(2,1)S(1)} %pad_maximum_fusion.7), channel_id=1, source_target_pairs={{0,24},{8,16},{16,8},{24,0},{1,25},{9,17},{17,9},{25,1},{2,26},{10... | collective-permute-start | bytes 245768 | tf_op jit(solution)/shard_map/ppermute | solution.py:367
  44.9 0.0 collective-permute-done.16.odd_ref
  44.9 1.2 %shard_map.101.taps_ref = f32[27,32,64]{2,1,0:T(8,128)S(1)} custom-call(bf16[4,256,128]{2,1,0:T(8,128)(2,1)S(1)} %pad_maximum_fusion.1.even_ref, bf16[4,256,128]{2,1,0:T(8,128)(2,1)S(1)} %collective-permute-done.16.odd_ref, bf16[256,128]{1,0:T(8,128)(2,1)S(1)} %get-tuple-element.47.own_ref, bf16[320,128]{1,0:T(8,128)(2,1)S(1)} %collective-permute-done.10.refs_0_, ...), custom_call_target="tpu_custom_call" | custom-call | tf_op jit(solution)/shard_map/pallas_call | solution.py:466
  46.1 0.0 collective-permute-done.17.refs_0_
  46.1 5.0 %collective-permute-done.18.refs_1_ = bf16[320,128]{1,0:T(8,128)(2,1)S(1)} collective-permute-done((bf16[320,128]{1,0:T(8,128)(2,1)S(1)}, bf16[320,128]{1,0:T(8,128)(2,1)S(1)}, u32[]{:S(2)}, u32[]{:S(2)}) %collective-permute-start.18) | collective-permute-done | bytes 81952 | tf_op jit(solution)/shard_map/ppermute | solution.py:367
  51.2 1.0 %shard_map.102 = (bf16[64,2,256]{2,1,0:T(2,128)(2,1)}, f32[31,32,64]{2,1,0:T(8,128)}) custom-call(bf16[4,64,128]{2,1,0:T(8,128)(2,1)S(1)} %shard_map.100.own_piece, f32[2,64,256]{2,1,0:T(8,128)S(1)} %get-tuple-element.48.base_ref, f32[27,32,64]{2,1,0:T(8,128)S(1)} %shard_map.101.taps_ref, bf16[320,128]{1,0:T(8,128)(2,1)S(1)} %collective-permute-done.17.refs_0_, ...), custom_call_target="tpu_custom_call" | custom-call | tf_op jit(solution)/shard_map/pallas_call | solution.py:476
  (24 shorter events, 0.3 us)
Async XLA Ops:
  2.0 8.6 %collective-permute-start.5 = (bf16[2,64,256]{2,1,0:T(8,128)(2,1)S(1)}, bf16[2,64,256]{2,1,0:T(8,128)(2,1)S(1)}, u32[]{:S(2)}, u32[]{:S(2)}) collective-permute-start(bf16[2,64,256]{2,1,0:T(8,128)(2,1)S(1)} %get-tuple-element.38), channel_id=1, source_target_pairs={{0,6},{1,7},{2,4},{3,5},{4,2},{5,3},{6,0},{7,1},{8,14},{9,15},{10,... | collective-permute-start | bytes 196616 | tf_op jit(solution)/shard_map/ppermute | solution.py:376
  6.0 5.2 %collective-permute-start.4 = (bf16[2,64,256]{2,1,0:T(8,128)(2,1)S(1)}, bf16[2,64,256]{2,1,0:T(8,128)(2,1)S(1)}, u32[]{:S(2)}, u32[]{:S(2)}) collective-permute-start(bf16[2,64,256]{2,1,0:T(8,128)(2,1)S(1)} %get-tuple-element.38), channel_id=1, source_target_pairs={{0,4},{1,5},{2,6},{3,7},{4,0},{5,1},{6,2},{7,3},{8,12},{9,13},{10,... | collective-permute-start | bytes 196616 | tf_op jit(solution)/shard_map/ppermute | solution.py:376
  6.5 4.7 %collective-permute-start.3 = (bf16[2,64,256]{2,1,0:T(8,128)(2,1)S(1)}, bf16[2,64,256]{2,1,0:T(8,128)(2,1)S(1)}, u32[]{:S(2)}, u32[]{:S(2)}) collective-permute-start(bf16[2,64,256]{2,1,0:T(8,128)(2,1)S(1)} %get-tuple-element.38), channel_id=1, source_target_pairs={{0,2},{1,3},{2,0},{3,1},{4,6},{5,7},{6,4},{7,5},{8,10},{9,11},{10,... | collective-permute-start | bytes 196616 | tf_op jit(solution)/shard_map/ppermute | solution.py:376
  6.6 6.7 %collective-permute-start.2 = (bf16[2,64,256]{2,1,0:T(8,128)(2,1)S(1)}, bf16[2,64,256]{2,1,0:T(8,128)(2,1)S(1)}, u32[]{:S(2)}, u32[]{:S(2)}) collective-permute-start(bf16[2,64,256]{2,1,0:T(8,128)(2,1)S(1)} %get-tuple-element.28.refs_1_), channel_id=1, source_target_pairs={{0,24},{8,16},{16,8},{24,0},{1,25},{9,17},{17,9},{25,1},{2,26},{10... | collective-permute-start | bytes 196616 | tf_op jit(solution)/shard_map/ppermute | solution.py:367
  10.6 5.4 %collective-permute-start.1 = (bf16[2,64,256]{2,1,0:T(8,128)(2,1)S(1)}, bf16[2,64,256]{2,1,0:T(8,128)(2,1)S(1)}, u32[]{:S(2)}, u32[]{:S(2)}) collective-permute-start(bf16[2,64,256]{2,1,0:T(8,128)(2,1)S(1)} %get-tuple-element.28.refs_1_), channel_id=1, source_target_pairs={{0,16},{8,24},{16,0},{24,8},{1,17},{9,25},{17,1},{25,9},{2,18},{10... | collective-permute-start | bytes 196616 | tf_op jit(solution)/shard_map/ppermute | solution.py:367
  10.6 5.4 %collective-permute-start = (bf16[2,64,256]{2,1,0:T(8,128)(2,1)S(1)}, bf16[2,64,256]{2,1,0:T(8,128)(2,1)S(1)}, u32[]{:S(2)}, u32[]{:S(2)}) collective-permute-start(bf16[2,64,256]{2,1,0:T(8,128)(2,1)S(1)} %get-tuple-element.28.refs_1_), channel_id=1, source_target_pairs={{0,8},{8,0},{16,24},{24,16},{1,9},{9,1},{17,25},{25,17},{2,10},{10... | collective-permute-start | bytes 196616 | tf_op jit(solution)/shard_map/ppermute | solution.py:367
  11.3 6.8 %collective-permute-start.6 = (bf16[4,2,64,256]{3,2,1,0:T(8,128)(2,1)S(1)}, bf16[4,2,64,256]{3,2,1,0:T(8,128)(2,1)S(1)}, u32[]{:S(2)}, u32[]{:S(2)}) collective-permute-start(bf16[4,2,64,256]{3,2,1,0:T(8,128)(2,1)S(1)} %pad_maximum_fusion.even_ref), channel_id=1, source_target_pairs={{0,1},{1,0},{2,3},{3,2},{4,5},{5,4},{6,7},{7,6},{8,9},{9,8},{10,11... | collective-permute-start | bytes 786440 | tf_op jit(solution)/shard_map/ppermute | solution.py:376
  18.4 6.9 %collective-permute-start.8 = (bf16[2,16,256]{2,1,0:T(8,128)(2,1)S(1)}, bf16[2,16,256]{2,1,0:T(8,128)(2,1)S(1)}, u32[]{:S(2)}, u32[]{:S(2)}) collective-permute-start(bf16[2,16,256]{2,1,0:T(8,128)(2,1)S(1)} %get-tuple-element.39), channel_id=1, source_target_pairs={{0,24},{8,16},{16,8},{24,0},{1,25},{9,17},{17,9},{25,1},{2,26},{10... | collective-permute-start | bytes 49160 | tf_op jit(solution)/shard_map/ppermute | solution.py:367
  20.7 4.6 %collective-permute-start.7 = (bf16[2,16,256]{2,1,0:T(8,128)(2,1)S(1)}, bf16[2,16,256]{2,1,0:T(8,128)(2,1)S(1)}, u32[]{:S(2)}, u32[]{:S(2)}) collective-permute-start(bf16[2,16,256]{2,1,0:T(8,128)(2,1)S(1)} %get-tuple-element.39), channel_id=1, source_target_pairs={{0,8},{8,0},{16,24},{24,16},{1,9},{9,1},{17,25},{25,17},{2,10},{10... | collective-permute-start | bytes 49160 | tf_op jit(solution)/shard_map/ppermute | solution.py:367
  20.9 8.8 %collective-permute-start.12 = (bf16[320,128]{1,0:T(8,128)(2,1)S(1)}, bf16[320,128]{1,0:T(8,128)(2,1)S(1)}, u32[]{:S(2)}, u32[]{:S(2)}) collective-permute-start(bf16[320,128]{1,0:T(8,128)(2,1)S(1)} %get-tuple-element.70), channel_id=1, source_target_pairs={{0,24},{8,16},{16,8},{24,0},{1,25},{9,17},{17,9},{25,1},{2,26},{10... | collective-permute-start | bytes 245768 | tf_op jit(solution)/shard_map/ppermute | solution.py:367
  22.4 7.2 %collective-permute-start.11 = (bf16[320,128]{1,0:T(8,128)(2,1)S(1)}, bf16[320,128]{1,0:T(8,128)(2,1)S(1)}, u32[]{:S(2)}, u32[]{:S(2)}) collective-permute-start(bf16[320,128]{1,0:T(8,128)(2,1)S(1)} %get-tuple-element.71), channel_id=1, source_target_pairs={{0,16},{8,24},{16,0},{24,8},{1,17},{9,25},{17,1},{25,9},{2,18},{10... | collective-permute-start | bytes 245768 | tf_op jit(solution)/shard_map/ppermute | solution.py:367
  24.3 5.3 %collective-permute-start.10 = (bf16[320,128]{1,0:T(8,128)(2,1)S(1)}, bf16[320,128]{1,0:T(8,128)(2,1)S(1)}, u32[]{:S(2)}, u32[]{:S(2)}) collective-permute-start(bf16[320,128]{1,0:T(8,128)(2,1)S(1)} %get-tuple-element.72), channel_id=1, source_target_pairs={{0,8},{8,0},{16,24},{24,16},{1,9},{9,1},{17,25},{25,17},{2,10},{10... | collective-permute-start | bytes 245768 | tf_op jit(solution)/shard_map/ppermute | solution.py:367
  28.7 1.6 %collective-permute-start.9 = (bf16[4,256,128]{2,1,0:T(8,128)(2,1)S(1)}, bf16[4,256,128]{2,1,0:T(8,128)(2,1)S(1)}, u32[]{:S(2)}, u32[]{:S(2)}) collective-permute-start(bf16[4,256,128]{2,1,0:T(8,128)(2,1)S(1)} %get-tuple-element.45), channel_id=1, source_target_pairs={{0,1},{1,0},{2,3},{3,2},{4,5},{5,4},{6,7},{7,6},{8,9},{9,8},{10,11... | collective-permute-start | bytes 786440 | tf_op jit(solution)/shard_map/ppermute | solution.py:376
  30.5 5.9 %collective-permute-start.13 = (bf16[512,128]{1,0:T(8,128)(2,1)S(1)}, bf16[512,128]{1,0:T(8,128)(2,1)S(1)}, u32[]{:S(2)}, u32[]{:S(2)}) collective-permute-start(bf16[512,128]{1,0:T(8,128)(2,1)S(1)} %fusion.2), channel_id=1, source_target_pairs={{0,2},{1,3},{2,0},{3,1},{4,6},{5,7},{6,4},{7,5},{8,10},{9,11},{10,... | collective-permute-start | bytes 393224 | tf_op jit(solution)/shard_map/ppermute | solution.py:376
  32.0 8.1 %collective-permute-start.14 = (bf16[512,128]{1,0:T(8,128)(2,1)S(1)}, bf16[512,128]{1,0:T(8,128)(2,1)S(1)}, u32[]{:S(2)}, u32[]{:S(2)}) collective-permute-start(bf16[512,128]{1,0:T(8,128)(2,1)S(1)} %fusion.1), channel_id=1, source_target_pairs={{0,4},{1,5},{2,6},{3,7},{4,0},{5,1},{6,2},{7,3},{8,12},{9,13},{10,... | collective-permute-start | bytes 393224 | tf_op jit(solution)/shard_map/ppermute | solution.py:376
  33.6 6.5 %collective-permute-start.15 = (bf16[512,128]{1,0:T(8,128)(2,1)S(1)}, bf16[512,128]{1,0:T(8,128)(2,1)S(1)}, u32[]{:S(2)}, u32[]{:S(2)}) collective-permute-start(bf16[512,128]{1,0:T(8,128)(2,1)S(1)} %fusion), channel_id=1, source_target_pairs={{0,6},{1,7},{2,4},{3,5},{4,2},{5,3},{6,0},{7,1},{8,14},{9,15},{10,... | collective-permute-start | bytes 393224 | tf_op jit(solution)/shard_map/ppermute | solution.py:376
  40.2 5.9 %collective-permute-start.17 = (bf16[320,128]{1,0:T(8,128)(2,1)S(1)}, bf16[320,128]{1,0:T(8,128)(2,1)S(1)}, u32[]{:S(2)}, u32[]{:S(2)}) collective-permute-start(bf16[320,128]{1,0:T(8,128)(2,1)S(1)} %pad_maximum_fusion.5), channel_id=1, source_target_pairs={{0,8},{8,0},{16,24},{24,16},{1,9},{9,1},{17,25},{25,17},{2,10},{10... | collective-permute-start | bytes 245768 | tf_op jit(solution)/shard_map/ppermute | solution.py:367
  41.4 3.6 %collective-permute-start.16 = (bf16[4,256,128]{2,1,0:T(8,128)(2,1)S(1)}, bf16[4,256,128]{2,1,0:T(8,128)(2,1)S(1)}, u32[]{:S(2)}, u32[]{:S(2)}) collective-permute-start(bf16[4,256,128]{2,1,0:T(8,128)(2,1)S(1)} %pad_maximum_fusion.1.even_ref), channel_id=1, source_target_pairs={{0,1},{1,0},{2,3},{3,2},{4,5},{5,4},{6,7},{7,6},{8,9},{9,8},{10,11... | collective-permute-start | bytes 786440 | tf_op jit(solution)/shard_map/ppermute | solution.py:376
  41.5 9.7 %collective-permute-start.18 = (bf16[320,128]{1,0:T(8,128)(2,1)S(1)}, bf16[320,128]{1,0:T(8,128)(2,1)S(1)}, u32[]{:S(2)}, u32[]{:S(2)}) collective-permute-start(bf16[320,128]{1,0:T(8,128)(2,1)S(1)} %pad_maximum_fusion.6), channel_id=1, source_target_pairs={{0,16},{8,24},{16,0},{24,8},{1,17},{9,25},{17,1},{25,9},{2,18},{10... | collective-permute-start | bytes 245768 | tf_op jit(solution)/shard_map/ppermute | solution.py:367
  42.6 8.6 %collective-permute-start.19 = (bf16[320,128]{1,0:T(8,128)(2,1)S(1)}, bf16[320,128]{1,0:T(8,128)(2,1)S(1)}, u32[]{:S(2)}, u32[]{:S(2)}) collective-permute-start(bf16[320,128]{1,0:T(8,128)(2,1)S(1)} %pad_maximum_fusion.7), channel_id=1, source_target_pairs={{0,24},{8,16},{16,8},{24,0},{1,25},{9,17},{17,9},{25,1},{2,26},{10... | collective-permute-start | bytes 245768 | tf_op jit(solution)/shard_map/ppermute | solution.py:367

commit v4 on v3

--- a/solution.py
+++ b/solution.py
@@ -28,9 +28,10 @@
     return lax.dot_general(left, right, (dims, ((), ())), preferred_element_type=F32)
 
 
-def call(kernel, outs, in_specs, scratch=(), limit=40):
+def call(kernel, outs, in_specs, scratch=(), limit=40, micros=2):
     return pl.pallas_call(
         kernel,
+        cost_estimate=pl.CostEstimate(flops=int(micros * 1e9), bytes_accessed=0, transcendentals=0),
         out_shape=[jax.ShapeDtypeStruct(shape, dtype) for shape, dtype in outs],
         in_specs=in_specs,
         out_specs=[VMEM] * len(outs),
@@ -117,7 +118,7 @@
 def conv_kernel(count, even_ref, odd_ref, *refs):
     distances = neighbour_distances(count)
     edge_refs = refs[: len(distances)]
-    w_ref, w_out_ref, layer_out, layer_bf_out, attended_out, padded, edges, shifted = refs[len(distances) :]
+    w_low_ref, w_high_ref, w_out_ref, layer_out, layer_bf_out, attended_out, padded, edges, shifted = refs[len(distances) :]
     me = group_index()
     column = lax.axis_index("azim")
     sweep = lax.axis_index("sweep")
@@ -156,7 +157,10 @@
         for j in (-1, 0, 1):
             for k in (-1, 0, 1):
                 rows = shifted[i + 1, 1 - j, (1 - k) * cols : (1 - k + beams) * cols, :]
-                total = total + dot(rows, w_ref[9 * (i + 1) + 3 * (j + 1) + (k + 1)], NT)
+                tap = 9 * (i + 1) + 3 * (j + 1) + (k + 1)
+                low = w_low_ref.shape[0]
+                w_tap = w_low_ref[tap] if tap < low else w_high_ref[tap - low]
+                total = total + dot(rows, w_tap, NT)
     rounded = total.astype(BF)
     layer_out[...] = total.reshape(beams, cols, channels)
     layer_bf_out[...] = rounded.reshape(beams, cols, channels)
@@ -188,12 +192,10 @@
     return jnp.where(allowed, jnp.exp(scores - logsum), 0.0)
 
 
-def forward_kernel(count, *refs):
-    allowed_ref = refs[0]
-    feature_refs = refs[1 : 1 + count]
-    w_query, w_key, w_value, w_out, w_conv_hbm = refs[1 + count : 6 + count]
-    all_out, query_out, key_out, value_out, attended_out, pieces_out, w_conv_out, sem = refs[6 + count :]
-    copy = pltpu.make_async_copy(w_conv_hbm, w_conv_out, sem)
+def project_kernel(count, *refs):
+    feature_refs = refs[:count]
+    w_query, w_key, w_value, w_conv_hbm, all_out, query_out, key_out, value_out, w_conv_out, sem = refs[count:]
+    copy = pltpu.make_async_copy(w_conv_hbm.at[: w_conv_out.shape[0]], w_conv_out, sem)
     copy.start()
     beams, cols, channels = feature_refs[0].shape
     for ahead in range(count):
@@ -203,10 +205,25 @@
     query_out[...] = dot(own, w_query[...]).astype(BF).reshape(beams, cols, channels)
     key_out[...] = dot(every, w_key[...]).astype(BF).reshape(beams, count * cols, channels)
     value_out[...] = dot(every, w_value[...]).astype(BF).reshape(beams, count * cols, channels)
+    copy.wait()
+
+
+def stack_kernel(after_ref, *refs):
+    out = refs[-1]
+    for index, ref in enumerate(refs[:-1]):
+        out[index] = ref[...]
+
+
+def attention_kernel(count, allowed_ref, own_ref, query_ref, key_ref, value_ref, w_out, w_conv_hbm,
+                     attended_out, pieces_out, w_conv_out, sem):
+    copy = pltpu.make_async_copy(w_conv_hbm.at[TAPS - w_conv_out.shape[0] :], w_conv_out, sem)
+    copy.start()
+    beams, cols, channels = query_ref.shape
     allowed = allowed_ref[0:1, :] > 0.5
     for b in range(beams):
-        weights = weights_of(by_head(query_out[b]), key_out[b], allowed)
-        attended_out[b] = own_head(dot(weights.astype(BF), value_out[b])).astype(BF)
+        weights = weights_of(by_head(query_ref[b]), key_ref[b], allowed)
+        attended_out[b] = own_head(dot(weights.astype(BF), value_ref[b])).astype(BF)
+    own = own_ref[...].reshape(beams * cols, channels)
     mixed = own.astype(F32) + dot(attended_out[...].reshape(beams * cols, channels), w_out[...])
     me = lax.axis_index("azim")
     width = channels // count
@@ -220,8 +237,8 @@
 
 
 def backward_kernel(count, allowed_ref, all_ref, query_ref, key_ref, value_ref, attended_ref, grad_ref, layer_bf_ref,
-                    layer_ref, w_query, w_key, w_value, base_out, send_out, keep_out, pass_out,
-                    grad_query, grad_key, grad_value, sums):
+                    layer_ref, w_query, w_key, w_value, base_out, send_out, keep_out, *refs):
+    *pass_outs, grad_query, grad_key, grad_value, sums = refs
     beams, cols, channels = query_ref.shape
     scale = (channels // HEADS) ** (-0.5)
     allowed = allowed_ref[0:1, :] > 0.5
@@ -265,12 +282,26 @@
         sums[index] = dot(left, right, TN).astype(BF).reshape(8, width, channels)
     me = group_index()
     for differ in range(8):
-        target = pass_out if differ & 1 else keep_out
+        target = pass_outs[differ >> 1] if differ & 1 else keep_out.at[differ >> 1]
         for index in range(4):
             part = sums[index, me ^ differ]
             for half in range(channels // LANES):
                 row = (half * 4 + index) * width
-                target[differ >> 1, row : row + width, :] = part[:, half * LANES : (half + 1) * LANES]
+                target[row : row + width, :] = part[:, half * LANES : (half + 1) * LANES]
+
+
+def pack_kernel(keep_ref, layer_ref, send_ref, *refs):
+    come_refs = refs[:4]
+    mine_out, *give_outs, send_out = refs[4:]
+    rows = layer_ref.shape[0]
+    for block, ref in enumerate(come_refs):
+        total = (keep_ref[block].astype(F32) + ref[...].astype(F32)).astype(BF)
+        if block == 0:
+            mine_out[...] = total
+        else:
+            give_outs[block - 1][:rows, :] = layer_ref[...]
+            give_outs[block - 1][rows:, :] = total
+    send_out[...] = send_ref[...]
 
 
 def pieces_kernel(count, keep_ref, *refs):
@@ -337,18 +368,18 @@
 
 
 def last_kernel(count, own_piece, base_ref, taps_ref, *refs):
-    come_refs = refs[: count - 1]
-    features_out, weights_out = refs[count - 1 :]
+    grad_refs, piece_refs = refs[: count - 1], refs[count - 1 : 2 * count - 2]
+    features_out, weights_out = refs[2 * count - 2 :]
     beams, cols, channels = base_ref.shape
     rows = beams * cols
     total = base_ref[...].reshape(rows, channels)
     piece = own_piece[0].astype(F32)
-    start = rows * (channels // LANES)
-    for ref in come_refs:
+    for ref in grad_refs:
         total = total + jnp.concatenate(
             [ref[half * rows : (half + 1) * rows, :].astype(F32) for half in range(channels // LANES)], axis=1
         )
-        piece = piece + ref[start:, :].astype(F32)
+    for ref in piece_refs:
+        piece = piece + ref[...].astype(F32)
     features_out[...] = jnp.stack([total[b * cols : (b + 1) * cols] for b in range(beams)], axis=1).astype(BF)
     width, lanes = weights_out.shape[1:]
     for index in range(4):
@@ -374,10 +405,6 @@
 
 def swap(value, bits):
     return lax.ppermute(value, GROUP, [(i, i ^ bits) for i in range(8)])
-
-
-def add(left, right):
-    return (left.astype(F32) + right.astype(F32)).astype(BF)
 
 
 def per_device(features, cotangent, w_query, w_key, w_value, w_out, w_conv, sector_mask):
@@ -405,41 +432,51 @@
     )(*map(in_hbm, (features.reshape(token), cotangent.reshape(token), sector_mask, w_query, w_key, w_value, w_out)))
     distances = range(1, count)
     all_features = [own_features] + exchange({distance: own_features for distance in distances})
-    even = jnp.stack([own_cot] + [swap(own_cot, bits) for bits in (2, 4, 6)])
+    low = TAPS // 2
+    taps_hbm = in_hbm(w_conv.transpose(1, 0, 2))
+    every, queries, keys, values, w_low = call(
+        functools.partial(project_kernel, count),
+        [(whole, BF), (block, BF), (whole, BF), (whole, BF), ((low,) + square, BF)],
+        [VMEM] * (count + 3) + [HBM],
+        scratch=[pltpu.SemaphoreType.DMA],
+    )(*all_features, w_query, w_key, w_value, taps_hbm)
+
+    even = call(stack_kernel, [((4,) + block, BF)], [VMEM] * 5)(
+        queries, own_cot, *[swap(own_cot, bits) for bits in (2, 4, 6)]
+    )[0]
     odd = swap(even, 1)
+
+    pieces_shape = (count, cols, max(LANES, beams * lanes))
+    attended, pieces, w_high = call(
+        functools.partial(attention_kernel, count),
+        [(block, BF), (pieces_shape, BF), ((TAPS - low,) + square, BF)],
+        [VMEM] * 6 + [HBM],
+        scratch=[pltpu.SemaphoreType.DMA],
+    )(allowed, own_features, queries, keys, values, w_out, taps_hbm)
 
     spread = (4 * cols, 4 * width)
     edge = (8 * beams, channels)
     slices, edges = call(slices_kernel, [(spread, BF), ((2,) + edge, BF)], [VMEM] * 2)(even, odd)
     neighbours = exchange({distance: edges for distance in neighbour_distances(count)})
 
-    pieces_shape = (count, cols, max(LANES, beams * lanes))
-    every, queries, keys, values, attended, pieces, w_conv = call(
-        functools.partial(forward_kernel, count),
-        [(whole, BF), (block, BF), (whole, BF), (whole, BF), (block, BF), (pieces_shape, BF),
-         ((TAPS,) + square, BF)],
-        [VMEM] * (count + 5) + [HBM],
-        scratch=[pltpu.SemaphoreType.DMA],
-    )(allowed, *all_features, w_query, w_key, w_value, w_out, in_hbm(w_conv.transpose(1, 0, 2)))
-
     packed = exchange({distance: jnp.concatenate([slices, pieces[distance]]) for distance in distances})
     layer_block = jnp.concatenate([pieces[0]] + [part[4 * cols :] for part in packed])
 
     grad_layer, grad_layer_bf, grad_attended = call(
         functools.partial(conv_kernel, count),
         [(block, F32), (block, BF), (block, BF)],
-        [VMEM] * (4 + len(neighbours)),
+        [VMEM] * (5 + len(neighbours)),
         scratch=[
             pltpu.VMEM((3, beams + 2, cols + 16, channels), F32),
             pltpu.VMEM((2,) + edge, F32),
             pltpu.VMEM((3, 3, (beams + 2) * cols, channels), BF),
         ],
-    )(even, odd, *neighbours, w_conv, w_out)
+    )(even, odd, *neighbours, w_low, w_high, w_out)
 
     quarter = (4, 4 * width * channels // LANES, LANES)
-    base, send, keep, give = call(
+    base, send, keep, *gives = call(
         functools.partial(backward_kernel, count),
-        [(block, F32), ((count - 1, beams * cols * channels // LANES, LANES), BF), (quarter, BF), (quarter, BF)],
+        [(block, F32), ((count - 1, beams * cols * channels // LANES, LANES), BF), (quarter, BF)] + [(quarter[1:], BF)] * 4,
         [VMEM] * 12,
         scratch=[
             pltpu.VMEM(block, BF),
@@ -452,16 +489,20 @@
         w_query, w_key, w_value,
     )
 
-    sums = add(keep, swap(give, 1))
-    both = [swap(jnp.concatenate([layer_block, sums[bits // 2]]), bits) for bits in (2, 4, 6)]
+    rows = quarter[1] + layer_block.shape[0]
+    mine, *gives, send = call(
+        pack_kernel, [(quarter[1:], BF)] + [((rows, LANES), BF)] * 3 + [(send.shape, BF)], [VMEM] * 7
+    )(keep, layer_block, send, *[swap(give, 1) for give in gives])
+    both = [swap(give, bits) for give, bits in zip(gives, (2, 4, 6))]
+    come_grads = exchange({distance: send[distance - 1] for distance in distances})
     even_layers = jnp.stack([layer_block] + [part[: layer_block.shape[0]] for part in both])
     odd_layers = swap(even_layers, 1)
     sum_pieces = call(
         functools.partial(pieces_kernel, count),
         [((count, 2 * width, max(LANES, 2 * lanes)), BF)],
         [VMEM] * 4,
-    )(sums[0], *both)[0]
-    come = exchange({distance: jnp.concatenate([send[distance - 1], sum_pieces[distance]]) for distance in distances})
+    )(mine, *both)[0]
+    come_pieces = exchange({distance: sum_pieces[distance] for distance in distances})
 
     taps = call(
         functools.partial(taps_kernel, count),
@@ -476,8 +517,8 @@
     features_grad, weight_grads = call(
         functools.partial(last_kernel, count),
         [((cols, beams, channels), BF), ((4 + TAPS, width, lanes), F32)],
-        [VMEM] * (2 + count),
-    )(sum_pieces, base, taps, *come)
+        [VMEM] * (1 + 2 * count),
+    )(sum_pieces, base, taps, *come_grads, *come_pieces)
     return features_grad.reshape(features.shape), weight_grads.transpose(2, 0, 1)
 
 

time: 52.3 us -> 49.6 us (0.948)
  waiting for transfers between devices: 17.2 us -> 7.86 us
  starting transfers between devices: 24.4 us -> 30.2 us
  Pallas kernels: 9.35 us -> 10.4 us
    ppermute x11 -> x14, waiting for transfers between devices: 10.5 us -> 4.09 us  [swap_columns(): lax.ppermute(value, 'azim', [(i, i ^ distance) for i in range(count)])]
    ppermute x11 -> x14, starting transfers between devices: 16 us -> 22.1 us  [swap_columns(): lax.ppermute(value, 'azim', [(i, i ^ distance) for i in range(count)])]
    ppermute x9 -> x12, waiting for transfers between devices: 6.7 us -> 3.78 us  [swap(): return lax.ppermute(value, GROUP, [(i, i ^ bits) for i in range(8)])]
    pallas_call x1 -> x4, Pallas kernels: 2.01 us -> 3.09 us  [the longest x1 1.52 us: per_device(): call(functools.partial(attention_kernel, count), [(block, BF), (pieces_sh...]
    ppermute x9 -> x12, starting transfers between devices: 8.37 us -> 8.13 us  [swap(): return lax.ppermute(value, GROUP, [(i, i ^ bits) for i in range(8)])]
  transfers between devices with their start and end apart: 20 -> 26, of which waited for: 7 -> 11; matrix products, arithmetic and copies ran while one was open for 0% -> 0% of each run, Pallas kernels for 13% -> 15%
where the time goes in v4:
time: 49.6 us; the launch traced here: 49.4 us
  starting transfers between devices  30.2 us (61%)
  Pallas kernels  10.4 us (21%)
  waiting for transfers between devices  7.86 us (16%)
  between operations  0.84 us (2%)
    ppermute x14, starting transfers between devices, swap_columns(): lax.ppermute(value, 'azim', [(i, i ^ distance) for i in range(count)])  22.1 us
    ppermute x12, starting transfers between devices, swap(): return lax.ppermute(value, GROUP, [(i, i ^ bits) for i in range(8)])  8.13 us
    ppermute x14, waiting for transfers between devices, swap_columns(): lax.ppermute(value, 'azim', [(i, i ^ distance) for i in range(count)])  4.09 us
    ppermute x12, waiting for transfers between devices, swap(): return lax.ppermute(value, GROUP, [(i, i ^ bits) for i in range(8)])  3.78 us
    pallas_call x1, Pallas kernels, per_device(): call(functools.partial(backward_kernel, count), [(block, F32), ((count -...  1.88 us
    pallas_call x1, Pallas kernels, per_device(): call(functools.partial(attention_kernel, count), [(block, BF), (pieces_sh...  1.52 us
    pallas_call x1, Pallas kernels, per_device(): call(functools.partial(project_kernel, count), [(whole, BF), (block, BF),...  1.48 us
    pallas_call x1, Pallas kernels, per_device(): call(functools.partial(conv_kernel, count), [(block, F32), (block, BF), (...  1.45 us
  transfers between devices with their start and end apart: 26, of which 11 were waited for; matrix products, arithmetic and copies ran while one was open for 0% of the time, Pallas kernels for 15%

profile of v4, /device:TPU:0, one launch (start us, length us, event | category | flops | bytes accessed | tf_op | source)
XLA Modules:
  0.0 49.4 jit_solution(4206316758755432183)
XLA Ops:
  0.6 1.4 %shard_map.95 = (bf16[2,64,256]{2,1,0:T(8,128)(2,1)S(1)}, bf16[2,64,256]{2,1,0:T(8,128)(2,1)S(1)}, f32[8,256]{1,0:T(8,128)S(1)}, bf16[256,256]{1,0:T(8,128)(2,1)...) custom-call(bf16[64,2,256]{2,1,0:T(2,128)(2,1)} %bitcast.37, ...), custom_call_target="tpu_custom_call" | custom-call | flops 2000000000 | tf_op jit(solution)/shard_map/pallas_call | solution.py:422
  2.0 5.1 %collective-permute-start.2 = (bf16[2,64,256]{2,1,0:T(8,128)(2,1)S(1)}, bf16[2,64,256]{2,1,0:T(8,128)(2,1)S(1)}, u32[]{:S(2)}, u32[]{:S(2)}) collective-permute-start(bf16[2,64,256]{2,1,0:T(8,128)(2,1)S(1)} %get-tuple-element.37.refs_0_.own_ref), channel_id=1, source_target_pairs={{0,24},{8,16},{16,8},{24,0},{1,25},{9,17},{17,9},{25,1},{2,26},{10... | collective-permute-start | bytes 196616 | tf_op jit(solution)/shard_map/ppermute | solution.py:398
  7.2 0.6 %collective-permute-start = (bf16[2,64,256]{2,1,0:T(8,128)(2,1)S(1)}, bf16[2,64,256]{2,1,0:T(8,128)(2,1)S(1)}, u32[]{:S(2)}, u32[]{:S(2)}) collective-permute-start(bf16[2,64,256]{2,1,0:T(8,128)(2,1)S(1)} %get-tuple-element.37.refs_0_.own_ref), channel_id=1, source_target_pairs={{0,8},{8,0},{16,24},{24,16},{1,9},{9,1},{17,25},{25,17},{2,10},{10... | collective-permute-start | bytes 196616 | tf_op jit(solution)/shard_map/ppermute | solution.py:398
  7.8 2.6 %collective-permute-start.5 = (bf16[2,64,256]{2,1,0:T(8,128)(2,1)S(1)}, bf16[2,64,256]{2,1,0:T(8,128)(2,1)S(1)}, u32[]{:S(2)}, u32[]{:S(2)}) collective-permute-start(bf16[2,64,256]{2,1,0:T(8,128)(2,1)S(1)} %get-tuple-element.47.refs_0_), channel_id=1, source_target_pairs={{0,6},{1,7},{2,4},{3,5},{4,2},{5,3},{6,0},{7,1},{8,14},{9,15},{10,... | collective-permute-start | bytes 196616 | tf_op jit(solution)/shard_map/ppermute | solution.py:407
  10.4 0.5 %collective-permute-start.4 = (bf16[2,64,256]{2,1,0:T(8,128)(2,1)S(1)}, bf16[2,64,256]{2,1,0:T(8,128)(2,1)S(1)}, u32[]{:S(2)}, u32[]{:S(2)}) collective-permute-start(bf16[2,64,256]{2,1,0:T(8,128)(2,1)S(1)} %get-tuple-element.47.refs_0_), channel_id=1, source_target_pairs={{0,4},{1,5},{2,6},{3,7},{4,0},{5,1},{6,2},{7,3},{8,12},{9,13},{10,... | collective-permute-start | bytes 196616 | tf_op jit(solution)/shard_map/ppermute | solution.py:407
  10.9 0.0 collective-permute-done.2.refs_3_
  10.9 0.7 %collective-permute-start.3 = (bf16[2,64,256]{2,1,0:T(8,128)(2,1)S(1)}, bf16[2,64,256]{2,1,0:T(8,128)(2,1)S(1)}, u32[]{:S(2)}, u32[]{:S(2)}) collective-permute-start(bf16[2,64,256]{2,1,0:T(8,128)(2,1)S(1)} %get-tuple-element.47.refs_0_), channel_id=1, source_target_pairs={{0,2},{1,3},{2,0},{3,1},{4,6},{5,7},{6,4},{7,5},{8,10},{9,11},{10,... | collective-permute-start | bytes 196616 | tf_op jit(solution)/shard_map/ppermute | solution.py:407
  11.6 1.2 %collective-permute-done.1.refs_2_ = bf16[2,64,256]{2,1,0:T(8,128)(2,1)S(1)} collective-permute-done((bf16[2,64,256]{2,1,0:T(8,128)(2,1)S(1)}, bf16[2,64,256]{2,1,0:T(8,128)(2,1)S(1)}, u32[]{:S(2)}, u32[]{:S(2)}) %collective-permute-start.1) | collective-permute-done | bytes 65568 | tf_op jit(solution)/shard_map/ppermute | solution.py:398
  12.8 1.5 %shard_map.96 = (bf16[2,256,256]{2,1,0:T(8,128)(2,1)S(1)}, bf16[2,64,256]{2,1,0:T(8,128)(2,1)S(1)}, bf16[2,256,256]{2,1,0:T(8,128)(2,1)S(1)}, bf16[2,256,256]{2,1,0:T(8,128)(2,1)S(1)}, bf16[13,256,256]{2,1,0:T(8,128)(2,1)S(1)}) custom-call(bf16[2,64,256]{2,1,0:T(8,128)(2,1)S(1)} %get-tuple-element.37.refs_0_.own_ref, ...), custom_call_target="tpu_custom_call" | custom-call | flops 2000000000 | tf_op jit(solution)/shard_map/pallas_call | solution.py:437
  14.3 0.4 collective-permute-done.4.refs_2_
  14.6 0.5 %collective-permute-done.3.refs_1_ = bf16[2,64,256]{2,1,0:T(8,128)(2,1)S(1)} collective-permute-done((bf16[2,64,256]{2,1,0:T(8,128)(2,1)S(1)}, bf16[2,64,256]{2,1,0:T(8,128)(2,1)S(1)}, u32[]{:S(2)}, u32[]{:S(2)}) %collective-permute-start.3) | collective-permute-done | bytes 65568 | tf_op jit(solution)/shard_map/ppermute | solution.py:407
  15.2 0.1 collective-permute-start.6
  15.3 1.5 %shard_map.97 = (bf16[2,64,256]{2,1,0:T(8,128)(2,1)S(1)}, bf16[4,64,128]{2,1,0:T(8,128)(2,1)S(1)}, bf16[14,256,256]{2,1,0:T(8,128)(2,1)S(1)}) custom-call(f32[8,256]{1,0:T(8,128)S(1)} %get-tuple-element.36.allowed_ref, bf16[2,64,256]{2,1,0:T(8,128)(2,1)S(1)} %get-tuple-element.37.refs_0_.own_ref, ...), custom_call_target="tpu_custom_call" | custom-call | flops 2000000000 | tf_op jit(solution)/shard_map/pallas_call | solution.py:450
  16.8 0.4 shard_map.99
  17.2 3.7 %collective-permute-start.8 = (bf16[2,16,256]{2,1,0:T(8,128)(2,1)S(1)}, bf16[2,16,256]{2,1,0:T(8,128)(2,1)S(1)}, u32[]{:S(2)}, u32[]{:S(2)}) collective-permute-start(bf16[2,16,256]{2,1,0:T(8,128)(2,1)S(1)} %get-tuple-element.48), channel_id=1, source_target_pairs={{0,24},{8,16},{16,8},{24,0},{1,25},{9,17},{17,9},{25,1},{2,26},{10... | collective-permute-start | bytes 49160 | tf_op jit(solution)/shard_map/ppermute | solution.py:398
  20.8 0.0 collective-permute-start.7
  20.9 2.1 %collective-permute-start.9 = (bf16[320,128]{1,0:T(8,128)(2,1)S(1)}, bf16[320,128]{1,0:T(8,128)(2,1)S(1)}, u32[]{:S(2)}, u32[]{:S(2)}) collective-permute-start(bf16[320,128]{1,0:T(8,128)(2,1)S(1)} %get-tuple-element.84), channel_id=1, source_target_pairs={{0,8},{8,0},{16,24},{24,16},{1,9},{9,1},{17,25},{25,17},{2,10},{10... | collective-permute-start | bytes 245768 | tf_op jit(solution)/shard_map/ppermute | solution.py:398
  23.0 2.4 %collective-permute-start.11 = (bf16[320,128]{1,0:T(8,128)(2,1)S(1)}, bf16[320,128]{1,0:T(8,128)(2,1)S(1)}, u32[]{:S(2)}, u32[]{:S(2)}) collective-permute-start(bf16[320,128]{1,0:T(8,128)(2,1)S(1)} %get-tuple-element.86), channel_id=1, source_target_pairs={{0,24},{8,16},{16,8},{24,0},{1,25},{9,17},{17,9},{25,1},{2,26},{10... | collective-permute-start | bytes 245768 | tf_op jit(solution)/shard_map/ppermute | solution.py:398
  25.4 0.0 collective-permute-done.8.refs_1_
  25.4 0.0 collective-permute-done.7.refs_0_
  25.4 1.4 %shard_map.100 = (f32[2,64,256]{2,1,0:T(8,128)S(1)}, bf16[2,64,256]{2,1,0:T(8,128)(2,1)S(1)}, bf16[2,64,256]{2,1,0:T(8,128)(2,1)S(1)}) custom-call(bf16[4,2,64,256]{3,2,1,0:T(8,128)(2,1)S(1)} %shard_map.98.even_ref, bf16[4,2,64,256]{3,2,1,0:T(8,128)(2,1)S(1)} %collective-permute-done.6.odd_ref, bf16[2,16,256]{2,1,0:T(8,128)(2,1)S(1)} %collective-permute-done.7.refs_0_, ...), custom_call_target="tpu_custom_call" | custom-call | flops 2000000000 | tf_op jit(solution)/shard_map/pallas_call | solution.py:465
  26.9 1.9 %shard_map.101 = (f32[2,64,256]{2,1,0:T(8,128)S(1)}, bf16[3,256,128]{2,1,0:T(8,128)(2,1)S(1)}, bf16[4,256,128]{2,1,0:T(8,128)(2,1)S(1)}, bf16[256,128]{1,0:T(8,1...) custom-call(f32[8,256]{1,0:T(8,128)S(1)} %get-tuple-element.36.allowed_ref, ...), custom_call_target="tpu_custom_call" | custom-call | flops 2000000000 | tf_op jit(solution)/shard_map/pallas_call | solution.py:477
  28.7 0.1 collective-permute-start.12
  28.8 0.5 %collective-permute-start.13 = (bf16[256,128]{1,0:T(8,128)(2,1)S(1)}, bf16[256,128]{1,0:T(8,128)(2,1)S(1)}, u32[]{:S(2)}, u32[]{:S(2)}) collective-permute-start(bf16[256,128]{1,0:T(8,128)(2,1)S(1)} %get-tuple-element.59), channel_id=1, source_target_pairs={{0,1},{1,0},{2,3},{3,2},{4,5},{5,4},{6,7},{7,6},{8,9},{9,8},{10,11... | collective-permute-start | bytes 196616 | tf_op jit(solution)/shard_map/ppermute | solution.py:407
  29.3 0.0 collective-permute-done.9.refs_0_
  29.3 0.1 collective-permute-start.14
  29.4 1.9 %collective-permute-done.10.refs_1_ = bf16[320,128]{1,0:T(8,128)(2,1)S(1)} collective-permute-done((bf16[320,128]{1,0:T(8,128)(2,1)S(1)}, bf16[320,128]{1,0:T(8,128)(2,1)S(1)}, u32[]{:S(2)}, u32[]{:S(2)}) %collective-permute-start.10) | collective-permute-done | bytes 81952 | tf_op jit(solution)/shard_map/ppermute | solution.py:398
  31.4 1.2 %collective-permute-done.15.refs_3_ = bf16[256,128]{1,0:T(8,128)(2,1)S(1)} collective-permute-done((bf16[256,128]{1,0:T(8,128)(2,1)S(1)}, bf16[256,128]{1,0:T(8,128)(2,1)S(1)}, u32[]{:S(2)}, u32[]{:S(2)}) %collective-permute-start.15) | collective-permute-done | bytes 65568 | tf_op jit(solution)/shard_map/ppermute | solution.py:407
  32.6 0.1 shard_map.102
  32.7 1.0 %collective-permute-start.16 = (bf16[512,128]{1,0:T(8,128)(2,1)S(1)}, bf16[512,128]{1,0:T(8,128)(2,1)S(1)}, u32[]{:S(2)}, u32[]{:S(2)}) collective-permute-start(bf16[512,128]{1,0:T(8,128)(2,1)S(1)} %get-tuple-element.63), channel_id=1, source_target_pairs={{0,2},{1,3},{2,0},{3,1},{4,6},{5,7},{6,4},{7,5},{8,10},{9,11},{10,... | collective-permute-start | bytes 393224 | tf_op jit(solution)/shard_map/ppermute | solution.py:407
  33.7 1.5 %collective-permute-start.17 = (bf16[512,128]{1,0:T(8,128)(2,1)S(1)}, bf16[512,128]{1,0:T(8,128)(2,1)S(1)}, u32[]{:S(2)}, u32[]{:S(2)}) collective-permute-start(bf16[512,128]{1,0:T(8,128)(2,1)S(1)} %get-tuple-element.64), channel_id=1, source_target_pairs={{0,4},{1,5},{2,6},{3,7},{4,0},{5,1},{6,2},{7,3},{8,12},{9,13},{10,... | collective-permute-start | bytes 393224 | tf_op jit(solution)/shard_map/ppermute | solution.py:407
  35.2 1.0 %collective-permute-start.18 = (bf16[512,128]{1,0:T(8,128)(2,1)S(1)}, bf16[512,128]{1,0:T(8,128)(2,1)S(1)}, u32[]{:S(2)}, u32[]{:S(2)}) collective-permute-start(bf16[512,128]{1,0:T(8,128)(2,1)S(1)} %get-tuple-element.65), channel_id=1, source_target_pairs={{0,6},{1,7},{2,4},{3,5},{4,2},{5,3},{6,0},{7,1},{8,14},{9,15},{10,... | collective-permute-start | bytes 393224 | tf_op jit(solution)/shard_map/ppermute | solution.py:407
  36.2 0.2 collective-permute-start.22
  36.4 2.3 %collective-permute-start.21 = (bf16[256,128]{1,0:T(8,128)(2,1)S(1)}, bf16[256,128]{1,0:T(8,128)(2,1)S(1)}, u32[]{:S(2)}, u32[]{:S(2)}) collective-permute-start(bf16[256,128]{1,0:T(8,128)(2,1)S(1)} %get-tuple-element.73), channel_id=1, source_target_pairs={{0,16},{8,24},{16,0},{24,8},{1,17},{9,25},{17,1},{25,9},{2,18},{10... | collective-permute-start | bytes 196616 | tf_op jit(solution)/shard_map/ppermute | solution.py:398
  38.7 0.3 collective-permute-done.16.refs_0_
  39.1 1.6 %collective-permute-start.20 = (bf16[256,128]{1,0:T(8,128)(2,1)S(1)}, bf16[256,128]{1,0:T(8,128)(2,1)S(1)}, u32[]{:S(2)}, u32[]{:S(2)}) collective-permute-start(bf16[256,128]{1,0:T(8,128)(2,1)S(1)} %get-tuple-element.74), channel_id=1, source_target_pairs={{0,8},{8,0},{16,24},{24,16},{1,9},{9,1},{17,25},{25,17},{2,10},{10... | collective-permute-start | bytes 196616 | tf_op jit(solution)/shard_map/ppermute | solution.py:398
  40.7 0.1 collective-permute-done.17.refs_1_
  40.8 1.2 %collective-permute-done.18.refs_2_ = bf16[512,128]{1,0:T(8,128)(2,1)S(1)} collective-permute-done((bf16[512,128]{1,0:T(8,128)(2,1)S(1)}, bf16[512,128]{1,0:T(8,128)(2,1)S(1)}, u32[]{:S(2)}, u32[]{:S(2)}) %collective-permute-start.18) | collective-permute-done | bytes 131104 | tf_op jit(solution)/shard_map/ppermute | solution.py:407
  42.1 0.1 collective-permute-start.19
  42.2 0.1 shard_map.103.own_piece
  42.3 0.1 collective-permute-start.25
  42.4 0.5 collective-permute-done.22.refs_2_
  42.8 1.8 %collective-permute-start.24 = (bf16[64,128]{1,0:T(8,128)(2,1)S(1)}, bf16[64,128]{1,0:T(8,128)(2,1)S(1)}, u32[]{:S(2)}, u32[]{:S(2)}) collective-permute-start(bf16[64,128]{1,0:T(8,128)(2,1)S(1)} %get-tuple-element.76), channel_id=1, source_target_pairs={{0,16},{8,24},{16,0},{24,8},{1,17},{9,25},{17,1},{25,9},{2,18},{10... | collective-permute-start | bytes 49160 | tf_op jit(solution)/shard_map/ppermute | solution.py:398
  44.6 2.2 %collective-permute-start.23 = (bf16[64,128]{1,0:T(8,128)(2,1)S(1)}, bf16[64,128]{1,0:T(8,128)(2,1)S(1)}, u32[]{:S(2)}, u32[]{:S(2)}) collective-permute-start(bf16[64,128]{1,0:T(8,128)(2,1)S(1)} %get-tuple-element.77), channel_id=1, source_target_pairs={{0,8},{8,0},{16,24},{24,16},{1,9},{9,1},{17,25},{25,17},{2,10},{10... | collective-permute-start | bytes 49160 | tf_op jit(solution)/shard_map/ppermute | solution.py:398
  46.8 1.2 %shard_map.104.taps_ref = f32[27,32,64]{2,1,0:T(8,128)S(1)} custom-call(bf16[4,256,128]{2,1,0:T(8,128)(2,1)S(1)} %pad_maximum_fusion.even_ref, bf16[4,256,128]{2,1,0:T(8,128)(2,1)S(1)} %collective-permute-done.19.odd_ref, bf16[256,128]{1,0:T(8,128)(2,1)S(1)} %get-tuple-element.56.own_ref, bf16[320,128]{1,0:T(8,128)(2,1)S(1)} %collective-permute-done.9.refs_0_, ...), custom_call_target="tpu_custom_call" | custom-call | flops 2000000000 | tf_op jit(solution)/shard_map/pallas_call | solution.py:507
  48.0 0.1 collective-permute-done.25.refs_5_
  48.0 0.4 collective-permute-done.23.refs_3_
  48.5 1.0 %shard_map.105 = (bf16[64,2,256]{2,1,0:T(2,128)(2,1)}, f32[31,32,64]{2,1,0:T(8,128)}) custom-call(bf16[4,64,128]{2,1,0:T(8,128)(2,1)S(1)} %shard_map.103.own_piece, f32[2,64,256]{2,1,0:T(8,128)S(1)} %get-tuple-element.66.base_ref, f32[27,32,64]{2,1,0:T(8,128)S(1)} %shard_map.104.taps_ref, bf16[256,128]{1,0:T(8,128)(2,1)S(1)} %collective-permute-done.20.refs_0_, ...), custom_call_target="tpu_custom_call" | custom-call | flops 2000000000 | tf_op jit(solution)/shard_map/pallas_call | solution.py:517
  (27 shorter events, 0.2 us)
Async XLA Ops:
  2.0 8.9 %collective-permute-start.2 = (bf16[2,64,256]{2,1,0:T(8,128)(2,1)S(1)}, bf16[2,64,256]{2,1,0:T(8,128)(2,1)S(1)}, u32[]{:S(2)}, u32[]{:S(2)}) collective-permute-start(bf16[2,64,256]{2,1,0:T(8,128)(2,1)S(1)} %get-tuple-element.37.refs_0_.own_ref), channel_id=1, source_target_pairs={{0,24},{8,16},{16,8},{24,0},{1,25},{9,17},{17,9},{25,1},{2,26},{10... | collective-permute-start | bytes 196616 | tf_op jit(solution)/shard_map/ppermute | solution.py:398
  7.1 5.6 %collective-permute-start.1 = (bf16[2,64,256]{2,1,0:T(8,128)(2,1)S(1)}, bf16[2,64,256]{2,1,0:T(8,128)(2,1)S(1)}, u32[]{:S(2)}, u32[]{:S(2)}) collective-permute-start(bf16[2,64,256]{2,1,0:T(8,128)(2,1)S(1)} %get-tuple-element.37.refs_0_.own_ref), channel_id=1, source_target_pairs={{0,16},{8,24},{16,0},{24,8},{1,17},{9,25},{17,1},{25,9},{2,18},{10... | collective-permute-start | bytes 196616 | tf_op jit(solution)/shard_map/ppermute | solution.py:398
  7.2 5.6 %collective-permute-start = (bf16[2,64,256]{2,1,0:T(8,128)(2,1)S(1)}, bf16[2,64,256]{2,1,0:T(8,128)(2,1)S(1)}, u32[]{:S(2)}, u32[]{:S(2)}) collective-permute-start(bf16[2,64,256]{2,1,0:T(8,128)(2,1)S(1)} %get-tuple-element.37.refs_0_.own_ref), channel_id=1, source_target_pairs={{0,8},{8,0},{16,24},{24,16},{1,9},{9,1},{17,25},{25,17},{2,10},{10... | collective-permute-start | bytes 196616 | tf_op jit(solution)/shard_map/ppermute | solution.py:398
  7.8 6.5 %collective-permute-start.5 = (bf16[2,64,256]{2,1,0:T(8,128)(2,1)S(1)}, bf16[2,64,256]{2,1,0:T(8,128)(2,1)S(1)}, u32[]{:S(2)}, u32[]{:S(2)}) collective-permute-start(bf16[2,64,256]{2,1,0:T(8,128)(2,1)S(1)} %get-tuple-element.47.refs_0_), channel_id=1, source_target_pairs={{0,6},{1,7},{2,4},{3,5},{4,2},{5,3},{6,0},{7,1},{8,14},{9,15},{10,... | collective-permute-start | bytes 196616 | tf_op jit(solution)/shard_map/ppermute | solution.py:407
  10.4 4.3 %collective-permute-start.4 = (bf16[2,64,256]{2,1,0:T(8,128)(2,1)S(1)}, bf16[2,64,256]{2,1,0:T(8,128)(2,1)S(1)}, u32[]{:S(2)}, u32[]{:S(2)}) collective-permute-start(bf16[2,64,256]{2,1,0:T(8,128)(2,1)S(1)} %get-tuple-element.47.refs_0_), channel_id=1, source_target_pairs={{0,4},{1,5},{2,6},{3,7},{4,0},{5,1},{6,2},{7,3},{8,12},{9,13},{10,... | collective-permute-start | bytes 196616 | tf_op jit(solution)/shard_map/ppermute | solution.py:407
  10.9 4.3 %collective-permute-start.3 = (bf16[2,64,256]{2,1,0:T(8,128)(2,1)S(1)}, bf16[2,64,256]{2,1,0:T(8,128)(2,1)S(1)}, u32[]{:S(2)}, u32[]{:S(2)}) collective-permute-start(bf16[2,64,256]{2,1,0:T(8,128)(2,1)S(1)} %get-tuple-element.47.refs_0_), channel_id=1, source_target_pairs={{0,2},{1,3},{2,0},{3,1},{4,6},{5,7},{6,4},{7,5},{8,10},{9,11},{10,... | collective-permute-start | bytes 196616 | tf_op jit(solution)/shard_map/ppermute | solution.py:407
  15.2 1.6 %collective-permute-start.6 = (bf16[4,2,64,256]{3,2,1,0:T(8,128)(2,1)S(1)}, bf16[4,2,64,256]{3,2,1,0:T(8,128)(2,1)S(1)}, u32[]{:S(2)}, u32[]{:S(2)}) collective-permute-start(bf16[4,2,64,256]{3,2,1,0:T(8,128)(2,1)S(1)} %shard_map.98.even_ref), channel_id=1, source_target_pairs={{0,1},{1,0},{2,3},{3,2},{4,5},{5,4},{6,7},{7,6},{8,9},{9,8},{10,11... | collective-permute-start | bytes 786440 | tf_op jit(solution)/shard_map/ppermute | solution.py:407
  17.2 8.2 %collective-permute-start.8 = (bf16[2,16,256]{2,1,0:T(8,128)(2,1)S(1)}, bf16[2,16,256]{2,1,0:T(8,128)(2,1)S(1)}, u32[]{:S(2)}, u32[]{:S(2)}) collective-permute-start(bf16[2,16,256]{2,1,0:T(8,128)(2,1)S(1)} %get-tuple-element.48), channel_id=1, source_target_pairs={{0,24},{8,16},{16,8},{24,0},{1,25},{9,17},{17,9},{25,1},{2,26},{10... | collective-permute-start | bytes 49160 | tf_op jit(solution)/shard_map/ppermute | solution.py:398
  20.8 4.6 %collective-permute-start.7 = (bf16[2,16,256]{2,1,0:T(8,128)(2,1)S(1)}, bf16[2,16,256]{2,1,0:T(8,128)(2,1)S(1)}, u32[]{:S(2)}, u32[]{:S(2)}) collective-permute-start(bf16[2,16,256]{2,1,0:T(8,128)(2,1)S(1)} %get-tuple-element.48), channel_id=1, source_target_pairs={{0,8},{8,0},{16,24},{24,16},{1,9},{9,1},{17,25},{25,17},{2,10},{10... | collective-permute-start | bytes 49160 | tf_op jit(solution)/shard_map/ppermute | solution.py:398
  20.9 8.5 %collective-permute-start.9 = (bf16[320,128]{1,0:T(8,128)(2,1)S(1)}, bf16[320,128]{1,0:T(8,128)(2,1)S(1)}, u32[]{:S(2)}, u32[]{:S(2)}) collective-permute-start(bf16[320,128]{1,0:T(8,128)(2,1)S(1)} %get-tuple-element.84), channel_id=1, source_target_pairs={{0,8},{8,0},{16,24},{24,16},{1,9},{9,1},{17,25},{25,17},{2,10},{10... | collective-permute-start | bytes 245768 | tf_op jit(solution)/shard_map/ppermute | solution.py:398
  23.0 8.4 %collective-permute-start.10 = (bf16[320,128]{1,0:T(8,128)(2,1)S(1)}, bf16[320,128]{1,0:T(8,128)(2,1)S(1)}, u32[]{:S(2)}, u32[]{:S(2)}) collective-permute-start(bf16[320,128]{1,0:T(8,128)(2,1)S(1)} %get-tuple-element.85), channel_id=1, source_target_pairs={{0,16},{8,24},{16,0},{24,8},{1,17},{9,25},{17,1},{25,9},{2,18},{10... | collective-permute-start | bytes 245768 | tf_op jit(solution)/shard_map/ppermute | solution.py:398
  23.0 8.4 %collective-permute-start.11 = (bf16[320,128]{1,0:T(8,128)(2,1)S(1)}, bf16[320,128]{1,0:T(8,128)(2,1)S(1)}, u32[]{:S(2)}, u32[]{:S(2)}) collective-permute-start(bf16[320,128]{1,0:T(8,128)(2,1)S(1)} %get-tuple-element.86), channel_id=1, source_target_pairs={{0,24},{8,16},{16,8},{24,0},{1,25},{9,17},{17,9},{25,1},{2,26},{10... | collective-permute-start | bytes 245768 | tf_op jit(solution)/shard_map/ppermute | solution.py:398
  28.7 2.6 %collective-permute-start.12 = (bf16[256,128]{1,0:T(8,128)(2,1)S(1)}, bf16[256,128]{1,0:T(8,128)(2,1)S(1)}, u32[]{:S(2)}, u32[]{:S(2)}) collective-permute-start(bf16[256,128]{1,0:T(8,128)(2,1)S(1)} %get-tuple-element.58), channel_id=1, source_target_pairs={{0,1},{1,0},{2,3},{3,2},{4,5},{5,4},{6,7},{7,6},{8,9},{9,8},{10,11... | collective-permute-start | bytes 196616 | tf_op jit(solution)/shard_map/ppermute | solution.py:407
  28.8 2.6 %collective-permute-start.13 = (bf16[256,128]{1,0:T(8,128)(2,1)S(1)}, bf16[256,128]{1,0:T(8,128)(2,1)S(1)}, u32[]{:S(2)}, u32[]{:S(2)}) collective-permute-start(bf16[256,128]{1,0:T(8,128)(2,1)S(1)} %get-tuple-element.59), channel_id=1, source_target_pairs={{0,1},{1,0},{2,3},{3,2},{4,5},{5,4},{6,7},{7,6},{8,9},{9,8},{10,11... | collective-permute-start | bytes 196616 | tf_op jit(solution)/shard_map/ppermute | solution.py:407
  29.3 2.1 %collective-permute-start.14 = (bf16[256,128]{1,0:T(8,128)(2,1)S(1)}, bf16[256,128]{1,0:T(8,128)(2,1)S(1)}, u32[]{:S(2)}, u32[]{:S(2)}) collective-permute-start(bf16[256,128]{1,0:T(8,128)(2,1)S(1)} %get-tuple-element.60), channel_id=1, source_target_pairs={{0,1},{1,0},{2,3},{3,2},{4,5},{5,4},{6,7},{7,6},{8,9},{9,8},{10,11... | collective-permute-start | bytes 196616 | tf_op jit(solution)/shard_map/ppermute | solution.py:407
  31.3 1.3 %collective-permute-start.15 = (bf16[256,128]{1,0:T(8,128)(2,1)S(1)}, bf16[256,128]{1,0:T(8,128)(2,1)S(1)}, u32[]{:S(2)}, u32[]{:S(2)}) collective-permute-start(bf16[256,128]{1,0:T(8,128)(2,1)S(1)} %get-tuple-element.61), channel_id=1, source_target_pairs={{0,1},{1,0},{2,3},{3,2},{4,5},{5,4},{6,7},{7,6},{8,9},{9,8},{10,11... | collective-permute-start | bytes 196616 | tf_op jit(solution)/shard_map/ppermute | solution.py:407
  32.7 6.4 %collective-permute-start.16 = (bf16[512,128]{1,0:T(8,128)(2,1)S(1)}, bf16[512,128]{1,0:T(8,128)(2,1)S(1)}, u32[]{:S(2)}, u32[]{:S(2)}) collective-permute-start(bf16[512,128]{1,0:T(8,128)(2,1)S(1)} %get-tuple-element.63), channel_id=1, source_target_pairs={{0,2},{1,3},{2,0},{3,1},{4,6},{5,7},{6,4},{7,5},{8,10},{9,11},{10,... | collective-permute-start | bytes 393224 | tf_op jit(solution)/shard_map/ppermute | solution.py:407
  33.7 7.2 %collective-permute-start.17 = (bf16[512,128]{1,0:T(8,128)(2,1)S(1)}, bf16[512,128]{1,0:T(8,128)(2,1)S(1)}, u32[]{:S(2)}, u32[]{:S(2)}) collective-permute-start(bf16[512,128]{1,0:T(8,128)(2,1)S(1)} %get-tuple-element.64), channel_id=1, source_target_pairs={{0,4},{1,5},{2,6},{3,7},{4,0},{5,1},{6,2},{7,3},{8,12},{9,13},{10,... | collective-permute-start | bytes 393224 | tf_op jit(solution)/shard_map/ppermute | solution.py:407
  35.2 6.9 %collective-permute-start.18 = (bf16[512,128]{1,0:T(8,128)(2,1)S(1)}, bf16[512,128]{1,0:T(8,128)(2,1)S(1)}, u32[]{:S(2)}, u32[]{:S(2)}) collective-permute-start(bf16[512,128]{1,0:T(8,128)(2,1)S(1)} %get-tuple-element.65), channel_id=1, source_target_pairs={{0,6},{1,7},{2,4},{3,5},{4,2},{5,3},{6,0},{7,1},{8,14},{9,15},{10,... | collective-permute-start | bytes 393224 | tf_op jit(solution)/shard_map/ppermute | solution.py:407
  36.2 6.6 %collective-permute-start.22 = (bf16[256,128]{1,0:T(8,128)(2,1)S(1)}, bf16[256,128]{1,0:T(8,128)(2,1)S(1)}, u32[]{:S(2)}, u32[]{:S(2)}) collective-permute-start(bf16[256,128]{1,0:T(8,128)(2,1)S(1)} %get-tuple-element.72), channel_id=1, source_target_pairs={{0,24},{8,16},{16,8},{24,0},{1,25},{9,17},{17,9},{25,1},{2,26},{10... | collective-permute-start | bytes 196616 | tf_op jit(solution)/shard_map/ppermute | solution.py:398
  36.4 11.5 %collective-permute-start.21 = (bf16[256,128]{1,0:T(8,128)(2,1)S(1)}, bf16[256,128]{1,0:T(8,128)(2,1)S(1)}, u32[]{:S(2)}, u32[]{:S(2)}) collective-permute-start(bf16[256,128]{1,0:T(8,128)(2,1)S(1)} %get-tuple-element.73), channel_id=1, source_target_pairs={{0,16},{8,24},{16,0},{24,8},{1,17},{9,25},{17,1},{25,9},{2,18},{10... | collective-permute-start | bytes 196616 | tf_op jit(solution)/shard_map/ppermute | solution.py:398
  39.1 8.9 %collective-permute-start.20 = (bf16[256,128]{1,0:T(8,128)(2,1)S(1)}, bf16[256,128]{1,0:T(8,128)(2,1)S(1)}, u32[]{:S(2)}, u32[]{:S(2)}) collective-permute-start(bf16[256,128]{1,0:T(8,128)(2,1)S(1)} %get-tuple-element.74), channel_id=1, source_target_pairs={{0,8},{8,0},{16,24},{24,16},{1,9},{9,1},{17,25},{25,17},{2,10},{10... | collective-permute-start | bytes 196616 | tf_op jit(solution)/shard_map/ppermute | solution.py:398
  42.1 2.5 %collective-permute-start.19 = (bf16[4,256,128]{2,1,0:T(8,128)(2,1)S(1)}, bf16[4,256,128]{2,1,0:T(8,128)(2,1)S(1)}, u32[]{:S(2)}, u32[]{:S(2)}) collective-permute-start(bf16[4,256,128]{2,1,0:T(8,128)(2,1)S(1)} %pad_maximum_fusion.even_ref), channel_id=1, source_target_pairs={{0,1},{1,0},{2,3},{3,2},{4,5},{5,4},{6,7},{7,6},{8,9},{9,8},{10,11... | collective-permute-start | bytes 786440 | tf_op jit(solution)/shard_map/ppermute | solution.py:407
  42.3 5.8 %collective-permute-start.25 = (bf16[64,128]{1,0:T(8,128)(2,1)S(1)}, bf16[64,128]{1,0:T(8,128)(2,1)S(1)}, u32[]{:S(2)}, u32[]{:S(2)}) collective-permute-start(bf16[64,128]{1,0:T(8,128)(2,1)S(1)} %get-tuple-element.75), channel_id=1, source_target_pairs={{0,24},{8,16},{16,8},{24,0},{1,25},{9,17},{17,9},{25,1},{2,26},{10... | collective-permute-start | bytes 49160 | tf_op jit(solution)/shard_map/ppermute | solution.py:398
  42.8 5.2 %collective-permute-start.24 = (bf16[64,128]{1,0:T(8,128)(2,1)S(1)}, bf16[64,128]{1,0:T(8,128)(2,1)S(1)}, u32[]{:S(2)}, u32[]{:S(2)}) collective-permute-start(bf16[64,128]{1,0:T(8,128)(2,1)S(1)} %get-tuple-element.76), channel_id=1, source_target_pairs={{0,16},{8,24},{16,0},{24,8},{1,17},{9,25},{17,1},{25,9},{2,18},{10... | collective-permute-start | bytes 49160 | tf_op jit(solution)/shard_map/ppermute | solution.py:398
  44.6 3.9 %collective-permute-start.23 = (bf16[64,128]{1,0:T(8,128)(2,1)S(1)}, bf16[64,128]{1,0:T(8,128)(2,1)S(1)}, u32[]{:S(2)}, u32[]{:S(2)}) collective-permute-start(bf16[64,128]{1,0:T(8,128)(2,1)S(1)} %get-tuple-element.77), channel_id=1, source_target_pairs={{0,8},{8,0},{16,24},{24,16},{1,9},{9,1},{17,25},{25,17},{2,10},{10... | collective-permute-start | bytes 49160 | tf_op jit(solution)/shard_map/ppermute | solution.py:398

commit v5 on v4

--- a/solution.py
+++ b/solution.py
@@ -28,13 +28,14 @@
     return lax.dot_general(left, right, (dims, ((), ())), preferred_element_type=F32)
 
 
-def call(kernel, outs, in_specs, scratch=(), limit=40, micros=2):
+def call(kernel, outs, in_specs, out_specs=None, scratch=(), aliases=None, limit=40, micros=2):
     return pl.pallas_call(
         kernel,
         cost_estimate=pl.CostEstimate(flops=int(micros * 1e9), bytes_accessed=0, transcendentals=0),
         out_shape=[jax.ShapeDtypeStruct(shape, dtype) for shape, dtype in outs],
         in_specs=in_specs,
-        out_specs=[VMEM] * len(outs),
+        out_specs=out_specs or [VMEM] * len(outs),
+        input_output_aliases=aliases or {},
         scratch_shapes=list(scratch),
         compiler_params=pltpu.CompilerParams(vmem_limit_bytes=limit << 20),
     )
@@ -49,36 +50,15 @@
     return lax.axis_index("beam") * lax.axis_size("sweep") + lax.axis_index("sweep")
 
 
-def prep_kernel(count, features_hbm, cot_hbm, mask_hbm, *refs):
-    weights_hbm = refs[:4]
-    features_out, cot_out, allowed_out = refs[4:7]
-    weights_out = refs[7:11]
-    features, cot, mask, sems = refs[11:]
-    copies = [
-        pltpu.make_async_copy(source, target, sems.at[index])
-        for index, (source, target) in enumerate(
-            zip((features_hbm, cot_hbm, mask_hbm) + weights_hbm, (features, cot, mask) + weights_out)
-        )
-    ]
-    for copy in copies:
-        copy.start()
-    for copy, source, target in ((copies[0], features, features_out), (copies[1], cot, cot_out)):
-        copy.wait()
-        wide = source[...].astype(F32)
-        for b in range(wide.shape[1]):
-            target[b] = wide[:, b, :].astype(BF)
-    copies[2].wait()
+def allowed_row(mask, count, keys):
     me = lax.axis_index("azim")
-    square = mask[...].astype(F32)
+    square = mask.astype(F32)
     row = lax.broadcasted_iota(jnp.int32, square.shape, 0)
     own = jnp.sum(jnp.where(row == me, square, 0.0), axis=0, keepdims=True)
-    keys = allowed_out.shape[1]
     sector = lax.broadcasted_iota(jnp.int32, (count, keys), 0)
     block = lax.broadcasted_iota(jnp.int32, (count, keys), 1) // SECTOR
     spread = jnp.where(sector == block ^ me, 1.0, 0.0).astype(BF)
-    allowed_out[...] = dot(jnp.broadcast_to(own, (8, count)).astype(BF), spread)
-    for copy in copies[3:]:
-        copy.wait()
+    return dot(jnp.broadcast_to(own, (8, count)).astype(BF), spread)
 
 
 def slices_kernel(even_ref, odd_ref, slices_out, edges_out):
@@ -118,7 +98,7 @@
 def conv_kernel(count, even_ref, odd_ref, *refs):
     distances = neighbour_distances(count)
     edge_refs = refs[: len(distances)]
-    w_low_ref, w_high_ref, w_out_ref, layer_out, layer_bf_out, attended_out, padded, edges, shifted = refs[len(distances) :]
+    w_ref, w_out_ref, layer_out, layer_bf_out, attended_out, padded, edges, shifted = refs[len(distances) :]
     me = group_index()
     column = lax.axis_index("azim")
     sweep = lax.axis_index("sweep")
@@ -158,9 +138,7 @@
             for k in (-1, 0, 1):
                 rows = shifted[i + 1, 1 - j, (1 - k) * cols : (1 - k + beams) * cols, :]
                 tap = 9 * (i + 1) + 3 * (j + 1) + (k + 1)
-                low = w_low_ref.shape[0]
-                w_tap = w_low_ref[tap] if tap < low else w_high_ref[tap - low]
-                total = total + dot(rows, w_tap, NT)
+                total = total + dot(rows, w_ref[tap], NT)
     rounded = total.astype(BF)
     layer_out[...] = total.reshape(beams, cols, channels)
     layer_bf_out[...] = rounded.reshape(beams, cols, channels)
@@ -193,37 +171,54 @@
 
 
 def project_kernel(count, *refs):
-    feature_refs = refs[:count]
-    w_query, w_key, w_value, w_conv_hbm, all_out, query_out, key_out, value_out, w_conv_out, sem = refs[count:]
-    copy = pltpu.make_async_copy(w_conv_hbm.at[: w_conv_out.shape[0]], w_conv_out, sem)
-    copy.start()
-    beams, cols, channels = feature_refs[0].shape
-    for ahead in range(count):
-        all_out[:, ahead * cols : (ahead + 1) * cols, :] = feature_refs[ahead][...]
-    own = feature_refs[0][...].reshape(beams * cols, channels)
+    come_refs = refs[: count - 1]
+    own_hbm, cot_hbm, *weights_hbm, mask_hbm = refs[count - 1 : count + 6]
+    all_out, query_out, key_out, value_out, allowed_out, w_out_out, cot_out = refs[count + 6 : count + 13]
+    own, cot, w_query, w_key, w_value, mask, sems = refs[count + 13 :]
+    targets = (own, w_key, w_value, w_query, mask, w_out_out, cot)
+    sources = (own_hbm, weights_hbm[1], weights_hbm[2], weights_hbm[0], mask_hbm, weights_hbm[3], cot_hbm)
+    copies = [
+        pltpu.make_async_copy(source, target, sems.at[index])
+        for index, (source, target) in enumerate(zip(sources, targets))
+    ]
+    for copy in copies:
+        copy.start()
+    cols, beams, channels = own.shape
+    for distance in range(1, count):
+        all_out[:, distance * cols : (distance + 1) * cols, :] = jnp.swapaxes(come_refs[distance - 1][...], 0, 1)
+    copies[0].wait()
+    all_out[:, :cols, :] = jnp.swapaxes(own[...], 0, 1)
     every = all_out[...].reshape(beams * count * cols, channels)
-    query_out[...] = dot(own, w_query[...]).astype(BF).reshape(beams, cols, channels)
+    copies[1].wait()
     key_out[...] = dot(every, w_key[...]).astype(BF).reshape(beams, count * cols, channels)
+    copies[2].wait()
     value_out[...] = dot(every, w_value[...]).astype(BF).reshape(beams, count * cols, channels)
-    copy.wait()
-
-
-def stack_kernel(after_ref, *refs):
-    out = refs[-1]
-    for index, ref in enumerate(refs[:-1]):
-        out[index] = ref[...]
-
-
-def attention_kernel(count, allowed_ref, own_ref, query_ref, key_ref, value_ref, w_out, w_conv_hbm,
-                     attended_out, pieces_out, w_conv_out, sem):
-    copy = pltpu.make_async_copy(w_conv_hbm.at[TAPS - w_conv_out.shape[0] :], w_conv_out, sem)
-    copy.start()
+    copies[3].wait()
+    mine = all_out[:, :cols, :].reshape(beams * cols, channels)
+    query_out[...] = dot(mine, w_query[...]).astype(BF).reshape(beams, cols, channels)
+    copies[4].wait()
+    allowed_out[...] = allowed_row(mask[...], count, count * cols)
+    copies[5].wait()
+    copies[6].wait()
+    cot_out[...] = jnp.swapaxes(cot[...], 0, 1)
+
+
+def stack_kernel(own_ref, *refs):
+    *come_refs, out = refs
+    out[0] = own_ref[...]
+    for index, ref in enumerate(come_refs, 1):
+        out[index] = jnp.swapaxes(ref[...], 0, 1)
+
+
+def attention_kernel(count, allowed_ref, all_ref, query_ref, key_ref, value_ref, w_out,
+                     attended_out, pieces_out, weights_out):
     beams, cols, channels = query_ref.shape
     allowed = allowed_ref[0:1, :] > 0.5
     for b in range(beams):
         weights = weights_of(by_head(query_ref[b]), key_ref[b], allowed)
+        weights_out[b] = weights
         attended_out[b] = own_head(dot(weights.astype(BF), value_ref[b])).astype(BF)
-    own = own_ref[...].reshape(beams * cols, channels)
+    own = all_ref[:, :cols, :].reshape(beams * cols, channels)
     mixed = own.astype(F32) + dot(attended_out[...].reshape(beams * cols, channels), w_out[...])
     me = lax.axis_index("azim")
     width = channels // count
@@ -233,19 +228,17 @@
         if spare:
             part.append(jnp.zeros((cols, spare), F32))
         pieces_out[owner ^ me] = jnp.concatenate(part, axis=1).astype(BF)
-    copy.wait()
-
-
-def backward_kernel(count, allowed_ref, all_ref, query_ref, key_ref, value_ref, attended_ref, grad_ref, layer_bf_ref,
+
+
+def backward_kernel(count, weights_ref, all_ref, query_ref, key_ref, value_ref, attended_ref, grad_ref, layer_bf_ref,
                     layer_ref, w_query, w_key, w_value, base_out, send_out, keep_out, *refs):
     *pass_outs, grad_query, grad_key, grad_value, sums = refs
     beams, cols, channels = query_ref.shape
     scale = (channels // HEADS) ** (-0.5)
-    allowed = allowed_ref[0:1, :] > 0.5
     for b in range(beams):
         queries = by_head(query_ref[b])
         keys = key_ref[b]
-        weights = weights_of(queries, keys, allowed)
+        weights = weights_ref[b]
         grads = by_head(grad_ref[b])
         attended = jnp.concatenate([attended_ref[b].astype(F32)] * HEADS, axis=0)
         delta = jnp.sum(grads.astype(F32) * attended, axis=-1, keepdims=True)
@@ -380,7 +373,7 @@
         )
     for ref in piece_refs:
         piece = piece + ref[...].astype(F32)
-    features_out[...] = jnp.stack([total[b * cols : (b + 1) * cols] for b in range(beams)], axis=1).astype(BF)
+    features_out[...] = jnp.swapaxes(total.reshape(beams, cols, channels).astype(BF), 0, 1)
     width, lanes = weights_out.shape[1:]
     for index in range(4):
         weights_out[index] = piece[
@@ -419,40 +412,28 @@
 
     token = (cols, beams, channels)
     square = (channels, channels)
-    own_features, own_cot, allowed, w_query, w_key, w_value, w_out = call(
-        functools.partial(prep_kernel, count),
-        [(block, BF), (block, BF), ((8, count * cols), F32)] + [(square, BF)] * 4,
-        [HBM] * 7,
-        scratch=[
-            pltpu.VMEM(token, BF),
-            pltpu.VMEM(token, BF),
-            pltpu.VMEM(sector_mask.shape, jnp.int32),
-            pltpu.SemaphoreType.DMA((7,)),
-        ],
-    )(*map(in_hbm, (features.reshape(token), cotangent.reshape(token), sector_mask, w_query, w_key, w_value, w_out)))
     distances = range(1, count)
-    all_features = [own_features] + exchange({distance: own_features for distance in distances})
-    low = TAPS // 2
-    taps_hbm = in_hbm(w_conv.transpose(1, 0, 2))
-    every, queries, keys, values, w_low = call(
+    raw_features, raw_cot = features.reshape(token), cotangent.reshape(token)
+    come_features = exchange({distance: raw_features for distance in distances})
+    come_cot = [swap(raw_cot, bits) for bits in (2, 4, 6)]
+
+    every, queries, keys, values, allowed, w_out, own_cot = call(
         functools.partial(project_kernel, count),
-        [(whole, BF), (block, BF), (whole, BF), (whole, BF), ((low,) + square, BF)],
-        [VMEM] * (count + 3) + [HBM],
-        scratch=[pltpu.SemaphoreType.DMA],
-    )(*all_features, w_query, w_key, w_value, taps_hbm)
-
-    even = call(stack_kernel, [((4,) + block, BF)], [VMEM] * 5)(
-        queries, own_cot, *[swap(own_cot, bits) for bits in (2, 4, 6)]
-    )[0]
+        [(whole, BF), (block, BF), (whole, BF), (whole, BF), ((8, count * cols), F32), (square, BF), (block, BF)],
+        [VMEM] * (count - 1) + [HBM] * 7,
+        scratch=[pltpu.VMEM(token, BF)] * 2 + [pltpu.VMEM(square, BF)] * 3
+        + [pltpu.VMEM(sector_mask.shape, jnp.int32), pltpu.SemaphoreType.DMA((7,))],
+    )(*come_features, *map(in_hbm, (raw_features, raw_cot, w_query, w_key, w_value, w_out, sector_mask)))
+
+    even = call(stack_kernel, [((4,) + block, BF)], [VMEM] * 4)(own_cot, *come_cot)[0]
     odd = swap(even, 1)
 
     pieces_shape = (count, cols, max(LANES, beams * lanes))
-    attended, pieces, w_high = call(
+    attended, pieces, weights = call(
         functools.partial(attention_kernel, count),
-        [(block, BF), (pieces_shape, BF), ((TAPS - low,) + square, BF)],
-        [VMEM] * 6 + [HBM],
-        scratch=[pltpu.SemaphoreType.DMA],
-    )(allowed, own_features, queries, keys, values, w_out, taps_hbm)
+        [(block, BF), (pieces_shape, BF), ((beams, HEADS * cols, count * cols), F32)],
+        [VMEM] * 6,
+    )(allowed, every, queries, keys, values, w_out)
 
     spread = (4 * cols, 4 * width)
     edge = (8 * beams, channels)
@@ -465,13 +446,13 @@
     grad_layer, grad_layer_bf, grad_attended = call(
         functools.partial(conv_kernel, count),
         [(block, F32), (block, BF), (block, BF)],
-        [VMEM] * (5 + len(neighbours)),
+        [VMEM] * (4 + len(neighbours)),
         scratch=[
             pltpu.VMEM((3, beams + 2, cols + 16, channels), F32),
             pltpu.VMEM((2,) + edge, F32),
             pltpu.VMEM((3, 3, (beams + 2) * cols, channels), BF),
         ],
-    )(even, odd, *neighbours, w_low, w_high, w_out)
+    )(even, odd, *neighbours, w_conv.transpose(1, 0, 2), w_out)
 
     quarter = (4, 4 * width * channels // LANES, LANES)
     base, send, keep, *gives = call(
@@ -485,7 +466,7 @@
             pltpu.VMEM((4, 8, width, channels), BF),
         ],
     )(
-        allowed, every, queries, keys, values, attended, grad_attended, grad_layer_bf, grad_layer,
+        weights, every, queries, keys, values, attended, grad_attended, grad_layer_bf, grad_layer,
         w_query, w_key, w_value,
     )
 

time: 49.6 us -> 48.4 us (0.976)
  Pallas kernels: 10.4 us -> 8.98 us
    pallas_call x2 -> x1, Pallas kernels: 1.41 us -> 0.1 us  [per_device(): call(stack_kernel, [((4,) + block, BF)], [VMEM] * 4)(own_cot, *come_cot)[0]]
  transfers between devices with their start and end apart: 26 -> 26, of which waited for: 11 -> 11; matrix products, arithmetic and copies ran while one was open for 0% -> 0% of each run, Pallas kernels for 15% -> 16%
where the time goes in v5:
time: 48.4 us; the launch traced here: 48.2 us
  starting transfers between devices  30.4 us (63%)
  Pallas kernels  8.98 us (19%)
  waiting for transfers between devices  7.83 us (16%)
  between operations  0.89 us (2%)
    ppermute x14, starting transfers between devices, swap_columns(): lax.ppermute(value, 'azim', [(i, i ^ distance) for i in range(count)])  22 us
    ppermute x12, starting transfers between devices, swap(): return lax.ppermute(value, GROUP, [(i, i ^ bits) for i in range(8)])  8.34 us
    ppermute x14, waiting for transfers between devices, swap_columns(): lax.ppermute(value, 'azim', [(i, i ^ distance) for i in range(count)])  4.4 us
    ppermute x12, waiting for transfers between devices, swap(): return lax.ppermute(value, GROUP, [(i, i ^ bits) for i in range(8)])  3.43 us
    pallas_call x1, Pallas kernels, per_device(): call(functools.partial(project_kernel, count), [(whole, BF), (block, BF),...  1.92 us
    pallas_call x1, Pallas kernels, per_device(): call(functools.partial(backward_kernel, count), [(block, F32), ((count -...  1.48 us
    pallas_call x1, Pallas kernels, per_device(): call(functools.partial(conv_kernel, count), [(block, F32), (block, BF), (...  1.45 us
    pallas_call x1, Pallas kernels, per_device(): call(functools.partial(attention_kernel, count), [(block, BF), (pieces_sh...  1.41 us
  transfers between devices with their start and end apart: 26, of which 11 were waited for; matrix products, arithmetic and copies ran while one was open for 0% of the time, Pallas kernels for 16%

profile of v5, /device:TPU:0, one launch (start us, length us, event | category | flops | bytes accessed | tf_op | source)
XLA Modules:
  0.0 48.2 jit_solution(10011329748528440112)
XLA Ops:
  0.6 5.1 %collective-permute-start.2 = (bf16[64,2,256]{2,1,0:T(2,128)(2,1)}, bf16[64,2,256]{2,1,0:T(2,128)(2,1)S(1)}, u32[]{:S(2)}, u32[]{:S(2)}) collective-permute-start(bf16[64,2,256]{2,1,0:T(2,128)(2,1)} %bitcast.36), channel_id=1, source_target_pairs={{0,24},{8,16},{16,8},{24,0},{1,25},{9,17},{17,9},{25,1},{2,26},{10... | collective-permute-start | bytes 196616 | tf_op jit(solution)/shard_map/ppermute | solution.py:391
  5.7 0.6 %collective-permute-start = (bf16[64,2,256]{2,1,0:T(2,128)(2,1)}, bf16[64,2,256]{2,1,0:T(2,128)(2,1)S(1)}, u32[]{:S(2)}, u32[]{:S(2)}) collective-permute-start(bf16[64,2,256]{2,1,0:T(2,128)(2,1)} %bitcast.38), channel_id=1, source_target_pairs={{0,8},{8,0},{16,24},{24,16},{1,9},{9,1},{17,25},{25,17},{2,10},{10... | collective-permute-start | bytes 196616 | tf_op jit(solution)/shard_map/ppermute | solution.py:391
  6.4 2.6 %collective-permute-start.5 = (bf16[64,2,256]{2,1,0:T(2,128)(2,1)}, bf16[64,2,256]{2,1,0:T(2,128)(2,1)S(1)}, u32[]{:S(2)}, u32[]{:S(2)}) collective-permute-start(bf16[64,2,256]{2,1,0:T(2,128)(2,1)} %bitcast.40), channel_id=1, source_target_pairs={{0,6},{1,7},{2,4},{3,5},{4,2},{5,3},{6,0},{7,1},{8,14},{9,15},{10,... | collective-permute-start | bytes 196616 | tf_op jit(solution)/shard_map/ppermute | solution.py:400
  9.0 0.5 %collective-permute-start.4 = (bf16[64,2,256]{2,1,0:T(2,128)(2,1)}, bf16[64,2,256]{2,1,0:T(2,128)(2,1)S(1)}, u32[]{:S(2)}, u32[]{:S(2)}) collective-permute-start(bf16[64,2,256]{2,1,0:T(2,128)(2,1)} %bitcast.41), channel_id=1, source_target_pairs={{0,4},{1,5},{2,6},{3,7},{4,0},{5,1},{6,2},{7,3},{8,12},{9,13},{10,... | collective-permute-start | bytes 196616 | tf_op jit(solution)/shard_map/ppermute | solution.py:400
  9.5 0.0 collective-permute-done.2.refs_2_
  9.5 0.9 %collective-permute-start.3 = (bf16[64,2,256]{2,1,0:T(2,128)(2,1)}, bf16[64,2,256]{2,1,0:T(2,128)(2,1)S(1)}, u32[]{:S(2)}, u32[]{:S(2)}) collective-permute-start(bf16[64,2,256]{2,1,0:T(2,128)(2,1)} %bitcast.42), channel_id=1, source_target_pairs={{0,2},{1,3},{2,0},{3,1},{4,6},{5,7},{6,4},{7,5},{8,10},{9,11},{10,... | collective-permute-start | bytes 196616 | tf_op jit(solution)/shard_map/ppermute | solution.py:400
  10.4 1.2 %collective-permute-done.1.refs_1_ = bf16[64,2,256]{2,1,0:T(2,128)(2,1)S(1)} collective-permute-done((bf16[64,2,256]{2,1,0:T(2,128)(2,1)}, bf16[64,2,256]{2,1,0:T(2,128)(2,1)S(1)}, u32[]{:S(2)}, u32[]{:S(2)}) %collective-permute-start.1) | collective-permute-done | bytes 65568 | tf_op jit(solution)/shard_map/ppermute | solution.py:391
  11.6 1.9 %shard_map.95 = (bf16[2,256,256]{2,1,0:T(8,128)(2,1)S(1)}, bf16[2,64,256]{2,1,0:T(8,128)(2,1)S(1)}, bf16[2,256,256]{2,1,0:T(8,128)(2,1)S(1)}, bf16[2,256,256]{2,...) custom-call(bf16[64,2,256]{2,1,0:T(2,128)(2,1)S(1)} %collective-permute-d, ...), custom_call_target="tpu_custom_call" | custom-call | flops 2000000000 | tf_op jit(solution)/shard_map/pallas_call | solution.py:420
  13.5 0.5 collective-permute-done.3.refs_0_
  14.0 0.1 shard_map.97.even_ref
  14.1 0.1 collective-permute-start.6
  14.2 1.4 %shard_map.96 = (bf16[2,64,256]{2,1,0:T(8,128)(2,1)S(1)}, bf16[4,64,128]{2,1,0:T(8,128)(2,1)S(1)}, f32[2,512,256]{2,1,0:T(8,128)S(1)}) custom-call(f32[8,256]{1,0:T(8,128)S(1)} %get-tuple-element.31.allowed_ref, bf16[2,256,256]{2,1,0:T(8,128)(2,1)S(1)} %get-tuple-element.32.all_ref, bf16[2,64,256]{2,1,0:T(8,128)(2,1)S(1)} %get-tuple-element.33.query_ref, ...), custom_call_target="tpu_custom_call" | custom-call | flops 2000000000 | tf_op jit(solution)/shard_map/pallas_call | solution.py:432
  15.6 0.0 copy-start
  15.6 0.1 collective-permute-done.6.odd_ref
  15.7 0.4 shard_map.98
  16.0 3.7 %collective-permute-start.8 = (bf16[2,16,256]{2,1,0:T(8,128)(2,1)S(1)}, bf16[2,16,256]{2,1,0:T(8,128)(2,1)S(1)}, u32[]{:S(2)}, u32[]{:S(2)}) collective-permute-start(bf16[2,16,256]{2,1,0:T(8,128)(2,1)S(1)} %get-tuple-element.40), channel_id=1, source_target_pairs={{0,24},{8,16},{16,8},{24,0},{1,25},{9,17},{17,9},{25,1},{2,26},{10... | collective-permute-start | bytes 49160 | tf_op jit(solution)/shard_map/ppermute | solution.py:391
  19.7 2.1 %collective-permute-start.9 = (bf16[320,128]{1,0:T(8,128)(2,1)S(1)}, bf16[320,128]{1,0:T(8,128)(2,1)S(1)}, u32[]{:S(2)}, u32[]{:S(2)}) collective-permute-start(bf16[320,128]{1,0:T(8,128)(2,1)S(1)} %get-tuple-element.74), channel_id=1, source_target_pairs={{0,8},{8,0},{16,24},{24,16},{1,9},{9,1},{17,25},{25,17},{2,10},{10... | collective-permute-start | bytes 245768 | tf_op jit(solution)/shard_map/ppermute | solution.py:391
  21.8 2.4 %collective-permute-start.11 = (bf16[320,128]{1,0:T(8,128)(2,1)S(1)}, bf16[320,128]{1,0:T(8,128)(2,1)S(1)}, u32[]{:S(2)}, u32[]{:S(2)}) collective-permute-start(bf16[320,128]{1,0:T(8,128)(2,1)S(1)} %get-tuple-element.76), channel_id=1, source_target_pairs={{0,24},{8,16},{16,8},{24,0},{1,25},{9,17},{17,9},{25,1},{2,26},{10... | collective-permute-start | bytes 245768 | tf_op jit(solution)/shard_map/ppermute | solution.py:391
  24.3 0.0 copy-start.1
  24.3 0.0 copy-start.2
  24.3 0.0 copy-start.3
  24.3 1.5 %shard_map.99 = (f32[2,64,256]{2,1,0:T(8,128)S(1)}, bf16[2,64,256]{2,1,0:T(8,128)(2,1)S(1)}, bf16[2,64,256]{2,1,0:T(8,128)(2,1)S(1)}) custom-call(bf16[4,2,64,256]{3,2,1,0:T(8,128)(2,1)S(1)} %shard_map.97.even_ref, bf16[4,2,64,256]{3,2,1,0:T(8,128)(2,1)S(1)} %collective-permute-done.6.odd_ref, bf16[2,16,256]{2,1,0:T(8,128)(2,1)S(1)} %collective-permute-done.7.refs_0_, ...), custom_call_target="tpu_custom_call" | custom-call | flops 2000000000 | tf_op jit(solution)/shard_map/pallas_call | solution.py:446
  25.8 1.5 %shard_map.100 = (f32[2,64,256]{2,1,0:T(8,128)S(1)}, bf16[3,256,128]{2,1,0:T(8,128)(2,1)S(1)}, bf16[4,256,128]{2,1,0:T(8,128)(2,1)S(1)}, bf16[256,128]{1,0:T(8,1...) custom-call(f32[2,512,256]{2,1,0:T(8,128)S(1)} %get-tuple-element.37.weights_, ...), custom_call_target="tpu_custom_call" | custom-call | flops 2000000000 | tf_op jit(solution)/shard_map/pallas_call | solution.py:458
  27.3 0.1 collective-permute-start.12
  27.4 0.5 %collective-permute-start.13 = (bf16[256,128]{1,0:T(8,128)(2,1)S(1)}, bf16[256,128]{1,0:T(8,128)(2,1)S(1)}, u32[]{:S(2)}, u32[]{:S(2)}) collective-permute-start(bf16[256,128]{1,0:T(8,128)(2,1)S(1)} %get-tuple-element.49), channel_id=1, source_target_pairs={{0,1},{1,0},{2,3},{3,2},{4,5},{5,4},{6,7},{7,6},{8,9},{9,8},{10,11... | collective-permute-start | bytes 196616 | tf_op jit(solution)/shard_map/ppermute | solution.py:400
  27.9 0.1 collective-permute-start.14
  27.9 2.2 %collective-permute-done.10.refs_1_ = bf16[320,128]{1,0:T(8,128)(2,1)S(1)} collective-permute-done((bf16[320,128]{1,0:T(8,128)(2,1)S(1)}, bf16[320,128]{1,0:T(8,128)(2,1)S(1)}, u32[]{:S(2)}, u32[]{:S(2)}) %collective-permute-start.10) | collective-permute-done | bytes 81952 | tf_op jit(solution)/shard_map/ppermute | solution.py:391
  30.3 1.2 %collective-permute-done.15.refs_3_ = bf16[256,128]{1,0:T(8,128)(2,1)S(1)} collective-permute-done((bf16[256,128]{1,0:T(8,128)(2,1)S(1)}, bf16[256,128]{1,0:T(8,128)(2,1)S(1)}, u32[]{:S(2)}, u32[]{:S(2)}) %collective-permute-start.15) | collective-permute-done | bytes 65568 | tf_op jit(solution)/shard_map/ppermute | solution.py:400
  31.4 0.1 shard_map.101
  31.5 1.2 %collective-permute-start.16 = (bf16[512,128]{1,0:T(8,128)(2,1)S(1)}, bf16[512,128]{1,0:T(8,128)(2,1)S(1)}, u32[]{:S(2)}, u32[]{:S(2)}) collective-permute-start(bf16[512,128]{1,0:T(8,128)(2,1)S(1)} %get-tuple-element.53), channel_id=1, source_target_pairs={{0,2},{1,3},{2,0},{3,1},{4,6},{5,7},{6,4},{7,5},{8,10},{9,11},{10,... | collective-permute-start | bytes 393224 | tf_op jit(solution)/shard_map/ppermute | solution.py:400
  32.7 1.5 %collective-permute-start.17 = (bf16[512,128]{1,0:T(8,128)(2,1)S(1)}, bf16[512,128]{1,0:T(8,128)(2,1)S(1)}, u32[]{:S(2)}, u32[]{:S(2)}) collective-permute-start(bf16[512,128]{1,0:T(8,128)(2,1)S(1)} %get-tuple-element.54), channel_id=1, source_target_pairs={{0,4},{1,5},{2,6},{3,7},{4,0},{5,1},{6,2},{7,3},{8,12},{9,13},{10,... | collective-permute-start | bytes 393224 | tf_op jit(solution)/shard_map/ppermute | solution.py:400
  34.2 0.8 %collective-permute-start.18 = (bf16[512,128]{1,0:T(8,128)(2,1)S(1)}, bf16[512,128]{1,0:T(8,128)(2,1)S(1)}, u32[]{:S(2)}, u32[]{:S(2)}) collective-permute-start(bf16[512,128]{1,0:T(8,128)(2,1)S(1)} %get-tuple-element.55), channel_id=1, source_target_pairs={{0,6},{1,7},{2,4},{3,5},{4,2},{5,3},{6,0},{7,1},{8,14},{9,15},{10,... | collective-permute-start | bytes 393224 | tf_op jit(solution)/shard_map/ppermute | solution.py:400
  35.1 0.1 collective-permute-start.22
  35.2 2.3 %collective-permute-start.21 = (bf16[256,128]{1,0:T(8,128)(2,1)S(1)}, bf16[256,128]{1,0:T(8,128)(2,1)S(1)}, u32[]{:S(2)}, u32[]{:S(2)}) collective-permute-start(bf16[256,128]{1,0:T(8,128)(2,1)S(1)} %get-tuple-element.63), channel_id=1, source_target_pairs={{0,16},{8,24},{16,0},{24,8},{1,17},{9,25},{17,1},{25,9},{2,18},{10... | collective-permute-start | bytes 196616 | tf_op jit(solution)/shard_map/ppermute | solution.py:391
  37.5 0.3 collective-permute-done.16.refs_0_
  37.9 1.7 %collective-permute-start.20 = (bf16[256,128]{1,0:T(8,128)(2,1)S(1)}, bf16[256,128]{1,0:T(8,128)(2,1)S(1)}, u32[]{:S(2)}, u32[]{:S(2)}) collective-permute-start(bf16[256,128]{1,0:T(8,128)(2,1)S(1)} %get-tuple-element.64), channel_id=1, source_target_pairs={{0,8},{8,0},{16,24},{24,16},{1,9},{9,1},{17,25},{25,17},{2,10},{10... | collective-permute-start | bytes 196616 | tf_op jit(solution)/shard_map/ppermute | solution.py:391
  39.6 0.3 collective-permute-done.17.refs_1_
  39.9 1.1 %collective-permute-done.18.refs_2_ = bf16[512,128]{1,0:T(8,128)(2,1)S(1)} collective-permute-done((bf16[512,128]{1,0:T(8,128)(2,1)S(1)}, bf16[512,128]{1,0:T(8,128)(2,1)S(1)}, u32[]{:S(2)}, u32[]{:S(2)}) %collective-permute-start.18) | collective-permute-done | bytes 131104 | tf_op jit(solution)/shard_map/ppermute | solution.py:400
  41.0 0.1 collective-permute-start.19
  41.0 0.1 shard_map.102.own_piece
  41.2 0.1 collective-permute-start.25
  41.2 0.5 collective-permute-done.22.refs_2_
  41.7 1.6 %collective-permute-start.24 = (bf16[64,128]{1,0:T(8,128)(2,1)S(1)}, bf16[64,128]{1,0:T(8,128)(2,1)S(1)}, u32[]{:S(2)}, u32[]{:S(2)}) collective-permute-start(bf16[64,128]{1,0:T(8,128)(2,1)S(1)} %get-tuple-element.66), channel_id=1, source_target_pairs={{0,16},{8,24},{16,0},{24,8},{1,17},{9,25},{17,1},{25,9},{2,18},{10... | collective-permute-start | bytes 49160 | tf_op jit(solution)/shard_map/ppermute | solution.py:391
  43.3 2.3 %collective-permute-start.23 = (bf16[64,128]{1,0:T(8,128)(2,1)S(1)}, bf16[64,128]{1,0:T(8,128)(2,1)S(1)}, u32[]{:S(2)}, u32[]{:S(2)}) collective-permute-start(bf16[64,128]{1,0:T(8,128)(2,1)S(1)} %get-tuple-element.67), channel_id=1, source_target_pairs={{0,8},{8,0},{16,24},{24,16},{1,9},{9,1},{17,25},{25,17},{2,10},{10... | collective-permute-start | bytes 49160 | tf_op jit(solution)/shard_map/ppermute | solution.py:391
  45.6 1.2 %shard_map.103.taps_ref = f32[27,32,64]{2,1,0:T(8,128)S(1)} custom-call(bf16[4,256,128]{2,1,0:T(8,128)(2,1)S(1)} %pad_maximum_fusion.even_ref, bf16[4,256,128]{2,1,0:T(8,128)(2,1)S(1)} %collective-permute-done.19.odd_ref, bf16[256,128]{1,0:T(8,128)(2,1)S(1)} %get-tuple-element.46.own_ref, bf16[320,128]{1,0:T(8,128)(2,1)S(1)} %collective-permute-done.9.refs_0_, ...), custom_call_target="tpu_custom_call" | custom-call | flops 2000000000 | tf_op jit(solution)/shard_map/pallas_call | solution.py:488
  46.8 0.1 collective-permute-done.25.refs_5_
  46.9 0.4 collective-permute-done.23.refs_3_
  47.3 0.9 %shard_map.104 = (bf16[64,2,256]{2,1,0:T(2,128)(2,1)}, f32[31,32,64]{2,1,0:T(8,128)}) custom-call(bf16[4,64,128]{2,1,0:T(8,128)(2,1)S(1)} %shard_map.102.own_piece, f32[2,64,256]{2,1,0:T(8,128)S(1)} %get-tuple-element.56.base_ref, f32[27,32,64]{2,1,0:T(8,128)S(1)} %shard_map.103.taps_ref, bf16[256,128]{1,0:T(8,128)(2,1)S(1)} %collective-permute-done.20.refs_0_, ...), custom_call_target="tpu_custom_call" | custom-call | flops 2000000000 | tf_op jit(solution)/shard_map/pallas_call | solution.py:498
  (34 shorter events, 0.2 us)
Async XLA Ops:
  0.6 8.9 %collective-permute-start.2 = (bf16[64,2,256]{2,1,0:T(2,128)(2,1)}, bf16[64,2,256]{2,1,0:T(2,128)(2,1)S(1)}, u32[]{:S(2)}, u32[]{:S(2)}) collective-permute-start(bf16[64,2,256]{2,1,0:T(2,128)(2,1)} %bitcast.36), channel_id=1, source_target_pairs={{0,24},{8,16},{16,8},{24,0},{1,25},{9,17},{17,9},{25,1},{2,26},{10... | collective-permute-start | bytes 196616 | tf_op jit(solution)/shard_map/ppermute | solution.py:391
  5.7 5.8 %collective-permute-start.1 = (bf16[64,2,256]{2,1,0:T(2,128)(2,1)}, bf16[64,2,256]{2,1,0:T(2,128)(2,1)S(1)}, u32[]{:S(2)}, u32[]{:S(2)}) collective-permute-start(bf16[64,2,256]{2,1,0:T(2,128)(2,1)} %bitcast.37), channel_id=1, source_target_pairs={{0,16},{8,24},{16,0},{24,8},{1,17},{9,25},{17,1},{25,9},{2,18},{10... | collective-permute-start | bytes 196616 | tf_op jit(solution)/shard_map/ppermute | solution.py:391
  5.7 5.8 %collective-permute-start = (bf16[64,2,256]{2,1,0:T(2,128)(2,1)}, bf16[64,2,256]{2,1,0:T(2,128)(2,1)S(1)}, u32[]{:S(2)}, u32[]{:S(2)}) collective-permute-start(bf16[64,2,256]{2,1,0:T(2,128)(2,1)} %bitcast.38), channel_id=1, source_target_pairs={{0,8},{8,0},{16,24},{24,16},{1,9},{9,1},{17,25},{25,17},{2,10},{10... | collective-permute-start | bytes 196616 | tf_op jit(solution)/shard_map/ppermute | solution.py:391
  6.4 7.1 %collective-permute-start.5 = (bf16[64,2,256]{2,1,0:T(2,128)(2,1)}, bf16[64,2,256]{2,1,0:T(2,128)(2,1)S(1)}, u32[]{:S(2)}, u32[]{:S(2)}) collective-permute-start(bf16[64,2,256]{2,1,0:T(2,128)(2,1)} %bitcast.40), channel_id=1, source_target_pairs={{0,6},{1,7},{2,4},{3,5},{4,2},{5,3},{6,0},{7,1},{8,14},{9,15},{10,... | collective-permute-start | bytes 196616 | tf_op jit(solution)/shard_map/ppermute | solution.py:400
  9.0 4.5 %collective-permute-start.4 = (bf16[64,2,256]{2,1,0:T(2,128)(2,1)}, bf16[64,2,256]{2,1,0:T(2,128)(2,1)S(1)}, u32[]{:S(2)}, u32[]{:S(2)}) collective-permute-start(bf16[64,2,256]{2,1,0:T(2,128)(2,1)} %bitcast.41), channel_id=1, source_target_pairs={{0,4},{1,5},{2,6},{3,7},{4,0},{5,1},{6,2},{7,3},{8,12},{9,13},{10,... | collective-permute-start | bytes 196616 | tf_op jit(solution)/shard_map/ppermute | solution.py:400
  9.5 4.5 %collective-permute-start.3 = (bf16[64,2,256]{2,1,0:T(2,128)(2,1)}, bf16[64,2,256]{2,1,0:T(2,128)(2,1)S(1)}, u32[]{:S(2)}, u32[]{:S(2)}) collective-permute-start(bf16[64,2,256]{2,1,0:T(2,128)(2,1)} %bitcast.42), channel_id=1, source_target_pairs={{0,2},{1,3},{2,0},{3,1},{4,6},{5,7},{6,4},{7,5},{8,10},{9,11},{10,... | collective-permute-start | bytes 196616 | tf_op jit(solution)/shard_map/ppermute | solution.py:400
  14.1 1.6 %collective-permute-start.6 = (bf16[4,2,64,256]{3,2,1,0:T(8,128)(2,1)S(1)}, bf16[4,2,64,256]{3,2,1,0:T(8,128)(2,1)S(1)}, u32[]{:S(2)}, u32[]{:S(2)}) collective-permute-start(bf16[4,2,64,256]{3,2,1,0:T(8,128)(2,1)S(1)} %shard_map.97.even_ref), channel_id=1, source_target_pairs={{0,1},{1,0},{2,3},{3,2},{4,5},{5,4},{6,7},{7,6},{8,9},{9,8},{10,11... | collective-permute-start | bytes 786440 | tf_op jit(solution)/shard_map/ppermute | solution.py:400
  15.6 8.7 %copy-start = (bf16[256,27,256]{2,0,1:T(8,128)(2,1)S(1)}, bf16[256,27,256]{2,0,1:T(8,128)(2,1)}, u32[]{:S(2)}) copy-start(bf16[256,27,256]{2,0,1:T(8,128)(2,1)} %param.14) | copy-start | bytes 10616836
  16.0 8.2 %collective-permute-start.8 = (bf16[2,16,256]{2,1,0:T(8,128)(2,1)S(1)}, bf16[2,16,256]{2,1,0:T(8,128)(2,1)S(1)}, u32[]{:S(2)}, u32[]{:S(2)}) collective-permute-start(bf16[2,16,256]{2,1,0:T(8,128)(2,1)S(1)} %get-tuple-element.40), channel_id=1, source_target_pairs={{0,24},{8,16},{16,8},{24,0},{1,25},{9,17},{17,9},{25,1},{2,26},{10... | collective-permute-start | bytes 49160 | tf_op jit(solution)/shard_map/ppermute | solution.py:391
  19.7 4.6 %collective-permute-start.7 = (bf16[2,16,256]{2,1,0:T(8,128)(2,1)S(1)}, bf16[2,16,256]{2,1,0:T(8,128)(2,1)S(1)}, u32[]{:S(2)}, u32[]{:S(2)}) collective-permute-start(bf16[2,16,256]{2,1,0:T(8,128)(2,1)S(1)} %get-tuple-element.40), channel_id=1, source_target_pairs={{0,8},{8,0},{16,24},{24,16},{1,9},{9,1},{17,25},{25,17},{2,10},{10... | collective-permute-start | bytes 49160 | tf_op jit(solution)/shard_map/ppermute | solution.py:391
  19.7 8.1 %collective-permute-start.9 = (bf16[320,128]{1,0:T(8,128)(2,1)S(1)}, bf16[320,128]{1,0:T(8,128)(2,1)S(1)}, u32[]{:S(2)}, u32[]{:S(2)}) collective-permute-start(bf16[320,128]{1,0:T(8,128)(2,1)S(1)} %get-tuple-element.74), channel_id=1, source_target_pairs={{0,8},{8,0},{16,24},{24,16},{1,9},{9,1},{17,25},{25,17},{2,10},{10... | collective-permute-start | bytes 245768 | tf_op jit(solution)/shard_map/ppermute | solution.py:391
  21.8 8.4 %collective-permute-start.10 = (bf16[320,128]{1,0:T(8,128)(2,1)S(1)}, bf16[320,128]{1,0:T(8,128)(2,1)S(1)}, u32[]{:S(2)}, u32[]{:S(2)}) collective-permute-start(bf16[320,128]{1,0:T(8,128)(2,1)S(1)} %get-tuple-element.75), channel_id=1, source_target_pairs={{0,16},{8,24},{16,0},{24,8},{1,17},{9,25},{17,1},{25,9},{2,18},{10... | collective-permute-start | bytes 245768 | tf_op jit(solution)/shard_map/ppermute | solution.py:391
  21.8 8.4 %collective-permute-start.11 = (bf16[320,128]{1,0:T(8,128)(2,1)S(1)}, bf16[320,128]{1,0:T(8,128)(2,1)S(1)}, u32[]{:S(2)}, u32[]{:S(2)}) collective-permute-start(bf16[320,128]{1,0:T(8,128)(2,1)S(1)} %get-tuple-element.76), channel_id=1, source_target_pairs={{0,24},{8,16},{16,8},{24,0},{1,25},{9,17},{17,9},{25,1},{2,26},{10... | collective-permute-start | bytes 245768 | tf_op jit(solution)/shard_map/ppermute | solution.py:391
  24.3 1.5 %copy-start.1 = (bf16[256,256]{1,0:T(8,128)(2,1)S(1)}, bf16[256,256]{1,0:T(8,128)(2,1)}, u32[]{:S(2)}) copy-start(bf16[256,256]{1,0:T(8,128)(2,1)} %w_query.1) | copy-start | bytes 393220
  24.3 1.5 %copy-start.2 = (bf16[256,256]{1,0:T(8,128)(2,1)S(1)}, bf16[256,256]{1,0:T(8,128)(2,1)}, u32[]{:S(2)}) copy-start(bf16[256,256]{1,0:T(8,128)(2,1)} %w_key.1) | copy-start | bytes 393220
  24.3 1.5 %copy-start.3 = (bf16[256,256]{1,0:T(8,128)(2,1)S(1)}, bf16[256,256]{1,0:T(8,128)(2,1)}, u32[]{:S(2)}) copy-start(bf16[256,256]{1,0:T(8,128)(2,1)} %w_value.1) | copy-start | bytes 393220
  27.3 2.9 %collective-permute-start.12 = (bf16[256,128]{1,0:T(8,128)(2,1)S(1)}, bf16[256,128]{1,0:T(8,128)(2,1)S(1)}, u32[]{:S(2)}, u32[]{:S(2)}) collective-permute-start(bf16[256,128]{1,0:T(8,128)(2,1)S(1)} %get-tuple-element.48), channel_id=1, source_target_pairs={{0,1},{1,0},{2,3},{3,2},{4,5},{5,4},{6,7},{7,6},{8,9},{9,8},{10,11... | collective-permute-start | bytes 196616 | tf_op jit(solution)/shard_map/ppermute | solution.py:400
  27.4 2.9 %collective-permute-start.13 = (bf16[256,128]{1,0:T(8,128)(2,1)S(1)}, bf16[256,128]{1,0:T(8,128)(2,1)S(1)}, u32[]{:S(2)}, u32[]{:S(2)}) collective-permute-start(bf16[256,128]{1,0:T(8,128)(2,1)S(1)} %get-tuple-element.49), channel_id=1, source_target_pairs={{0,1},{1,0},{2,3},{3,2},{4,5},{5,4},{6,7},{7,6},{8,9},{9,8},{10,11... | collective-permute-start | bytes 196616 | tf_op jit(solution)/shard_map/ppermute | solution.py:400
  27.9 2.4 %collective-permute-start.14 = (bf16[256,128]{1,0:T(8,128)(2,1)S(1)}, bf16[256,128]{1,0:T(8,128)(2,1)S(1)}, u32[]{:S(2)}, u32[]{:S(2)}) collective-permute-start(bf16[256,128]{1,0:T(8,128)(2,1)S(1)} %get-tuple-element.50), channel_id=1, source_target_pairs={{0,1},{1,0},{2,3},{3,2},{4,5},{5,4},{6,7},{7,6},{8,9},{9,8},{10,11... | collective-permute-start | bytes 196616 | tf_op jit(solution)/shard_map/ppermute | solution.py:400
  30.2 1.3 %collective-permute-start.15 = (bf16[256,128]{1,0:T(8,128)(2,1)S(1)}, bf16[256,128]{1,0:T(8,128)(2,1)S(1)}, u32[]{:S(2)}, u32[]{:S(2)}) collective-permute-start(bf16[256,128]{1,0:T(8,128)(2,1)S(1)} %get-tuple-element.51), channel_id=1, source_target_pairs={{0,1},{1,0},{2,3},{3,2},{4,5},{5,4},{6,7},{7,6},{8,9},{9,8},{10,11... | collective-permute-start | bytes 196616 | tf_op jit(solution)/shard_map/ppermute | solution.py:400
  31.5 6.4 %collective-permute-start.16 = (bf16[512,128]{1,0:T(8,128)(2,1)S(1)}, bf16[512,128]{1,0:T(8,128)(2,1)S(1)}, u32[]{:S(2)}, u32[]{:S(2)}) collective-permute-start(bf16[512,128]{1,0:T(8,128)(2,1)S(1)} %get-tuple-element.53), channel_id=1, source_target_pairs={{0,2},{1,3},{2,0},{3,1},{4,6},{5,7},{6,4},{7,5},{8,10},{9,11},{10,... | collective-permute-start | bytes 393224 | tf_op jit(solution)/shard_map/ppermute | solution.py:400
  32.7 7.1 %collective-permute-start.17 = (bf16[512,128]{1,0:T(8,128)(2,1)S(1)}, bf16[512,128]{1,0:T(8,128)(2,1)S(1)}, u32[]{:S(2)}, u32[]{:S(2)}) collective-permute-start(bf16[512,128]{1,0:T(8,128)(2,1)S(1)} %get-tuple-element.54), channel_id=1, source_target_pairs={{0,4},{1,5},{2,6},{3,7},{4,0},{5,1},{6,2},{7,3},{8,12},{9,13},{10,... | collective-permute-start | bytes 393224 | tf_op jit(solution)/shard_map/ppermute | solution.py:400
  34.2 6.7 %collective-permute-start.18 = (bf16[512,128]{1,0:T(8,128)(2,1)S(1)}, bf16[512,128]{1,0:T(8,128)(2,1)S(1)}, u32[]{:S(2)}, u32[]{:S(2)}) collective-permute-start(bf16[512,128]{1,0:T(8,128)(2,1)S(1)} %get-tuple-element.55), channel_id=1, source_target_pairs={{0,6},{1,7},{2,4},{3,5},{4,2},{5,3},{6,0},{7,1},{8,14},{9,15},{10,... | collective-permute-start | bytes 393224 | tf_op jit(solution)/shard_map/ppermute | solution.py:400
  35.1 6.6 %collective-permute-start.22 = (bf16[256,128]{1,0:T(8,128)(2,1)S(1)}, bf16[256,128]{1,0:T(8,128)(2,1)S(1)}, u32[]{:S(2)}, u32[]{:S(2)}) collective-permute-start(bf16[256,128]{1,0:T(8,128)(2,1)S(1)} %get-tuple-element.62), channel_id=1, source_target_pairs={{0,24},{8,16},{16,8},{24,0},{1,25},{9,17},{17,9},{25,1},{2,26},{10... | collective-permute-start | bytes 196616 | tf_op jit(solution)/shard_map/ppermute | solution.py:391
  35.2 11.6 %collective-permute-start.21 = (bf16[256,128]{1,0:T(8,128)(2,1)S(1)}, bf16[256,128]{1,0:T(8,128)(2,1)S(1)}, u32[]{:S(2)}, u32[]{:S(2)}) collective-permute-start(bf16[256,128]{1,0:T(8,128)(2,1)S(1)} %get-tuple-element.63), channel_id=1, source_target_pairs={{0,16},{8,24},{16,0},{24,8},{1,17},{9,25},{17,1},{25,9},{2,18},{10... | collective-permute-start | bytes 196616 | tf_op jit(solution)/shard_map/ppermute | solution.py:391
  37.9 8.9 %collective-permute-start.20 = (bf16[256,128]{1,0:T(8,128)(2,1)S(1)}, bf16[256,128]{1,0:T(8,128)(2,1)S(1)}, u32[]{:S(2)}, u32[]{:S(2)}) collective-permute-start(bf16[256,128]{1,0:T(8,128)(2,1)S(1)} %get-tuple-element.64), channel_id=1, source_target_pairs={{0,8},{8,0},{16,24},{24,16},{1,9},{9,1},{17,25},{25,17},{2,10},{10... | collective-permute-start | bytes 196616 | tf_op jit(solution)/shard_map/ppermute | solution.py:391
  41.0 2.4 %collective-permute-start.19 = (bf16[4,256,128]{2,1,0:T(8,128)(2,1)S(1)}, bf16[4,256,128]{2,1,0:T(8,128)(2,1)S(1)}, u32[]{:S(2)}, u32[]{:S(2)}) collective-permute-start(bf16[4,256,128]{2,1,0:T(8,128)(2,1)S(1)} %pad_maximum_fusion.even_ref), channel_id=1, source_target_pairs={{0,1},{1,0},{2,3},{3,2},{4,5},{5,4},{6,7},{7,6},{8,9},{9,8},{10,11... | collective-permute-start | bytes 786440 | tf_op jit(solution)/shard_map/ppermute | solution.py:400
  41.2 5.8 %collective-permute-start.25 = (bf16[64,128]{1,0:T(8,128)(2,1)S(1)}, bf16[64,128]{1,0:T(8,128)(2,1)S(1)}, u32[]{:S(2)}, u32[]{:S(2)}) collective-permute-start(bf16[64,128]{1,0:T(8,128)(2,1)S(1)} %get-tuple-element.65), channel_id=1, source_target_pairs={{0,24},{8,16},{16,8},{24,0},{1,25},{9,17},{17,9},{25,1},{2,26},{10... | collective-permute-start | bytes 49160 | tf_op jit(solution)/shard_map/ppermute | solution.py:391
  41.7 5.2 %collective-permute-start.24 = (bf16[64,128]{1,0:T(8,128)(2,1)S(1)}, bf16[64,128]{1,0:T(8,128)(2,1)S(1)}, u32[]{:S(2)}, u32[]{:S(2)}) collective-permute-start(bf16[64,128]{1,0:T(8,128)(2,1)S(1)} %get-tuple-element.66), channel_id=1, source_target_pairs={{0,16},{8,24},{16,0},{24,8},{1,17},{9,25},{17,1},{25,9},{2,18},{10... | collective-permute-start | bytes 49160 | tf_op jit(solution)/shard_map/ppermute | solution.py:391
  43.3 4.0 %collective-permute-start.23 = (bf16[64,128]{1,0:T(8,128)(2,1)S(1)}, bf16[64,128]{1,0:T(8,128)(2,1)S(1)}, u32[]{:S(2)}, u32[]{:S(2)}) collective-permute-start(bf16[64,128]{1,0:T(8,128)(2,1)S(1)} %get-tuple-element.67), channel_id=1, source_target_pairs={{0,8},{8,0},{16,24},{24,16},{1,9},{9,1},{17,25},{25,17},{2,10},{10... | collective-permute-start | bytes 49160 | tf_op jit(solution)/shard_map/ppermute | solution.py:391

commit v6 on v5

--- a/solution.py
+++ b/solution.py
@@ -61,7 +61,8 @@
     return dot(jnp.broadcast_to(own, (8, count)).astype(BF), spread)
 
 
-def slices_kernel(even_ref, odd_ref, slices_out, edges_out):
+def slices_kernel(even_ref, odd_ref, pieces_ref, slices_out, edges_out, pieces_out):
+    pieces_out[...] = pieces_ref[...]
     me = group_index()
     _, beams, cols, channels = even_ref.shape
     width = channels // 8
@@ -98,7 +99,7 @@
 def conv_kernel(count, even_ref, odd_ref, *refs):
     distances = neighbour_distances(count)
     edge_refs = refs[: len(distances)]
-    w_ref, w_out_ref, layer_out, layer_bf_out, attended_out, padded, edges, shifted = refs[len(distances) :]
+    w_ref, w_out_ref, layer_out, layer_bf_out, attended_out, main, edges, halo = refs[len(distances) :]
     me = group_index()
     column = lax.axis_index("azim")
     sweep = lax.axis_index("sweep")
@@ -124,21 +125,31 @@
             odd = slot // 4
             block = lax.rem(slot, 4)
             value = jnp.where(odd == 1, odd_ref[block, within], even_ref[block, within])
-            padded[j, m, 8 : 8 + cols, :] = value.astype(F32) * keep
+            main[j, m * cols : (m + 1) * cols, :] = (value.astype(F32) * keep).astype(BF)
             row = slot * beams + within
-            padded[j, m, 7:8, :] = edges[0, pl.ds(row, 1), :] * keep
-            padded[j, m, 8 + cols : 9 + cols, :] = edges[1, pl.ds(row, 1), :] * keep
-    for i in (-1, 0, 1):
-        for j in range(3):
-            for m in range(beams + 2):
-                shifted[i + 1, j, m * cols : (m + 1) * cols, :] = padded[j, m, 8 - i : 8 - i + cols, :].astype(BF)
-    total = even_ref[0].reshape(beams * cols, channels).astype(F32)
-    for i in (-1, 0, 1):
+            for side in range(2):
+                halo[side, j, m : m + 1, :] = edges[side, pl.ds(row, 1), :] * keep
+    rows = beams * cols
+    total = even_ref[0].reshape(rows, channels).astype(F32)
+    spare = jnp.zeros((16 - beams, channels), F32)
+    for i in (0, 1, -1):
+        found = None
         for j in (-1, 0, 1):
             for k in (-1, 0, 1):
-                rows = shifted[i + 1, 1 - j, (1 - k) * cols : (1 - k + beams) * cols, :]
-                tap = 9 * (i + 1) + 3 * (j + 1) + (k + 1)
-                total = total + dot(rows, w_ref[tap], NT)
+                left = main[1 - j, (1 - k) * cols : (1 - k + beams) * cols, :]
+                if i:
+                    edge = halo[0 if i == 1 else 1, 1 - j, 1 - k : 1 - k + beams, :]
+                    left = jnp.concatenate([left, jnp.concatenate([edge, spare]).astype(BF)])
+                part = dot(w_ref[9 * (i + 1) + 3 * (j + 1) + (k + 1)], left, NT)
+                found = part if found is None else found + part
+        found = found.T
+        if i == 1:
+            parts = [[found[rows + b : rows + b + 1], found[b * cols : (b + 1) * cols - 1]] for b in range(beams)]
+        elif i == -1:
+            parts = [[found[b * cols + 1 : (b + 1) * cols], found[rows + b : rows + b + 1]] for b in range(beams)]
+        else:
+            parts = [[found]]
+        total = total + jnp.concatenate([part for pair in parts for part in pair], axis=0)
     rounded = total.astype(BF)
     layer_out[...] = total.reshape(beams, cols, channels)
     layer_bf_out[...] = rounded.reshape(beams, cols, channels)
@@ -170,40 +181,40 @@
     return jnp.where(allowed, jnp.exp(scores - logsum), 0.0)
 
 
-def project_kernel(count, *refs):
-    come_refs = refs[: count - 1]
-    own_hbm, cot_hbm, *weights_hbm, mask_hbm = refs[count - 1 : count + 6]
-    all_out, query_out, key_out, value_out, allowed_out, w_out_out, cot_out = refs[count + 6 : count + 13]
-    own, cot, w_query, w_key, w_value, mask, sems = refs[count + 13 :]
-    targets = (own, w_key, w_value, w_query, mask, w_out_out, cot)
-    sources = (own_hbm, weights_hbm[1], weights_hbm[2], weights_hbm[0], mask_hbm, weights_hbm[3], cot_hbm)
+def load_kernel(count, *refs):
+    own_hbm, cot_hbm, mask_hbm, *weights_hbm = refs[:7]
+    own_out, cot_out, allowed_out, *weights_out = refs[7:14]
+    own, cot, mask, sems = refs[14:]
     copies = [
         pltpu.make_async_copy(source, target, sems.at[index])
-        for index, (source, target) in enumerate(zip(sources, targets))
+        for index, (source, target) in enumerate(
+            zip((own_hbm, cot_hbm, mask_hbm, *weights_hbm), (own, cot, mask, *weights_out))
+        )
     ]
     for copy in copies:
         copy.start()
-    cols, beams, channels = own.shape
+    for copy in copies:
+        copy.wait()
+    own_out[...] = jnp.swapaxes(own[...], 0, 1)
+    cot_out[...] = jnp.swapaxes(cot[...], 0, 1)
+    allowed_out[...] = allowed_row(mask[...], count, allowed_out.shape[1])
+
+
+def project_kernel(count, *refs):
+    own_ref, *come_refs = refs[:count]
+    w_query, w_key, w_value, all_out, query_out, key_out, value_out = refs[count:]
+    beams, cols, channels = own_ref.shape
     for distance in range(1, count):
         all_out[:, distance * cols : (distance + 1) * cols, :] = jnp.swapaxes(come_refs[distance - 1][...], 0, 1)
-    copies[0].wait()
-    all_out[:, :cols, :] = jnp.swapaxes(own[...], 0, 1)
+    all_out[:, :cols, :] = own_ref[...]
     every = all_out[...].reshape(beams * count * cols, channels)
-    copies[1].wait()
     key_out[...] = dot(every, w_key[...]).astype(BF).reshape(beams, count * cols, channels)
-    copies[2].wait()
     value_out[...] = dot(every, w_value[...]).astype(BF).reshape(beams, count * cols, channels)
-    copies[3].wait()
     mine = all_out[:, :cols, :].reshape(beams * cols, channels)
     query_out[...] = dot(mine, w_query[...]).astype(BF).reshape(beams, cols, channels)
-    copies[4].wait()
-    allowed_out[...] = allowed_row(mask[...], count, count * cols)
-    copies[5].wait()
-    copies[6].wait()
-    cot_out[...] = jnp.swapaxes(cot[...], 0, 1)
-
-
-def stack_kernel(own_ref, *refs):
+
+
+def stack_kernel(after_ref, own_ref, *refs):
     *come_refs, out = refs
     out[0] = own_ref[...]
     for index, ref in enumerate(come_refs, 1):
@@ -319,8 +330,16 @@
 
 
 def taps_kernel(count, even_ref, odd_ref, own_ref, *refs):
-    packed_refs = refs[: count - 1]
-    taps_out, layers, turned, held = refs[count - 1 :]
+    packed_refs, base_ref, grad_refs = refs[: count - 1], refs[count - 1], refs[count : 2 * count - 1]
+    taps_out, features_out, layers, turned, held = refs[2 * count - 1 :]
+    beams, cols, channels = base_ref.shape
+    rows = beams * cols
+    total = base_ref[...].reshape(rows, channels)
+    for ref in grad_refs:
+        total = total + jnp.concatenate(
+            [ref[half * rows : (half + 1) * rows, :].astype(F32) for half in range(channels // LANES)], axis=1
+        )
+    features_out[...] = jnp.swapaxes(total.reshape(beams, cols, channels).astype(BF), 0, 1)
     me = group_index()
     column = lax.axis_index("azim")
     lanes = taps_out.shape[2]
@@ -328,7 +347,8 @@
     per_sweep, rows = own_ref.shape[1], own_ref.shape[0] // 4
     held[0] = own_ref[...]
     for distance in range(1, count):
-        held[distance] = packed_refs[distance - 1][: 4 * rows, :]
+        ref = packed_refs[distance - 1]
+        held[distance] = ref[ref.shape[0] - 4 * rows :, :]
     for s in range(4):
         for y in range(2):
             slot = slot_of(y * 4 + s, me)
@@ -360,20 +380,11 @@
                 taps_out[9 * (i + 1) + 3 * (j + 1) + (k + 1)] = tap
 
 
-def last_kernel(count, own_piece, base_ref, taps_ref, *refs):
-    grad_refs, piece_refs = refs[: count - 1], refs[count - 1 : 2 * count - 2]
-    features_out, weights_out = refs[2 * count - 2 :]
-    beams, cols, channels = base_ref.shape
-    rows = beams * cols
-    total = base_ref[...].reshape(rows, channels)
+def last_kernel(own_piece, taps_ref, *refs):
+    *piece_refs, weights_out = refs
     piece = own_piece[0].astype(F32)
-    for ref in grad_refs:
-        total = total + jnp.concatenate(
-            [ref[half * rows : (half + 1) * rows, :].astype(F32) for half in range(channels // LANES)], axis=1
-        )
     for ref in piece_refs:
         piece = piece + ref[...].astype(F32)
-    features_out[...] = jnp.swapaxes(total.reshape(beams, cols, channels).astype(BF), 0, 1)
     width, lanes = weights_out.shape[1:]
     for index in range(4):
         weights_out[index] = piece[
@@ -417,15 +428,22 @@
     come_features = exchange({distance: raw_features for distance in distances})
     come_cot = [swap(raw_cot, bits) for bits in (2, 4, 6)]
 
-    every, queries, keys, values, allowed, w_out, own_cot = call(
+    own_features, own_cot, allowed, w_query, w_key, w_value, w_out = call(
+        functools.partial(load_kernel, count),
+        [(block, BF), (block, BF), ((8, count * cols), F32)] + [(square, BF)] * 4,
+        [HBM] * 7,
+        scratch=[pltpu.VMEM(token, BF)] * 2
+        + [pltpu.VMEM(sector_mask.shape, jnp.int32), pltpu.SemaphoreType.DMA((7,))],
+        micros=2,
+    )(*map(in_hbm, (raw_features, raw_cot, sector_mask, w_query, w_key, w_value, w_out)))
+    every, queries, keys, values = call(
         functools.partial(project_kernel, count),
-        [(whole, BF), (block, BF), (whole, BF), (whole, BF), ((8, count * cols), F32), (square, BF), (block, BF)],
-        [VMEM] * (count - 1) + [HBM] * 7,
-        scratch=[pltpu.VMEM(token, BF)] * 2 + [pltpu.VMEM(square, BF)] * 3
-        + [pltpu.VMEM(sector_mask.shape, jnp.int32), pltpu.SemaphoreType.DMA((7,))],
-    )(*come_features, *map(in_hbm, (raw_features, raw_cot, w_query, w_key, w_value, w_out, sector_mask)))
-
-    even = call(stack_kernel, [((4,) + block, BF)], [VMEM] * 4)(own_cot, *come_cot)[0]
+        [(whole, BF), (block, BF), (whole, BF), (whole, BF)],
+        [VMEM] * (count + 3),
+        micros=0.01,
+    )(own_features, *come_features, w_query, w_key, w_value)
+
+    even = call(stack_kernel, [((4,) + block, BF)], [VMEM] * 5)(queries, own_cot, *come_cot)[0]
     odd = swap(even, 1)
 
     pieces_shape = (count, cols, max(LANES, beams * lanes))
@@ -437,20 +455,28 @@
 
     spread = (4 * cols, 4 * width)
     edge = (8 * beams, channels)
-    slices, edges = call(slices_kernel, [(spread, BF), ((2,) + edge, BF)], [VMEM] * 2)(even, odd)
+    slices, edges, pieces = call(
+        slices_kernel, [(spread, BF), ((2,) + edge, BF), (pieces_shape, BF)], [VMEM] * 3
+    )(even, odd, pieces)
     neighbours = exchange({distance: edges for distance in neighbour_distances(count)})
 
-    packed = exchange({distance: jnp.concatenate([slices, pieces[distance]]) for distance in distances})
-    layer_block = jnp.concatenate([pieces[0]] + [part[4 * cols :] for part in packed])
+    far = count - 1
+    packed = exchange(
+        {
+            distance: pieces[distance] if distance == far else jnp.concatenate([pieces[distance], slices])
+            for distance in distances
+        }
+    )
+    layer_block = jnp.concatenate([pieces[0]] + [part[:cols] for part in packed])
 
     grad_layer, grad_layer_bf, grad_attended = call(
         functools.partial(conv_kernel, count),
         [(block, F32), (block, BF), (block, BF)],
         [VMEM] * (4 + len(neighbours)),
         scratch=[
-            pltpu.VMEM((3, beams + 2, cols + 16, channels), F32),
+            pltpu.VMEM((3, (beams + 2) * cols, channels), BF),
             pltpu.VMEM((2,) + edge, F32),
-            pltpu.VMEM((3, 3, (beams + 2) * cols, channels), BF),
+            pltpu.VMEM((2, 3, 8, channels), F32),
         ],
     )(even, odd, *neighbours, w_conv.transpose(1, 0, 2), w_out)
 
@@ -475,7 +501,14 @@
         pack_kernel, [(quarter[1:], BF)] + [((rows, LANES), BF)] * 3 + [(send.shape, BF)], [VMEM] * 7
     )(keep, layer_block, send, *[swap(give, 1) for give in gives])
     both = [swap(give, bits) for give, bits in zip(gives, (2, 4, 6))]
-    come_grads = exchange({distance: send[distance - 1] for distance in distances})
+    relayed = packed[far - 2][cols:]
+    come_grads = exchange(
+        {
+            distance: jnp.concatenate([send[distance - 1], relayed]) if distance == 1 else send[distance - 1]
+            for distance in distances
+        }
+    )
+    held_slices = packed[: far - 1] + [come_grads[0]]
     even_layers = jnp.stack([layer_block] + [part[: layer_block.shape[0]] for part in both])
     odd_layers = swap(even_layers, 1)
     sum_pieces = call(
@@ -485,21 +518,19 @@
     )(mine, *both)[0]
     come_pieces = exchange({distance: sum_pieces[distance] for distance in distances})
 
-    taps = call(
+    taps, features_grad = call(
         functools.partial(taps_kernel, count),
-        [((TAPS, width, lanes), F32)],
-        [VMEM] * (2 + count),
+        [((TAPS, width, lanes), F32), (token, BF)],
+        [VMEM] * (2 + 2 * count),
         scratch=[
             pltpu.VMEM((4, count * cols, 4 * lanes), BF),
             pltpu.VMEM((3, 16 * width, count * cols), BF),
             pltpu.VMEM((count,) + spread, BF),
         ],
-    )(even_layers, odd_layers, slices, *packed)[0]
-    features_grad, weight_grads = call(
-        functools.partial(last_kernel, count),
-        [((cols, beams, channels), BF), ((4 + TAPS, width, lanes), F32)],
-        [VMEM] * (1 + 2 * count),
-    )(sum_pieces, base, taps, *come_grads, *come_pieces)
+    )(even_layers, odd_layers, slices, *held_slices, base, *come_grads)
+    weight_grads = call(last_kernel, [((4 + TAPS, width, lanes), F32)], [VMEM] * (1 + count))(
+        sum_pieces, taps, *come_pieces
+    )[0]
     return features_grad.reshape(features.shape), weight_grads.transpose(2, 0, 1)
 
 

time: 48.4 us -> 47.8 us (0.988)
  waiting for transfers between devices: 7.83 us -> 6.29 us
  starting transfers between devices: 30.4 us -> 31 us
    ppermute x14, waiting for transfers between devices: 4.4 us -> 1.71 us  [swap_columns(): lax.ppermute(value, 'azim', [(i, i ^ distance) for i in range(count)])]
    pallas_call x4 -> x5, Pallas kernels: 2.53 us -> 4.61 us  [the longest x1 1.84 us: per_device(): call(functools.partial(taps_kernel, count), [((TAPS, width, lanes), F32),...]
    pallas_call x1, Pallas kernels: 1.92 us -> 0.34 us  [per_device(): call(functools.partial(project_kernel, count), [(whole, BF), (block, BF),...]
    ppermute x12, waiting for transfers between devices: 3.43 us -> 4.58 us  [swap(): return lax.ppermute(value, GROUP, [(i, i ^ bits) for i in range(8)])]
    ppermute x14, starting transfers between devices: 22 us -> 22.7 us  [swap_columns(): lax.ppermute(value, 'azim', [(i, i ^ distance) for i in range(count)])]
  transfers between devices with their start and end apart: 26 -> 26, of which waited for: 11 -> 10; matrix products, arithmetic and copies ran while one was open for 0% -> 0% of each run, Pallas kernels for 16% -> 17%
where the time goes in v6:
time: 47.8 us; the launch traced here: 47.6 us
  starting transfers between devices  31 us (65%)
  Pallas kernels  9.36 us (20%)
  waiting for transfers between devices  6.29 us (13%)
  between operations  0.82 us (2%)
    ppermute x14, starting transfers between devices, swap_columns(): lax.ppermute(value, 'azim', [(i, i ^ distance) for i in range(count)])  22.7 us
    ppermute x12, starting transfers between devices, swap(): return lax.ppermute(value, GROUP, [(i, i ^ bits) for i in range(8)])  8.34 us
    ppermute x12, waiting for transfers between devices, swap(): return lax.ppermute(value, GROUP, [(i, i ^ bits) for i in range(8)])  4.58 us
    pallas_call x1, Pallas kernels, per_device(): call(functools.partial(taps_kernel, count), [((TAPS, width, lanes), F32),...  1.84 us
    ppermute x14, waiting for transfers between devices, swap_columns(): lax.ppermute(value, 'azim', [(i, i ^ distance) for i in range(count)])  1.71 us
    pallas_call x1, Pallas kernels, per_device(): call(functools.partial(backward_kernel, count), [(block, F32), ((count -...  1.48 us
    pallas_call x1, Pallas kernels, per_device(): call(functools.partial(load_kernel, count), [(block, BF), (block, BF), ((...  1.43 us
    pallas_call x1, Pallas kernels, per_device(): call(functools.partial(attention_kernel, count), [(block, BF), (pieces_sh...  1.41 us
  transfers between devices with their start and end apart: 26, of which 10 were waited for; matrix products, arithmetic and copies ran while one was open for 0% of the time, Pallas kernels for 17%

profile of v6, /device:TPU:0, one launch (start us, length us, event | category | flops | bytes accessed | tf_op | source)
XLA Modules:
  0.0 47.6 jit_solution(10056122384281766672)
XLA Ops:
  0.6 5.1 %collective-permute-start.2 = (bf16[64,2,256]{2,1,0:T(2,128)(2,1)}, bf16[64,2,256]{2,1,0:T(2,128)(2,1)S(1)}, u32[]{:S(2)}, u32[]{:S(2)}) collective-permute-start(bf16[64,2,256]{2,1,0:T(2,128)(2,1)} %bitcast.36), channel_id=1, source_target_pairs={{0,24},{8,16},{16,8},{24,0},{1,25},{9,17},{17,9},{25,1},{2,26},{10... | collective-permute-start | bytes 196616 | tf_op jit(solution)/shard_map/ppermute | solution.py:402
  5.7 0.0 collective-permute-start.1
  5.7 0.6 %collective-permute-start = (bf16[64,2,256]{2,1,0:T(2,128)(2,1)}, bf16[64,2,256]{2,1,0:T(2,128)(2,1)S(1)}, u32[]{:S(2)}, u32[]{:S(2)}) collective-permute-start(bf16[64,2,256]{2,1,0:T(2,128)(2,1)} %bitcast.38), channel_id=1, source_target_pairs={{0,8},{8,0},{16,24},{24,16},{1,9},{9,1},{17,25},{25,17},{2,10},{10... | collective-permute-start | bytes 196616 | tf_op jit(solution)/shard_map/ppermute | solution.py:402
  6.4 2.6 %collective-permute-start.5 = (bf16[64,2,256]{2,1,0:T(2,128)(2,1)}, bf16[64,2,256]{2,1,0:T(2,128)(2,1)S(1)}, u32[]{:S(2)}, u32[]{:S(2)}) collective-permute-start(bf16[64,2,256]{2,1,0:T(2,128)(2,1)} %bitcast.40), channel_id=1, source_target_pairs={{0,6},{1,7},{2,4},{3,5},{4,2},{5,3},{6,0},{7,1},{8,14},{9,15},{10,... | collective-permute-start | bytes 196616 | tf_op jit(solution)/shard_map/ppermute | solution.py:411
  9.0 0.5 %collective-permute-start.4 = (bf16[64,2,256]{2,1,0:T(2,128)(2,1)}, bf16[64,2,256]{2,1,0:T(2,128)(2,1)S(1)}, u32[]{:S(2)}, u32[]{:S(2)}) collective-permute-start(bf16[64,2,256]{2,1,0:T(2,128)(2,1)} %bitcast.41), channel_id=1, source_target_pairs={{0,4},{1,5},{2,6},{3,7},{4,0},{5,1},{6,2},{7,3},{8,12},{9,13},{10,... | collective-permute-start | bytes 196616 | tf_op jit(solution)/shard_map/ppermute | solution.py:411
  9.5 0.0 collective-permute-done.2.refs_3_
  9.5 0.9 %collective-permute-start.3 = (bf16[64,2,256]{2,1,0:T(2,128)(2,1)}, bf16[64,2,256]{2,1,0:T(2,128)(2,1)S(1)}, u32[]{:S(2)}, u32[]{:S(2)}) collective-permute-start(bf16[64,2,256]{2,1,0:T(2,128)(2,1)} %bitcast.42), channel_id=1, source_target_pairs={{0,2},{1,3},{2,0},{3,1},{4,6},{5,7},{6,4},{7,5},{8,10},{9,11},{10,... | collective-permute-start | bytes 196616 | tf_op jit(solution)/shard_map/ppermute | solution.py:411
  10.4 1.4 %shard_map.95 = (bf16[2,64,256]{2,1,0:T(8,128)(2,1)S(1)}, bf16[2,64,256]{2,1,0:T(8,128)(2,1)S(1)}, f32[8,256]{1,0:T(8,128)S(1)}, bf16[256,256]{1,0:T(8,128)(2,1)...) custom-call(bf16[64,2,256]{2,1,0:T(2,128)(2,1)} %bitcast.39, ...), custom_call_target="tpu_custom_call" | custom-call | flops 2000000000 | tf_op jit(solution)/shard_map/pallas_call | solution.py:431
  11.8 0.0 collective-permute-done.1.refs_2_
  11.8 0.0 collective-permute-done.refs_1_
  11.9 0.3 shard_map.96
  12.2 0.0 collective-permute-done.5.refs_2_
  12.2 1.2 %collective-permute-done.4.refs_1_ = bf16[64,2,256]{2,1,0:T(2,128)(2,1)S(1)} collective-permute-done((bf16[64,2,256]{2,1,0:T(2,128)(2,1)}, bf16[64,2,256]{2,1,0:T(2,128)(2,1)S(1)}, u32[]{:S(2)}, u32[]{:S(2)}) %collective-permute-start.4) | collective-permute-done | bytes 65568 | tf_op jit(solution)/shard_map/ppermute | solution.py:411
  13.5 0.5 %collective-permute-done.3.refs_0_ = bf16[64,2,256]{2,1,0:T(2,128)(2,1)S(1)} collective-permute-done((bf16[64,2,256]{2,1,0:T(2,128)(2,1)}, bf16[64,2,256]{2,1,0:T(2,128)(2,1)S(1)}, u32[]{:S(2)}, u32[]{:S(2)}) %collective-permute-start.3) | collective-permute-done | bytes 65568 | tf_op jit(solution)/shard_map/ppermute | solution.py:411
  14.0 0.1 shard_map.97.even_ref
  14.1 0.1 collective-permute-start.6
  14.2 1.4 %shard_map.98 = (bf16[2,64,256]{2,1,0:T(8,128)(2,1)S(1)}, bf16[4,64,128]{2,1,0:T(8,128)(2,1)S(1)}, f32[2,512,256]{2,1,0:T(8,128)S(1)}) custom-call(f32[8,256]{1,0:T(8,128)S(1)} %get-tuple-element.42.allowed_ref, bf16[2,256,256]{2,1,0:T(8,128)(2,1)S(1)} %get-tuple-element.43.all_ref, bf16[2,64,256]{2,1,0:T(8,128)(2,1)S(1)} %get-tuple-element.40.after_ref.query_ref, ...), custom_call_target="tpu_custom_call" | custom-call | flops 2000000000 | tf_op jit(solution)/shard_map/pallas_call | solution.py:450
  15.6 0.1 collective-permute-done.6.odd_ref
  15.7 0.4 shard_map.99
  16.0 3.7 %collective-permute-start.11 = (bf16[2,16,256]{2,1,0:T(8,128)(2,1)S(1)}, bf16[2,16,256]{2,1,0:T(8,128)(2,1)S(1)}, u32[]{:S(2)}, u32[]{:S(2)}) collective-permute-start(bf16[2,16,256]{2,1,0:T(8,128)(2,1)S(1)} %get-tuple-element.52), channel_id=1, source_target_pairs={{0,24},{8,16},{16,8},{24,0},{1,25},{9,17},{17,9},{25,1},{2,26},{10... | collective-permute-start | bytes 49160 | tf_op jit(solution)/shard_map/ppermute | solution.py:402
  19.7 1.0 %collective-permute-start.9 = (bf16[64,128]{1,0:T(8,128)(2,1)S(1)}, bf16[64,128]{1,0:T(8,128)(2,1)S(1)}, u32[]{:S(2)}, u32[]{:S(2)}) collective-permute-start(bf16[64,128]{1,0:T(8,128)(2,1)S(1)} %get-tuple-element.81), channel_id=1, source_target_pairs={{0,24},{8,16},{16,8},{24,0},{1,25},{9,17},{17,9},{25,1},{2,26},{10... | collective-permute-start | bytes 49160 | tf_op jit(solution)/shard_map/ppermute | solution.py:402
  20.7 1.1 %collective-permute-start.7 = (bf16[320,128]{1,0:T(8,128)(2,1)S(1)}, bf16[320,128]{1,0:T(8,128)(2,1)S(1)}, u32[]{:S(2)}, u32[]{:S(2)}) collective-permute-start(bf16[320,128]{1,0:T(8,128)(2,1)S(1)} %get-tuple-element.84), channel_id=1, source_target_pairs={{0,8},{8,0},{16,24},{24,16},{1,9},{9,1},{17,25},{25,17},{2,10},{10... | collective-permute-start | bytes 245768 | tf_op jit(solution)/shard_map/ppermute | solution.py:402
  21.8 2.4 %collective-permute-start.8 = (bf16[320,128]{1,0:T(8,128)(2,1)S(1)}, bf16[320,128]{1,0:T(8,128)(2,1)S(1)}, u32[]{:S(2)}, u32[]{:S(2)}) collective-permute-start(bf16[320,128]{1,0:T(8,128)(2,1)S(1)} %get-tuple-element.85), channel_id=1, source_target_pairs={{0,16},{8,24},{16,0},{24,8},{1,17},{9,25},{17,1},{25,9},{2,18},{10... | collective-permute-start | bytes 245768 | tf_op jit(solution)/shard_map/ppermute | solution.py:402
  24.3 0.0 collective-permute-done.11.refs_1_
  24.3 1.3 %shard_map.100 = (f32[2,64,256]{2,1,0:T(8,128)S(1)}, bf16[2,64,256]{2,1,0:T(8,128)(2,1)S(1)}, bf16[2,64,256]{2,1,0:T(8,128)(2,1)S(1)}) custom-call(bf16[4,2,64,256]{3,2,1,0:T(8,128)(2,1)S(1)} %shard_map.97.even_ref, bf16[4,2,64,256]{3,2,1,0:T(8,128)(2,1)S(1)} %collective-permute-done.6.odd_ref, bf16[2,16,256]{2,1,0:T(8,128)(2,1)S(1)} %collective-permute-done.10.refs_0_, ...), custom_call_target="tpu_custom_call" | custom-call | flops 2000000000 | tf_op jit(solution)/shard_map/pallas_call | solution.py:472
  25.6 1.5 %shard_map.101 = (f32[2,64,256]{2,1,0:T(8,128)S(1)}, bf16[3,256,128]{2,1,0:T(8,128)(2,1)S(1)}, bf16[4,256,128]{2,1,0:T(8,128)(2,1)S(1)}, bf16[256,128]{1,0:T(8,1...) custom-call(f32[2,512,256]{2,1,0:T(8,128)S(1)} %get-tuple-element.50.weights_, ...), custom_call_target="tpu_custom_call" | custom-call | flops 2000000000 | tf_op jit(solution)/shard_map/pallas_call | solution.py:484
  27.1 0.1 collective-permute-start.12
  27.2 0.5 %collective-permute-start.13 = (bf16[256,128]{1,0:T(8,128)(2,1)S(1)}, bf16[256,128]{1,0:T(8,128)(2,1)S(1)}, u32[]{:S(2)}, u32[]{:S(2)}) collective-permute-start(bf16[256,128]{1,0:T(8,128)(2,1)S(1)} %get-tuple-element.59), channel_id=1, source_target_pairs={{0,1},{1,0},{2,3},{3,2},{4,5},{5,4},{6,7},{7,6},{8,9},{9,8},{10,11... | collective-permute-start | bytes 196616 | tf_op jit(solution)/shard_map/ppermute | solution.py:411
  27.7 0.1 collective-permute-start.14
  27.8 0.8 %collective-permute-done.8.refs_1_ = bf16[320,128]{1,0:T(8,128)(2,1)S(1)} collective-permute-done((bf16[320,128]{1,0:T(8,128)(2,1)S(1)}, bf16[320,128]{1,0:T(8,128)(2,1)S(1)}, u32[]{:S(2)}, u32[]{:S(2)}) %collective-permute-start.8) | collective-permute-done | bytes 81952 | tf_op jit(solution)/shard_map/ppermute | solution.py:402
  28.7 0.3 collective-permute-done.14.refs_2_
  28.9 0.9 %collective-permute-done.15.refs_3_ = bf16[256,128]{1,0:T(8,128)(2,1)S(1)} collective-permute-done((bf16[256,128]{1,0:T(8,128)(2,1)S(1)}, bf16[256,128]{1,0:T(8,128)(2,1)S(1)}, u32[]{:S(2)}, u32[]{:S(2)}) %collective-permute-start.15) | collective-permute-done | bytes 65568 | tf_op jit(solution)/shard_map/ppermute | solution.py:411
  29.9 0.1 shard_map.102
  29.9 1.2 %collective-permute-start.16 = (bf16[512,128]{1,0:T(8,128)(2,1)S(1)}, bf16[512,128]{1,0:T(8,128)(2,1)S(1)}, u32[]{:S(2)}, u32[]{:S(2)}) collective-permute-start(bf16[512,128]{1,0:T(8,128)(2,1)S(1)} %get-tuple-element.62), channel_id=1, source_target_pairs={{0,2},{1,3},{2,0},{3,1},{4,6},{5,7},{6,4},{7,5},{8,10},{9,11},{10,... | collective-permute-start | bytes 393224 | tf_op jit(solution)/shard_map/ppermute | solution.py:411
  31.1 1.5 %collective-permute-start.17 = (bf16[512,128]{1,0:T(8,128)(2,1)S(1)}, bf16[512,128]{1,0:T(8,128)(2,1)S(1)}, u32[]{:S(2)}, u32[]{:S(2)}) collective-permute-start(bf16[512,128]{1,0:T(8,128)(2,1)S(1)} %get-tuple-element.63), channel_id=1, source_target_pairs={{0,4},{1,5},{2,6},{3,7},{4,0},{5,1},{6,2},{7,3},{8,12},{9,13},{10,... | collective-permute-start | bytes 393224 | tf_op jit(solution)/shard_map/ppermute | solution.py:411
  32.7 0.8 %collective-permute-start.18 = (bf16[512,128]{1,0:T(8,128)(2,1)S(1)}, bf16[512,128]{1,0:T(8,128)(2,1)S(1)}, u32[]{:S(2)}, u32[]{:S(2)}) collective-permute-start(bf16[512,128]{1,0:T(8,128)(2,1)S(1)} %get-tuple-element.64), channel_id=1, source_target_pairs={{0,6},{1,7},{2,4},{3,5},{4,2},{5,3},{6,0},{7,1},{8,14},{9,15},{10,... | collective-permute-start | bytes 393224 | tf_op jit(solution)/shard_map/ppermute | solution.py:411
  33.5 2.5 %collective-permute-start.22 = (bf16[256,128]{1,0:T(8,128)(2,1)S(1)}, bf16[256,128]{1,0:T(8,128)(2,1)S(1)}, u32[]{:S(2)}, u32[]{:S(2)}) collective-permute-start(bf16[256,128]{1,0:T(8,128)(2,1)S(1)} %get-tuple-element.72), channel_id=1, source_target_pairs={{0,24},{8,16},{16,8},{24,0},{1,25},{9,17},{17,9},{25,1},{2,26},{10... | collective-permute-start | bytes 196616 | tf_op jit(solution)/shard_map/ppermute | solution.py:402
  36.1 0.2 collective-permute-done.16.refs_0_
  36.3 1.8 %collective-permute-start.20 = (bf16[512,128]{1,0:T(8,128)(2,1)S(1)}, bf16[512,128]{1,0:T(8,128)(2,1)S(1)}, u32[]{:S(2)}, u32[]{:S(2)}) collective-permute-start(bf16[512,128]{1,0:T(8,128)(2,1)S(1)} %pad_maximum_fusion.1), channel_id=1, source_target_pairs={{0,8},{8,0},{16,24},{24,16},{1,9},{9,1},{17,25},{25,17},{2,10},{10... | collective-permute-start | bytes 393224 | tf_op jit(solution)/shard_map/ppermute | solution.py:402
  38.1 0.2 collective-permute-done.17.refs_1_
  38.3 1.1 %collective-permute-done.18.refs_2_ = bf16[512,128]{1,0:T(8,128)(2,1)S(1)} collective-permute-done((bf16[512,128]{1,0:T(8,128)(2,1)S(1)}, bf16[512,128]{1,0:T(8,128)(2,1)S(1)}, u32[]{:S(2)}, u32[]{:S(2)}) %collective-permute-start.18) | collective-permute-done | bytes 131104 | tf_op jit(solution)/shard_map/ppermute | solution.py:411
  39.4 0.1 collective-permute-start.19
  39.5 0.1 shard_map.104.own_piece
  39.6 2.5 %collective-permute-start.25 = (bf16[64,128]{1,0:T(8,128)(2,1)S(1)}, bf16[64,128]{1,0:T(8,128)(2,1)S(1)}, u32[]{:S(2)}, u32[]{:S(2)}) collective-permute-start(bf16[64,128]{1,0:T(8,128)(2,1)S(1)} %get-tuple-element.75), channel_id=1, source_target_pairs={{0,24},{8,16},{16,8},{24,0},{1,25},{9,17},{17,9},{25,1},{2,26},{10... | collective-permute-start | bytes 49160 | tf_op jit(solution)/shard_map/ppermute | solution.py:402
  42.1 1.9 %collective-permute-start.23 = (bf16[64,128]{1,0:T(8,128)(2,1)S(1)}, bf16[64,128]{1,0:T(8,128)(2,1)S(1)}, u32[]{:S(2)}, u32[]{:S(2)}) collective-permute-start(bf16[64,128]{1,0:T(8,128)(2,1)S(1)} %get-tuple-element.77), channel_id=1, source_target_pairs={{0,8},{8,0},{16,24},{24,16},{1,9},{9,1},{17,25},{25,17},{2,10},{10... | collective-permute-start | bytes 49160 | tf_op jit(solution)/shard_map/ppermute | solution.py:402
  44.0 1.8 %shard_map.103 = (f32[27,32,64]{2,1,0:T(8,128)S(1)}, bf16[64,2,256]{2,1,0:T(2,128)(2,1)}) custom-call(bf16[4,256,128]{2,1,0:T(8,128)(2,1)S(1)} %pad_maximum_fusion.even_ref, bf16[4,256,128]{2,1,0:T(8,128)(2,1)S(1)} %collective-permute-done.19.odd_ref, bf16[256,128]{1,0:T(8,128)(2,1)S(1)} %get-tuple-element.49.own_ref, ...), custom_call_target="tpu_custom_call" | custom-call | flops 2000000000 | tf_op jit(solution)/shard_map/pallas_call | solution.py:521
  45.9 0.8 %collective-permute-done.24.refs_1_ = bf16[64,128]{1,0:T(8,128)(2,1)S(1)} collective-permute-done((bf16[64,128]{1,0:T(8,128)(2,1)S(1)}, bf16[64,128]{1,0:T(8,128)(2,1)S(1)}, u32[]{:S(2)}, u32[]{:S(2)}) %collective-permute-start.24) | collective-permute-done | bytes 16416 | tf_op jit(solution)/shard_map/ppermute | solution.py:402
  46.7 0.9 %shard_map.105 = f32[31,32,64]{2,1,0:T(8,128)} custom-call(bf16[4,64,128]{2,1,0:T(8,128)(2,1)S(1)} %shard_map.104.own_piece, f32[27,32,64]{2,1,0:T(8,128)S(1)} %get-tuple-element.69.taps_ref, bf16[64,128]{1,0:T(8,128)(2,1)S(1)} %collective-permute-done.23.refs_0_, bf16[64,128]{1,0:T(8,128)(2,1)S(1)} %collective-permute-done.24.refs_1_, ...), custom_call_target="tpu_custom_call" | custom-call | flops 2000000000 | tf_op jit(solution)/shard_map/pallas_call | solution.py:531
  (30 shorter events, 0.2 us)
Async XLA Ops:
  0.6 8.9 %collective-permute-start.2 = (bf16[64,2,256]{2,1,0:T(2,128)(2,1)}, bf16[64,2,256]{2,1,0:T(2,128)(2,1)S(1)}, u32[]{:S(2)}, u32[]{:S(2)}) collective-permute-start(bf16[64,2,256]{2,1,0:T(2,128)(2,1)} %bitcast.36), channel_id=1, source_target_pairs={{0,24},{8,16},{16,8},{24,0},{1,25},{9,17},{17,9},{25,1},{2,26},{10... | collective-permute-start | bytes 196616 | tf_op jit(solution)/shard_map/ppermute | solution.py:402
  5.7 6.1 %collective-permute-start.1 = (bf16[64,2,256]{2,1,0:T(2,128)(2,1)}, bf16[64,2,256]{2,1,0:T(2,128)(2,1)S(1)}, u32[]{:S(2)}, u32[]{:S(2)}) collective-permute-start(bf16[64,2,256]{2,1,0:T(2,128)(2,1)} %bitcast.37), channel_id=1, source_target_pairs={{0,16},{8,24},{16,0},{24,8},{1,17},{9,25},{17,1},{25,9},{2,18},{10... | collective-permute-start | bytes 196616 | tf_op jit(solution)/shard_map/ppermute | solution.py:402
  5.7 6.1 %collective-permute-start = (bf16[64,2,256]{2,1,0:T(2,128)(2,1)}, bf16[64,2,256]{2,1,0:T(2,128)(2,1)S(1)}, u32[]{:S(2)}, u32[]{:S(2)}) collective-permute-start(bf16[64,2,256]{2,1,0:T(2,128)(2,1)} %bitcast.38), channel_id=1, source_target_pairs={{0,8},{8,0},{16,24},{24,16},{1,9},{9,1},{17,25},{25,17},{2,10},{10... | collective-permute-start | bytes 196616 | tf_op jit(solution)/shard_map/ppermute | solution.py:402
  6.4 5.8 %collective-permute-start.5 = (bf16[64,2,256]{2,1,0:T(2,128)(2,1)}, bf16[64,2,256]{2,1,0:T(2,128)(2,1)S(1)}, u32[]{:S(2)}, u32[]{:S(2)}) collective-permute-start(bf16[64,2,256]{2,1,0:T(2,128)(2,1)} %bitcast.40), channel_id=1, source_target_pairs={{0,6},{1,7},{2,4},{3,5},{4,2},{5,3},{6,0},{7,1},{8,14},{9,15},{10,... | collective-permute-start | bytes 196616 | tf_op jit(solution)/shard_map/ppermute | solution.py:411
  9.0 4.5 %collective-permute-start.4 = (bf16[64,2,256]{2,1,0:T(2,128)(2,1)}, bf16[64,2,256]{2,1,0:T(2,128)(2,1)S(1)}, u32[]{:S(2)}, u32[]{:S(2)}) collective-permute-start(bf16[64,2,256]{2,1,0:T(2,128)(2,1)} %bitcast.41), channel_id=1, source_target_pairs={{0,4},{1,5},{2,6},{3,7},{4,0},{5,1},{6,2},{7,3},{8,12},{9,13},{10,... | collective-permute-start | bytes 196616 | tf_op jit(solution)/shard_map/ppermute | solution.py:411
  9.5 4.5 %collective-permute-start.3 = (bf16[64,2,256]{2,1,0:T(2,128)(2,1)}, bf16[64,2,256]{2,1,0:T(2,128)(2,1)S(1)}, u32[]{:S(2)}, u32[]{:S(2)}) collective-permute-start(bf16[64,2,256]{2,1,0:T(2,128)(2,1)} %bitcast.42), channel_id=1, source_target_pairs={{0,2},{1,3},{2,0},{3,1},{4,6},{5,7},{6,4},{7,5},{8,10},{9,11},{10,... | collective-permute-start | bytes 196616 | tf_op jit(solution)/shard_map/ppermute | solution.py:411
  14.1 1.6 %collective-permute-start.6 = (bf16[4,2,64,256]{3,2,1,0:T(8,128)(2,1)S(1)}, bf16[4,2,64,256]{3,2,1,0:T(8,128)(2,1)S(1)}, u32[]{:S(2)}, u32[]{:S(2)}) collective-permute-start(bf16[4,2,64,256]{3,2,1,0:T(8,128)(2,1)S(1)} %shard_map.97.even_ref), channel_id=1, source_target_pairs={{0,1},{1,0},{2,3},{3,2},{4,5},{5,4},{6,7},{7,6},{8,9},{9,8},{10,11... | collective-permute-start | bytes 786440 | tf_op jit(solution)/shard_map/ppermute | solution.py:411
  15.7 8.6 %copy-start = (bf16[256,27,256]{2,0,1:T(8,128)(2,1)S(1)}, bf16[256,27,256]{2,0,1:T(8,128)(2,1)}, u32[]{:S(2)}) copy-start(bf16[256,27,256]{2,0,1:T(8,128)(2,1)} %param.14) | copy-start | bytes 10616836
  16.0 8.2 %collective-permute-start.11 = (bf16[2,16,256]{2,1,0:T(8,128)(2,1)S(1)}, bf16[2,16,256]{2,1,0:T(8,128)(2,1)S(1)}, u32[]{:S(2)}, u32[]{:S(2)}) collective-permute-start(bf16[2,16,256]{2,1,0:T(8,128)(2,1)S(1)} %get-tuple-element.52), channel_id=1, source_target_pairs={{0,24},{8,16},{16,8},{24,0},{1,25},{9,17},{17,9},{25,1},{2,26},{10... | collective-permute-start | bytes 49160 | tf_op jit(solution)/shard_map/ppermute | solution.py:402
  19.7 4.6 %collective-permute-start.10 = (bf16[2,16,256]{2,1,0:T(8,128)(2,1)S(1)}, bf16[2,16,256]{2,1,0:T(8,128)(2,1)S(1)}, u32[]{:S(2)}, u32[]{:S(2)}) collective-permute-start(bf16[2,16,256]{2,1,0:T(8,128)(2,1)S(1)} %get-tuple-element.52), channel_id=1, source_target_pairs={{0,8},{8,0},{16,24},{24,16},{1,9},{9,1},{17,25},{25,17},{2,10},{10... | collective-permute-start | bytes 49160 | tf_op jit(solution)/shard_map/ppermute | solution.py:402
  19.7 8.9 %collective-permute-start.9 = (bf16[64,128]{1,0:T(8,128)(2,1)S(1)}, bf16[64,128]{1,0:T(8,128)(2,1)S(1)}, u32[]{:S(2)}, u32[]{:S(2)}) collective-permute-start(bf16[64,128]{1,0:T(8,128)(2,1)S(1)} %get-tuple-element.81), channel_id=1, source_target_pairs={{0,24},{8,16},{16,8},{24,0},{1,25},{9,17},{17,9},{25,1},{2,26},{10... | collective-permute-start | bytes 49160 | tf_op jit(solution)/shard_map/ppermute | solution.py:402
  20.7 7.0 %collective-permute-start.7 = (bf16[320,128]{1,0:T(8,128)(2,1)S(1)}, bf16[320,128]{1,0:T(8,128)(2,1)S(1)}, u32[]{:S(2)}, u32[]{:S(2)}) collective-permute-start(bf16[320,128]{1,0:T(8,128)(2,1)S(1)} %get-tuple-element.84), channel_id=1, source_target_pairs={{0,8},{8,0},{16,24},{24,16},{1,9},{9,1},{17,25},{25,17},{2,10},{10... | collective-permute-start | bytes 245768 | tf_op jit(solution)/shard_map/ppermute | solution.py:402
  21.8 6.8 %collective-permute-start.8 = (bf16[320,128]{1,0:T(8,128)(2,1)S(1)}, bf16[320,128]{1,0:T(8,128)(2,1)S(1)}, u32[]{:S(2)}, u32[]{:S(2)}) collective-permute-start(bf16[320,128]{1,0:T(8,128)(2,1)S(1)} %get-tuple-element.85), channel_id=1, source_target_pairs={{0,16},{8,24},{16,0},{24,8},{1,17},{9,25},{17,1},{25,9},{2,18},{10... | collective-permute-start | bytes 245768 | tf_op jit(solution)/shard_map/ppermute | solution.py:402
  27.1 1.5 %collective-permute-start.12 = (bf16[256,128]{1,0:T(8,128)(2,1)S(1)}, bf16[256,128]{1,0:T(8,128)(2,1)S(1)}, u32[]{:S(2)}, u32[]{:S(2)}) collective-permute-start(bf16[256,128]{1,0:T(8,128)(2,1)S(1)} %get-tuple-element.58), channel_id=1, source_target_pairs={{0,1},{1,0},{2,3},{3,2},{4,5},{5,4},{6,7},{7,6},{8,9},{9,8},{10,11... | collective-permute-start | bytes 196616 | tf_op jit(solution)/shard_map/ppermute | solution.py:411
  27.2 1.5 %collective-permute-start.13 = (bf16[256,128]{1,0:T(8,128)(2,1)S(1)}, bf16[256,128]{1,0:T(8,128)(2,1)S(1)}, u32[]{:S(2)}, u32[]{:S(2)}) collective-permute-start(bf16[256,128]{1,0:T(8,128)(2,1)S(1)} %get-tuple-element.59), channel_id=1, source_target_pairs={{0,1},{1,0},{2,3},{3,2},{4,5},{5,4},{6,7},{7,6},{8,9},{9,8},{10,11... | collective-permute-start | bytes 196616 | tf_op jit(solution)/shard_map/ppermute | solution.py:411
  27.7 1.3 %collective-permute-start.14 = (bf16[256,128]{1,0:T(8,128)(2,1)S(1)}, bf16[256,128]{1,0:T(8,128)(2,1)S(1)}, u32[]{:S(2)}, u32[]{:S(2)}) collective-permute-start(bf16[256,128]{1,0:T(8,128)(2,1)S(1)} %get-tuple-element.60), channel_id=1, source_target_pairs={{0,1},{1,0},{2,3},{3,2},{4,5},{5,4},{6,7},{7,6},{8,9},{9,8},{10,11... | collective-permute-start | bytes 196616 | tf_op jit(solution)/shard_map/ppermute | solution.py:411
  28.6 1.3 %collective-permute-start.15 = (bf16[256,128]{1,0:T(8,128)(2,1)S(1)}, bf16[256,128]{1,0:T(8,128)(2,1)S(1)}, u32[]{:S(2)}, u32[]{:S(2)}) collective-permute-start(bf16[256,128]{1,0:T(8,128)(2,1)S(1)} %get-tuple-element.61), channel_id=1, source_target_pairs={{0,1},{1,0},{2,3},{3,2},{4,5},{5,4},{6,7},{7,6},{8,9},{9,8},{10,11... | collective-permute-start | bytes 196616 | tf_op jit(solution)/shard_map/ppermute | solution.py:411
  29.9 6.4 %collective-permute-start.16 = (bf16[512,128]{1,0:T(8,128)(2,1)S(1)}, bf16[512,128]{1,0:T(8,128)(2,1)S(1)}, u32[]{:S(2)}, u32[]{:S(2)}) collective-permute-start(bf16[512,128]{1,0:T(8,128)(2,1)S(1)} %get-tuple-element.62), channel_id=1, source_target_pairs={{0,2},{1,3},{2,0},{3,1},{4,6},{5,7},{6,4},{7,5},{8,10},{9,11},{10,... | collective-permute-start | bytes 393224 | tf_op jit(solution)/shard_map/ppermute | solution.py:411
  31.1 7.1 %collective-permute-start.17 = (bf16[512,128]{1,0:T(8,128)(2,1)S(1)}, bf16[512,128]{1,0:T(8,128)(2,1)S(1)}, u32[]{:S(2)}, u32[]{:S(2)}) collective-permute-start(bf16[512,128]{1,0:T(8,128)(2,1)S(1)} %get-tuple-element.63), channel_id=1, source_target_pairs={{0,4},{1,5},{2,6},{3,7},{4,0},{5,1},{6,2},{7,3},{8,12},{9,13},{10,... | collective-permute-start | bytes 393224 | tf_op jit(solution)/shard_map/ppermute | solution.py:411
  32.7 6.7 %collective-permute-start.18 = (bf16[512,128]{1,0:T(8,128)(2,1)S(1)}, bf16[512,128]{1,0:T(8,128)(2,1)S(1)}, u32[]{:S(2)}, u32[]{:S(2)}) collective-permute-start(bf16[512,128]{1,0:T(8,128)(2,1)S(1)} %get-tuple-element.64), channel_id=1, source_target_pairs={{0,6},{1,7},{2,4},{3,5},{4,2},{5,3},{6,0},{7,1},{8,14},{9,15},{10,... | collective-permute-start | bytes 393224 | tf_op jit(solution)/shard_map/ppermute | solution.py:411
  33.5 8.6 %collective-permute-start.22 = (bf16[256,128]{1,0:T(8,128)(2,1)S(1)}, bf16[256,128]{1,0:T(8,128)(2,1)S(1)}, u32[]{:S(2)}, u32[]{:S(2)}) collective-permute-start(bf16[256,128]{1,0:T(8,128)(2,1)S(1)} %get-tuple-element.72), channel_id=1, source_target_pairs={{0,24},{8,16},{16,8},{24,0},{1,25},{9,17},{17,9},{25,1},{2,26},{10... | collective-permute-start | bytes 196616 | tf_op jit(solution)/shard_map/ppermute | solution.py:402
  36.0 6.1 %collective-permute-start.21 = (bf16[256,128]{1,0:T(8,128)(2,1)S(1)}, bf16[256,128]{1,0:T(8,128)(2,1)S(1)}, u32[]{:S(2)}, u32[]{:S(2)}) collective-permute-start(bf16[256,128]{1,0:T(8,128)(2,1)S(1)} %get-tuple-element.73), channel_id=1, source_target_pairs={{0,16},{8,24},{16,0},{24,8},{1,17},{9,25},{17,1},{25,9},{2,18},{10... | collective-permute-start | bytes 196616 | tf_op jit(solution)/shard_map/ppermute | solution.py:402
  36.3 7.7 %collective-permute-start.20 = (bf16[512,128]{1,0:T(8,128)(2,1)S(1)}, bf16[512,128]{1,0:T(8,128)(2,1)S(1)}, u32[]{:S(2)}, u32[]{:S(2)}) collective-permute-start(bf16[512,128]{1,0:T(8,128)(2,1)S(1)} %pad_maximum_fusion.1), channel_id=1, source_target_pairs={{0,8},{8,0},{16,24},{24,16},{1,9},{9,1},{17,25},{25,17},{2,10},{10... | collective-permute-start | bytes 393224 | tf_op jit(solution)/shard_map/ppermute | solution.py:402
  39.4 4.7 %collective-permute-start.19 = (bf16[4,256,128]{2,1,0:T(8,128)(2,1)S(1)}, bf16[4,256,128]{2,1,0:T(8,128)(2,1)S(1)}, u32[]{:S(2)}, u32[]{:S(2)}) collective-permute-start(bf16[4,256,128]{2,1,0:T(8,128)(2,1)S(1)} %pad_maximum_fusion.even_ref), channel_id=1, source_target_pairs={{0,1},{1,0},{2,3},{3,2},{4,5},{5,4},{6,7},{7,6},{8,9},{9,8},{10,11... | collective-permute-start | bytes 786440 | tf_op jit(solution)/shard_map/ppermute | solution.py:411
  39.6 6.3 %collective-permute-start.25 = (bf16[64,128]{1,0:T(8,128)(2,1)S(1)}, bf16[64,128]{1,0:T(8,128)(2,1)S(1)}, u32[]{:S(2)}, u32[]{:S(2)}) collective-permute-start(bf16[64,128]{1,0:T(8,128)(2,1)S(1)} %get-tuple-element.75), channel_id=1, source_target_pairs={{0,24},{8,16},{16,8},{24,0},{1,25},{9,17},{17,9},{25,1},{2,26},{10... | collective-permute-start | bytes 49160 | tf_op jit(solution)/shard_map/ppermute | solution.py:402
  42.1 4.6 %collective-permute-start.24 = (bf16[64,128]{1,0:T(8,128)(2,1)S(1)}, bf16[64,128]{1,0:T(8,128)(2,1)S(1)}, u32[]{:S(2)}, u32[]{:S(2)}) collective-permute-start(bf16[64,128]{1,0:T(8,128)(2,1)S(1)} %get-tuple-element.76), channel_id=1, source_target_pairs={{0,16},{8,24},{16,0},{24,8},{1,17},{9,25},{17,1},{25,9},{2,18},{10... | collective-permute-start | bytes 49160 | tf_op jit(solution)/shard_map/ppermute | solution.py:402
  42.1 4.6 %collective-permute-start.23 = (bf16[64,128]{1,0:T(8,128)(2,1)S(1)}, bf16[64,128]{1,0:T(8,128)(2,1)S(1)}, u32[]{:S(2)}, u32[]{:S(2)}) collective-permute-start(bf16[64,128]{1,0:T(8,128)(2,1)S(1)} %get-tuple-element.77), channel_id=1, source_target_pairs={{0,8},{8,0},{16,24},{24,16},{1,9},{9,1},{17,25},{25,17},{2,10},{10... | collective-permute-start | bytes 49160 | tf_op jit(solution)/shard_map/ppermute | solution.py:402

commit v7 on v6

--- a/solution.py
+++ b/solution.py
@@ -294,25 +294,21 @@
                 target[row : row + width, :] = part[:, half * LANES : (half + 1) * LANES]
 
 
-def pack_kernel(keep_ref, layer_ref, send_ref, *refs):
-    come_refs = refs[:4]
-    mine_out, *give_outs, send_out = refs[4:]
+def pack_kernel(keep_ref, layer_ref, send_ref, give_ref, *refs):
+    come_refs, give_outs, (send_out, give_out) = refs[:3], refs[3:6], refs[6:]
     rows = layer_ref.shape[0]
-    for block, ref in enumerate(come_refs):
-        total = (keep_ref[block].astype(F32) + ref[...].astype(F32)).astype(BF)
-        if block == 0:
-            mine_out[...] = total
-        else:
-            give_outs[block - 1][:rows, :] = layer_ref[...]
-            give_outs[block - 1][rows:, :] = total
+    for block, (ref, out) in enumerate(zip(come_refs, give_outs), 1):
+        out[:rows, :] = layer_ref[...]
+        out[rows:, :] = (keep_ref[block].astype(F32) + ref[...].astype(F32)).astype(BF)
     send_out[...] = send_ref[...]
-
-
-def pieces_kernel(count, keep_ref, *refs):
+    give_out[...] = give_ref[...]
+
+
+def pieces_kernel(count, keep_ref, mine_ref, *refs):
     pieces_out = refs[-1]
     me = lax.axis_index("azim")
-    rows = keep_ref.shape[0]
-    total = keep_ref[...].astype(F32)
+    rows = keep_ref.shape[1]
+    total = keep_ref[0].astype(F32) + mine_ref[...].astype(F32)
     for ref in refs[:-1]:
         total = total + ref[ref.shape[0] - rows :, :].astype(F32)
     halves = 2
@@ -497,10 +493,11 @@
     )
 
     rows = quarter[1] + layer_block.shape[0]
-    mine, *gives, send = call(
-        pack_kernel, [(quarter[1:], BF)] + [((rows, LANES), BF)] * 3 + [(send.shape, BF)], [VMEM] * 7
-    )(keep, layer_block, send, *[swap(give, 1) for give in gives])
-    both = [swap(give, bits) for give, bits in zip(gives, (2, 4, 6))]
+    *packs, send, give = call(
+        pack_kernel, [((rows, LANES), BF)] * 3 + [(send.shape, BF), (quarter[1:], BF)], [VMEM] * 7
+    )(keep, layer_block, send, gives[0], *[swap(part, 1) for part in gives[1:]])
+    mine = swap(give, 1)
+    both = [swap(give, bits) for give, bits in zip(packs, (2, 4, 6))]
     relayed = packed[far - 2][cols:]
     come_grads = exchange(
         {
@@ -514,8 +511,8 @@
     sum_pieces = call(
         functools.partial(pieces_kernel, count),
         [((count, 2 * width, max(LANES, 2 * lanes)), BF)],
-        [VMEM] * 4,
-    )(mine, *both)[0]
+        [VMEM] * 5,
+    )(keep, mine, *both)[0]
     come_pieces = exchange({distance: sum_pieces[distance] for distance in distances})
 
     taps, features_grad = call(

time: 47.8 us -> 46.9 us (0.981)
  waiting for transfers between devices: 6.29 us -> 5.76 us
  transfers between devices with their start and end apart: 26 -> 26, of which waited for: 10 -> 8; matrix products, arithmetic and copies ran while one was open for 0% -> 0% of each run, Pallas kernels for 17% -> 17%
where the time goes in v7:
time: 46.9 us; the launch traced here: 46.8 us
  starting transfers between devices  30.7 us (65%)
  Pallas kernels  9.36 us (20%)
  waiting for transfers between devices  5.76 us (12%)
  between operations  0.83 us (2%)
    ppermute x14, starting transfers between devices, swap_columns(): lax.ppermute(value, 'azim', [(i, i ^ distance) for i in range(count)])  22.2 us
    ppermute x12, starting transfers between devices, swap(): return lax.ppermute(value, GROUP, [(i, i ^ bits) for i in range(8)])  8.5 us
    ppermute x12, waiting for transfers between devices, swap(): return lax.ppermute(value, GROUP, [(i, i ^ bits) for i in range(8)])  4.33 us
    pallas_call x1, Pallas kernels, per_device(): call(functools.partial(taps_kernel, count), [((TAPS, width, lanes), F32),...  1.84 us
    pallas_call x1, Pallas kernels, per_device(): call(functools.partial(backward_kernel, count), [(block, F32), ((count -...  1.48 us
    pallas_call x1, Pallas kernels, per_device(): call(functools.partial(load_kernel, count), [(block, BF), (block, BF), ((...  1.43 us
    ppermute x14, waiting for transfers between devices, swap_columns(): lax.ppermute(value, 'azim', [(i, i ^ distance) for i in range(count)])  1.43 us
    pallas_call x1, Pallas kernels, per_device(): call(functools.partial(attention_kernel, count), [(block, BF), (pieces_sh...  1.41 us
  transfers between devices with their start and end apart: 26, of which 8 were waited for; matrix products, arithmetic and copies ran while one was open for 0% of the time, Pallas kernels for 17%

profile of v7, /device:TPU:0, one launch (start us, length us, event | category | flops | bytes accessed | tf_op | source)
XLA Modules:
  0.0 46.8 jit_solution(18405069455492814932)
XLA Ops:
  0.6 5.1 %collective-permute-start.2 = (bf16[64,2,256]{2,1,0:T(2,128)(2,1)}, bf16[64,2,256]{2,1,0:T(2,128)(2,1)S(1)}, u32[]{:S(2)}, u32[]{:S(2)}) collective-permute-start(bf16[64,2,256]{2,1,0:T(2,128)(2,1)} %bitcast.36), channel_id=1, source_target_pairs={{0,24},{8,16},{16,8},{24,0},{1,25},{9,17},{17,9},{25,1},{2,26},{10... | collective-permute-start | bytes 196616 | tf_op jit(solution)/shard_map/ppermute | solution.py:398
  5.7 0.6 %collective-permute-start = (bf16[64,2,256]{2,1,0:T(2,128)(2,1)}, bf16[64,2,256]{2,1,0:T(2,128)(2,1)S(1)}, u32[]{:S(2)}, u32[]{:S(2)}) collective-permute-start(bf16[64,2,256]{2,1,0:T(2,128)(2,1)} %bitcast.38), channel_id=1, source_target_pairs={{0,8},{8,0},{16,24},{24,16},{1,9},{9,1},{17,25},{25,17},{2,10},{10... | collective-permute-start | bytes 196616 | tf_op jit(solution)/shard_map/ppermute | solution.py:398
  6.4 2.6 %collective-permute-start.5 = (bf16[64,2,256]{2,1,0:T(2,128)(2,1)}, bf16[64,2,256]{2,1,0:T(2,128)(2,1)S(1)}, u32[]{:S(2)}, u32[]{:S(2)}) collective-permute-start(bf16[64,2,256]{2,1,0:T(2,128)(2,1)} %bitcast.40), channel_id=1, source_target_pairs={{0,6},{1,7},{2,4},{3,5},{4,2},{5,3},{6,0},{7,1},{8,14},{9,15},{10,... | collective-permute-start | bytes 196616 | tf_op jit(solution)/shard_map/ppermute | solution.py:407
  9.0 0.5 %collective-permute-start.4 = (bf16[64,2,256]{2,1,0:T(2,128)(2,1)}, bf16[64,2,256]{2,1,0:T(2,128)(2,1)S(1)}, u32[]{:S(2)}, u32[]{:S(2)}) collective-permute-start(bf16[64,2,256]{2,1,0:T(2,128)(2,1)} %bitcast.41), channel_id=1, source_target_pairs={{0,4},{1,5},{2,6},{3,7},{4,0},{5,1},{6,2},{7,3},{8,12},{9,13},{10,... | collective-permute-start | bytes 196616 | tf_op jit(solution)/shard_map/ppermute | solution.py:407
  9.5 0.0 collective-permute-done.2.refs_3_
  9.5 0.9 %collective-permute-start.3 = (bf16[64,2,256]{2,1,0:T(2,128)(2,1)}, bf16[64,2,256]{2,1,0:T(2,128)(2,1)S(1)}, u32[]{:S(2)}, u32[]{:S(2)}) collective-permute-start(bf16[64,2,256]{2,1,0:T(2,128)(2,1)} %bitcast.42), channel_id=1, source_target_pairs={{0,2},{1,3},{2,0},{3,1},{4,6},{5,7},{6,4},{7,5},{8,10},{9,11},{10,... | collective-permute-start | bytes 196616 | tf_op jit(solution)/shard_map/ppermute | solution.py:407
  10.4 1.4 %shard_map.95 = (bf16[2,64,256]{2,1,0:T(8,128)(2,1)S(1)}, bf16[2,64,256]{2,1,0:T(8,128)(2,1)S(1)}, f32[8,256]{1,0:T(8,128)S(1)}, bf16[256,256]{1,0:T(8,128)(2,1)...) custom-call(bf16[64,2,256]{2,1,0:T(2,128)(2,1)} %bitcast.39, ...), custom_call_target="tpu_custom_call" | custom-call | flops 2000000000 | tf_op jit(solution)/shard_map/pallas_call | solution.py:427
  11.8 0.0 collective-permute-done.1.refs_2_
  11.9 0.3 shard_map.96
  12.2 1.2 %collective-permute-done.4.refs_1_ = bf16[64,2,256]{2,1,0:T(2,128)(2,1)S(1)} collective-permute-done((bf16[64,2,256]{2,1,0:T(2,128)(2,1)}, bf16[64,2,256]{2,1,0:T(2,128)(2,1)S(1)}, u32[]{:S(2)}, u32[]{:S(2)}) %collective-permute-start.4) | collective-permute-done | bytes 65568 | tf_op jit(solution)/shard_map/ppermute | solution.py:407
  13.5 0.5 %collective-permute-done.3.refs_0_ = bf16[64,2,256]{2,1,0:T(2,128)(2,1)S(1)} collective-permute-done((bf16[64,2,256]{2,1,0:T(2,128)(2,1)}, bf16[64,2,256]{2,1,0:T(2,128)(2,1)S(1)}, u32[]{:S(2)}, u32[]{:S(2)}) %collective-permute-start.3) | collective-permute-done | bytes 65568 | tf_op jit(solution)/shard_map/ppermute | solution.py:407
  14.0 0.1 shard_map.97.even_ref
  14.1 0.1 collective-permute-start.6
  14.2 1.4 %shard_map.98 = (bf16[2,64,256]{2,1,0:T(8,128)(2,1)S(1)}, bf16[4,64,128]{2,1,0:T(8,128)(2,1)S(1)}, f32[2,512,256]{2,1,0:T(8,128)S(1)}) custom-call(f32[8,256]{1,0:T(8,128)S(1)} %get-tuple-element.42.allowed_ref, bf16[2,256,256]{2,1,0:T(8,128)(2,1)S(1)} %get-tuple-element.43.all_ref, bf16[2,64,256]{2,1,0:T(8,128)(2,1)S(1)} %get-tuple-element.40.after_ref.query_ref, ...), custom_call_target="tpu_custom_call" | custom-call | flops 2000000000 | tf_op jit(solution)/shard_map/pallas_call | solution.py:446
  15.6 0.1 collective-permute-done.6.odd_ref
  15.7 0.4 shard_map.99
  16.0 3.7 %collective-permute-start.11 = (bf16[2,16,256]{2,1,0:T(8,128)(2,1)S(1)}, bf16[2,16,256]{2,1,0:T(8,128)(2,1)S(1)}, u32[]{:S(2)}, u32[]{:S(2)}) collective-permute-start(bf16[2,16,256]{2,1,0:T(8,128)(2,1)S(1)} %get-tuple-element.52), channel_id=1, source_target_pairs={{0,24},{8,16},{16,8},{24,0},{1,25},{9,17},{17,9},{25,1},{2,26},{10... | collective-permute-start | bytes 49160 | tf_op jit(solution)/shard_map/ppermute | solution.py:398
  19.7 1.0 %collective-permute-start.9 = (bf16[64,128]{1,0:T(8,128)(2,1)S(1)}, bf16[64,128]{1,0:T(8,128)(2,1)S(1)}, u32[]{:S(2)}, u32[]{:S(2)}) collective-permute-start(bf16[64,128]{1,0:T(8,128)(2,1)S(1)} %get-tuple-element.81), channel_id=1, source_target_pairs={{0,24},{8,16},{16,8},{24,0},{1,25},{9,17},{17,9},{25,1},{2,26},{10... | collective-permute-start | bytes 49160 | tf_op jit(solution)/shard_map/ppermute | solution.py:398
  20.7 1.1 %collective-permute-start.7 = (bf16[320,128]{1,0:T(8,128)(2,1)S(1)}, bf16[320,128]{1,0:T(8,128)(2,1)S(1)}, u32[]{:S(2)}, u32[]{:S(2)}) collective-permute-start(bf16[320,128]{1,0:T(8,128)(2,1)S(1)} %get-tuple-element.84), channel_id=1, source_target_pairs={{0,8},{8,0},{16,24},{24,16},{1,9},{9,1},{17,25},{25,17},{2,10},{10... | collective-permute-start | bytes 245768 | tf_op jit(solution)/shard_map/ppermute | solution.py:398
  21.8 2.4 %collective-permute-start.8 = (bf16[320,128]{1,0:T(8,128)(2,1)S(1)}, bf16[320,128]{1,0:T(8,128)(2,1)S(1)}, u32[]{:S(2)}, u32[]{:S(2)}) collective-permute-start(bf16[320,128]{1,0:T(8,128)(2,1)S(1)} %get-tuple-element.85), channel_id=1, source_target_pairs={{0,16},{8,24},{16,0},{24,8},{1,17},{9,25},{17,1},{25,9},{2,18},{10... | collective-permute-start | bytes 245768 | tf_op jit(solution)/shard_map/ppermute | solution.py:398
  24.3 0.0 collective-permute-done.11.refs_1_
  24.3 0.0 collective-permute-done.10.refs_0_
  24.3 1.3 %shard_map.100 = (f32[2,64,256]{2,1,0:T(8,128)S(1)}, bf16[2,64,256]{2,1,0:T(8,128)(2,1)S(1)}, bf16[2,64,256]{2,1,0:T(8,128)(2,1)S(1)}) custom-call(bf16[4,2,64,256]{3,2,1,0:T(8,128)(2,1)S(1)} %shard_map.97.even_ref, bf16[4,2,64,256]{3,2,1,0:T(8,128)(2,1)S(1)} %collective-permute-done.6.odd_ref, bf16[2,16,256]{2,1,0:T(8,128)(2,1)S(1)} %collective-permute-done.10.refs_0_, ...), custom_call_target="tpu_custom_call" | custom-call | flops 2000000000 | tf_op jit(solution)/shard_map/pallas_call | solution.py:468
  25.6 1.5 %shard_map.101 = (f32[2,64,256]{2,1,0:T(8,128)S(1)}, bf16[3,256,128]{2,1,0:T(8,128)(2,1)S(1)}, bf16[4,256,128]{2,1,0:T(8,128)(2,1)S(1)}, bf16[256,128]{1,0:T(8,1...) custom-call(f32[2,512,256]{2,1,0:T(8,128)S(1)} %get-tuple-element.50.weights_, ...), custom_call_target="tpu_custom_call" | custom-call | flops 2000000000 | tf_op jit(solution)/shard_map/pallas_call | solution.py:480
  27.1 0.1 collective-permute-start.12
  27.2 0.5 %collective-permute-start.13 = (bf16[256,128]{1,0:T(8,128)(2,1)S(1)}, bf16[256,128]{1,0:T(8,128)(2,1)S(1)}, u32[]{:S(2)}, u32[]{:S(2)}) collective-permute-start(bf16[256,128]{1,0:T(8,128)(2,1)S(1)} %get-tuple-element.60), channel_id=1, source_target_pairs={{0,1},{1,0},{2,3},{3,2},{4,5},{5,4},{6,7},{7,6},{8,9},{9,8},{10,11... | collective-permute-start | bytes 196616 | tf_op jit(solution)/shard_map/ppermute | solution.py:407
  27.7 0.0 collective-permute-done.7.refs_0_
  27.7 0.1 collective-permute-start.14
  27.8 0.8 %collective-permute-done.8.refs_1_ = bf16[320,128]{1,0:T(8,128)(2,1)S(1)} collective-permute-done((bf16[320,128]{1,0:T(8,128)(2,1)S(1)}, bf16[320,128]{1,0:T(8,128)(2,1)S(1)}, u32[]{:S(2)}, u32[]{:S(2)}) %collective-permute-start.8) | collective-permute-done | bytes 81952 | tf_op jit(solution)/shard_map/ppermute | solution.py:398
  28.6 0.3 collective-permute-done.14.refs_2_
  28.9 0.1 shard_map.102
  29.0 0.2 collective-permute-start.22
  29.2 1.1 %collective-permute-start.15 = (bf16[512,128]{1,0:T(8,128)(2,1)S(1)}, bf16[512,128]{1,0:T(8,128)(2,1)S(1)}, u32[]{:S(2)}, u32[]{:S(2)}) collective-permute-start(bf16[512,128]{1,0:T(8,128)(2,1)S(1)} %get-tuple-element.62), channel_id=1, source_target_pairs={{0,2},{1,3},{2,0},{3,1},{4,6},{5,7},{6,4},{7,5},{8,10},{9,11},{10,... | collective-permute-start | bytes 393224 | tf_op jit(solution)/shard_map/ppermute | solution.py:407
  30.4 1.5 %collective-permute-start.16 = (bf16[512,128]{1,0:T(8,128)(2,1)S(1)}, bf16[512,128]{1,0:T(8,128)(2,1)S(1)}, u32[]{:S(2)}, u32[]{:S(2)}) collective-permute-start(bf16[512,128]{1,0:T(8,128)(2,1)S(1)} %get-tuple-element.63), channel_id=1, source_target_pairs={{0,4},{1,5},{2,6},{3,7},{4,0},{5,1},{6,2},{7,3},{8,12},{9,13},{10,... | collective-permute-start | bytes 393224 | tf_op jit(solution)/shard_map/ppermute | solution.py:407
  31.9 0.8 %collective-permute-start.17 = (bf16[512,128]{1,0:T(8,128)(2,1)S(1)}, bf16[512,128]{1,0:T(8,128)(2,1)S(1)}, u32[]{:S(2)}, u32[]{:S(2)}) collective-permute-start(bf16[512,128]{1,0:T(8,128)(2,1)S(1)} %get-tuple-element.64), channel_id=1, source_target_pairs={{0,6},{1,7},{2,4},{3,5},{4,2},{5,3},{6,0},{7,1},{8,14},{9,15},{10,... | collective-permute-start | bytes 393224 | tf_op jit(solution)/shard_map/ppermute | solution.py:407
  32.8 2.2 %collective-permute-start.21 = (bf16[256,128]{1,0:T(8,128)(2,1)S(1)}, bf16[256,128]{1,0:T(8,128)(2,1)S(1)}, u32[]{:S(2)}, u32[]{:S(2)}) collective-permute-start(bf16[256,128]{1,0:T(8,128)(2,1)S(1)} %get-tuple-element.72), channel_id=1, source_target_pairs={{0,24},{8,16},{16,8},{24,0},{1,25},{9,17},{17,9},{25,1},{2,26},{10... | collective-permute-start | bytes 196616 | tf_op jit(solution)/shard_map/ppermute | solution.py:398
  34.9 0.6 %collective-permute-done.15.refs_0_ = bf16[512,128]{1,0:T(8,128)(2,1)S(1)} collective-permute-done((bf16[512,128]{1,0:T(8,128)(2,1)S(1)}, bf16[512,128]{1,0:T(8,128)(2,1)S(1)}, u32[]{:S(2)}, u32[]{:S(2)}) %collective-permute-start.15) | collective-permute-done | bytes 131104 | tf_op jit(solution)/shard_map/ppermute | solution.py:407
  35.6 0.6 %collective-permute-start.20 = (bf16[256,128]{1,0:T(8,128)(2,1)S(1)}, bf16[256,128]{1,0:T(8,128)(2,1)S(1)}, u32[]{:S(2)}, u32[]{:S(2)}) collective-permute-start(bf16[256,128]{1,0:T(8,128)(2,1)S(1)} %get-tuple-element.73), channel_id=1, source_target_pairs={{0,16},{8,24},{16,0},{24,8},{1,17},{9,25},{17,1},{25,9},{2,18},{10... | collective-permute-start | bytes 196616 | tf_op jit(solution)/shard_map/ppermute | solution.py:398
  36.2 1.5 %collective-permute-done.16.refs_1_ = bf16[512,128]{1,0:T(8,128)(2,1)S(1)} collective-permute-done((bf16[512,128]{1,0:T(8,128)(2,1)S(1)}, bf16[512,128]{1,0:T(8,128)(2,1)S(1)}, u32[]{:S(2)}, u32[]{:S(2)}) %collective-permute-start.16) | collective-permute-done | bytes 131104 | tf_op jit(solution)/shard_map/ppermute | solution.py:407
  37.7 1.1 %collective-permute-start.19 = (bf16[512,128]{1,0:T(8,128)(2,1)S(1)}, bf16[512,128]{1,0:T(8,128)(2,1)S(1)}, u32[]{:S(2)}, u32[]{:S(2)}) collective-permute-start(bf16[512,128]{1,0:T(8,128)(2,1)S(1)} %pad_maximum_fusion.1), channel_id=1, source_target_pairs={{0,8},{8,0},{16,24},{24,16},{1,9},{9,1},{17,25},{25,17},{2,10},{10... | collective-permute-start | bytes 393224 | tf_op jit(solution)/shard_map/ppermute | solution.py:398
  38.8 0.1 collective-permute-start.18
  38.9 0.1 shard_map.104.own_piece
  39.1 2.2 %collective-permute-start.25 = (bf16[64,128]{1,0:T(8,128)(2,1)S(1)}, bf16[64,128]{1,0:T(8,128)(2,1)S(1)}, u32[]{:S(2)}, u32[]{:S(2)}) collective-permute-start(bf16[64,128]{1,0:T(8,128)(2,1)S(1)} %get-tuple-element.75), channel_id=1, source_target_pairs={{0,24},{8,16},{16,8},{24,0},{1,25},{9,17},{17,9},{25,1},{2,26},{10... | collective-permute-start | bytes 49160 | tf_op jit(solution)/shard_map/ppermute | solution.py:398
  41.3 0.3 collective-permute-start.24
  41.6 1.9 %collective-permute-start.23 = (bf16[64,128]{1,0:T(8,128)(2,1)S(1)}, bf16[64,128]{1,0:T(8,128)(2,1)S(1)}, u32[]{:S(2)}, u32[]{:S(2)}) collective-permute-start(bf16[64,128]{1,0:T(8,128)(2,1)S(1)} %get-tuple-element.77), channel_id=1, source_target_pairs={{0,8},{8,0},{16,24},{24,16},{1,9},{9,1},{17,25},{25,17},{2,10},{10... | collective-permute-start | bytes 49160 | tf_op jit(solution)/shard_map/ppermute | solution.py:398
  43.5 1.8 %shard_map.103 = (f32[27,32,64]{2,1,0:T(8,128)S(1)}, bf16[64,2,256]{2,1,0:T(2,128)(2,1)}) custom-call(bf16[4,256,128]{2,1,0:T(8,128)(2,1)S(1)} %pad_maximum_fusion.even_ref, bf16[4,256,128]{2,1,0:T(8,128)(2,1)S(1)} %collective-permute-done.18.odd_ref, bf16[256,128]{1,0:T(8,128)(2,1)S(1)} %get-tuple-element.49.own_ref, ...), custom_call_target="tpu_custom_call" | custom-call | flops 2000000000 | tf_op jit(solution)/shard_map/pallas_call | solution.py:518
  45.4 0.6 %collective-permute-done.24.refs_1_ = bf16[64,128]{1,0:T(8,128)(2,1)S(1)} collective-permute-done((bf16[64,128]{1,0:T(8,128)(2,1)S(1)}, bf16[64,128]{1,0:T(8,128)(2,1)S(1)}, u32[]{:S(2)}, u32[]{:S(2)}) %collective-permute-start.24) | collective-permute-done | bytes 16416 | tf_op jit(solution)/shard_map/ppermute | solution.py:398
  45.9 0.9 %shard_map.105 = f32[31,32,64]{2,1,0:T(8,128)} custom-call(bf16[4,64,128]{2,1,0:T(8,128)(2,1)S(1)} %shard_map.104.own_piece, f32[27,32,64]{2,1,0:T(8,128)S(1)} %get-tuple-element.69.taps_ref, bf16[64,128]{1,0:T(8,128)(2,1)S(1)} %collective-permute-done.23.refs_0_, bf16[64,128]{1,0:T(8,128)(2,1)S(1)} %collective-permute-done.24.refs_1_, ...), custom_call_target="tpu_custom_call" | custom-call | flops 2000000000 | tf_op jit(solution)/shard_map/pallas_call | solution.py:528
  (30 shorter events, 0.2 us)
Async XLA Ops:
  0.6 8.9 %collective-permute-start.2 = (bf16[64,2,256]{2,1,0:T(2,128)(2,1)}, bf16[64,2,256]{2,1,0:T(2,128)(2,1)S(1)}, u32[]{:S(2)}, u32[]{:S(2)}) collective-permute-start(bf16[64,2,256]{2,1,0:T(2,128)(2,1)} %bitcast.36), channel_id=1, source_target_pairs={{0,24},{8,16},{16,8},{24,0},{1,25},{9,17},{17,9},{25,1},{2,26},{10... | collective-permute-start | bytes 196616 | tf_op jit(solution)/shard_map/ppermute | solution.py:398
  5.7 6.1 %collective-permute-start.1 = (bf16[64,2,256]{2,1,0:T(2,128)(2,1)}, bf16[64,2,256]{2,1,0:T(2,128)(2,1)S(1)}, u32[]{:S(2)}, u32[]{:S(2)}) collective-permute-start(bf16[64,2,256]{2,1,0:T(2,128)(2,1)} %bitcast.37), channel_id=1, source_target_pairs={{0,16},{8,24},{16,0},{24,8},{1,17},{9,25},{17,1},{25,9},{2,18},{10... | collective-permute-start | bytes 196616 | tf_op jit(solution)/shard_map/ppermute | solution.py:398
  5.7 6.1 %collective-permute-start = (bf16[64,2,256]{2,1,0:T(2,128)(2,1)}, bf16[64,2,256]{2,1,0:T(2,128)(2,1)S(1)}, u32[]{:S(2)}, u32[]{:S(2)}) collective-permute-start(bf16[64,2,256]{2,1,0:T(2,128)(2,1)} %bitcast.38), channel_id=1, source_target_pairs={{0,8},{8,0},{16,24},{24,16},{1,9},{9,1},{17,25},{25,17},{2,10},{10... | collective-permute-start | bytes 196616 | tf_op jit(solution)/shard_map/ppermute | solution.py:398
  6.4 5.8 %collective-permute-start.5 = (bf16[64,2,256]{2,1,0:T(2,128)(2,1)}, bf16[64,2,256]{2,1,0:T(2,128)(2,1)S(1)}, u32[]{:S(2)}, u32[]{:S(2)}) collective-permute-start(bf16[64,2,256]{2,1,0:T(2,128)(2,1)} %bitcast.40), channel_id=1, source_target_pairs={{0,6},{1,7},{2,4},{3,5},{4,2},{5,3},{6,0},{7,1},{8,14},{9,15},{10,... | collective-permute-start | bytes 196616 | tf_op jit(solution)/shard_map/ppermute | solution.py:407
  9.0 4.5 %collective-permute-start.4 = (bf16[64,2,256]{2,1,0:T(2,128)(2,1)}, bf16[64,2,256]{2,1,0:T(2,128)(2,1)S(1)}, u32[]{:S(2)}, u32[]{:S(2)}) collective-permute-start(bf16[64,2,256]{2,1,0:T(2,128)(2,1)} %bitcast.41), channel_id=1, source_target_pairs={{0,4},{1,5},{2,6},{3,7},{4,0},{5,1},{6,2},{7,3},{8,12},{9,13},{10,... | collective-permute-start | bytes 196616 | tf_op jit(solution)/shard_map/ppermute | solution.py:407
  9.5 4.5 %collective-permute-start.3 = (bf16[64,2,256]{2,1,0:T(2,128)(2,1)}, bf16[64,2,256]{2,1,0:T(2,128)(2,1)S(1)}, u32[]{:S(2)}, u32[]{:S(2)}) collective-permute-start(bf16[64,2,256]{2,1,0:T(2,128)(2,1)} %bitcast.42), channel_id=1, source_target_pairs={{0,2},{1,3},{2,0},{3,1},{4,6},{5,7},{6,4},{7,5},{8,10},{9,11},{10,... | collective-permute-start | bytes 196616 | tf_op jit(solution)/shard_map/ppermute | solution.py:407
  14.1 1.6 %collective-permute-start.6 = (bf16[4,2,64,256]{3,2,1,0:T(8,128)(2,1)S(1)}, bf16[4,2,64,256]{3,2,1,0:T(8,128)(2,1)S(1)}, u32[]{:S(2)}, u32[]{:S(2)}) collective-permute-start(bf16[4,2,64,256]{3,2,1,0:T(8,128)(2,1)S(1)} %shard_map.97.even_ref), channel_id=1, source_target_pairs={{0,1},{1,0},{2,3},{3,2},{4,5},{5,4},{6,7},{7,6},{8,9},{9,8},{10,11... | collective-permute-start | bytes 786440 | tf_op jit(solution)/shard_map/ppermute | solution.py:407
  15.7 8.6 %copy-start = (bf16[256,27,256]{2,0,1:T(8,128)(2,1)S(1)}, bf16[256,27,256]{2,0,1:T(8,128)(2,1)}, u32[]{:S(2)}) copy-start(bf16[256,27,256]{2,0,1:T(8,128)(2,1)} %param.14) | copy-start | bytes 10616836
  16.0 8.2 %collective-permute-start.11 = (bf16[2,16,256]{2,1,0:T(8,128)(2,1)S(1)}, bf16[2,16,256]{2,1,0:T(8,128)(2,1)S(1)}, u32[]{:S(2)}, u32[]{:S(2)}) collective-permute-start(bf16[2,16,256]{2,1,0:T(8,128)(2,1)S(1)} %get-tuple-element.52), channel_id=1, source_target_pairs={{0,24},{8,16},{16,8},{24,0},{1,25},{9,17},{17,9},{25,1},{2,26},{10... | collective-permute-start | bytes 49160 | tf_op jit(solution)/shard_map/ppermute | solution.py:398
  19.7 4.6 %collective-permute-start.10 = (bf16[2,16,256]{2,1,0:T(8,128)(2,1)S(1)}, bf16[2,16,256]{2,1,0:T(8,128)(2,1)S(1)}, u32[]{:S(2)}, u32[]{:S(2)}) collective-permute-start(bf16[2,16,256]{2,1,0:T(8,128)(2,1)S(1)} %get-tuple-element.52), channel_id=1, source_target_pairs={{0,8},{8,0},{16,24},{24,16},{1,9},{9,1},{17,25},{25,17},{2,10},{10... | collective-permute-start | bytes 49160 | tf_op jit(solution)/shard_map/ppermute | solution.py:398
  19.7 8.9 %collective-permute-start.9 = (bf16[64,128]{1,0:T(8,128)(2,1)S(1)}, bf16[64,128]{1,0:T(8,128)(2,1)S(1)}, u32[]{:S(2)}, u32[]{:S(2)}) collective-permute-start(bf16[64,128]{1,0:T(8,128)(2,1)S(1)} %get-tuple-element.81), channel_id=1, source_target_pairs={{0,24},{8,16},{16,8},{24,0},{1,25},{9,17},{17,9},{25,1},{2,26},{10... | collective-permute-start | bytes 49160 | tf_op jit(solution)/shard_map/ppermute | solution.py:398
  20.7 7.0 %collective-permute-start.7 = (bf16[320,128]{1,0:T(8,128)(2,1)S(1)}, bf16[320,128]{1,0:T(8,128)(2,1)S(1)}, u32[]{:S(2)}, u32[]{:S(2)}) collective-permute-start(bf16[320,128]{1,0:T(8,128)(2,1)S(1)} %get-tuple-element.84), channel_id=1, source_target_pairs={{0,8},{8,0},{16,24},{24,16},{1,9},{9,1},{17,25},{25,17},{2,10},{10... | collective-permute-start | bytes 245768 | tf_op jit(solution)/shard_map/ppermute | solution.py:398
  21.8 6.8 %collective-permute-start.8 = (bf16[320,128]{1,0:T(8,128)(2,1)S(1)}, bf16[320,128]{1,0:T(8,128)(2,1)S(1)}, u32[]{:S(2)}, u32[]{:S(2)}) collective-permute-start(bf16[320,128]{1,0:T(8,128)(2,1)S(1)} %get-tuple-element.85), channel_id=1, source_target_pairs={{0,16},{8,24},{16,0},{24,8},{1,17},{9,25},{17,1},{25,9},{2,18},{10... | collective-permute-start | bytes 245768 | tf_op jit(solution)/shard_map/ppermute | solution.py:398
  27.1 1.5 %collective-permute-start.12 = (bf16[256,128]{1,0:T(8,128)(2,1)S(1)}, bf16[256,128]{1,0:T(8,128)(2,1)S(1)}, u32[]{:S(2)}, u32[]{:S(2)}) collective-permute-start(bf16[256,128]{1,0:T(8,128)(2,1)S(1)} %get-tuple-element.59), channel_id=1, source_target_pairs={{0,1},{1,0},{2,3},{3,2},{4,5},{5,4},{6,7},{7,6},{8,9},{9,8},{10,11... | collective-permute-start | bytes 196616 | tf_op jit(solution)/shard_map/ppermute | solution.py:407
  27.2 1.4 %collective-permute-start.13 = (bf16[256,128]{1,0:T(8,128)(2,1)S(1)}, bf16[256,128]{1,0:T(8,128)(2,1)S(1)}, u32[]{:S(2)}, u32[]{:S(2)}) collective-permute-start(bf16[256,128]{1,0:T(8,128)(2,1)S(1)} %get-tuple-element.60), channel_id=1, source_target_pairs={{0,1},{1,0},{2,3},{3,2},{4,5},{5,4},{6,7},{7,6},{8,9},{9,8},{10,11... | collective-permute-start | bytes 196616 | tf_op jit(solution)/shard_map/ppermute | solution.py:407
  27.7 1.3 %collective-permute-start.14 = (bf16[256,128]{1,0:T(8,128)(2,1)S(1)}, bf16[256,128]{1,0:T(8,128)(2,1)S(1)}, u32[]{:S(2)}, u32[]{:S(2)}) collective-permute-start(bf16[256,128]{1,0:T(8,128)(2,1)S(1)} %get-tuple-element.61), channel_id=1, source_target_pairs={{0,1},{1,0},{2,3},{3,2},{4,5},{5,4},{6,7},{7,6},{8,9},{9,8},{10,11... | collective-permute-start | bytes 196616 | tf_op jit(solution)/shard_map/ppermute | solution.py:407
  29.0 9.9 %collective-permute-start.22 = (bf16[256,128]{1,0:T(8,128)(2,1)S(1)}, bf16[256,128]{1,0:T(8,128)(2,1)S(1)}, u32[]{:S(2)}, u32[]{:S(2)}) collective-permute-start(bf16[256,128]{1,0:T(8,128)(2,1)S(1)} %get-tuple-element.68), channel_id=1, source_target_pairs={{0,1},{1,0},{2,3},{3,2},{4,5},{5,4},{6,7},{7,6},{8,9},{9,8},{10,11... | collective-permute-start | bytes 196616 | tf_op jit(solution)/shard_map/ppermute | solution.py:407
  29.2 6.3 %collective-permute-start.15 = (bf16[512,128]{1,0:T(8,128)(2,1)S(1)}, bf16[512,128]{1,0:T(8,128)(2,1)S(1)}, u32[]{:S(2)}, u32[]{:S(2)}) collective-permute-start(bf16[512,128]{1,0:T(8,128)(2,1)S(1)} %get-tuple-element.62), channel_id=1, source_target_pairs={{0,2},{1,3},{2,0},{3,1},{4,6},{5,7},{6,4},{7,5},{8,10},{9,11},{10,... | collective-permute-start | bytes 393224 | tf_op jit(solution)/shard_map/ppermute | solution.py:407
  30.4 7.3 %collective-permute-start.16 = (bf16[512,128]{1,0:T(8,128)(2,1)S(1)}, bf16[512,128]{1,0:T(8,128)(2,1)S(1)}, u32[]{:S(2)}, u32[]{:S(2)}) collective-permute-start(bf16[512,128]{1,0:T(8,128)(2,1)S(1)} %get-tuple-element.63), channel_id=1, source_target_pairs={{0,4},{1,5},{2,6},{3,7},{4,0},{5,1},{6,2},{7,3},{8,12},{9,13},{10,... | collective-permute-start | bytes 393224 | tf_op jit(solution)/shard_map/ppermute | solution.py:407
  31.9 6.9 %collective-permute-start.17 = (bf16[512,128]{1,0:T(8,128)(2,1)S(1)}, bf16[512,128]{1,0:T(8,128)(2,1)S(1)}, u32[]{:S(2)}, u32[]{:S(2)}) collective-permute-start(bf16[512,128]{1,0:T(8,128)(2,1)S(1)} %get-tuple-element.64), channel_id=1, source_target_pairs={{0,6},{1,7},{2,4},{3,5},{4,2},{5,3},{6,0},{7,1},{8,14},{9,15},{10,... | collective-permute-start | bytes 393224 | tf_op jit(solution)/shard_map/ppermute | solution.py:407
  32.8 8.5 %collective-permute-start.21 = (bf16[256,128]{1,0:T(8,128)(2,1)S(1)}, bf16[256,128]{1,0:T(8,128)(2,1)S(1)}, u32[]{:S(2)}, u32[]{:S(2)}) collective-permute-start(bf16[256,128]{1,0:T(8,128)(2,1)S(1)} %get-tuple-element.72), channel_id=1, source_target_pairs={{0,24},{8,16},{16,8},{24,0},{1,25},{9,17},{17,9},{25,1},{2,26},{10... | collective-permute-start | bytes 196616 | tf_op jit(solution)/shard_map/ppermute | solution.py:398
  35.6 6.1 %collective-permute-start.20 = (bf16[256,128]{1,0:T(8,128)(2,1)S(1)}, bf16[256,128]{1,0:T(8,128)(2,1)S(1)}, u32[]{:S(2)}, u32[]{:S(2)}) collective-permute-start(bf16[256,128]{1,0:T(8,128)(2,1)S(1)} %get-tuple-element.73), channel_id=1, source_target_pairs={{0,16},{8,24},{16,0},{24,8},{1,17},{9,25},{17,1},{25,9},{2,18},{10... | collective-permute-start | bytes 196616 | tf_op jit(solution)/shard_map/ppermute | solution.py:398
  37.7 5.8 %collective-permute-start.19 = (bf16[512,128]{1,0:T(8,128)(2,1)S(1)}, bf16[512,128]{1,0:T(8,128)(2,1)S(1)}, u32[]{:S(2)}, u32[]{:S(2)}) collective-permute-start(bf16[512,128]{1,0:T(8,128)(2,1)S(1)} %pad_maximum_fusion.1), channel_id=1, source_target_pairs={{0,8},{8,0},{16,24},{24,16},{1,9},{9,1},{17,25},{25,17},{2,10},{10... | collective-permute-start | bytes 393224 | tf_op jit(solution)/shard_map/ppermute | solution.py:398
  38.8 4.7 %collective-permute-start.18 = (bf16[4,256,128]{2,1,0:T(8,128)(2,1)S(1)}, bf16[4,256,128]{2,1,0:T(8,128)(2,1)S(1)}, u32[]{:S(2)}, u32[]{:S(2)}) collective-permute-start(bf16[4,256,128]{2,1,0:T(8,128)(2,1)S(1)} %pad_maximum_fusion.even_ref), channel_id=1, source_target_pairs={{0,1},{1,0},{2,3},{3,2},{4,5},{5,4},{6,7},{7,6},{8,9},{9,8},{10,11... | collective-permute-start | bytes 786440 | tf_op jit(solution)/shard_map/ppermute | solution.py:407
  39.1 6.3 %collective-permute-start.25 = (bf16[64,128]{1,0:T(8,128)(2,1)S(1)}, bf16[64,128]{1,0:T(8,128)(2,1)S(1)}, u32[]{:S(2)}, u32[]{:S(2)}) collective-permute-start(bf16[64,128]{1,0:T(8,128)(2,1)S(1)} %get-tuple-element.75), channel_id=1, source_target_pairs={{0,24},{8,16},{16,8},{24,0},{1,25},{9,17},{17,9},{25,1},{2,26},{10... | collective-permute-start | bytes 49160 | tf_op jit(solution)/shard_map/ppermute | solution.py:398
  41.3 4.6 %collective-permute-start.24 = (bf16[64,128]{1,0:T(8,128)(2,1)S(1)}, bf16[64,128]{1,0:T(8,128)(2,1)S(1)}, u32[]{:S(2)}, u32[]{:S(2)}) collective-permute-start(bf16[64,128]{1,0:T(8,128)(2,1)S(1)} %get-tuple-element.76), channel_id=1, source_target_pairs={{0,16},{8,24},{16,0},{24,8},{1,17},{9,25},{17,1},{25,9},{2,18},{10... | collective-permute-start | bytes 49160 | tf_op jit(solution)/shard_map/ppermute | solution.py:398
  41.6 4.3 %collective-permute-start.23 = (bf16[64,128]{1,0:T(8,128)(2,1)S(1)}, bf16[64,128]{1,0:T(8,128)(2,1)S(1)}, u32[]{:S(2)}, u32[]{:S(2)}) collective-permute-start(bf16[64,128]{1,0:T(8,128)(2,1)S(1)} %get-tuple-element.77), channel_id=1, source_target_pairs={{0,8},{8,0},{16,24},{24,16},{1,9},{9,1},{17,25},{25,17},{2,10},{10... | collective-permute-start | bytes 49160 | tf_op jit(solution)/shard_map/ppermute | solution.py:398

commit v8 on v7

--- a/solution.py
+++ b/solution.py
@@ -439,15 +439,16 @@
         micros=0.01,
     )(own_features, *come_features, w_query, w_key, w_value)
 
-    even = call(stack_kernel, [((4,) + block, BF)], [VMEM] * 5)(queries, own_cot, *come_cot)[0]
-    odd = swap(even, 1)
-
     pieces_shape = (count, cols, max(LANES, beams * lanes))
     attended, pieces, weights = call(
         functools.partial(attention_kernel, count),
         [(block, BF), (pieces_shape, BF), ((beams, HEADS * cols, count * cols), F32)],
         [VMEM] * 6,
+        micros=0.01,
     )(allowed, every, queries, keys, values, w_out)
+
+    even = call(stack_kernel, [((4,) + block, BF)], [VMEM] * 5)(attended, own_cot, *come_cot)[0]
+    odd = swap(even, 1)
 
     spread = (4 * cols, 4 * width)
     edge = (8 * beams, channels)

time: 46.9 us -> 46.8 us (level)
  no operation moved by 1% of the time
where the time goes in v8:
time: 46.8 us; the launch traced here: 46.7 us
  starting transfers between devices  30.7 us (66%)
  Pallas kernels  9.36 us (20%)
  waiting for transfers between devices  5.65 us (12%)
  between operations  0.83 us (2%)
    ppermute x14, starting transfers between devices, swap_columns(): lax.ppermute(value, 'azim', [(i, i ^ distance) for i in range(count)])  22.3 us
    ppermute x12, starting transfers between devices, swap(): return lax.ppermute(value, GROUP, [(i, i ^ bits) for i in range(8)])  8.5 us
    ppermute x12, waiting for transfers between devices, swap(): return lax.ppermute(value, GROUP, [(i, i ^ bits) for i in range(8)])  4.43 us
    pallas_call x1, Pallas kernels, per_device(): call(functools.partial(taps_kernel, count), [((TAPS, width, lanes), F32),...  1.84 us
    pallas_call x1, Pallas kernels, per_device(): call(functools.partial(backward_kernel, count), [(block, F32), ((count -...  1.48 us
    pallas_call x1, Pallas kernels, per_device(): call(functools.partial(load_kernel, count), [(block, BF), (block, BF), ((...  1.43 us
    pallas_call x1, Pallas kernels, per_device(): call(functools.partial(attention_kernel, count), [(block, BF), (pieces_sh...  1.4 us
    pallas_call x1, Pallas kernels, per_device(): call(functools.partial(conv_kernel, count), [(block, F32), (block, BF), (...  1.34 us
  transfers between devices with their start and end apart: 26, of which 8 were waited for; matrix products, arithmetic and copies ran while one was open for 0% of the time, Pallas kernels for 17%

profile of v8, /device:TPU:0, one launch (start us, length us, event | category | flops | bytes accessed | tf_op | source)
XLA Modules:
  0.0 46.7 jit_solution(4384880570682874922)
XLA Ops:
  0.6 5.1 %collective-permute-start.2 = (bf16[64,2,256]{2,1,0:T(2,128)(2,1)}, bf16[64,2,256]{2,1,0:T(2,128)(2,1)S(1)}, u32[]{:S(2)}, u32[]{:S(2)}) collective-permute-start(bf16[64,2,256]{2,1,0:T(2,128)(2,1)} %bitcast.36), channel_id=1, source_target_pairs={{0,24},{8,16},{16,8},{24,0},{1,25},{9,17},{17,9},{25,1},{2,26},{10... | collective-permute-start | bytes 196616 | tf_op jit(solution)/shard_map/ppermute | solution.py:398
  5.7 0.6 %collective-permute-start = (bf16[64,2,256]{2,1,0:T(2,128)(2,1)}, bf16[64,2,256]{2,1,0:T(2,128)(2,1)S(1)}, u32[]{:S(2)}, u32[]{:S(2)}) collective-permute-start(bf16[64,2,256]{2,1,0:T(2,128)(2,1)} %bitcast.38), channel_id=1, source_target_pairs={{0,8},{8,0},{16,24},{24,16},{1,9},{9,1},{17,25},{25,17},{2,10},{10... | collective-permute-start | bytes 196616 | tf_op jit(solution)/shard_map/ppermute | solution.py:398
  6.4 2.6 %collective-permute-start.5 = (bf16[64,2,256]{2,1,0:T(2,128)(2,1)}, bf16[64,2,256]{2,1,0:T(2,128)(2,1)S(1)}, u32[]{:S(2)}, u32[]{:S(2)}) collective-permute-start(bf16[64,2,256]{2,1,0:T(2,128)(2,1)} %bitcast.40), channel_id=1, source_target_pairs={{0,6},{1,7},{2,4},{3,5},{4,2},{5,3},{6,0},{7,1},{8,14},{9,15},{10,... | collective-permute-start | bytes 196616 | tf_op jit(solution)/shard_map/ppermute | solution.py:407
  9.0 0.5 %collective-permute-start.4 = (bf16[64,2,256]{2,1,0:T(2,128)(2,1)}, bf16[64,2,256]{2,1,0:T(2,128)(2,1)S(1)}, u32[]{:S(2)}, u32[]{:S(2)}) collective-permute-start(bf16[64,2,256]{2,1,0:T(2,128)(2,1)} %bitcast.41), channel_id=1, source_target_pairs={{0,4},{1,5},{2,6},{3,7},{4,0},{5,1},{6,2},{7,3},{8,12},{9,13},{10,... | collective-permute-start | bytes 196616 | tf_op jit(solution)/shard_map/ppermute | solution.py:407
  9.5 0.0 collective-permute-done.2.refs_3_
  9.5 0.9 %collective-permute-start.3 = (bf16[64,2,256]{2,1,0:T(2,128)(2,1)}, bf16[64,2,256]{2,1,0:T(2,128)(2,1)S(1)}, u32[]{:S(2)}, u32[]{:S(2)}) collective-permute-start(bf16[64,2,256]{2,1,0:T(2,128)(2,1)} %bitcast.42), channel_id=1, source_target_pairs={{0,2},{1,3},{2,0},{3,1},{4,6},{5,7},{6,4},{7,5},{8,10},{9,11},{10,... | collective-permute-start | bytes 196616 | tf_op jit(solution)/shard_map/ppermute | solution.py:407
  10.4 1.4 %shard_map.95 = (bf16[2,64,256]{2,1,0:T(8,128)(2,1)S(1)}, bf16[2,64,256]{2,1,0:T(8,128)(2,1)S(1)}, f32[8,256]{1,0:T(8,128)S(1)}, bf16[256,256]{1,0:T(8,128)(2,1)...) custom-call(bf16[64,2,256]{2,1,0:T(2,128)(2,1)} %bitcast.39, ...), custom_call_target="tpu_custom_call" | custom-call | flops 2000000000 | tf_op jit(solution)/shard_map/pallas_call | solution.py:427
  11.8 0.0 collective-permute-done.1.refs_2_
  11.9 0.3 shard_map.96
  12.2 1.4 %shard_map.97 = (bf16[2,64,256]{2,1,0:T(8,128)(2,1)S(1)}, bf16[4,64,128]{2,1,0:T(8,128)(2,1)S(1)}, f32[2,512,256]{2,1,0:T(8,128)S(1)}) custom-call(f32[8,256]{1,0:T(8,128)S(1)} %get-tuple-element.36.allowed_ref, bf16[2,256,256]{2,1,0:T(8,128)(2,1)S(1)} %get-tuple-element.41.all_ref, bf16[2,64,256]{2,1,0:T(8,128)(2,1)S(1)} %get-tuple-element.42.query_ref, ...), custom_call_target="tpu_custom_call" | custom-call | flops 10000000 | tf_op jit(solution)/shard_map/pallas_call | solution.py:443
  13.6 0.0 collective-permute-done.5.refs_2_
  13.6 0.0 collective-permute-done.4.refs_1_
  13.6 0.3 collective-permute-done.3.refs_0_
  14.0 0.1 shard_map.98.even_ref
  14.1 0.1 collective-permute-start.6
  14.2 1.5 %collective-permute-done.6.odd_ref = bf16[4,2,64,256]{3,2,1,0:T(8,128)(2,1)S(1)} collective-permute-done((bf16[4,2,64,256]{3,2,1,0:T(8,128)(2,1)S(1)}, bf16[4,2,64,256]{3,2,1,0:T(8,128)(2,1)S(1)}, u32[]{:S(2)}, u32[]{:S(2)}) %collective-permute-start.6) | collective-permute-done | bytes 262176 | tf_op jit(solution)/shard_map/ppermute | solution.py:407
  15.7 0.4 shard_map.99
  16.0 3.7 %collective-permute-start.11 = (bf16[2,16,256]{2,1,0:T(8,128)(2,1)S(1)}, bf16[2,16,256]{2,1,0:T(8,128)(2,1)S(1)}, u32[]{:S(2)}, u32[]{:S(2)}) collective-permute-start(bf16[2,16,256]{2,1,0:T(8,128)(2,1)S(1)} %get-tuple-element.52), channel_id=1, source_target_pairs={{0,24},{8,16},{16,8},{24,0},{1,25},{9,17},{17,9},{25,1},{2,26},{10... | collective-permute-start | bytes 49160 | tf_op jit(solution)/shard_map/ppermute | solution.py:398
  19.7 1.0 %collective-permute-start.9 = (bf16[64,128]{1,0:T(8,128)(2,1)S(1)}, bf16[64,128]{1,0:T(8,128)(2,1)S(1)}, u32[]{:S(2)}, u32[]{:S(2)}) collective-permute-start(bf16[64,128]{1,0:T(8,128)(2,1)S(1)} %get-tuple-element.81), channel_id=1, source_target_pairs={{0,24},{8,16},{16,8},{24,0},{1,25},{9,17},{17,9},{25,1},{2,26},{10... | collective-permute-start | bytes 49160 | tf_op jit(solution)/shard_map/ppermute | solution.py:398
  20.8 1.1 %collective-permute-start.7 = (bf16[320,128]{1,0:T(8,128)(2,1)S(1)}, bf16[320,128]{1,0:T(8,128)(2,1)S(1)}, u32[]{:S(2)}, u32[]{:S(2)}) collective-permute-start(bf16[320,128]{1,0:T(8,128)(2,1)S(1)} %get-tuple-element.84), channel_id=1, source_target_pairs={{0,8},{8,0},{16,24},{24,16},{1,9},{9,1},{17,25},{25,17},{2,10},{10... | collective-permute-start | bytes 245768 | tf_op jit(solution)/shard_map/ppermute | solution.py:398
  21.8 2.4 %collective-permute-start.8 = (bf16[320,128]{1,0:T(8,128)(2,1)S(1)}, bf16[320,128]{1,0:T(8,128)(2,1)S(1)}, u32[]{:S(2)}, u32[]{:S(2)}) collective-permute-start(bf16[320,128]{1,0:T(8,128)(2,1)S(1)} %get-tuple-element.85), channel_id=1, source_target_pairs={{0,16},{8,24},{16,0},{24,8},{1,17},{9,25},{17,1},{25,9},{2,18},{10... | collective-permute-start | bytes 245768 | tf_op jit(solution)/shard_map/ppermute | solution.py:398
  24.3 0.0 collective-permute-done.11.refs_1_
  24.3 1.3 %shard_map.100 = (f32[2,64,256]{2,1,0:T(8,128)S(1)}, bf16[2,64,256]{2,1,0:T(8,128)(2,1)S(1)}, bf16[2,64,256]{2,1,0:T(8,128)(2,1)S(1)}) custom-call(bf16[4,2,64,256]{3,2,1,0:T(8,128)(2,1)S(1)} %shard_map.98.even_ref, bf16[4,2,64,256]{3,2,1,0:T(8,128)(2,1)S(1)} %collective-permute-done.6.odd_ref, bf16[2,16,256]{2,1,0:T(8,128)(2,1)S(1)} %collective-permute-done.10.refs_0_, ...), custom_call_target="tpu_custom_call" | custom-call | flops 2000000000 | tf_op jit(solution)/shard_map/pallas_call | solution.py:469
  25.6 1.5 %shard_map.101 = (f32[2,64,256]{2,1,0:T(8,128)S(1)}, bf16[3,256,128]{2,1,0:T(8,128)(2,1)S(1)}, bf16[4,256,128]{2,1,0:T(8,128)(2,1)S(1)}, bf16[256,128]{1,0:T(8,1...) custom-call(f32[2,512,256]{2,1,0:T(8,128)S(1)} %get-tuple-element.51.weights_, ...), custom_call_target="tpu_custom_call" | custom-call | flops 2000000000 | tf_op jit(solution)/shard_map/pallas_call | solution.py:481
  27.1 0.1 collective-permute-start.12
  27.2 0.5 %collective-permute-start.13 = (bf16[256,128]{1,0:T(8,128)(2,1)S(1)}, bf16[256,128]{1,0:T(8,128)(2,1)S(1)}, u32[]{:S(2)}, u32[]{:S(2)}) collective-permute-start(bf16[256,128]{1,0:T(8,128)(2,1)S(1)} %get-tuple-element.60), channel_id=1, source_target_pairs={{0,1},{1,0},{2,3},{3,2},{4,5},{5,4},{6,7},{7,6},{8,9},{9,8},{10,11... | collective-permute-start | bytes 196616 | tf_op jit(solution)/shard_map/ppermute | solution.py:407
  27.7 0.1 collective-permute-start.14
  27.8 0.7 %collective-permute-done.8.refs_1_ = bf16[320,128]{1,0:T(8,128)(2,1)S(1)} collective-permute-done((bf16[320,128]{1,0:T(8,128)(2,1)S(1)}, bf16[320,128]{1,0:T(8,128)(2,1)S(1)}, u32[]{:S(2)}, u32[]{:S(2)}) %collective-permute-start.8) | collective-permute-done | bytes 81952 | tf_op jit(solution)/shard_map/ppermute | solution.py:398
  28.5 0.1 collective-permute-done.13.refs_1_
  28.6 0.4 collective-permute-done.14.refs_2_
  28.9 0.1 shard_map.102
  29.0 0.2 collective-permute-start.22
  29.2 1.1 %collective-permute-start.15 = (bf16[512,128]{1,0:T(8,128)(2,1)S(1)}, bf16[512,128]{1,0:T(8,128)(2,1)S(1)}, u32[]{:S(2)}, u32[]{:S(2)}) collective-permute-start(bf16[512,128]{1,0:T(8,128)(2,1)S(1)} %get-tuple-element.62), channel_id=1, source_target_pairs={{0,2},{1,3},{2,0},{3,1},{4,6},{5,7},{6,4},{7,5},{8,10},{9,11},{10,... | collective-permute-start | bytes 393224 | tf_op jit(solution)/shard_map/ppermute | solution.py:407
  30.4 1.5 %collective-permute-start.16 = (bf16[512,128]{1,0:T(8,128)(2,1)S(1)}, bf16[512,128]{1,0:T(8,128)(2,1)S(1)}, u32[]{:S(2)}, u32[]{:S(2)}) collective-permute-start(bf16[512,128]{1,0:T(8,128)(2,1)S(1)} %get-tuple-element.63), channel_id=1, source_target_pairs={{0,4},{1,5},{2,6},{3,7},{4,0},{5,1},{6,2},{7,3},{8,12},{9,13},{10,... | collective-permute-start | bytes 393224 | tf_op jit(solution)/shard_map/ppermute | solution.py:407
  31.9 0.8 %collective-permute-start.17 = (bf16[512,128]{1,0:T(8,128)(2,1)S(1)}, bf16[512,128]{1,0:T(8,128)(2,1)S(1)}, u32[]{:S(2)}, u32[]{:S(2)}) collective-permute-start(bf16[512,128]{1,0:T(8,128)(2,1)S(1)} %get-tuple-element.64), channel_id=1, source_target_pairs={{0,6},{1,7},{2,4},{3,5},{4,2},{5,3},{6,0},{7,1},{8,14},{9,15},{10,... | collective-permute-start | bytes 393224 | tf_op jit(solution)/shard_map/ppermute | solution.py:407
  32.7 2.1 %collective-permute-start.21 = (bf16[256,128]{1,0:T(8,128)(2,1)S(1)}, bf16[256,128]{1,0:T(8,128)(2,1)S(1)}, u32[]{:S(2)}, u32[]{:S(2)}) collective-permute-start(bf16[256,128]{1,0:T(8,128)(2,1)S(1)} %get-tuple-element.72), channel_id=1, source_target_pairs={{0,24},{8,16},{16,8},{24,0},{1,25},{9,17},{17,9},{25,1},{2,26},{10... | collective-permute-start | bytes 196616 | tf_op jit(solution)/shard_map/ppermute | solution.py:398
  34.8 0.7 %collective-permute-done.15.refs_0_ = bf16[512,128]{1,0:T(8,128)(2,1)S(1)} collective-permute-done((bf16[512,128]{1,0:T(8,128)(2,1)S(1)}, bf16[512,128]{1,0:T(8,128)(2,1)S(1)}, u32[]{:S(2)}, u32[]{:S(2)}) %collective-permute-start.15) | collective-permute-done | bytes 131104 | tf_op jit(solution)/shard_map/ppermute | solution.py:407
  35.6 0.7 %collective-permute-start.20 = (bf16[256,128]{1,0:T(8,128)(2,1)S(1)}, bf16[256,128]{1,0:T(8,128)(2,1)S(1)}, u32[]{:S(2)}, u32[]{:S(2)}) collective-permute-start(bf16[256,128]{1,0:T(8,128)(2,1)S(1)} %get-tuple-element.73), channel_id=1, source_target_pairs={{0,16},{8,24},{16,0},{24,8},{1,17},{9,25},{17,1},{25,9},{2,18},{10... | collective-permute-start | bytes 196616 | tf_op jit(solution)/shard_map/ppermute | solution.py:398
  36.3 1.4 %collective-permute-done.16.refs_1_ = bf16[512,128]{1,0:T(8,128)(2,1)S(1)} collective-permute-done((bf16[512,128]{1,0:T(8,128)(2,1)S(1)}, bf16[512,128]{1,0:T(8,128)(2,1)S(1)}, u32[]{:S(2)}, u32[]{:S(2)}) %collective-permute-start.16) | collective-permute-done | bytes 131104 | tf_op jit(solution)/shard_map/ppermute | solution.py:407
  37.7 1.1 %collective-permute-start.19 = (bf16[512,128]{1,0:T(8,128)(2,1)S(1)}, bf16[512,128]{1,0:T(8,128)(2,1)S(1)}, u32[]{:S(2)}, u32[]{:S(2)}) collective-permute-start(bf16[512,128]{1,0:T(8,128)(2,1)S(1)} %pad_maximum_fusion.1), channel_id=1, source_target_pairs={{0,8},{8,0},{16,24},{24,16},{1,9},{9,1},{17,25},{25,17},{2,10},{10... | collective-permute-start | bytes 393224 | tf_op jit(solution)/shard_map/ppermute | solution.py:398
  38.8 0.1 collective-permute-start.18
  38.9 0.1 shard_map.104.own_piece
  39.0 2.1 %collective-permute-start.25 = (bf16[64,128]{1,0:T(8,128)(2,1)S(1)}, bf16[64,128]{1,0:T(8,128)(2,1)S(1)}, u32[]{:S(2)}, u32[]{:S(2)}) collective-permute-start(bf16[64,128]{1,0:T(8,128)(2,1)S(1)} %get-tuple-element.75), channel_id=1, source_target_pairs={{0,24},{8,16},{16,8},{24,0},{1,25},{9,17},{17,9},{25,1},{2,26},{10... | collective-permute-start | bytes 49160 | tf_op jit(solution)/shard_map/ppermute | solution.py:398
  41.2 0.4 collective-permute-start.24
  41.6 1.9 %collective-permute-start.23 = (bf16[64,128]{1,0:T(8,128)(2,1)S(1)}, bf16[64,128]{1,0:T(8,128)(2,1)S(1)}, u32[]{:S(2)}, u32[]{:S(2)}) collective-permute-start(bf16[64,128]{1,0:T(8,128)(2,1)S(1)} %get-tuple-element.77), channel_id=1, source_target_pairs={{0,8},{8,0},{16,24},{24,16},{1,9},{9,1},{17,25},{25,17},{2,10},{10... | collective-permute-start | bytes 49160 | tf_op jit(solution)/shard_map/ppermute | solution.py:398
  43.5 1.8 %shard_map.103 = (f32[27,32,64]{2,1,0:T(8,128)S(1)}, bf16[64,2,256]{2,1,0:T(2,128)(2,1)}) custom-call(bf16[4,256,128]{2,1,0:T(8,128)(2,1)S(1)} %pad_maximum_fusion.even_ref, bf16[4,256,128]{2,1,0:T(8,128)(2,1)S(1)} %collective-permute-done.18.odd_ref, bf16[256,128]{1,0:T(8,128)(2,1)S(1)} %get-tuple-element.50.own_ref, ...), custom_call_target="tpu_custom_call" | custom-call | flops 2000000000 | tf_op jit(solution)/shard_map/pallas_call | solution.py:519
  45.4 0.5 %collective-permute-done.24.refs_1_ = bf16[64,128]{1,0:T(8,128)(2,1)S(1)} collective-permute-done((bf16[64,128]{1,0:T(8,128)(2,1)S(1)}, bf16[64,128]{1,0:T(8,128)(2,1)S(1)}, u32[]{:S(2)}, u32[]{:S(2)}) %collective-permute-start.24) | collective-permute-done | bytes 16416 | tf_op jit(solution)/shard_map/ppermute | solution.py:398
  45.8 0.9 %shard_map.105 = f32[31,32,64]{2,1,0:T(8,128)} custom-call(bf16[4,64,128]{2,1,0:T(8,128)(2,1)S(1)} %shard_map.104.own_piece, f32[27,32,64]{2,1,0:T(8,128)S(1)} %get-tuple-element.69.taps_ref, bf16[64,128]{1,0:T(8,128)(2,1)S(1)} %collective-permute-done.23.refs_0_, bf16[64,128]{1,0:T(8,128)(2,1)S(1)} %collective-permute-done.24.refs_1_, ...), custom_call_target="tpu_custom_call" | custom-call | flops 2000000000 | tf_op jit(solution)/shard_map/pallas_call | solution.py:529
  (30 shorter events, 0.2 us)
Async XLA Ops:
  0.6 8.9 %collective-permute-start.2 = (bf16[64,2,256]{2,1,0:T(2,128)(2,1)}, bf16[64,2,256]{2,1,0:T(2,128)(2,1)S(1)}, u32[]{:S(2)}, u32[]{:S(2)}) collective-permute-start(bf16[64,2,256]{2,1,0:T(2,128)(2,1)} %bitcast.36), channel_id=1, source_target_pairs={{0,24},{8,16},{16,8},{24,0},{1,25},{9,17},{17,9},{25,1},{2,26},{10... | collective-permute-start | bytes 196616 | tf_op jit(solution)/shard_map/ppermute | solution.py:398
  5.7 6.1 %collective-permute-start.1 = (bf16[64,2,256]{2,1,0:T(2,128)(2,1)}, bf16[64,2,256]{2,1,0:T(2,128)(2,1)S(1)}, u32[]{:S(2)}, u32[]{:S(2)}) collective-permute-start(bf16[64,2,256]{2,1,0:T(2,128)(2,1)} %bitcast.37), channel_id=1, source_target_pairs={{0,16},{8,24},{16,0},{24,8},{1,17},{9,25},{17,1},{25,9},{2,18},{10... | collective-permute-start | bytes 196616 | tf_op jit(solution)/shard_map/ppermute | solution.py:398
  5.7 6.1 %collective-permute-start = (bf16[64,2,256]{2,1,0:T(2,128)(2,1)}, bf16[64,2,256]{2,1,0:T(2,128)(2,1)S(1)}, u32[]{:S(2)}, u32[]{:S(2)}) collective-permute-start(bf16[64,2,256]{2,1,0:T(2,128)(2,1)} %bitcast.38), channel_id=1, source_target_pairs={{0,8},{8,0},{16,24},{24,16},{1,9},{9,1},{17,25},{25,17},{2,10},{10... | collective-permute-start | bytes 196616 | tf_op jit(solution)/shard_map/ppermute | solution.py:398
  6.4 7.2 %collective-permute-start.5 = (bf16[64,2,256]{2,1,0:T(2,128)(2,1)}, bf16[64,2,256]{2,1,0:T(2,128)(2,1)S(1)}, u32[]{:S(2)}, u32[]{:S(2)}) collective-permute-start(bf16[64,2,256]{2,1,0:T(2,128)(2,1)} %bitcast.40), channel_id=1, source_target_pairs={{0,6},{1,7},{2,4},{3,5},{4,2},{5,3},{6,0},{7,1},{8,14},{9,15},{10,... | collective-permute-start | bytes 196616 | tf_op jit(solution)/shard_map/ppermute | solution.py:407
  9.0 4.6 %collective-permute-start.4 = (bf16[64,2,256]{2,1,0:T(2,128)(2,1)}, bf16[64,2,256]{2,1,0:T(2,128)(2,1)S(1)}, u32[]{:S(2)}, u32[]{:S(2)}) collective-permute-start(bf16[64,2,256]{2,1,0:T(2,128)(2,1)} %bitcast.41), channel_id=1, source_target_pairs={{0,4},{1,5},{2,6},{3,7},{4,0},{5,1},{6,2},{7,3},{8,12},{9,13},{10,... | collective-permute-start | bytes 196616 | tf_op jit(solution)/shard_map/ppermute | solution.py:407
  9.5 4.5 %collective-permute-start.3 = (bf16[64,2,256]{2,1,0:T(2,128)(2,1)}, bf16[64,2,256]{2,1,0:T(2,128)(2,1)S(1)}, u32[]{:S(2)}, u32[]{:S(2)}) collective-permute-start(bf16[64,2,256]{2,1,0:T(2,128)(2,1)} %bitcast.42), channel_id=1, source_target_pairs={{0,2},{1,3},{2,0},{3,1},{4,6},{5,7},{6,4},{7,5},{8,10},{9,11},{10,... | collective-permute-start | bytes 196616 | tf_op jit(solution)/shard_map/ppermute | solution.py:407
  14.1 1.6 %collective-permute-start.6 = (bf16[4,2,64,256]{3,2,1,0:T(8,128)(2,1)S(1)}, bf16[4,2,64,256]{3,2,1,0:T(8,128)(2,1)S(1)}, u32[]{:S(2)}, u32[]{:S(2)}) collective-permute-start(bf16[4,2,64,256]{3,2,1,0:T(8,128)(2,1)S(1)} %shard_map.98.even_ref), channel_id=1, source_target_pairs={{0,1},{1,0},{2,3},{3,2},{4,5},{5,4},{6,7},{7,6},{8,9},{9,8},{10,11... | collective-permute-start | bytes 786440 | tf_op jit(solution)/shard_map/ppermute | solution.py:407
  15.7 8.6 %copy-start = (bf16[256,27,256]{2,0,1:T(8,128)(2,1)S(1)}, bf16[256,27,256]{2,0,1:T(8,128)(2,1)}, u32[]{:S(2)}) copy-start(bf16[256,27,256]{2,0,1:T(8,128)(2,1)} %param.14) | copy-start | bytes 10616836
  16.0 8.2 %collective-permute-start.11 = (bf16[2,16,256]{2,1,0:T(8,128)(2,1)S(1)}, bf16[2,16,256]{2,1,0:T(8,128)(2,1)S(1)}, u32[]{:S(2)}, u32[]{:S(2)}) collective-permute-start(bf16[2,16,256]{2,1,0:T(8,128)(2,1)S(1)} %get-tuple-element.52), channel_id=1, source_target_pairs={{0,24},{8,16},{16,8},{24,0},{1,25},{9,17},{17,9},{25,1},{2,26},{10... | collective-permute-start | bytes 49160 | tf_op jit(solution)/shard_map/ppermute | solution.py:398
  19.7 4.6 %collective-permute-start.10 = (bf16[2,16,256]{2,1,0:T(8,128)(2,1)S(1)}, bf16[2,16,256]{2,1,0:T(8,128)(2,1)S(1)}, u32[]{:S(2)}, u32[]{:S(2)}) collective-permute-start(bf16[2,16,256]{2,1,0:T(8,128)(2,1)S(1)} %get-tuple-element.52), channel_id=1, source_target_pairs={{0,8},{8,0},{16,24},{24,16},{1,9},{9,1},{17,25},{25,17},{2,10},{10... | collective-permute-start | bytes 49160 | tf_op jit(solution)/shard_map/ppermute | solution.py:398
  19.7 8.8 %collective-permute-start.9 = (bf16[64,128]{1,0:T(8,128)(2,1)S(1)}, bf16[64,128]{1,0:T(8,128)(2,1)S(1)}, u32[]{:S(2)}, u32[]{:S(2)}) collective-permute-start(bf16[64,128]{1,0:T(8,128)(2,1)S(1)} %get-tuple-element.81), channel_id=1, source_target_pairs={{0,24},{8,16},{16,8},{24,0},{1,25},{9,17},{17,9},{25,1},{2,26},{10... | collective-permute-start | bytes 49160 | tf_op jit(solution)/shard_map/ppermute | solution.py:398
  20.8 6.9 %collective-permute-start.7 = (bf16[320,128]{1,0:T(8,128)(2,1)S(1)}, bf16[320,128]{1,0:T(8,128)(2,1)S(1)}, u32[]{:S(2)}, u32[]{:S(2)}) collective-permute-start(bf16[320,128]{1,0:T(8,128)(2,1)S(1)} %get-tuple-element.84), channel_id=1, source_target_pairs={{0,8},{8,0},{16,24},{24,16},{1,9},{9,1},{17,25},{25,17},{2,10},{10... | collective-permute-start | bytes 245768 | tf_op jit(solution)/shard_map/ppermute | solution.py:398
  21.8 6.6 %collective-permute-start.8 = (bf16[320,128]{1,0:T(8,128)(2,1)S(1)}, bf16[320,128]{1,0:T(8,128)(2,1)S(1)}, u32[]{:S(2)}, u32[]{:S(2)}) collective-permute-start(bf16[320,128]{1,0:T(8,128)(2,1)S(1)} %get-tuple-element.85), channel_id=1, source_target_pairs={{0,16},{8,24},{16,0},{24,8},{1,17},{9,25},{17,1},{25,9},{2,18},{10... | collective-permute-start | bytes 245768 | tf_op jit(solution)/shard_map/ppermute | solution.py:398
  27.1 1.4 %collective-permute-start.12 = (bf16[256,128]{1,0:T(8,128)(2,1)S(1)}, bf16[256,128]{1,0:T(8,128)(2,1)S(1)}, u32[]{:S(2)}, u32[]{:S(2)}) collective-permute-start(bf16[256,128]{1,0:T(8,128)(2,1)S(1)} %get-tuple-element.59), channel_id=1, source_target_pairs={{0,1},{1,0},{2,3},{3,2},{4,5},{5,4},{6,7},{7,6},{8,9},{9,8},{10,11... | collective-permute-start | bytes 196616 | tf_op jit(solution)/shard_map/ppermute | solution.py:407
  27.2 1.4 %collective-permute-start.13 = (bf16[256,128]{1,0:T(8,128)(2,1)S(1)}, bf16[256,128]{1,0:T(8,128)(2,1)S(1)}, u32[]{:S(2)}, u32[]{:S(2)}) collective-permute-start(bf16[256,128]{1,0:T(8,128)(2,1)S(1)} %get-tuple-element.60), channel_id=1, source_target_pairs={{0,1},{1,0},{2,3},{3,2},{4,5},{5,4},{6,7},{7,6},{8,9},{9,8},{10,11... | collective-permute-start | bytes 196616 | tf_op jit(solution)/shard_map/ppermute | solution.py:407
  27.7 1.3 %collective-permute-start.14 = (bf16[256,128]{1,0:T(8,128)(2,1)S(1)}, bf16[256,128]{1,0:T(8,128)(2,1)S(1)}, u32[]{:S(2)}, u32[]{:S(2)}) collective-permute-start(bf16[256,128]{1,0:T(8,128)(2,1)S(1)} %get-tuple-element.61), channel_id=1, source_target_pairs={{0,1},{1,0},{2,3},{3,2},{4,5},{5,4},{6,7},{7,6},{8,9},{9,8},{10,11... | collective-permute-start | bytes 196616 | tf_op jit(solution)/shard_map/ppermute | solution.py:407
  29.0 9.9 %collective-permute-start.22 = (bf16[256,128]{1,0:T(8,128)(2,1)S(1)}, bf16[256,128]{1,0:T(8,128)(2,1)S(1)}, u32[]{:S(2)}, u32[]{:S(2)}) collective-permute-start(bf16[256,128]{1,0:T(8,128)(2,1)S(1)} %get-tuple-element.68), channel_id=1, source_target_pairs={{0,1},{1,0},{2,3},{3,2},{4,5},{5,4},{6,7},{7,6},{8,9},{9,8},{10,11... | collective-permute-start | bytes 196616 | tf_op jit(solution)/shard_map/ppermute | solution.py:407
  29.2 6.3 %collective-permute-start.15 = (bf16[512,128]{1,0:T(8,128)(2,1)S(1)}, bf16[512,128]{1,0:T(8,128)(2,1)S(1)}, u32[]{:S(2)}, u32[]{:S(2)}) collective-permute-start(bf16[512,128]{1,0:T(8,128)(2,1)S(1)} %get-tuple-element.62), channel_id=1, source_target_pairs={{0,2},{1,3},{2,0},{3,1},{4,6},{5,7},{6,4},{7,5},{8,10},{9,11},{10,... | collective-permute-start | bytes 393224 | tf_op jit(solution)/shard_map/ppermute | solution.py:407
  30.4 7.3 %collective-permute-start.16 = (bf16[512,128]{1,0:T(8,128)(2,1)S(1)}, bf16[512,128]{1,0:T(8,128)(2,1)S(1)}, u32[]{:S(2)}, u32[]{:S(2)}) collective-permute-start(bf16[512,128]{1,0:T(8,128)(2,1)S(1)} %get-tuple-element.63), channel_id=1, source_target_pairs={{0,4},{1,5},{2,6},{3,7},{4,0},{5,1},{6,2},{7,3},{8,12},{9,13},{10,... | collective-permute-start | bytes 393224 | tf_op jit(solution)/shard_map/ppermute | solution.py:407
  31.9 6.9 %collective-permute-start.17 = (bf16[512,128]{1,0:T(8,128)(2,1)S(1)}, bf16[512,128]{1,0:T(8,128)(2,1)S(1)}, u32[]{:S(2)}, u32[]{:S(2)}) collective-permute-start(bf16[512,128]{1,0:T(8,128)(2,1)S(1)} %get-tuple-element.64), channel_id=1, source_target_pairs={{0,6},{1,7},{2,4},{3,5},{4,2},{5,3},{6,0},{7,1},{8,14},{9,15},{10,... | collective-permute-start | bytes 393224 | tf_op jit(solution)/shard_map/ppermute | solution.py:407
  32.7 8.4 %collective-permute-start.21 = (bf16[256,128]{1,0:T(8,128)(2,1)S(1)}, bf16[256,128]{1,0:T(8,128)(2,1)S(1)}, u32[]{:S(2)}, u32[]{:S(2)}) collective-permute-start(bf16[256,128]{1,0:T(8,128)(2,1)S(1)} %get-tuple-element.72), channel_id=1, source_target_pairs={{0,24},{8,16},{16,8},{24,0},{1,25},{9,17},{17,9},{25,1},{2,26},{10... | collective-permute-start | bytes 196616 | tf_op jit(solution)/shard_map/ppermute | solution.py:398
  35.6 6.1 %collective-permute-start.20 = (bf16[256,128]{1,0:T(8,128)(2,1)S(1)}, bf16[256,128]{1,0:T(8,128)(2,1)S(1)}, u32[]{:S(2)}, u32[]{:S(2)}) collective-permute-start(bf16[256,128]{1,0:T(8,128)(2,1)S(1)} %get-tuple-element.73), channel_id=1, source_target_pairs={{0,16},{8,24},{16,0},{24,8},{1,17},{9,25},{17,1},{25,9},{2,18},{10... | collective-permute-start | bytes 196616 | tf_op jit(solution)/shard_map/ppermute | solution.py:398
  37.7 5.8 %collective-permute-start.19 = (bf16[512,128]{1,0:T(8,128)(2,1)S(1)}, bf16[512,128]{1,0:T(8,128)(2,1)S(1)}, u32[]{:S(2)}, u32[]{:S(2)}) collective-permute-start(bf16[512,128]{1,0:T(8,128)(2,1)S(1)} %pad_maximum_fusion.1), channel_id=1, source_target_pairs={{0,8},{8,0},{16,24},{24,16},{1,9},{9,1},{17,25},{25,17},{2,10},{10... | collective-permute-start | bytes 393224 | tf_op jit(solution)/shard_map/ppermute | solution.py:398
  38.8 4.7 %collective-permute-start.18 = (bf16[4,256,128]{2,1,0:T(8,128)(2,1)S(1)}, bf16[4,256,128]{2,1,0:T(8,128)(2,1)S(1)}, u32[]{:S(2)}, u32[]{:S(2)}) collective-permute-start(bf16[4,256,128]{2,1,0:T(8,128)(2,1)S(1)} %pad_maximum_fusion.even_ref), channel_id=1, source_target_pairs={{0,1},{1,0},{2,3},{3,2},{4,5},{5,4},{6,7},{7,6},{8,9},{9,8},{10,11... | collective-permute-start | bytes 786440 | tf_op jit(solution)/shard_map/ppermute | solution.py:407
  39.0 6.3 %collective-permute-start.25 = (bf16[64,128]{1,0:T(8,128)(2,1)S(1)}, bf16[64,128]{1,0:T(8,128)(2,1)S(1)}, u32[]{:S(2)}, u32[]{:S(2)}) collective-permute-start(bf16[64,128]{1,0:T(8,128)(2,1)S(1)} %get-tuple-element.75), channel_id=1, source_target_pairs={{0,24},{8,16},{16,8},{24,0},{1,25},{9,17},{17,9},{25,1},{2,26},{10... | collective-permute-start | bytes 49160 | tf_op jit(solution)/shard_map/ppermute | solution.py:398
  41.2 4.6 %collective-permute-start.24 = (bf16[64,128]{1,0:T(8,128)(2,1)S(1)}, bf16[64,128]{1,0:T(8,128)(2,1)S(1)}, u32[]{:S(2)}, u32[]{:S(2)}) collective-permute-start(bf16[64,128]{1,0:T(8,128)(2,1)S(1)} %get-tuple-element.76), channel_id=1, source_target_pairs={{0,16},{8,24},{16,0},{24,8},{1,17},{9,25},{17,1},{25,9},{2,18},{10... | collective-permute-start | bytes 49160 | tf_op jit(solution)/shard_map/ppermute | solution.py:398
  41.6 4.2 %collective-permute-start.23 = (bf16[64,128]{1,0:T(8,128)(2,1)S(1)}, bf16[64,128]{1,0:T(8,128)(2,1)S(1)}, u32[]{:S(2)}, u32[]{:S(2)}) collective-permute-start(bf16[64,128]{1,0:T(8,128)(2,1)S(1)} %get-tuple-element.77), channel_id=1, source_target_pairs={{0,8},{8,0},{16,24},{24,16},{1,9},{9,1},{17,25},{25,17},{2,10},{10... | collective-permute-start | bytes 49160 | tf_op jit(solution)/shard_map/ppermute | solution.py:398
